TPU v7x, 32 devices: a whole 2x2x4 slice. The times are simulated.
32 devices in a mesh: groups: 2 (over x), nodes: 16 (over z, y, core).
Axes of the slice: x: 2, y: 2, z: 4, core: 2. Of those that a mesh axis runs over, the one named last changes fastest.
Arguments:
- grid_in: bfloat16 [131072, 227], P(('groups', 'nodes')), parts along dimension 0, may hold values from -6 to 6
- w_embed: bfloat16 [227, 512], replicated, may hold values from -0.375 to 0.375
- enc_coef: bfloat16 [6144, 32, 128], P('nodes'), may hold values from -0.125 to 0.125
- enc_owner: int32 [6144], P('nodes'), may hold values from 0 to 15, as said below
- slot_block: int32 [256], P('nodes'), may hold values from 0 to 3
- mesh_in: bfloat16 [4096, 512], P(('groups', 'nodes')), parts along dimension 0, may hold values from -6 to 6
- w_enc: bfloat16 [512, 512], replicated, may hold values from -0.25 to 0.25
- proc_adj: int32 [64, 6], P('nodes'), may hold values from -1 to 63, as said below
- proc_coef: bfloat16 [64, 6, 32, 32], P('nodes'), may hold values from -0.4375 to 0.4375
- proc_gain: float32 [512], replicated, may hold values from 0.1 to 1.9
- w_proc: bfloat16 [512, 512], replicated, may hold values from -0.25 to 0.25
- dec_coef: bfloat16 [6144, 128, 32], P('nodes'), may hold values from -0.3125 to 0.3125
- w_out: bfloat16 [512, 227], replicated, may hold values from -0.25 to 0.25
Outputs:
- grid_pred: bfloat16 [131072, 227], P(('groups', 'nodes')), parts along dimension 0
- mesh_out: bfloat16 [4096, 512], P(('groups', 'nodes')), parts along dimension 0
There are 2 independent parts, one for each index of `groups`. A program takes and returns all parts, laid end to end along the dimension named above; an argument that names none is the same for every part. Nothing has to cross between parts.
Inputs may be any that keep to these rules, and one draw needn't show every extreme that they name: `proc_adj`: each row lists between 2 and 6 neighbour blocks first, then -1 padding; a listed block belongs to the row's own partition or to one of the two partitions beside it, the first and last partition being beside each other. `enc_owner`: A tile of partition p feeds partition (p + d) mod 16 for some d of -2 to 2, or d = 8.
All inputs are finite; a program needn't handle non-finite values.
Results may differ from a plain program's by a relative error of at most 0.0075.
Values may be sent and summed in bfloat16 or wider, within the bound.
No kernel may reach another device: no remote copies, remote signals or barrier semaphores. Data moves between devices by JAX's collectives and lax.ppermute only.
A program may use at most 128 MiB of HBM per device.

v0:
```python
import jax
import jax.numpy as jnp
from jax import lax
from jax.sharding import PartitionSpec as P


def padded(cells, sides, width):
    for axis, dim in sides:
        count = lax.axis_size(axis)
        head = lax.slice_in_dim(cells, 0, width, axis=dim)
        tail = lax.slice_in_dim(cells, cells.shape[dim] - width, cells.shape[dim], axis=dim)
        cells = jnp.concatenate(
            [
                lax.ppermute(tail, axis, [(i, (i + 1) % count) for i in range(count)]),
                cells,
                lax.ppermute(head, axis, [((i + 1) % count, i) for i in range(count)]),
            ],
            axis=dim,
        )
    return cells


def one_hot_rows(indices, count, dtype):
    return (indices[:, None] == jnp.arange(count, dtype=jnp.int32)[None, :]).astype(dtype)


def local(
    grid_in,
    w_embed,
    enc_coef,
    enc_owner,
    slot_block,
    mesh_in,
    w_enc,
    proc_adj,
    proc_coef,
    proc_gain,
    w_proc,
    dec_coef,
    w_out,
):
    parts = lax.axis_size("nodes")
    myself = lax.axis_index("nodes")
    grid_count, channels = grid_in.shape
    latent = w_embed.shape[1]
    tile_count, block_mesh, block_grid = enc_coef.shape
    grid_blocks = grid_count // block_grid
    per_block = tile_count // grid_blocks
    group_count = grid_blocks // 4
    mesh_count = mesh_in.shape[0]
    mesh_blocks = mesh_count // block_mesh
    adj_width = proc_adj.shape[1]
    latent_grid = jax.nn.silu(jnp.dot(grid_in, w_embed, preferred_element_type=jnp.float32)).astype(
        jnp.bfloat16
    )
    latent_groups = latent_grid.reshape(group_count, 4, block_grid, latent)
    coef_groups = enc_coef.reshape(group_count, 4, per_block, block_mesh, block_grid)
    index_groups = enc_owner.reshape(group_count, 4 * per_block)

    def encode(current, inputs):
        coef_group, latent_group, owners = inputs
        products = jnp.einsum(
            "gkij,gjl->gkil", coef_group, latent_group, preferred_element_type=jnp.float32
        )
        selector = one_hot_rows(owners, parts, jnp.float32)
        added = jnp.einsum(
            "ts,til->sil",
            selector,
            products.reshape(-1, block_mesh, latent),
            precision=lax.Precision.HIGHEST,
            preferred_element_type=jnp.float32,
        )
        return (current + added, None)

    slot_sums, _ = lax.scan(
        encode,
        jnp.zeros((parts, block_mesh, latent), jnp.float32),
        (coef_groups, latent_groups, index_groups),
    )
    slot_sums = slot_sums.astype(jnp.bfloat16)
    received, block_ids = (
        lax.all_to_all(slot_sums, "nodes", split_axis=0, concat_axis=0, tiled=True),
        lax.all_to_all(slot_block, "nodes", split_axis=0, concat_axis=0, tiled=True),
    )
    selector = (block_ids[None, :] == jnp.arange(mesh_blocks, dtype=jnp.int32)[:, None]).astype(
        jnp.bfloat16
    )
    aggregate = jnp.einsum("bq,qil->bil", selector, received, preferred_element_type=jnp.float32)
    aggregate = aggregate.reshape(mesh_count, latent).astype(jnp.bfloat16)
    mesh_mid = (
        mesh_in.astype(jnp.float32)
        + jax.nn.silu(jnp.dot(aggregate, w_enc, preferred_element_type=jnp.float32))
    ).astype(jnp.bfloat16)
    extended = padded(mesh_mid, (("nodes", 0),), mesh_count)
    ext_blocks = extended.reshape(3 * mesh_blocks, block_mesh, latent)
    relative = (proc_adj // mesh_blocks - myself + 1) % parts
    position = jnp.clip(
        relative * mesh_blocks + proc_adj % mesh_blocks, 0, 3 * mesh_blocks - 1
    ).reshape(-1)
    live = (proc_adj >= 0).reshape(-1)
    pick_table = (one_hot_rows(position, 3 * mesh_blocks, jnp.bool_) & live[:, None]).astype(
        jnp.bfloat16
    )
    picked = jnp.einsum(
        "pe,eil->pil", pick_table, ext_blocks, preferred_element_type=jnp.float32
    ).astype(jnp.bfloat16)
    picked = picked.reshape(mesh_blocks, adj_width, block_mesh, latent)
    message = jnp.einsum(
        "bakj,bajl->bkl", proc_coef, picked, preferred_element_type=jnp.float32
    ).reshape(mesh_count, latent)
    scale_inv = lax.rsqrt(jnp.mean(message * message, axis=-1, keepdims=True) + 1e-05)
    normed = (message * scale_inv * proc_gain).astype(jnp.bfloat16)
    mesh_out = (
        mesh_mid.astype(jnp.float32)
        + jax.nn.silu(jnp.dot(normed, w_proc, preferred_element_type=jnp.float32))
    ).astype(jnp.bfloat16)
    out_blocks = mesh_out.reshape(mesh_blocks, block_mesh, latent)
    requested = lax.all_to_all(slot_block, "nodes", split_axis=0, concat_axis=0, tiled=True)
    request_table = one_hot_rows(requested, mesh_blocks, jnp.bfloat16)
    outgoing = jnp.einsum(
        "qb,bil->qil", request_table, out_blocks, preferred_element_type=jnp.float32
    ).astype(jnp.bfloat16)
    returned = lax.all_to_all(outgoing, "nodes", split_axis=0, concat_axis=0, tiled=True)
    dec_groups = dec_coef.reshape(group_count, 4, per_block, block_grid, block_mesh)
    grid_groups = grid_in.reshape(group_count, 4 * block_grid, channels)

    def decode(inputs):
        coef_group, latent_group, owners, grid_rows = inputs
        owner_table = one_hot_rows(owners, parts, jnp.bfloat16)
        fetched = jnp.einsum(
            "ts,sil->til", owner_table, returned, preferred_element_type=jnp.float32
        ).astype(jnp.bfloat16)
        fetched = fetched.reshape(4, per_block, block_mesh, latent)
        decoded = jnp.einsum(
            "gkij,gkjl->gil", coef_group, fetched, preferred_element_type=jnp.float32
        )
        hidden_grid = (
            jax.nn.silu(latent_group.astype(jnp.float32) + decoded)
            .astype(jnp.bfloat16)
            .reshape(-1, latent)
        )
        return (
            grid_rows.astype(jnp.float32)
            + jnp.dot(hidden_grid, w_out, preferred_element_type=jnp.float32)
        ).astype(jnp.bfloat16)

    grid_pred = lax.map(decode, (dec_groups, latent_groups, index_groups, grid_groups)).reshape(
        grid_count, channels
    )
    return (grid_pred, mesh_out)


def solution(mesh):
    return jax.shard_map(
        local,
        mesh=mesh,
        in_specs=(
            P(("groups", "nodes"), None),
            P(),
            P("nodes", None, None),
            P("nodes"),
            P("nodes"),
            P(("groups", "nodes"), None),
            P(),
            P("nodes", None),
            P("nodes", None, None, None),
            P(),
            P(),
            P("nodes", None, None),
            P(),
        ),
        out_specs=(P(("groups", "nodes"), None), P(("groups", "nodes"), None)),
        check_vma=False,
    )
```

profile of v0, /device:TPU:0, one launch (start us, length us, event | category | flops | bytes accessed | tf_op | source)
XLA Modules:
  0.0 175.5 jit_solution(8171632057646989496)
XLA Ops:
  0.6 1.4 copy.44
  2.0 7.4 %all-to-all-start = ((s32[16,1,1]{2,1,0:T(1,128)}), s32[16,1,1]{2,1,0:T(1,128)S(1)}, u32[]{:S(2)}, u32[]{:S(2)}) async-start(s32[16,1,1]{2,1,0:T(1,128)} %copy.44), calls=%async_computation | async-start | bytes 16384 | tf_op jit(solution)/shard_map/all_to_all | solution.py:118
  10.2 6.0 %multiply_convert_fusion.1 = bf16[4096,512]{1,0:T(8,128)(2,1)} fusion(bf16[4096,227]{0,1:T(8,128)(2,1)} %param.17, bf16[227,512]{1,0:T(8,128)(2,1)} %param.18), kind=kOutput, calls=%fused_computation.30 | convolution fusion | flops 962592768 | bytes 6286336 | tf_op jit(solution)/shard_map/dot_general | solution.py:53
  16.2 66.2 %while.22 = (s32[]{:T(128)}, f32[16,32,512]{2,0,1:T(8,128)S(1)}, s32[8,48]{1,0:T(8,128)S(1)}, bf16[8,4,12,32,128]{4,3,2,1,0:T(8,128)(2,1)}, bf16[8,4,128,512]{3,2,1,0:T(8,128)(2,1)}, /*index=5*/s32[]{:T(128)}, s32[]{:T(128)}) while((s32[]{:T(128)}, f32[16,32,512]{2,0,1:T(8,128)S(1)}, s32[8,48]{1,0:T(8,128)S(1)}, ...), condition=%wide.region_1.2_spmd.clone, body=%wide.region_0.1_spmd.clone.sunk | while | flops 352846592 | bytes 9307803 | solution.py:75
  16.2 3.4 %fusion.89 = f32[4,12,32,512]{3,2,1,0:T(8,128)} fusion(bf16[8,4,128,512]{3,2,1,0:T(8,128)(2,1)} %get-tuple-element.241, s32[]{:T(128)} %get-tuple-element.230, bf16[8,4,12,32,128]{4,3,2,1,0:T(8,128)(2,1)} %get-tuple-element.240), kind=kOutput, calls=%fused_computation.19.clone.1 | convolution fusion | flops 201326592 | bytes 4064256 | tf_op jit(solution)/shard_map/while/body/eval_jaxpr/gkij,gjl->gkil/dot_general | solution.py:62
  19.6 4.8 %fusion.91 = f32[16,32,512]{2,0,1:T(8,128)S(1)} fusion(f32[48,32,512]{2,1,0:T(8,128)} %bitcast.134, f32[16,32,512]{2,0,1:T(8,128)S(1)} %get-tuple-element.231, pred[]{:T(512)S(6)} %compare.7, s32[48]{0:T(128)S(1)} %fusion.90), kind=kOutput, calls=%fused_computation.18.clone.1 | convolution fusion | flops 151520000 | bytes 5243073 | tf_op jit(solution)/shard_map/while/body/eval_jaxpr/ts,til->sil/dot_general | solution.py:66
  24.4 3.4 %fusion.89 = f32[4,12,32,512]{3,2,1,0:T(8,128)} fusion(bf16[8,4,128,512]{3,2,1,0:T(8,128)(2,1)} %get-tuple-element.241, s32[]{:T(128)} %get-tuple-element.230, bf16[8,4,12,32,128]{4,3,2,1,0:T(8,128)(2,1)} %get-tuple-element.240), kind=kOutput, calls=%fused_computation.19.clone.1 | convolution fusion | flops 201326592 | bytes 4064256 | tf_op jit(solution)/shard_map/while/body/eval_jaxpr/gkij,gjl->gkil/dot_general | solution.py:62
  27.8 4.8 %fusion.91 = f32[16,32,512]{2,0,1:T(8,128)S(1)} fusion(f32[48,32,512]{2,1,0:T(8,128)} %bitcast.134, f32[16,32,512]{2,0,1:T(8,128)S(1)} %get-tuple-element.231, pred[]{:T(512)S(6)} %compare.7, s32[48]{0:T(128)S(1)} %fusion.90), kind=kOutput, calls=%fused_computation.18.clone.1 | convolution fusion | flops 151520000 | bytes 5243073 | tf_op jit(solution)/shard_map/while/body/eval_jaxpr/ts,til->sil/dot_general | solution.py:66
  32.7 3.4 %fusion.89 = f32[4,12,32,512]{3,2,1,0:T(8,128)} fusion(bf16[8,4,128,512]{3,2,1,0:T(8,128)(2,1)} %get-tuple-element.241, s32[]{:T(128)} %get-tuple-element.230, bf16[8,4,12,32,128]{4,3,2,1,0:T(8,128)(2,1)} %get-tuple-element.240), kind=kOutput, calls=%fused_computation.19.clone.1 | convolution fusion | flops 201326592 | bytes 4064256 | tf_op jit(solution)/shard_map/while/body/eval_jaxpr/gkij,gjl->gkil/dot_general | solution.py:62
  36.1 4.8 %fusion.91 = f32[16,32,512]{2,0,1:T(8,128)S(1)} fusion(f32[48,32,512]{2,1,0:T(8,128)} %bitcast.134, f32[16,32,512]{2,0,1:T(8,128)S(1)} %get-tuple-element.231, pred[]{:T(512)S(6)} %compare.7, s32[48]{0:T(128)S(1)} %fusion.90), kind=kOutput, calls=%fused_computation.18.clone.1 | convolution fusion | flops 151520000 | bytes 5243073 | tf_op jit(solution)/shard_map/while/body/eval_jaxpr/ts,til->sil/dot_general | solution.py:66
  41.0 3.4 %fusion.89 = f32[4,12,32,512]{3,2,1,0:T(8,128)} fusion(bf16[8,4,128,512]{3,2,1,0:T(8,128)(2,1)} %get-tuple-element.241, s32[]{:T(128)} %get-tuple-element.230, bf16[8,4,12,32,128]{4,3,2,1,0:T(8,128)(2,1)} %get-tuple-element.240), kind=kOutput, calls=%fused_computation.19.clone.1 | convolution fusion | flops 201326592 | bytes 4064256 | tf_op jit(solution)/shard_map/while/body/eval_jaxpr/gkij,gjl->gkil/dot_general | solution.py:62
  44.4 4.8 %fusion.91 = f32[16,32,512]{2,0,1:T(8,128)S(1)} fusion(f32[48,32,512]{2,1,0:T(8,128)} %bitcast.134, f32[16,32,512]{2,0,1:T(8,128)S(1)} %get-tuple-element.231, pred[]{:T(512)S(6)} %compare.7, s32[48]{0:T(128)S(1)} %fusion.90), kind=kOutput, calls=%fused_computation.18.clone.1 | convolution fusion | flops 151520000 | bytes 5243073 | tf_op jit(solution)/shard_map/while/body/eval_jaxpr/ts,til->sil/dot_general | solution.py:66
  49.3 3.4 %fusion.89 = f32[4,12,32,512]{3,2,1,0:T(8,128)} fusion(bf16[8,4,128,512]{3,2,1,0:T(8,128)(2,1)} %get-tuple-element.241, s32[]{:T(128)} %get-tuple-element.230, bf16[8,4,12,32,128]{4,3,2,1,0:T(8,128)(2,1)} %get-tuple-element.240), kind=kOutput, calls=%fused_computation.19.clone.1 | convolution fusion | flops 201326592 | bytes 4064256 | tf_op jit(solution)/shard_map/while/body/eval_jaxpr/gkij,gjl->gkil/dot_general | solution.py:62
  52.7 4.8 %fusion.91 = f32[16,32,512]{2,0,1:T(8,128)S(1)} fusion(f32[48,32,512]{2,1,0:T(8,128)} %bitcast.134, f32[16,32,512]{2,0,1:T(8,128)S(1)} %get-tuple-element.231, pred[]{:T(512)S(6)} %compare.7, s32[48]{0:T(128)S(1)} %fusion.90), kind=kOutput, calls=%fused_computation.18.clone.1 | convolution fusion | flops 151520000 | bytes 5243073 | tf_op jit(solution)/shard_map/while/body/eval_jaxpr/ts,til->sil/dot_general | solution.py:66
  57.5 3.4 %fusion.89 = f32[4,12,32,512]{3,2,1,0:T(8,128)} fusion(bf16[8,4,128,512]{3,2,1,0:T(8,128)(2,1)} %get-tuple-element.241, s32[]{:T(128)} %get-tuple-element.230, bf16[8,4,12,32,128]{4,3,2,1,0:T(8,128)(2,1)} %get-tuple-element.240), kind=kOutput, calls=%fused_computation.19.clone.1 | convolution fusion | flops 201326592 | bytes 4064256 | tf_op jit(solution)/shard_map/while/body/eval_jaxpr/gkij,gjl->gkil/dot_general | solution.py:62
  61.0 4.8 %fusion.91 = f32[16,32,512]{2,0,1:T(8,128)S(1)} fusion(f32[48,32,512]{2,1,0:T(8,128)} %bitcast.134, f32[16,32,512]{2,0,1:T(8,128)S(1)} %get-tuple-element.231, pred[]{:T(512)S(6)} %compare.7, s32[48]{0:T(128)S(1)} %fusion.90), kind=kOutput, calls=%fused_computation.18.clone.1 | convolution fusion | flops 151520000 | bytes 5243073 | tf_op jit(solution)/shard_map/while/body/eval_jaxpr/ts,til->sil/dot_general | solution.py:66
  65.8 3.4 %fusion.89 = f32[4,12,32,512]{3,2,1,0:T(8,128)} fusion(bf16[8,4,128,512]{3,2,1,0:T(8,128)(2,1)} %get-tuple-element.241, s32[]{:T(128)} %get-tuple-element.230, bf16[8,4,12,32,128]{4,3,2,1,0:T(8,128)(2,1)} %get-tuple-element.240), kind=kOutput, calls=%fused_computation.19.clone.1 | convolution fusion | flops 201326592 | bytes 4064256 | tf_op jit(solution)/shard_map/while/body/eval_jaxpr/gkij,gjl->gkil/dot_general | solution.py:62
  69.2 4.8 %fusion.91 = f32[16,32,512]{2,0,1:T(8,128)S(1)} fusion(f32[48,32,512]{2,1,0:T(8,128)} %bitcast.134, f32[16,32,512]{2,0,1:T(8,128)S(1)} %get-tuple-element.231, pred[]{:T(512)S(6)} %compare.7, s32[48]{0:T(128)S(1)} %fusion.90), kind=kOutput, calls=%fused_computation.18.clone.1 | convolution fusion | flops 151520000 | bytes 5243073 | tf_op jit(solution)/shard_map/while/body/eval_jaxpr/ts,til->sil/dot_general | solution.py:66
  74.1 3.4 %fusion.89 = f32[4,12,32,512]{3,2,1,0:T(8,128)} fusion(bf16[8,4,128,512]{3,2,1,0:T(8,128)(2,1)} %get-tuple-element.241, s32[]{:T(128)} %get-tuple-element.230, bf16[8,4,12,32,128]{4,3,2,1,0:T(8,128)(2,1)} %get-tuple-element.240), kind=kOutput, calls=%fused_computation.19.clone.1 | convolution fusion | flops 201326592 | bytes 4064256 | tf_op jit(solution)/shard_map/while/body/eval_jaxpr/gkij,gjl->gkil/dot_general | solution.py:62
  77.5 4.8 %fusion.91 = f32[16,32,512]{2,0,1:T(8,128)S(1)} fusion(f32[48,32,512]{2,1,0:T(8,128)} %bitcast.134, f32[16,32,512]{2,0,1:T(8,128)S(1)} %get-tuple-element.231, pred[]{:T(512)S(6)} %compare.7, s32[48]{0:T(128)S(1)} %fusion.90), kind=kOutput, calls=%fused_computation.18.clone.1 | convolution fusion | flops 151520000 | bytes 5243073 | tf_op jit(solution)/shard_map/while/body/eval_jaxpr/ts,til->sil/dot_general | solution.py:66
  82.4 1.4 copy.72
  83.7 6.0 %all-to-all-start.1 = ((bf16[16,32,512]{2,1,0:T(8,128)(2,1)}), bf16[16,32,512]{2,1,0:T(8,128)(2,1)S(1)}, u32[]{:S(2)}, u32[]{:S(2)}) async-start(bf16[16,32,512]{2,1,0:T(8,128)(2,1)} %copy.72), calls=%async_computation.1 | async-start | bytes 1048576 | tf_op jit(solution)/shard_map/all_to_all | solution.py:82
  90.3 14.0 %all-to-all-done.1 = bf16[16,32,512]{2,1,0:T(8,128)(2,1)S(1)} async-done(((bf16[16,32,512]{2,1,0:T(8,128)(2,1)}), bf16[16,32,512]{2,1,0:T(8,128)(2,1)S(1)}, u32[]{:S(2)}, u32[]{:S(2)}) %all-to-all-start.1) | async-done | bytes 524320 | tf_op jit(solution)/shard_map/all_to_all | solution.py:82
  105.0 4.4 %collective-permute-start.1 = (bf16[128,512]{1,0:T(8,128)(2,1)S(1)}, bf16[128,512]{1,0:T(8,128)(2,1)S(1)}, u32[]{:S(2)}, u32[]{:S(2)}) collective-permute-start(bf16[128,512]{1,0:T(8,128)(2,1)S(1)} %add_convert_fusion.1), channel_id=1, source_target_pairs={{1,0},{2,1},{3,2},{4,3},{5,4},{6,5},{7,6},{8,7},{9,8},{10,9},{11,1... | collective-permute-start | bytes 393224 | tf_op jit(solution)/shard_map/ppermute | solution.py:16
  109.6 2.6 %collective-permute-done = bf16[128,512]{1,0:T(8,128)(2,1)S(1)} collective-permute-done((bf16[128,512]{1,0:T(8,128)(2,1)S(1)}, bf16[128,512]{1,0:T(8,128)(2,1)S(1)}, u32[]{:S(2)}, u32[]{:S(2)}) %collective-permute-start) | collective-permute-done | bytes 131104 | tf_op jit(solution)/shard_map/ppermute | solution.py:14
  114.3 1.1 copy.51
  115.4 5.9 %all-to-all-start.2 = ((bf16[16,32,512]{2,1,0:T(8,128)(2,1)}), bf16[16,32,512]{2,1,0:T(8,128)(2,1)}, u32[]{:S(2)}, u32[]{:S(2)}) async-start(bf16[16,32,512]{2,1,0:T(8,128)(2,1)} %copy.51), calls=%async_computation.2 | async-start | bytes 1048576 | tf_op jit(solution)/shard_map/all_to_all | solution.py:123
  122.9 12.9 %all-to-all-done.2 = bf16[16,32,512]{2,1,0:T(8,128)(2,1)} async-done(((bf16[16,32,512]{2,1,0:T(8,128)(2,1)}), bf16[16,32,512]{2,1,0:T(8,128)(2,1)}, u32[]{:S(2)}, u32[]{:S(2)}) %all-to-all-start.2) | async-done | bytes 524320 | tf_op jit(solution)/shard_map/all_to_all | solution.py:123
  135.8 1.3 copy.53
  137.2 34.0 %while.21 = (s32[]{:T(128)}, bf16[8,512,227]{1,2,0:T(8,128)(2,1)}, bf16[8,512,227]{1,2,0:T(8,128)(2,1)S(1)}, bf16[8,4,128,512]{3,2,1,0:T(8,128)(2,1)}, bf16[8,4,...) while((s32[]{:T(128)}, bf16[8,512,227]{1,2,0:T(8,128)(2,1)}, ...), condition=%wide.region_4.5_spmd, body=%wide.region_3.4_spmd.sunk | while | flops 348476672 | bytes 9486497 | solution.py:147
  138.7 1.7 multiply_convert_fusion.3
  140.4 1.0 fusion.84
  142.9 1.7 multiply_convert_fusion.3
  144.7 1.0 fusion.84
  147.2 1.7 multiply_convert_fusion.3
  148.9 1.0 fusion.84
  151.4 1.7 multiply_convert_fusion.3
  153.2 1.0 fusion.84
  155.7 1.7 multiply_convert_fusion.3
  157.4 1.0 fusion.84
  160.0 1.7 multiply_convert_fusion.3
  161.7 1.0 fusion.84
  164.2 1.7 multiply_convert_fusion.3
  165.9 1.0 fusion.84
  168.5 1.7 multiply_convert_fusion.3
  170.2 1.0 fusion.84
  171.2 2.1 %copy.73 = bf16[8,512,227]{1,0,2:T(8,128)(2,1)S(1)} copy(bf16[8,512,227]{1,2,0:T(8,128)(2,1)} %get-tuple-element.72) | data formatting | bytes 3719168 | tf_op jit(solution)/shard_map/while | solution.py:147
  173.5 2.1 %copy.59 = bf16[29,8,8,512]{3,1,2,0:T(8,128)(2,1)} copy(bf16[29,8,8,512]{3,2,1,0:T(8,128)(2,1)S(1)} %bitcast.137) | data formatting | bytes 3801088
  (77 shorter events, 17.8 us)
Async XLA Ops:
  0.6 104.0 %copy-start = (bf16[512,512]{1,0:T(8,128)(2,1)S(1)}, bf16[512,512]{1,0:T(8,128)(2,1)}, u32[]{:S(2)}) copy-start(bf16[512,512]{1,0:T(8,128)(2,1)} %param.23) | copy-start | bytes 1572868
  2.0 81.7 %all-to-all-start = ((s32[16,1,1]{2,1,0:T(1,128)}), s32[16,1,1]{2,1,0:T(1,128)S(1)}, u32[]{:S(2)}, u32[]{:S(2)}) async-start(s32[16,1,1]{2,1,0:T(1,128)} %copy.44), calls=%async_computation | async-start | bytes 16384 | tf_op jit(solution)/shard_map/all_to_all | solution.py:118
  82.4 7.4 %copy-start.5 = (s32[4,6]{1,0:T(4,128)S(1)}, s32[4,6]{1,0:T(4,128)}, u32[]{:S(2)}) copy-start(s32[4,6]{1,0:T(4,128)} %param.24) | copy-start | bytes 292
  82.4 22.3 %copy-start.8 = (bf16[128,512]{1,0:T(8,128)(2,1)S(1)}, bf16[128,512]{1,0:T(8,128)(2,1)}, u32[]{:S(2)}) copy-start(bf16[128,512]{1,0:T(8,128)(2,1)} %param.22) | copy-start | bytes 393220
  83.7 20.5 %all-to-all-start.1 = ((bf16[16,32,512]{2,1,0:T(8,128)(2,1)}), bf16[16,32,512]{2,1,0:T(8,128)(2,1)S(1)}, u32[]{:S(2)}, u32[]{:S(2)}) async-start(bf16[16,32,512]{2,1,0:T(8,128)(2,1)} %copy.72), calls=%async_computation.1 | async-start | bytes 1048576 | tf_op jit(solution)/shard_map/all_to_all | solution.py:82
  105.0 7.9 %copy-start.3 = (bf16[4,6,32,32]{3,2,1,0:T(8,128)(2,1)S(1)}, bf16[4,6,32,32]{3,2,1,0:T(8,128)(2,1)}, u32[]{:S(2)}) copy-start(bf16[4,6,32,32]{3,2,1,0:T(8,128)(2,1)} %param.25) | copy-start | bytes 147460
  105.0 7.1 %collective-permute-start = (bf16[128,512]{1,0:T(8,128)(2,1)S(1)}, bf16[128,512]{1,0:T(8,128)(2,1)S(1)}, u32[]{:S(2)}, u32[]{:S(2)}) collective-permute-start(bf16[128,512]{1,0:T(8,128)(2,1)S(1)} %add_convert_fusion.1), channel_id=1, source_target_pairs={{0,1},{1,2},{2,3},{3,4},{4,5},{5,6},{6,7},{7,8},{8,9},{9,10},{10,1... | collective-permute-start | bytes 393224 | tf_op jit(solution)/shard_map/ppermute | solution.py:14
  105.0 7.1 %collective-permute-start.1 = (bf16[128,512]{1,0:T(8,128)(2,1)S(1)}, bf16[128,512]{1,0:T(8,128)(2,1)S(1)}, u32[]{:S(2)}, u32[]{:S(2)}) collective-permute-start(bf16[128,512]{1,0:T(8,128)(2,1)S(1)} %add_convert_fusion.1), channel_id=1, source_target_pairs={{1,0},{2,1},{3,2},{4,3},{5,4},{6,5},{7,6},{8,7},{9,8},{10,9},{11,1... | collective-permute-start | bytes 393224 | tf_op jit(solution)/shard_map/ppermute | solution.py:16
  112.2 1.2 copy-start.6
  112.6 1.0 copy-start.7
  113.6 7.7 %copy-start.2 = (bf16[4096,227]{0,1:T(8,128)(2,1)S(1)}, bf16[4096,227]{0,1:T(8,128)(2,1)}, u32[]{:S(2)}) copy-start(bf16[4096,227]{0,1:T(8,128)(2,1)} %param.17) | copy-start | bytes 5578756
  113.9 8.2 %copy-start.4 = (bf16[128,512]{1,0:T(8,128)(2,1)}, bf16[128,512]{1,0:T(8,128)(2,1)S(1)}, u32[]{:S(2)}) copy-start(bf16[128,512]{1,0:T(8,128)(2,1)S(1)} %add_convert_fusion) | copy-start | bytes 393220
  115.4 20.4 %all-to-all-start.2 = ((bf16[16,32,512]{2,1,0:T(8,128)(2,1)}), bf16[16,32,512]{2,1,0:T(8,128)(2,1)}, u32[]{:S(2)}, u32[]{:S(2)}) async-start(bf16[16,32,512]{2,1,0:T(8,128)(2,1)} %copy.51), calls=%async_computation.2 | async-start | bytes 1048576 | tf_op jit(solution)/shard_map/all_to_all | solution.py:123
  122.3 14.9 %copy-start.1 = (bf16[512,227]{0,1:T(8,128)(2,1)S(1)}, bf16[512,227]{0,1:T(8,128)(2,1)}, u32[]{:S(2)}) copy-start(bf16[512,227]{0,1:T(8,128)(2,1)} %param.29) | copy-start | bytes 697348
where the time goes:
time: 177 us; the launch traced here: 176 us
  matrix products  101 us (57%)
  waiting for transfers between devices  29.4 us (17%)
  starting transfers between devices  23.8 us (13%)
  local copies, waits for them, and re-layouts  19.5 us (11%)
    dot_general x8, matrix products, encode(): jnp.einsum('ts,til->sil', selector, products.reshape(-1, block_mesh, late...  38.7 us
    dot_general x8, matrix products, encode(): jnp.einsum('gkij,gjl->gkil', coef_group, latent_group, preferred_element_...  27.3 us
    all_to_all x1, waiting for transfers between devices, local(): lax.all_to_all(slot_sums, 'nodes', split_axis=0, concat_axis=0, tiled=True)  14 us
    dot_general x8, matrix products, decode(): jnp.einsum('gkij,gkjl->gil', coef_group, fetched, preferred_element_type=...  13.8 us
    all_to_all x1, waiting for transfers between devices, local(): lax.all_to_all(outgoing, 'nodes', split_axis=0, concat_axis=0, tiled=True)  12.9 us
    dot_general x8, matrix products, decode(): jnp.dot(hidden_grid, w_out, preferred_element_type=jnp.float32)  8.21 us
    all_to_all x1, starting transfers between devices, local(): lax.all_to_all(slot_block, 'nodes', split_axis=0, concat_axis=0, tiled=True)  7.39 us
    convert_element_type x8, local copies, waits for them, and re-layouts, decode(): fetched = jnp.einsum('ts,sil->til', owner_table, returned, preferred_elem...  6.93 us
  transfers between devices with their start and end apart: 5, of which 3 were waited for; matrix products, arithmetic and copies ran while one was open for 43% of the time, Pallas kernels for 0%

commit v1 on v0

v1 whole, which is shorter than its diff:
```python
import functools

import jax
import jax.numpy as jnp
from jax import lax
from jax.experimental import pallas as pl
from jax.experimental.pallas import tpu as pltpu
from jax.sharding import PartitionSpec as P

F32 = jnp.float32
BF16 = jnp.bfloat16
SLOTS = 6
MIB = 1 << 20


def offsets_of(parts):
    return (0, 1, 2, -2, -1, parts // 2)


def silu(x):
    half = 0.5 * x
    return half + half * jnp.tanh(half)


def encode_kernel(
    parts, per_block, owner_ref, grid_ref, w_ref, enc_ref, dec_ref,
    lat_ref, dsum_ref, *rest,
):
    slot_refs = rest[:SLOTS]
    wt_ref, tgt_ref, msum_ref, acc_ref = rest[SLOTS:]
    step = pl.program_id(0)
    block_mesh, block_grid = enc_ref.shape[1:]
    blocks = enc_ref.shape[0] // per_block
    wide = per_block * block_mesh
    rows = SLOTS * block_mesh

    @pl.when(step == 0)
    def _():
        channels, latent = w_ref.shape
        wt_ref[:, :channels] = w_ref[...].astype(F32).T.astype(BF16)
        me = lax.axis_index("nodes")
        off = owner_ref[...] - me
        off = jnp.where(off < 0, off + parts, off)
        slot = jnp.where(off == parts // 2, 5, jnp.where(off > 2, off - parts + 5, off))
        slot = slot.astype(F32)
        total = jnp.zeros(tgt_ref.shape, F32)
        groups, lanes = owner_ref.shape
        all_blocks = tgt_ref.shape[0]
        for r in range(groups):
            tile = lax.broadcasted_iota(jnp.int32, (all_blocks, lanes), 1) + r * lanes
            first = lax.broadcasted_iota(jnp.int32, (all_blocks, lanes), 0) * per_block
            mine = (tile >= first) & (tile < first + per_block)
            picked = jnp.where(mine, slot[r : r + 1, :], 0.0).astype(BF16)
            row = lax.broadcasted_iota(jnp.int32, (lanes, wide), 0) + r * lanes
            col = lax.broadcasted_iota(jnp.int32, (lanes, wide), 1)
            place = row - per_block * ((row * (2**19 // per_block + 1)) >> 19)
            spread = jnp.where(place == col // block_mesh, 1.0, 0.0).astype(BF16)
            total += jnp.dot(picked, spread, preferred_element_type=F32)
        col = lax.broadcasted_iota(jnp.int32, tgt_ref.shape, 1)
        tgt_ref[...] = total.astype(jnp.int32) * block_mesh + col % block_mesh
        acc_ref[...] = jnp.zeros_like(acc_ref)

    row_ids = lax.broadcasted_iota(jnp.int32, (rows, wide), 0)
    for b in range(blocks):
        target = tgt_ref[pl.ds(step * blocks + b, 1), :]
        hot = jnp.where(row_ids == target, 1.0, 0.0).astype(BF16)
        span = slice(b * per_block, (b + 1) * per_block)
        both = jnp.concatenate(
            [
                enc_ref[span].reshape(wide, block_grid),
                dec_ref[span].reshape(wide, block_grid),
            ],
            axis=1,
        )
        sums = jnp.dot(hot, both, preferred_element_type=F32).astype(BF16)
        cols = slice(b * block_grid, (b + 1) * block_grid)
        msum_ref[:, cols] = sums[:, :block_grid]
        dsum_ref[:, cols] = sums[:, block_grid:]
    channels = grid_ref.shape[0]
    lat = silu(
        jnp.dot(wt_ref[:, :channels], grid_ref[...], preferred_element_type=F32)
    ).astype(BF16)
    lat_ref[...] = lat
    acc_ref[...] += lax.dot_general(
        lat, msum_ref[...], (((1,), (1,)), ((), ())), preferred_element_type=F32
    )

    @pl.when(step == pl.num_programs(0) - 1)
    def _():
        flipped = acc_ref[...].T.astype(BF16)
        for s in range(SLOTS):
            slot_refs[s][...] = flipped[s * block_mesh : (s + 1) * block_mesh, :]


def encode(parts, grid_t, w_embed, enc_coef, dec_t, owners):
    channels, points = grid_t.shape
    latent = w_embed.shape[1]
    tiles, block_mesh, block_grid = enc_coef.shape
    grid_blocks = points // block_grid
    per_block = tiles // grid_blocks
    blocks = 4
    steps = grid_blocks // blocks
    width = blocks * block_grid
    rows = SLOTS * block_mesh
    wide = per_block * block_mesh
    return pl.pallas_call(
        functools.partial(encode_kernel, parts, per_block),
        grid=(steps,),
        in_specs=[
            pl.BlockSpec(owners.shape, lambda i: (0, 0)),
            pl.BlockSpec((channels, width), lambda i: (0, i)),
            pl.BlockSpec((channels, latent), lambda i: (0, 0)),
            pl.BlockSpec((blocks * per_block, block_mesh, block_grid), lambda i: (i, 0, 0)),
            pl.BlockSpec((blocks * per_block, block_mesh, block_grid), lambda i: (i, 0, 0)),
        ],
        out_specs=[
            pl.BlockSpec((latent, width), lambda i: (0, i)),
            pl.BlockSpec((rows, width), lambda i: (0, i)),
        ]
        + [pl.BlockSpec((block_mesh, latent), lambda i: (0, 0))] * SLOTS,
        out_shape=[
            jax.ShapeDtypeStruct((latent, points), BF16),
            jax.ShapeDtypeStruct((rows, points), BF16),
        ]
        + [jax.ShapeDtypeStruct((block_mesh, latent), BF16)] * SLOTS,
        scratch_shapes=[
            pltpu.VMEM((latent, 256), BF16),
            pltpu.VMEM((grid_blocks, wide), jnp.int32),
            pltpu.VMEM((rows, width), BF16),
            pltpu.VMEM((latent, rows), F32),
        ],
        compiler_params=pltpu.CompilerParams(vmem_limit_bytes=24 * MIB),
        name="encode",
    )(owners, grid_t, w_embed, enc_coef, dec_t)


def update_kernel(parts, ids_ref, *refs):
    slots = refs[:SLOTS]
    mesh_ref, w_ref, mid_ref, agg_ref = refs[SLOTS:]
    block_mesh = slots[0].shape[0]
    me = lax.axis_index("nodes")
    agg_ref[...] = jnp.zeros_like(agg_ref)
    for s, off in enumerate(offsets_of(parts)):
        block = ids_ref[lax.rem(me - off + parts, parts) * parts + me]
        span = pl.ds(pl.multiple_of(block * block_mesh, block_mesh), block_mesh)
        agg_ref[span, :] += slots[s][...].astype(F32)
    grown = jnp.dot(agg_ref[...].astype(BF16), w_ref[...], preferred_element_type=F32)
    mid_ref[...] = (mesh_ref[...].astype(F32) + silu(grown)).astype(BF16)


def update(parts, ids, slots, mesh_in, w_enc):
    vmem = pl.BlockSpec(memory_space=pltpu.VMEM)
    return pl.pallas_call(
        functools.partial(update_kernel, parts),
        in_specs=[pl.BlockSpec(memory_space=pltpu.SMEM)] + [vmem] * (SLOTS + 2),
        out_specs=vmem,
        out_shape=jax.ShapeDtypeStruct(mesh_in.shape, BF16),
        scratch_shapes=[pltpu.VMEM(mesh_in.shape, F32)],
        compiler_params=pltpu.CompilerParams(vmem_limit_bytes=8 * MIB),
        name="mesh_update",
    )(ids, *slots, mesh_in, w_enc)


def process_kernel(
    parts, ids_ref, adj_ref, mid_ref, left_ref, right_ref, coef_ref, gain_ref, w_ref,
    out_ref, *rest,
):
    sends = rest[:SLOTS]
    ext_ref, pick_ref, norm_ref = rest[SLOTS:]
    mesh_blocks, block_mesh, wide = coef_ref.shape
    adj_width = wide // block_mesh
    mesh_count = mid_ref.shape[0]
    me = lax.axis_index("nodes")
    ext_ref[0:mesh_count, :] = left_ref[...]
    ext_ref[mesh_count : 2 * mesh_count, :] = mid_ref[...]
    ext_ref[2 * mesh_count : 3 * mesh_count, :] = right_ref[...]
    for b in range(mesh_blocks):
        for a in range(adj_width):
            near = jnp.maximum(adj_ref[b, a], 0)
            side = lax.rem(near // mesh_blocks - me + 1 + parts, parts)
            place = side * mesh_blocks + lax.rem(near, mesh_blocks)
            place = jnp.minimum(place, 3 * mesh_blocks - 1)
            span = pl.ds(pl.multiple_of(place * block_mesh, block_mesh), block_mesh)
            pick_ref[b, a * block_mesh : (a + 1) * block_mesh, :] = ext_ref[span, :]
        message = jnp.dot(coef_ref[b], pick_ref[b], preferred_element_type=F32)
        power = jnp.mean(message * message, axis=-1, keepdims=True)
        normed = message * lax.rsqrt(power + 1e-05) * gain_ref[...]
        norm_ref[b * block_mesh : (b + 1) * block_mesh, :] = normed.astype(BF16)
    grown = jnp.dot(norm_ref[...], w_ref[...], preferred_element_type=F32)
    out_ref[...] = (mid_ref[...].astype(F32) + silu(grown)).astype(BF16)
    for s, off in enumerate(offsets_of(parts)):
        block = ids_ref[lax.rem(me - off + parts, parts) * parts + me]
        span = pl.ds(pl.multiple_of(block * block_mesh, block_mesh), block_mesh)
        sends[s][...] = out_ref[span, :]


def process(parts, ids, adj, mid, left, right, coef, gain, w_proc):
    vmem = pl.BlockSpec(memory_space=pltpu.VMEM)
    smem = pl.BlockSpec(memory_space=pltpu.SMEM)
    mesh_blocks, block_mesh, wide = coef.shape
    mesh_count, latent = mid.shape
    return pl.pallas_call(
        functools.partial(process_kernel, parts),
        in_specs=[smem] * 2 + [vmem] * 6,
        out_specs=[vmem] * (1 + SLOTS),
        out_shape=[jax.ShapeDtypeStruct(mid.shape, BF16)]
        + [jax.ShapeDtypeStruct((block_mesh, latent), BF16)] * SLOTS,
        scratch_shapes=[
            pltpu.VMEM((3 * mesh_count, latent), BF16),
            pltpu.VMEM((mesh_blocks, wide, latent), BF16),
            pltpu.VMEM((mesh_count, latent), BF16),
        ],
        compiler_params=pltpu.CompilerParams(vmem_limit_bytes=8 * MIB),
        name="mesh_process",
    )(ids, adj, mid, left, right, coef, gain, w_proc)


def decode_kernel(grid_ref, lat_ref, dsum_ref, w_ref, *rest):
    slots = rest[:SLOTS]
    out_ref, back_ref = rest[SLOTS:]

    @pl.when(pl.program_id(0) == 0)
    def _():
        joined = jnp.concatenate([slot[...] for slot in slots], axis=0)
        back_ref[...] = joined.astype(F32).T.astype(BF16)

    decoded = jnp.dot(back_ref[...], dsum_ref[...], preferred_element_type=F32)
    hidden = silu(lat_ref[...].astype(F32) + decoded).astype(BF16)
    out_ref[...] = (
        grid_ref[...].astype(F32)
        + jnp.dot(w_ref[...], hidden, preferred_element_type=F32)
    ).astype(BF16)


def decode(grid_t, lat_t, dsum, w_out_t, slots):
    channels, points = grid_t.shape
    latent = lat_t.shape[0]
    rows = dsum.shape[0]
    block_mesh = slots[0].shape[0]
    width = 512
    return pl.pallas_call(
        decode_kernel,
        grid=(points // width,),
        in_specs=[
            pl.BlockSpec((channels, width), lambda i: (0, i)),
            pl.BlockSpec((latent, width), lambda i: (0, i)),
            pl.BlockSpec((rows, width), lambda i: (0, i)),
            pl.BlockSpec((channels, latent), lambda i: (0, 0)),
        ]
        + [pl.BlockSpec((block_mesh, latent), lambda i: (0, 0))] * SLOTS,
        out_specs=pl.BlockSpec((channels, width), lambda i: (0, i)),
        out_shape=jax.ShapeDtypeStruct((channels, points), BF16),
        scratch_shapes=[pltpu.VMEM((latent, rows), BF16)],
        compiler_params=pltpu.CompilerParams(vmem_limit_bytes=24 * MIB),
        name="decode",
    )(grid_t, lat_t, dsum, w_out_t, *slots)


def local(
    grid_in, w_embed, enc_coef, enc_owner, slot_block, mesh_in, w_enc,
    proc_adj, proc_coef, proc_gain, w_proc, dec_coef, w_out,
):
    parts = lax.axis_size("nodes")
    offsets = offsets_of(parts)
    mesh_blocks, adj_width, block_mesh, _ = proc_coef.shape

    def shift(x, off):
        if off == 0:
            return x
        return lax.ppermute(x, "nodes", [(i, (i + off) % parts) for i in range(parts)])

    ids = lax.all_gather(slot_block, "nodes", axis=0, tiled=True)
    grid_t = grid_in.T
    lat_t, dsum, *sums = encode(
        parts, grid_t, w_embed, enc_coef, jnp.swapaxes(dec_coef, 1, 2),
        enc_owner.reshape(-1, 128),
    )
    received = [shift(x, off) for x, off in zip(sums, offsets)]
    mid = update(parts, ids, received, mesh_in, w_enc)
    left, right = shift(mid, 1), shift(mid, -1)
    live = (proc_adj >= 0)[:, :, None, None]
    coef = jnp.where(live, proc_coef, jnp.zeros_like(proc_coef))
    coef = coef.transpose(0, 2, 1, 3).reshape(mesh_blocks, block_mesh, adj_width * block_mesh)
    mesh_out, *sends = process(
        parts, ids, proc_adj, mid, left, right, coef, proc_gain.reshape(1, -1), w_proc
    )
    returned = [shift(x, -off) for x, off in zip(sends, offsets)]
    pred_t = decode(grid_t, lat_t, dsum, w_out.T, returned)
    return (pred_t.T, mesh_out)


def solution(mesh):
    return jax.shard_map(
        local,
        mesh=mesh,
        in_specs=(
            P(("groups", "nodes"), None),
            P(),
            P("nodes", None, None),
            P("nodes"),
            P("nodes"),
            P(("groups", "nodes"), None),
            P(),
            P("nodes", None),
            P("nodes", None, None, None),
            P(),
            P(),
            P("nodes", None, None),
            P(),
        ),
        out_specs=(P(("groups", "nodes"), None), P(("groups", "nodes"), None)),
        check_vma=False,
    )
```

time: 177 us -> 73.3 us (0.41)
  matrix products: 101 us -> 0 us
  waiting for transfers between devices: 29.4 us -> 9.51 us
  Pallas kernels: 0 us -> 19 us
  starting transfers between devices: 23.8 us -> 11.6 us
  blocking collectives: 0 us -> 10 us
    dot_general x47 -> x0, matrix products: 101 us -> none  [the longest x8 38.7 us: encode(): jnp.einsum('ts,til->sil', selector, products.reshape(-1, block_mesh, late...]
    all_to_all x3 -> x0, waiting for transfers between devices: 26.9 us -> none  [the longest x1 14 us: local(): lax.all_to_all(slot_sums, 'nodes', split_axis=0, concat_axis=0, tiled=True)]
    all_to_all x3 -> x0, starting transfers between devices: 19.3 us -> none  [the longest x1 7.39 us: local(): lax.all_to_all(slot_block, 'nodes', split_axis=0, concat_axis=0, tiled=True)]
    pallas_call x0 -> x4, Pallas kernels: none -> 19 us  [the longest x1 8.08 us: encode(): pl.pallas_call(functools.partial(encode_kernel, parts, per_block), grid=(...]
    unnamed x21 -> x33, local copies, waits for them, and re-layouts: 3.23 us -> 18.2 us
    unnamed x0 -> x1, blocking collectives: none -> 10 us
    convert_element_type x11 -> x0, local copies, waits for them, and re-layouts: 8.28 us -> none  [the longest x8 6.93 us: decode(): fetched = jnp.einsum('ts,sil->til', owner_table, returned, preferred_elem...]
    ppermute x2 -> x12, starting transfers between devices: 4.49 us -> 11.6 us  [shift(): lax.ppermute(x, 'nodes', [(i, (i + off) % parts) for i in range(parts)])]
  transfers between devices with their start and end apart: 5 -> 12, of which waited for: 3 -> 4; matrix products, arithmetic and copies ran while one was open for 43% -> 9% of each run, Pallas kernels for 0% -> 0%
where the time goes in v1:
time: 73.3 us; the launch traced here: 72.7 us
  local copies, waits for them, and re-layouts  20.1 us (27%)
  Pallas kernels  19 us (26%)
  starting transfers between devices  11.6 us (16%)
  blocking collectives  10 us (14%)
  waiting for transfers between devices  9.51 us (13%)
  between operations  1.4 us (2%)
  other arithmetic  1.02 us (1%)
    unnamed x33, local copies, waits for them, and re-layouts  18.2 us
    ppermute x12, starting transfers between devices, shift(): lax.ppermute(x, 'nodes', [(i, (i + off) % parts) for i in range(parts)])  11.6 us
    unnamed x1, blocking collectives  10 us
    ppermute x12, waiting for transfers between devices, shift(): lax.ppermute(x, 'nodes', [(i, (i + off) % parts) for i in range(parts)])  9.51 us
    pallas_call x1, Pallas kernels, encode(): pl.pallas_call(functools.partial(encode_kernel, parts, per_block), grid=(...  8.08 us
    pallas_call x1, Pallas kernels, decode(): pl.pallas_call(decode_kernel, grid=(points // width,), in_specs=[pl.Block...  6.78 us
    pallas_call x1, Pallas kernels, process(): pl.pallas_call(functools.partial(process_kernel, parts), in_specs=[smem]...  2.3 us
    pallas_call x1, Pallas kernels, update(): pl.pallas_call(functools.partial(update_kernel, parts), in_specs=[pl.Bloc...  1.8 us
  transfers between devices with their start and end apart: 12, of which 4 were waited for; matrix products, arithmetic and copies ran while one was open for 9% of the time, Pallas kernels for 0%

profile of v1, /device:TPU:0, one launch (start us, length us, event | category | flops | bytes accessed | tf_op | source)
XLA Modules:
  0.0 72.7 jit_solution(2929954333937405914)
XLA Ops:
  0.6 0.0 copy-start
  0.6 1.5 %copy-done = bf16[4096,227]{0,1:T(8,128)(2,1)S(1)} copy-done((bf16[4096,227]{0,1:T(8,128)(2,1)S(1)}, bf16[4096,227]{0,1:T(8,128)(2,1)}, u32[]{:S(2)}) %copy-start) | copy-done | bytes 1859608
  2.2 1.9 %copy-done.4 = bf16[384,32,128]{2,1,0:T(8,128)(2,1)S(1)} copy-done((bf16[384,32,128]{2,1,0:T(8,128)(2,1)S(1)}, bf16[384,32,128]{2,1,0:T(8,128)(2,1)}, u32[]{:S(2)}) %copy-start.4) | copy-done | bytes 3145752
  4.0 1.9 %copy-done.5 = bf16[384,128,32]{1,2,0:T(8,128)(2,1)S(1)} copy-done((bf16[384,128,32]{1,2,0:T(8,128)(2,1)S(1)}, bf16[384,128,32]{1,2,0:T(8,128)(2,1)}, u32[]{:S(2)}) %copy-start.5) | copy-done | bytes 3145752
  5.9 0.9 %copy-done.8 = bf16[227,512]{1,0:T(8,128)(2,1)S(1)} copy-done((bf16[227,512]{1,0:T(8,128)(2,1)S(1)}, bf16[227,512]{1,0:T(8,128)(2,1)}, u32[]{:S(2)}) %copy-start.8) | copy-done | bytes 232472
  6.9 0.7 copy-done.13
  7.6 8.1 %encode.1 = (bf16[512,4096]{1,0:T(8,128)(2,1)S(1)}, bf16[192,4096]{1,0:T(8,128)(2,1)S(1)}, bf16[32,512]{1,0:T(8,128)(2,1)S(1)}, bf16[32,512]{1,0:T(8,128)(2,1)},...) custom-call(s32[3,128]{1,0:T(4,128)S(1)} %bitcast.14, ...), custom_call_target="tpu_custom_call" | custom-call | tf_op jit(solution)/shard_map/encode/pallas_call | solution.py:106
  15.6 1.9 %copy-done.2 = bf16[512,4096]{1,0:T(8,128)(2,1)} copy-done((bf16[512,4096]{1,0:T(8,128)(2,1)}, bf16[512,4096]{1,0:T(8,128)(2,1)S(1)}, u32[]{:S(2)}) %copy-start.2) | copy-done | bytes 4194328
  17.6 0.5 collective-permute-start
  18.0 2.5 %collective-permute-start.1 = (bf16[32,512]{1,0:T(8,128)(2,1)}, bf16[32,512]{1,0:T(8,128)(2,1)}, u32[]{:S(2)}, u32[]{:S(2)}) collective-permute-start(bf16[32,512]{1,0:T(8,128)(2,1)} %get-tuple-element.21), channel_id=1, source_target_pairs={{0,2},{1,3},{2,4},{3,5},{4,6},{5,7},{6,8},{7,9},{8,10},{9,11},{10,... | collective-permute-start | bytes 98312 | tf_op jit(solution)/shard_map/ppermute | solution.py:270
  20.6 3.1 %collective-permute-start.2 = (bf16[32,512]{1,0:T(8,128)(2,1)}, bf16[32,512]{1,0:T(8,128)(2,1)}, u32[]{:S(2)}, u32[]{:S(2)}) collective-permute-start(bf16[32,512]{1,0:T(8,128)(2,1)} %get-tuple-element.22), channel_id=1, source_target_pairs={{0,14},{1,15},{2,0},{3,1},{4,2},{5,3},{6,4},{7,5},{8,6},{9,7},{10,... | collective-permute-start | bytes 98312 | tf_op jit(solution)/shard_map/ppermute | solution.py:270
  23.7 1.4 %collective-permute-start.3 = (bf16[32,512]{1,0:T(8,128)(2,1)}, bf16[32,512]{1,0:T(8,128)(2,1)}, u32[]{:S(2)}, u32[]{:S(2)}) collective-permute-start(bf16[32,512]{1,0:T(8,128)(2,1)} %get-tuple-element.23), channel_id=1, source_target_pairs={{0,15},{1,0},{2,1},{3,2},{4,3},{5,4},{6,5},{7,6},{8,7},{9,8},{10,9... | collective-permute-start | bytes 98312 | tf_op jit(solution)/shard_map/ppermute | solution.py:270
  25.1 0.7 collective-permute-start.4
  25.7 1.3 %dynamic-slice = u32[1]{0:T(128)} dynamic-slice(u32[32]{0:T(128)} %constant.8, u32[]{:T(128)S(6)} %add), dynamic_slice_sizes={1} | dynamic-slice | bytes 12
  27.7 0.6 broadcast.5
  28.3 1.3 %dynamic-update-slice = s32[256]{0:T(256)} dynamic-update-slice(s32[256]{0:T(256)} %broadcast.5, s32[16]{0:T(128)S(1)} %copy-done.14, u32[]{:T(128)} %bitcast.4) | dynamic-update-slice | bytes 132
  29.6 10.0 %all-reduce.ids_ref = s32[256]{0:T(256)S(1)} all-reduce(s32[256]{0:T(256)} %dynamic-update-slice), channel_id=1, replica_groups=mesh['groups'=2,'nodes'=16] {'nodes'}, use_global_device_ids=true, to_apply=%add | all-reduce | flops 256 | bytes 2048
  39.7 0.0 collective-permute-done.refs_1_
  39.7 0.0 collective-permute-done.1.refs_2_
  39.7 0.0 collective-permute-done.2.refs_3_
  39.7 0.0 collective-permute-done.3.refs_4_
  39.7 0.0 collective-permute-done.4.refs_5_
  39.7 0.0 copy-start.6
  39.7 1.0 %copy-done.6 = bf16[512,512]{1,0:T(8,128)(2,1)S(1)} copy-done((bf16[512,512]{1,0:T(8,128)(2,1)S(1)}, bf16[512,512]{1,0:T(8,128)(2,1)}, u32[]{:S(2)}) %copy-start.6) | copy-done | bytes 524312
  40.8 0.9 %copy-done.10 = bf16[128,512]{1,0:T(8,128)(2,1)S(1)} copy-done((bf16[128,512]{1,0:T(8,128)(2,1)S(1)}, bf16[128,512]{1,0:T(8,128)(2,1)}, u32[]{:S(2)}) %copy-start.10) | copy-done | bytes 131096
  41.7 1.8 %mesh_update.1.mid_ref = bf16[128,512]{1,0:T(8,128)(2,1)} custom-call(s32[256]{0:T(256)S(1)} %all-reduce.ids_ref, bf16[32,512]{1,0:T(8,128)(2,1)S(1)} %get-tuple-element.19.refs_0_, bf16[32,512]{1,0:T(8,128)(2,1)S(1)} %collective-permute-done.refs_1_, bf16[32,512]{1,0:T(8,128)(2,1)} %collective-permute-done.1.refs_2_, ...), custom_call_target="tpu_custom_call" | custom-call | tf_op jit(solution)/shard_map/mesh_update/pallas_call | solution.py:153
  43.5 0.0 collective-permute-start.6
  43.5 0.5 collective-permute-start.5
  44.0 1.0 %select_bitcast_fusion = bf16[4,32,6,32]{3,1,2,0:T(8,128)(2,1)S(1)} fusion(bf16[4,6,32,32]{3,2,1,0:T(8,128)(2,1)} %param.21, pred[4,6]{1,0:T(4,128)(4,1)S(1)} %broadcast_compare_fusion), kind=kLoop, calls=%fused_computation | loop fusion | flops 24576 | bytes 98328 | tf_op jit(solution)/shard_map/transpose | solution.py:283
  45.0 0.8 %copy.16 = bf16[4,32,6,32]{3,2,1,0:T(8,128)(2,1)} copy(bf16[4,32,6,32]{3,1,2,0:T(8,128)(2,1)S(1)} %select_bitcast_fusion) | data formatting | bytes 98304 | tf_op jit(solution)/shard_map/transpose | solution.py:283
  45.8 1.2 %reshape.15.coef_ref = bf16[4,32,192]{2,1,0:T(8,128)(2,1)S(1)} reshape(bf16[4,32,6,32]{3,2,1,0:T(8,128)(2,1)} %copy.16) | data formatting | bytes 98304 | tf_op jit(solution)/shard_map/reshape | solution.py:283
  47.0 0.0 collective-permute-done.6.right_ref
  47.0 3.9 %collective-permute-done.5.left_ref = bf16[128,512]{1,0:T(8,128)(2,1)} collective-permute-done((bf16[128,512]{1,0:T(8,128)(2,1)}, bf16[128,512]{1,0:T(8,128)(2,1)}, u32[]{:S(2)}, u32[]{:S(2)}) %collective-permute-start.5) | collective-permute-done | bytes 131104 | tf_op jit(solution)/shard_map/ppermute | solution.py:270
  50.9 1.0 %copy-done.7 = bf16[512,512]{1,0:T(8,128)(2,1)S(1)} copy-done((bf16[512,512]{1,0:T(8,128)(2,1)S(1)}, bf16[512,512]{1,0:T(8,128)(2,1)}, u32[]{:S(2)}) %copy-start.7) | copy-done | bytes 524312
  51.9 2.3 %mesh_process.1 = (bf16[128,512]{1,0:T(8,128)(2,1)}, bf16[32,512]{1,0:T(8,128)(2,1)S(1)}, bf16[32,512]{1,0:T(8,128)(2,1)S(1)}, bf16[32,512]{1,0:T(8,128)(2,1)S(1...) custom-call(s32[256]{0:T(256)S(1)} %all-reduce.ids_ref, ...), custom_call_target="tpu_custom_call" | custom-call | tf_op jit(solution)/shard_map/mesh_process/pallas_call | solution.py:202
  54.2 0.1 collective-permute-start.7
  54.3 1.4 %collective-permute-start.8 = (bf16[32,512]{1,0:T(8,128)(2,1)S(1)}, bf16[32,512]{1,0:T(8,128)(2,1)S(1)}, u32[]{:S(2)}, u32[]{:S(2)}) collective-permute-start(bf16[32,512]{1,0:T(8,128)(2,1)S(1)} %get-tuple-element.27), channel_id=1, source_target_pairs={{0,14},{1,15},{2,0},{3,1},{4,2},{5,3},{6,4},{7,5},{8,6},{9,7},{10,... | collective-permute-start | bytes 98312 | tf_op jit(solution)/shard_map/ppermute | solution.py:270
  55.7 0.7 collective-permute-start.9
  56.4 0.0 collective-permute-start.10
  56.4 0.8 %collective-permute-start.11 = (bf16[32,512]{1,0:T(8,128)(2,1)S(1)}, bf16[32,512]{1,0:T(8,128)(2,1)S(1)}, u32[]{:S(2)}, u32[]{:S(2)}) collective-permute-start(bf16[32,512]{1,0:T(8,128)(2,1)S(1)} %get-tuple-element.30), channel_id=1, source_target_pairs={{0,8},{1,9},{2,10},{3,11},{4,12},{5,13},{6,14},{7,15},{8,0},{9,1},... | collective-permute-start | bytes 98312 | tf_op jit(solution)/shard_map/ppermute | solution.py:270
  57.2 0.0 collective-permute-done.7.rest_1_
  57.2 1.1 %collective-permute-done.8.rest_2_ = bf16[32,512]{1,0:T(8,128)(2,1)S(1)} collective-permute-done((bf16[32,512]{1,0:T(8,128)(2,1)S(1)}, bf16[32,512]{1,0:T(8,128)(2,1)S(1)}, u32[]{:S(2)}, u32[]{:S(2)}) %collective-permute-start.8) | collective-permute-done | bytes 32800 | tf_op jit(solution)/shard_map/ppermute | solution.py:270
  58.2 4.3 %collective-permute-done.9.rest_3_ = bf16[32,512]{1,0:T(8,128)(2,1)S(1)} collective-permute-done((bf16[32,512]{1,0:T(8,128)(2,1)S(1)}, bf16[32,512]{1,0:T(8,128)(2,1)S(1)}, u32[]{:S(2)}, u32[]{:S(2)}) %collective-permute-start.9) | collective-permute-done | bytes 32800 | tf_op jit(solution)/shard_map/ppermute | solution.py:270
  62.6 0.2 collective-permute-done.10.rest_4_
  62.7 0.0 collective-permute-done.11.rest_5_
  62.8 2.2 %copy-done.3 = bf16[512,4096]{1,0:T(8,128)(2,1)S(1)} copy-done((bf16[512,4096]{1,0:T(8,128)(2,1)S(1)}, bf16[512,4096]{1,0:T(8,128)(2,1)}, u32[]{:S(2)}) %copy-start.3) | copy-done | bytes 4194328
  64.9 0.9 %copy-done.9 = bf16[512,227]{0,1:T(8,128)(2,1)S(1)} copy-done((bf16[512,227]{0,1:T(8,128)(2,1)S(1)}, bf16[512,227]{0,1:T(8,128)(2,1)}, u32[]{:S(2)}) %copy-start.9) | copy-done | bytes 232472
  65.9 6.8 %decode.1 = bf16[227,4096]{1,0:T(8,128)(2,1)} custom-call(bf16[227,4096]{1,0:T(8,128)(2,1)S(1)} %bitcast.10, bf16[512,4096]{1,0:T(8,128)(2,1)S(1)} %copy-done.3, bf16[192,4096]{1,0:T(8,128)(2,1)S(1)} %get-tuple-element.18.dsum_ref, bf16[227,512]{1,0:T(8,128)(2,1)S(1)} %bitcast.12, bf16[32,512]{1,0:T(8,128)(2,1)S(1)} %get-tuple-element.25.rest_0_, ...), custom_call_target="tpu_custom_call" | custom-call | tf_op jit(solution)/shard_map/decode/pallas_call | solution.py:241
  (18 shorter events, 0.0 us)
Async XLA Ops:
  0.6 1.5 %copy-start = (bf16[4096,227]{0,1:T(8,128)(2,1)S(1)}, bf16[4096,227]{0,1:T(8,128)(2,1)}, u32[]{:S(2)}) copy-start(bf16[4096,227]{0,1:T(8,128)(2,1)} %param.13) | copy-start | bytes 5578756
  2.2 1.9 %copy-start.4 = (bf16[384,32,128]{2,1,0:T(8,128)(2,1)S(1)}, bf16[384,32,128]{2,1,0:T(8,128)(2,1)}, u32[]{:S(2)}) copy-start(bf16[384,32,128]{2,1,0:T(8,128)(2,1)} %enc_ref.1) | copy-start | bytes 9437188
  4.0 1.9 %copy-start.5 = (bf16[384,128,32]{1,2,0:T(8,128)(2,1)S(1)}, bf16[384,128,32]{1,2,0:T(8,128)(2,1)}, u32[]{:S(2)}) copy-start(bf16[384,128,32]{1,2,0:T(8,128)(2,1)} %param.24) | copy-start | bytes 9437188
  5.9 0.9 %copy-start.8 = (bf16[227,512]{1,0:T(8,128)(2,1)S(1)}, bf16[227,512]{1,0:T(8,128)(2,1)}, u32[]{:S(2)}) copy-start(bf16[227,512]{1,0:T(8,128)(2,1)} %w_ref.2) | copy-start | bytes 697348
  6.9 0.7 copy-start.13
  7.6 18.2 %copy-start.11 = (s32[4,6]{1,0:T(4,128)S(1)}, s32[4,6]{1,0:T(4,128)}, u32[]{:S(2)}) copy-start(s32[4,6]{1,0:T(4,128)} %adj_ref.1) | copy-start | bytes 292
  7.6 20.7 %copy-start.14 = (s32[16]{0:T(128)S(1)}, s32[16]{0:T(128)}, u32[]{:S(2)}) copy-start(s32[16]{0:T(128)} %param.17) | copy-start | bytes 196
  7.6 43.3 %copy-start.12 = (f32[512]{0:T(512)S(1)}, f32[512]{0:T(512)}, u32[]{:S(2)}) copy-start(f32[512]{0:T(512)} %param.22) | copy-start | bytes 6148
  15.6 1.9 %copy-start.2 = (bf16[512,4096]{1,0:T(8,128)(2,1)}, bf16[512,4096]{1,0:T(8,128)(2,1)S(1)}, u32[]{:S(2)}) copy-start(bf16[512,4096]{1,0:T(8,128)(2,1)S(1)} %get-tuple-element.17.lat_ref) | copy-start | bytes 12582916
  17.6 45.2 %copy-start.1 = (bf16[4096,227]{0,1:T(8,128)(2,1)S(1)}, bf16[4096,227]{0,1:T(8,128)(2,1)}, u32[]{:S(2)}) copy-start(bf16[4096,227]{0,1:T(8,128)(2,1)} %param.13) | copy-start | bytes 5578756
  17.6 22.1 %collective-permute-start = (bf16[32,512]{1,0:T(8,128)(2,1)}, bf16[32,512]{1,0:T(8,128)(2,1)S(1)}, u32[]{:S(2)}, u32[]{:S(2)}) collective-permute-start(bf16[32,512]{1,0:T(8,128)(2,1)} %get-tuple-element.20), channel_id=1, source_target_pairs={{0,1},{1,2},{2,3},{3,4},{4,5},{5,6},{6,7},{7,8},{8,9},{9,10},{10,1... | collective-permute-start | bytes 98312 | tf_op jit(solution)/shard_map/ppermute | solution.py:270
  18.0 21.7 %collective-permute-start.1 = (bf16[32,512]{1,0:T(8,128)(2,1)}, bf16[32,512]{1,0:T(8,128)(2,1)}, u32[]{:S(2)}, u32[]{:S(2)}) collective-permute-start(bf16[32,512]{1,0:T(8,128)(2,1)} %get-tuple-element.21), channel_id=1, source_target_pairs={{0,2},{1,3},{2,4},{3,5},{4,6},{5,7},{6,8},{7,9},{8,10},{9,11},{10,... | collective-permute-start | bytes 98312 | tf_op jit(solution)/shard_map/ppermute | solution.py:270
  20.6 19.1 %collective-permute-start.2 = (bf16[32,512]{1,0:T(8,128)(2,1)}, bf16[32,512]{1,0:T(8,128)(2,1)}, u32[]{:S(2)}, u32[]{:S(2)}) collective-permute-start(bf16[32,512]{1,0:T(8,128)(2,1)} %get-tuple-element.22), channel_id=1, source_target_pairs={{0,14},{1,15},{2,0},{3,1},{4,2},{5,3},{6,4},{7,5},{8,6},{9,7},{10,... | collective-permute-start | bytes 98312 | tf_op jit(solution)/shard_map/ppermute | solution.py:270
  23.7 16.0 %collective-permute-start.3 = (bf16[32,512]{1,0:T(8,128)(2,1)}, bf16[32,512]{1,0:T(8,128)(2,1)}, u32[]{:S(2)}, u32[]{:S(2)}) collective-permute-start(bf16[32,512]{1,0:T(8,128)(2,1)} %get-tuple-element.23), channel_id=1, source_target_pairs={{0,15},{1,0},{2,1},{3,2},{4,3},{5,4},{6,5},{7,6},{8,7},{9,8},{10,9... | collective-permute-start | bytes 98312 | tf_op jit(solution)/shard_map/ppermute | solution.py:270
  25.1 14.7 %collective-permute-start.4 = (bf16[32,512]{1,0:T(8,128)(2,1)}, bf16[32,512]{1,0:T(8,128)(2,1)}, u32[]{:S(2)}, u32[]{:S(2)}) collective-permute-start(bf16[32,512]{1,0:T(8,128)(2,1)} %get-tuple-element.24), channel_id=1, source_target_pairs={{0,8},{1,9},{2,10},{3,11},{4,12},{5,13},{6,14},{7,15},{8,0},{9,1},... | collective-permute-start | bytes 98312 | tf_op jit(solution)/shard_map/ppermute | solution.py:270
  39.7 1.0 %copy-start.6 = (bf16[512,512]{1,0:T(8,128)(2,1)S(1)}, bf16[512,512]{1,0:T(8,128)(2,1)}, u32[]{:S(2)}) copy-start(bf16[512,512]{1,0:T(8,128)(2,1)} %refs_7_.1) | copy-start | bytes 1572868
  40.8 0.9 %copy-start.10 = (bf16[128,512]{1,0:T(8,128)(2,1)S(1)}, bf16[128,512]{1,0:T(8,128)(2,1)}, u32[]{:S(2)}) copy-start(bf16[128,512]{1,0:T(8,128)(2,1)} %refs_6_.1) | copy-start | bytes 393220
  43.5 3.5 %collective-permute-start.6 = (bf16[128,512]{1,0:T(8,128)(2,1)}, bf16[128,512]{1,0:T(8,128)(2,1)}, u32[]{:S(2)}, u32[]{:S(2)}) collective-permute-start(bf16[128,512]{1,0:T(8,128)(2,1)} %mesh_update.1.mid_ref), channel_id=1, source_target_pairs={{0,15},{1,0},{2,1},{3,2},{4,3},{5,4},{6,5},{7,6},{8,7},{9,8},{10,9... | collective-permute-start | bytes 393224 | tf_op jit(solution)/shard_map/ppermute | solution.py:270
  43.5 7.4 %collective-permute-start.5 = (bf16[128,512]{1,0:T(8,128)(2,1)}, bf16[128,512]{1,0:T(8,128)(2,1)}, u32[]{:S(2)}, u32[]{:S(2)}) collective-permute-start(bf16[128,512]{1,0:T(8,128)(2,1)} %mesh_update.1.mid_ref), channel_id=1, source_target_pairs={{0,1},{1,2},{2,3},{3,4},{4,5},{5,6},{6,7},{7,8},{8,9},{9,10},{10,1... | collective-permute-start | bytes 393224 | tf_op jit(solution)/shard_map/ppermute | solution.py:270
  50.9 1.0 %copy-start.7 = (bf16[512,512]{1,0:T(8,128)(2,1)S(1)}, bf16[512,512]{1,0:T(8,128)(2,1)}, u32[]{:S(2)}) copy-start(bf16[512,512]{1,0:T(8,128)(2,1)} %w_ref.3) | copy-start | bytes 1572868
  54.2 2.9 %collective-permute-start.7 = (bf16[32,512]{1,0:T(8,128)(2,1)S(1)}, bf16[32,512]{1,0:T(8,128)(2,1)S(1)}, u32[]{:S(2)}, u32[]{:S(2)}) collective-permute-start(bf16[32,512]{1,0:T(8,128)(2,1)S(1)} %get-tuple-element.26), channel_id=1, source_target_pairs={{0,15},{1,0},{2,1},{3,2},{4,3},{5,4},{6,5},{7,6},{8,7},{9,8},{10,9... | collective-permute-start | bytes 98312 | tf_op jit(solution)/shard_map/ppermute | solution.py:270
  54.3 3.9 %collective-permute-start.8 = (bf16[32,512]{1,0:T(8,128)(2,1)S(1)}, bf16[32,512]{1,0:T(8,128)(2,1)S(1)}, u32[]{:S(2)}, u32[]{:S(2)}) collective-permute-start(bf16[32,512]{1,0:T(8,128)(2,1)S(1)} %get-tuple-element.27), channel_id=1, source_target_pairs={{0,14},{1,15},{2,0},{3,1},{4,2},{5,3},{6,4},{7,5},{8,6},{9,7},{10,... | collective-permute-start | bytes 98312 | tf_op jit(solution)/shard_map/ppermute | solution.py:270
  55.7 6.9 %collective-permute-start.9 = (bf16[32,512]{1,0:T(8,128)(2,1)S(1)}, bf16[32,512]{1,0:T(8,128)(2,1)S(1)}, u32[]{:S(2)}, u32[]{:S(2)}) collective-permute-start(bf16[32,512]{1,0:T(8,128)(2,1)S(1)} %get-tuple-element.28), channel_id=1, source_target_pairs={{0,2},{1,3},{2,4},{3,5},{4,6},{5,7},{6,8},{7,9},{8,10},{9,11},{10,... | collective-permute-start | bytes 98312 | tf_op jit(solution)/shard_map/ppermute | solution.py:270
  56.4 6.4 %collective-permute-start.10 = (bf16[32,512]{1,0:T(8,128)(2,1)S(1)}, bf16[32,512]{1,0:T(8,128)(2,1)S(1)}, u32[]{:S(2)}, u32[]{:S(2)}) collective-permute-start(bf16[32,512]{1,0:T(8,128)(2,1)S(1)} %get-tuple-element.29), channel_id=1, source_target_pairs={{0,1},{1,2},{2,3},{3,4},{4,5},{5,6},{6,7},{7,8},{8,9},{9,10},{10,1... | collective-permute-start | bytes 98312 | tf_op jit(solution)/shard_map/ppermute | solution.py:270
  56.4 6.4 %collective-permute-start.11 = (bf16[32,512]{1,0:T(8,128)(2,1)S(1)}, bf16[32,512]{1,0:T(8,128)(2,1)S(1)}, u32[]{:S(2)}, u32[]{:S(2)}) collective-permute-start(bf16[32,512]{1,0:T(8,128)(2,1)S(1)} %get-tuple-element.30), channel_id=1, source_target_pairs={{0,8},{1,9},{2,10},{3,11},{4,12},{5,13},{6,14},{7,15},{8,0},{9,1},... | collective-permute-start | bytes 98312 | tf_op jit(solution)/shard_map/ppermute | solution.py:270
  62.8 2.2 %copy-start.3 = (bf16[512,4096]{1,0:T(8,128)(2,1)S(1)}, bf16[512,4096]{1,0:T(8,128)(2,1)}, u32[]{:S(2)}) copy-start(bf16[512,4096]{1,0:T(8,128)(2,1)} %copy-done.2) | copy-start | bytes 12582916
  64.9 0.9 %copy-start.9 = (bf16[512,227]{0,1:T(8,128)(2,1)S(1)}, bf16[512,227]{0,1:T(8,128)(2,1)}, u32[]{:S(2)}) copy-start(bf16[512,227]{0,1:T(8,128)(2,1)} %param.25) | copy-start | bytes 697348

commit v2 on v1

v2 whole, which is shorter than its diff:
```python
import functools

import jax
import jax.numpy as jnp
from jax import lax
from jax.experimental import pallas as pl
from jax.experimental.pallas import tpu as pltpu
from jax.sharding import PartitionSpec as P

F32 = jnp.float32
BF16 = jnp.bfloat16
MIB = 1 << 20
OWN, HALF, ODD, FAR, EVEN, NEAR = range(6)
SLOTS = 6
PAD = 16


def partner(slot, me, parts):
    chip = me // 2 % 2
    core = me % 2
    step = {
        OWN: 0,
        HALF: parts // 2,
        ODD: 4 * chip - 2,
        EVEN: 2 - 4 * chip,
        FAR: 2 * core - 1,
        NEAR: 1 - 2 * core,
    }[slot]
    return (me + step + parts) % parts


def scalar_partner(slot, me, parts):
    chip = lax.rem(lax.div(me, 2), 2)
    core = lax.rem(me, 2)
    step = {
        OWN: 0,
        HALF: parts // 2,
        ODD: 4 * chip - 2,
        EVEN: 2 - 4 * chip,
        FAR: 2 * core - 1,
        NEAR: 1 - 2 * core,
    }[slot]
    return lax.rem(me + step + parts, parts)


def silu(x):
    half = 0.5 * x
    return half + half * jnp.tanh(half)


def hot_rows(target, rows):
    ids = lax.broadcasted_iota(jnp.int32, (rows, target.shape[1]), 0)
    return jnp.where(ids == target, 1.0, 0.0).astype(BF16)


def fill_targets(parts, per_block, block_mesh, owner_ref, tgt_ref):
    wide = tgt_ref.shape[1]
    me = lax.axis_index("nodes")
    chip = lax.rem(lax.div(me, 2), 2)
    core = lax.rem(me, 2)
    up2 = EVEN + (ODD - EVEN) * chip
    up1 = NEAR + (FAR - NEAR) * core
    off = owner_ref[...] - me
    off = jnp.where(off < 0, off + parts, off)
    slot = jnp.where(off == parts // 2, HALF, OWN)
    slot = jnp.where(off == 2, up2, slot)
    slot = jnp.where(off == parts - 2, ODD + EVEN - up2, slot)
    slot = jnp.where(off == 1, up1, slot)
    slot = jnp.where(off == parts - 1, NEAR + FAR - up1, slot)
    slot = slot.astype(F32)
    groups, lanes = owner_ref.shape
    all_blocks = tgt_ref.shape[0]
    total = jnp.zeros(tgt_ref.shape, F32)
    for r in range(groups):
        tile = lax.broadcasted_iota(jnp.int32, (all_blocks, lanes), 1) + r * lanes
        first = lax.broadcasted_iota(jnp.int32, (all_blocks, lanes), 0) * per_block
        mine = (tile >= first) & (tile < first + per_block)
        picked = jnp.where(mine, slot[r : r + 1, :], 0.0).astype(BF16)
        row = lax.broadcasted_iota(jnp.int32, (lanes, wide), 0) + r * lanes
        col = lax.broadcasted_iota(jnp.int32, (lanes, wide), 1)
        place = row - per_block * ((row * (2**19 // per_block + 1)) >> 19)
        spread = jnp.where(place == col // block_mesh, 1.0, 0.0).astype(BF16)
        total += jnp.dot(picked, spread, preferred_element_type=F32)
    col = lax.broadcasted_iota(jnp.int32, tgt_ref.shape, 1)
    tgt_ref[...] = total.astype(jnp.int32) * block_mesh + col % block_mesh


def encode_kernel(
    parts, per_block, slot_ref, owner_ref, grid_ref, w_ref, enc_ref, lat_ref, tgt_ref, *rest
):
    send_refs = rest[:SLOTS]
    wt_ref, msum_ref, acc_ref = rest[SLOTS:]
    step = pl.program_id(0)
    block_mesh, block_grid = enc_ref.shape[1:]
    blocks = enc_ref.shape[0] // per_block
    wide = per_block * block_mesh
    rows = SLOTS * block_mesh
    channels, latent = w_ref.shape

    @pl.when(step == 0)
    def _():
        wt_ref[:, :channels] = w_ref[...].astype(F32).T.astype(BF16)
        fill_targets(parts, per_block, block_mesh, owner_ref, tgt_ref)
        acc_ref[...] = jnp.zeros_like(acc_ref)

    for b in range(blocks):
        hot = hot_rows(tgt_ref[pl.ds(step * blocks + b, 1), :], rows)
        tiles = enc_ref[b * per_block : (b + 1) * per_block].reshape(wide, block_grid)
        sums = jnp.dot(hot, tiles, preferred_element_type=F32)
        msum_ref[:, b * block_grid : (b + 1) * block_grid] = sums.astype(BF16)
    lat = silu(
        jnp.dot(wt_ref[:, :channels], grid_ref[...], preferred_element_type=F32)
    ).astype(BF16)
    lat_ref[...] = lat
    acc_ref[...] += lax.dot_general(
        lat, msum_ref[...], (((1,), (1,)), ((), ())), preferred_element_type=F32
    )

    @pl.when(step == pl.num_programs(0) - 1)
    def _():
        me = lax.axis_index("nodes")
        flipped = acc_ref[...].T.astype(BF16)
        for s in range(SLOTS):
            send_refs[s][:block_mesh, :] = flipped[s * block_mesh : (s + 1) * block_mesh, :]
            block = slot_ref[scalar_partner(s, me, parts)].astype(F32)
            send_refs[s][block_mesh:, :] = jnp.full((PAD, latent), block, F32).astype(BF16)


def encode(parts, slot_block, owners, grid_t, w_embed, enc_coef):
    channels, points = grid_t.shape
    latent = w_embed.shape[1]
    tiles, block_mesh, block_grid = enc_coef.shape
    grid_blocks = points // block_grid
    per_block = tiles // grid_blocks
    blocks = 4
    steps = grid_blocks // blocks
    width = blocks * block_grid
    rows = SLOTS * block_mesh
    wide = per_block * block_mesh
    return pl.pallas_call(
        functools.partial(encode_kernel, parts, per_block),
        grid=(steps,),
        in_specs=[
            pl.BlockSpec(memory_space=pltpu.SMEM),
            pl.BlockSpec(owners.shape, lambda i: (0, 0)),
            pl.BlockSpec((channels, width), lambda i: (0, i)),
            pl.BlockSpec((channels, latent), lambda i: (0, 0)),
            pl.BlockSpec((blocks * per_block, block_mesh, block_grid), lambda i: (i, 0, 0)),
        ],
        out_specs=[
            pl.BlockSpec((latent, width), lambda i: (0, i)),
            pl.BlockSpec((grid_blocks, wide), lambda i: (0, 0)),
        ]
        + [pl.BlockSpec((block_mesh + PAD, latent), lambda i: (0, 0))] * SLOTS,
        out_shape=[
            jax.ShapeDtypeStruct((latent, points), BF16),
            jax.ShapeDtypeStruct((grid_blocks, wide), jnp.int32),
        ]
        + [jax.ShapeDtypeStruct((block_mesh + PAD, latent), BF16)] * SLOTS,
        scratch_shapes=[
            pltpu.VMEM((latent, 256), BF16),
            pltpu.VMEM((rows, width), BF16),
            pltpu.VMEM((latent, rows), F32),
        ],
        compiler_params=pltpu.CompilerParams(vmem_limit_bytes=56 * MIB),
        name="encode",
    )(slot_block, owners, grid_t, w_embed, enc_coef)


def prepare_kernel(parts, per_block, adj_ref, coef_ref, tgt_ref, dec_ref, near_ref, dsum_ref):
    step = pl.program_id(0)
    block_mesh, block_grid = dec_ref.shape[1:]
    blocks = dec_ref.shape[0] // per_block
    wide = per_block * block_mesh
    rows = SLOTS * block_mesh
    for b in range(blocks):
        hot = hot_rows(tgt_ref[pl.ds(step * blocks + b, 1), :], rows)
        tiles = dec_ref[b * per_block : (b + 1) * per_block].reshape(wide, block_grid)
        sums = jnp.dot(hot, tiles, preferred_element_type=F32)
        dsum_ref[:, b * block_grid : (b + 1) * block_grid] = sums.astype(BF16)

    @pl.when(step == 0)
    def _():
        mesh_blocks, adj_width = adj_ref.shape
        me = lax.axis_index("nodes")
        core = lax.rem(me, 2)
        columns = near_ref.shape[1]
        row = lax.broadcasted_iota(jnp.int32, (block_mesh, columns), 0)
        col = lax.broadcasted_iota(jnp.int32, (block_mesh, columns), 1)
        for b in range(mesh_blocks):
            total = jnp.zeros((block_mesh, columns), F32)
            for a in range(adj_width):
                which = adj_ref[b, a]
                listed = jnp.maximum(which, 0)
                side = lax.rem(lax.div(listed, mesh_blocks) - me + 1 + parts, parts)
                side = jnp.where(core == 0, 2 - side, side)
                place = side * mesh_blocks + lax.rem(listed, mesh_blocks)
                place = jnp.where(which >= 0, place, -1)
                spot = jnp.where(col == place * block_mesh + row, 1.0, 0.0).astype(BF16)
                total += jnp.dot(coef_ref[b, a], spot, preferred_element_type=F32)
            near_ref[b * block_mesh : (b + 1) * block_mesh, :] = total.astype(BF16)


def prepare(parts, adj, coef, tgt, dec_t):
    tiles, block_mesh, block_grid = dec_t.shape
    grid_blocks, wide = tgt.shape
    per_block = tiles // grid_blocks
    mesh_blocks = adj.shape[0]
    blocks = 4
    width = blocks * block_grid
    rows = SLOTS * block_mesh
    count = mesh_blocks * block_mesh
    return pl.pallas_call(
        functools.partial(prepare_kernel, parts, per_block),
        grid=(grid_blocks // blocks,),
        in_specs=[
            pl.BlockSpec(memory_space=pltpu.SMEM),
            pl.BlockSpec(coef.shape, lambda i: (0, 0, 0, 0)),
            pl.BlockSpec(tgt.shape, lambda i: (0, 0)),
            pl.BlockSpec((blocks * per_block, block_mesh, block_grid), lambda i: (i, 0, 0)),
        ],
        out_specs=[
            pl.BlockSpec((count, 3 * count), lambda i: (0, 0)),
            pl.BlockSpec((rows, width), lambda i: (0, i)),
        ],
        out_shape=[
            jax.ShapeDtypeStruct((count, 3 * count), BF16),
            jax.ShapeDtypeStruct((rows, grid_blocks * block_grid), BF16),
        ],
        compiler_params=pltpu.CompilerParams(vmem_limit_bytes=56 * MIB),
        cost_estimate=pl.CostEstimate(
            flops=2 * rows * wide * block_grid * grid_blocks,
            bytes_accessed=2 * (tiles * block_mesh * block_grid + rows * width * 8),
            transcendentals=0,
        ),
        name="prepare",
    )(adj, coef, tgt, dec_t)


def update_kernel(*refs):
    slots = refs[:SLOTS]
    mesh_ref, w_ref, mid_ref, ids_ref = refs[SLOTS:]
    count, latent = mesh_ref.shape
    block_mesh = slots[0].shape[0] - PAD
    sums = [slot[:block_mesh, :].astype(F32) for slot in slots]
    ids = [slot[block_mesh:, :].astype(F32)[:1, :] for slot in slots]
    for s in range(SLOTS):
        ids_ref[s : s + 1, :] = ids[s]
    parts = []
    for b in range(count // block_mesh):
        total = jnp.zeros((block_mesh, latent), F32)
        for s in range(SLOTS):
            total += jnp.where(ids[s] == b, sums[s], 0.0)
        parts.append(total.astype(BF16))
    grown = jnp.dot(jnp.concatenate(parts, axis=0), w_ref[...], preferred_element_type=F32)
    mid_ref[...] = (mesh_ref[...].astype(F32) + silu(grown)).astype(BF16)


def update(slots, mesh_in, w_enc):
    vmem = pl.BlockSpec(memory_space=pltpu.VMEM)
    return pl.pallas_call(
        update_kernel,
        in_specs=[vmem] * (SLOTS + 2),
        out_specs=[vmem] * 2,
        out_shape=[
            jax.ShapeDtypeStruct(mesh_in.shape, BF16),
            jax.ShapeDtypeStruct((8, mesh_in.shape[1]), F32),
        ],
        compiler_params=pltpu.CompilerParams(vmem_limit_bytes=8 * MIB),
        name="mesh_update",
    )(*slots, mesh_in, w_enc)


def process_kernel(ids_ref, mid_ref, near_mid_ref, far_mid_ref, near_ref, gain_ref, w_ref, out_ref, *sends):
    count, latent = mid_ref.shape
    block_mesh = sends[0].shape[0]
    around = jnp.concatenate([near_mid_ref[...], mid_ref[...], far_mid_ref[...]], axis=0)
    message = jnp.dot(near_ref[...], around, preferred_element_type=F32)
    power = jnp.mean(message * message, axis=-1, keepdims=True)
    normed = (message * lax.rsqrt(power + 1e-05) * gain_ref[...]).astype(BF16)
    grown = jnp.dot(normed, w_ref[...], preferred_element_type=F32)
    grown = mid_ref[...].astype(F32) + silu(grown)
    out_ref[...] = grown.astype(BF16)
    for s in range(SLOTS):
        chosen = grown[:block_mesh, :]
        for b in range(1, count // block_mesh):
            block = grown[b * block_mesh : (b + 1) * block_mesh, :]
            chosen = jnp.where(ids_ref[s : s + 1, :] == b, block, chosen)
        sends[s][...] = chosen.astype(BF16)


def process(block_mesh, ids, mid, near_mid, far_mid, near, gain, w_proc):
    vmem = pl.BlockSpec(memory_space=pltpu.VMEM)
    latent = mid.shape[1]
    return pl.pallas_call(
        process_kernel,
        in_specs=[vmem] * 7,
        out_specs=[vmem] * (1 + SLOTS),
        out_shape=[jax.ShapeDtypeStruct(mid.shape, BF16)]
        + [jax.ShapeDtypeStruct((block_mesh, latent), BF16)] * SLOTS,
        compiler_params=pltpu.CompilerParams(vmem_limit_bytes=8 * MIB),
        name="mesh_process",
    )(ids, mid, near_mid, far_mid, near, gain, w_proc)


def decode_kernel(grid_ref, lat_ref, dsum_ref, w_ref, *rest):
    slots = rest[:SLOTS]
    out_ref, back_ref = rest[SLOTS:]

    @pl.when(pl.program_id(0) == 0)
    def _():
        joined = jnp.concatenate([slot[...] for slot in slots], axis=0)
        back_ref[...] = joined.astype(F32).T.astype(BF16)

    decoded = jnp.dot(back_ref[...], dsum_ref[...], preferred_element_type=F32)
    hidden = silu(lat_ref[...].astype(F32) + decoded).astype(BF16)
    out_ref[...] = (
        grid_ref[...].astype(F32)
        + jnp.dot(w_ref[...], hidden, preferred_element_type=F32)
    ).astype(BF16)


def decode(grid_t, lat_t, dsum, w_out_t, slots):
    channels, points = grid_t.shape
    latent = lat_t.shape[0]
    rows = dsum.shape[0]
    block_mesh = slots[0].shape[0]
    width = 512
    return pl.pallas_call(
        decode_kernel,
        grid=(points // width,),
        in_specs=[
            pl.BlockSpec((channels, width), lambda i: (0, i)),
            pl.BlockSpec((latent, width), lambda i: (0, i)),
            pl.BlockSpec((rows, width), lambda i: (0, i)),
            pl.BlockSpec((channels, latent), lambda i: (0, 0)),
        ]
        + [pl.BlockSpec((block_mesh, latent), lambda i: (0, 0))] * SLOTS,
        out_specs=pl.BlockSpec((channels, width), lambda i: (0, i)),
        out_shape=jax.ShapeDtypeStruct((channels, points), BF16),
        scratch_shapes=[pltpu.VMEM((latent, rows), BF16)],
        compiler_params=pltpu.CompilerParams(vmem_limit_bytes=56 * MIB),
        name="decode",
    )(grid_t, lat_t, dsum, w_out_t, *slots)


def local(
    grid_in, w_embed, enc_coef, enc_owner, slot_block, mesh_in, w_enc,
    proc_adj, proc_coef, proc_gain, w_proc, dec_coef, w_out,
):
    parts = lax.axis_size("nodes")
    block_mesh = enc_coef.shape[1]

    def swap(x, slot):
        pairs = [(i, partner(slot, i, parts)) for i in range(parts)]
        return lax.ppermute(x, "nodes", pairs)

    def swap_all(xs):
        return [xs[OWN]] + [swap(xs[s], s) for s in range(1, SLOTS)]

    grid_t = grid_in.T
    lat_t, tgt, *sums = encode(
        parts, slot_block, enc_owner.reshape(-1, 128), grid_t, w_embed, enc_coef
    )
    received = swap_all(sums)
    near, dsum = prepare(parts, proc_adj, proc_coef, tgt, jnp.swapaxes(dec_coef, 1, 2))
    mid, ids = update(received, mesh_in, w_enc)
    far_mid = swap(mid, FAR)
    near_mid = swap(mid, NEAR)
    mesh_out, *sends = process(
        block_mesh, ids, mid, near_mid, far_mid, near, proc_gain.reshape(1, -1), w_proc
    )
    returned = swap_all(sends)
    pred_t = decode(grid_t, lat_t, dsum, w_out.T, returned)
    return (pred_t.T, mesh_out)


def solution(mesh):
    return jax.shard_map(
        local,
        mesh=mesh,
        in_specs=(
            P(("groups", "nodes"), None),
            P(),
            P("nodes", None, None),
            P("nodes"),
            P("nodes"),
            P(("groups", "nodes"), None),
            P(),
            P("nodes", None),
            P("nodes", None, None, None),
            P(),
            P(),
            P("nodes", None, None),
            P(),
        ),
        out_specs=(P(("groups", "nodes"), None), P(("groups", "nodes"), None)),
        check_vma=False,
    )
```

time: 73.3 us -> 56.8 us (0.77)
  local copies, waits for them, and re-layouts: 20.1 us -> 2.9 us
  blocking collectives: 10 us -> 0 us
  Pallas kernels: 19 us -> 28.6 us
  starting transfers between devices: 11.6 us -> 14.7 us
  other arithmetic: 1.02 us -> 0 us
    unnamed x33 -> x24, local copies, waits for them, and re-layouts: 18.2 us -> 2.9 us
    unnamed x1 -> x0, blocking collectives: 10 us -> none
    pallas_call x2 -> x3, Pallas kernels: 4.1 us -> 8.96 us  [the longest x1 7.33 us: prepare(): pl.pallas_call(functools.partial(prepare_kernel, parts, per_block), grid=...]
    ppermute x12, starting transfers between devices: 11.6 us -> 14.7 us  [swap(): return lax.ppermute(x, 'nodes', pairs)]
    pallas_call x1, Pallas kernels: 6.78 us -> 9.61 us  [decode(): pl.pallas_call(decode_kernel, grid=(points // width,), in_specs=[pl.Block...]
    pallas_call x1, Pallas kernels: 8.08 us -> 10.1 us  [encode(): pl.pallas_call(functools.partial(encode_kernel, parts, per_block), grid=(...]
    reshape x1 -> x0, local copies, waits for them, and re-layouts: 1.16 us -> none  [local(): coef.transpose(0, 2, 1, 3)]
    transpose x1 -> x0, other arithmetic: 1.02 us -> none  [local(): coef.transpose(0, 2, 1, 3)]
  transfers between devices with their start and end apart: 12 -> 12, of which waited for: 4 -> 5; matrix products, arithmetic and copies ran while one was open for 9% -> 0% of each run, Pallas kernels for 0% -> 13%
where the time goes in v2:
time: 56.8 us; the launch traced here: 56.1 us
  Pallas kernels  28.6 us (50%)
  starting transfers between devices  14.7 us (26%)
  waiting for transfers between devices  9.09 us (16%)
  local copies, waits for them, and re-layouts  2.9 us (5%)
  between operations  0.77 us (1%)
    ppermute x12, starting transfers between devices, swap(): return lax.ppermute(x, 'nodes', pairs)  14.7 us
    pallas_call x1, Pallas kernels, encode(): pl.pallas_call(functools.partial(encode_kernel, parts, per_block), grid=(...  10.1 us
    pallas_call x1, Pallas kernels, decode(): pl.pallas_call(decode_kernel, grid=(points // width,), in_specs=[pl.Block...  9.61 us
    ppermute x12, waiting for transfers between devices, swap(): return lax.ppermute(x, 'nodes', pairs)  9.09 us
    pallas_call x1, Pallas kernels, prepare(): pl.pallas_call(functools.partial(prepare_kernel, parts, per_block), grid=...  7.33 us
    unnamed x24, local copies, waits for them, and re-layouts  2.9 us
    pallas_call x1, Pallas kernels, process(): pl.pallas_call(process_kernel, in_specs=[vmem] * 7, out_specs=[vmem] * (1...  1.3 us
  transfers between devices with their start and end apart: 12, of which 5 were waited for; matrix products, arithmetic and copies ran while one was open for 0% of the time, Pallas kernels for 13%

profile of v2, /device:TPU:0, one launch (start us, length us, event | category | flops | bytes accessed | tf_op | source)
XLA Modules:
  0.0 56.1 jit_solution(12184932201626152)
XLA Ops:
  0.6 0.0 copy-start
  0.6 0.0 copy-start.2
  0.7 0.0 copy-start.6
  0.7 10.1 %encode.1 = (bf16[512,4096]{1,0:T(8,128)(2,1)}, s32[32,384]{1,0:T(8,128)}, bf16[48,512]{1,0:T(8,128)(2,1)}, bf16[48,512]{1,0:T(8,128)(2,1)}, bf16[48,512]{1,0:T(...) custom-call(s32[16]{0:T(128)} %slot_ref.1, s32[3,128]{1,0:T(4,128)} %bitcast.12, ...), custom_call_target="tpu_custom_call" | custom-call | tf_op jit(solution)/shard_map/encode/pallas_call | solution.py:140
  10.7 0.0 copy-start.1
  10.8 4.1 %collective-permute-start = (bf16[48,512]{1,0:T(8,128)(2,1)}, bf16[48,512]{1,0:T(8,128)(2,1)S(1)}, u32[]{:S(2)}, u32[]{:S(2)}) collective-permute-start(bf16[48,512]{1,0:T(8,128)(2,1)} %get-tuple-element.25), channel_id=1, source_target_pairs={{0,8},{1,9},{2,10},{3,11},{4,12},{5,13},{6,14},{7,15},{8,0},{9,1},... | collective-permute-start | bytes 147464 | tf_op jit(solution)/shard_map/ppermute | solution.py:356
  14.9 2.3 %collective-permute-start.1 = (bf16[48,512]{1,0:T(8,128)(2,1)}, bf16[48,512]{1,0:T(8,128)(2,1)S(1)}, u32[]{:S(2)}, u32[]{:S(2)}) collective-permute-start(bf16[48,512]{1,0:T(8,128)(2,1)} %get-tuple-element.26), channel_id=1, source_target_pairs={{0,14},{1,15},{2,4},{3,5},{4,2},{5,3},{6,8},{7,9},{8,6},{9,7},{10,... | collective-permute-start | bytes 147464 | tf_op jit(solution)/shard_map/ppermute | solution.py:356
  17.2 1.3 %collective-permute-start.2 = (bf16[48,512]{1,0:T(8,128)(2,1)}, bf16[48,512]{1,0:T(8,128)(2,1)S(1)}, u32[]{:S(2)}, u32[]{:S(2)}) collective-permute-start(bf16[48,512]{1,0:T(8,128)(2,1)} %get-tuple-element.27), channel_id=1, source_target_pairs={{0,15},{1,2},{2,1},{3,4},{4,3},{5,6},{6,5},{7,8},{8,7},{9,10},{10,... | collective-permute-start | bytes 147464 | tf_op jit(solution)/shard_map/ppermute | solution.py:356
  18.5 0.0 collective-permute-start.3
  18.5 0.7 %collective-permute-start.4 = (bf16[48,512]{1,0:T(8,128)(2,1)}, bf16[48,512]{1,0:T(8,128)(2,1)S(1)}, u32[]{:S(2)}, u32[]{:S(2)}) collective-permute-start(bf16[48,512]{1,0:T(8,128)(2,1)} %get-tuple-element.29), channel_id=1, source_target_pairs={{0,1},{1,0},{2,3},{3,2},{4,5},{5,4},{6,7},{7,6},{8,9},{9,8},{10,11... | collective-permute-start | bytes 147464 | tf_op jit(solution)/shard_map/ppermute | solution.py:356
  19.1 0.0 collective-permute-done.refs_1_
  19.1 2.8 %collective-permute-done.1.refs_2_ = bf16[48,512]{1,0:T(8,128)(2,1)S(1)} collective-permute-done((bf16[48,512]{1,0:T(8,128)(2,1)}, bf16[48,512]{1,0:T(8,128)(2,1)S(1)}, u32[]{:S(2)}, u32[]{:S(2)}) %collective-permute-start.1) | collective-permute-done | bytes 49184 | tf_op jit(solution)/shard_map/ppermute | solution.py:356
  21.9 1.6 %collective-permute-done.2.refs_3_ = bf16[48,512]{1,0:T(8,128)(2,1)S(1)} collective-permute-done((bf16[48,512]{1,0:T(8,128)(2,1)}, bf16[48,512]{1,0:T(8,128)(2,1)S(1)}, u32[]{:S(2)}, u32[]{:S(2)}) %collective-permute-start.2) | collective-permute-done | bytes 49184 | tf_op jit(solution)/shard_map/ppermute | solution.py:356
  23.6 0.0 collective-permute-done.3.refs_4_
  23.6 0.0 collective-permute-done.4.refs_5_
  23.6 0.0 copy-done
  23.6 0.0 copy-done.2
  23.6 0.0 copy-start.4
  23.6 0.8 %copy-done.4 = bf16[48,512]{1,0:T(8,128)(2,1)S(1)} copy-done((bf16[48,512]{1,0:T(8,128)(2,1)S(1)}, bf16[48,512]{1,0:T(8,128)(2,1)}, u32[]{:S(2)}) %copy-start.4) | copy-done | bytes 49176
  24.4 0.3 mesh_update.1
  24.8 1.8 %collective-permute-start.6 = (bf16[128,512]{1,0:T(8,128)(2,1)S(1)}, bf16[128,512]{1,0:T(8,128)(2,1)S(1)}, u32[]{:S(2)}, u32[]{:S(2)}) collective-permute-start(bf16[128,512]{1,0:T(8,128)(2,1)S(1)} %get-tuple-element.31.mid_ref), channel_id=1, source_target_pairs={{0,15},{1,2},{2,1},{3,4},{4,3},{5,6},{6,5},{7,8},{8,7},{9,10},{10,... | collective-permute-start | bytes 393224 | tf_op jit(solution)/shard_map/ppermute | solution.py:356
  26.5 0.0 collective-permute-start.5
  26.5 7.3 %prepare.1 = (bf16[128,384]{1,0:T(8,128)(2,1)}, bf16[192,4096]{1,0:T(8,128)(2,1)}) custom-call(s32[4,6]{1,0:T(4,128)} %adj_ref.1, bf16[4,6,32,32]{3,2,1,0:T(8,128)(2,1)} %coef_ref.1, s32[32,384]{1,0:T(8,128)} %get-tuple-element.22.tgt_ref, bf16[384,32,128]{2,1,0:T(8,128)(2,1)} %bitcast.9), custom_call_target="tpu_custom_call" | custom-call | flops 603979776 | bytes 4718592 | tf_op jit(solution)/shard_map/prepare/pallas_call | solution.py:213
  33.8 0.0 collective-permute-done.6.far_mid_ref
  33.8 0.0 collective-permute-done.5.near_mid_ref
  33.8 0.0 copy-done.6
  33.9 0.0 copy-done.1
  33.9 0.0 copy-start.3
  33.9 0.9 %copy-done.3 = bf16[128,384]{1,0:T(8,128)(2,1)S(1)} copy-done((bf16[128,384]{1,0:T(8,128)(2,1)S(1)}, bf16[128,384]{1,0:T(8,128)(2,1)}, u32[]{:S(2)}) %copy-start.3) | copy-done | bytes 98328
  34.8 1.3 %mesh_process.1 = (bf16[128,512]{1,0:T(8,128)(2,1)}, bf16[32,512]{1,0:T(8,128)(2,1)S(1)}, bf16[32,512]{1,0:T(8,128)(2,1)S(1)}, bf16[32,512]{1,0:T(8,128)(2,1)S(1...) custom-call(f32[8,512]{1,0:T(8,128)S(1)} %get-tuple-element.30.ids_ref, ...), custom_call_target="tpu_custom_call" | custom-call | tf_op jit(solution)/shard_map/mesh_process/pallas_call | solution.py:295
  36.1 0.6 %copy-done.5 = bf16[32,512]{1,0:T(8,128)(2,1)} copy-done((bf16[32,512]{1,0:T(8,128)(2,1)}, bf16[32,512]{1,0:T(8,128)(2,1)S(1)}, u32[]{:S(2)}) %copy-start.5) | copy-done | bytes 32792
  36.7 0.0 collective-permute-start.7
  36.7 3.1 %collective-permute-start.8 = (bf16[32,512]{1,0:T(8,128)(2,1)S(1)}, bf16[32,512]{1,0:T(8,128)(2,1)S(1)}, u32[]{:S(2)}, u32[]{:S(2)}) collective-permute-start(bf16[32,512]{1,0:T(8,128)(2,1)S(1)} %get-tuple-element.35), channel_id=1, source_target_pairs={{0,14},{1,15},{2,4},{3,5},{4,2},{5,3},{6,8},{7,9},{8,6},{9,7},{10,... | collective-permute-start | bytes 98312 | tf_op jit(solution)/shard_map/ppermute | solution.py:356
  39.8 1.4 %collective-permute-start.9 = (bf16[32,512]{1,0:T(8,128)(2,1)S(1)}, bf16[32,512]{1,0:T(8,128)(2,1)S(1)}, u32[]{:S(2)}, u32[]{:S(2)}) collective-permute-start(bf16[32,512]{1,0:T(8,128)(2,1)S(1)} %get-tuple-element.36), channel_id=1, source_target_pairs={{0,15},{1,2},{2,1},{3,4},{4,3},{5,6},{6,5},{7,8},{8,7},{9,10},{10,... | collective-permute-start | bytes 98312 | tf_op jit(solution)/shard_map/ppermute | solution.py:356
  41.2 0.0 collective-permute-start.10
  41.2 0.0 collective-permute-start.11
  41.2 0.3 collective-permute-done.7.rest_1_
  41.5 1.8 %collective-permute-done.8.rest_2_ = bf16[32,512]{1,0:T(8,128)(2,1)S(1)} collective-permute-done((bf16[32,512]{1,0:T(8,128)(2,1)S(1)}, bf16[32,512]{1,0:T(8,128)(2,1)S(1)}, u32[]{:S(2)}, u32[]{:S(2)}) %collective-permute-start.8) | collective-permute-done | bytes 32800 | tf_op jit(solution)/shard_map/ppermute | solution.py:356
  43.3 2.5 %collective-permute-done.9.rest_3_ = bf16[32,512]{1,0:T(8,128)(2,1)S(1)} collective-permute-done((bf16[32,512]{1,0:T(8,128)(2,1)S(1)}, bf16[32,512]{1,0:T(8,128)(2,1)S(1)}, u32[]{:S(2)}, u32[]{:S(2)}) %collective-permute-start.9) | collective-permute-done | bytes 32800 | tf_op jit(solution)/shard_map/ppermute | solution.py:356
  45.8 0.0 collective-permute-done.10.rest_4_
  45.8 0.0 collective-permute-done.11.rest_5_
  45.9 0.0 copy-start.11
  45.9 0.0 copy-done.7
  45.9 0.0 copy-done.8
  45.9 0.6 copy-done.9
  46.4 0.0 copy-done.10
  46.5 0.0 copy-done.11
  46.5 9.6 %decode.1 = bf16[227,4096]{1,0:T(8,128)(2,1)} custom-call(bf16[227,4096]{1,0:T(8,128)(2,1)} %bitcast.8, bf16[512,4096]{1,0:T(8,128)(2,1)} %get-tuple-element.21.lat_ref, bf16[192,4096]{1,0:T(8,128)(2,1)} %get-tuple-element.23.dsum_ref, bf16[227,512]{1,0:T(8,128)(2,1)} %bitcast.11, bf16[32,512]{1,0:T(8,128)(2,1)} %copy-done.5, bf16[32,512]{1,0:T(8,128)(2,1)} %copy-done.7, ...), custom_call_target="tpu_custom_call" | custom-call | tf_op jit(solution)/shard_map/decode/pallas_call | solution.py:329
  (5 shorter events, 0.0 us)
Async XLA Ops:
  0.6 23.0 %copy-start = (bf16[512,512]{1,0:T(8,128)(2,1)S(1)}, bf16[512,512]{1,0:T(8,128)(2,1)}, u32[]{:S(2)}) copy-start(bf16[512,512]{1,0:T(8,128)(2,1)} %refs_7_.1) | copy-start | bytes 1572868
  0.6 23.0 %copy-start.2 = (bf16[128,512]{1,0:T(8,128)(2,1)S(1)}, bf16[128,512]{1,0:T(8,128)(2,1)}, u32[]{:S(2)}) copy-start(bf16[128,512]{1,0:T(8,128)(2,1)} %refs_6_.1) | copy-start | bytes 393220
  0.7 33.2 %copy-start.6 = (f32[512]{0:T(512)S(1)}, f32[512]{0:T(512)}, u32[]{:S(2)}) copy-start(f32[512]{0:T(512)} %param.22) | copy-start | bytes 6148
  10.7 23.1 %copy-start.1 = (bf16[512,512]{1,0:T(8,128)(2,1)S(1)}, bf16[512,512]{1,0:T(8,128)(2,1)}, u32[]{:S(2)}) copy-start(bf16[512,512]{1,0:T(8,128)(2,1)} %w_ref.3) | copy-start | bytes 1572868
  10.8 8.4 %collective-permute-start = (bf16[48,512]{1,0:T(8,128)(2,1)}, bf16[48,512]{1,0:T(8,128)(2,1)S(1)}, u32[]{:S(2)}, u32[]{:S(2)}) collective-permute-start(bf16[48,512]{1,0:T(8,128)(2,1)} %get-tuple-element.25), channel_id=1, source_target_pairs={{0,8},{1,9},{2,10},{3,11},{4,12},{5,13},{6,14},{7,15},{8,0},{9,1},... | collective-permute-start | bytes 147464 | tf_op jit(solution)/shard_map/ppermute | solution.py:356
  14.9 7.1 %collective-permute-start.1 = (bf16[48,512]{1,0:T(8,128)(2,1)}, bf16[48,512]{1,0:T(8,128)(2,1)S(1)}, u32[]{:S(2)}, u32[]{:S(2)}) collective-permute-start(bf16[48,512]{1,0:T(8,128)(2,1)} %get-tuple-element.26), channel_id=1, source_target_pairs={{0,14},{1,15},{2,4},{3,5},{4,2},{5,3},{6,8},{7,9},{8,6},{9,7},{10,... | collective-permute-start | bytes 147464 | tf_op jit(solution)/shard_map/ppermute | solution.py:356
  17.2 6.4 %collective-permute-start.2 = (bf16[48,512]{1,0:T(8,128)(2,1)}, bf16[48,512]{1,0:T(8,128)(2,1)S(1)}, u32[]{:S(2)}, u32[]{:S(2)}) collective-permute-start(bf16[48,512]{1,0:T(8,128)(2,1)} %get-tuple-element.27), channel_id=1, source_target_pairs={{0,15},{1,2},{2,1},{3,4},{4,3},{5,6},{6,5},{7,8},{8,7},{9,10},{10,... | collective-permute-start | bytes 147464 | tf_op jit(solution)/shard_map/ppermute | solution.py:356
  18.5 5.1 %collective-permute-start.3 = (bf16[48,512]{1,0:T(8,128)(2,1)}, bf16[48,512]{1,0:T(8,128)(2,1)S(1)}, u32[]{:S(2)}, u32[]{:S(2)}) collective-permute-start(bf16[48,512]{1,0:T(8,128)(2,1)} %get-tuple-element.28), channel_id=1, source_target_pairs={{0,2},{1,3},{2,0},{3,1},{4,6},{5,7},{6,4},{7,5},{8,10},{9,11},{10,... | collective-permute-start | bytes 147464 | tf_op jit(solution)/shard_map/ppermute | solution.py:356
  18.5 5.1 %collective-permute-start.4 = (bf16[48,512]{1,0:T(8,128)(2,1)}, bf16[48,512]{1,0:T(8,128)(2,1)S(1)}, u32[]{:S(2)}, u32[]{:S(2)}) collective-permute-start(bf16[48,512]{1,0:T(8,128)(2,1)} %get-tuple-element.29), channel_id=1, source_target_pairs={{0,1},{1,0},{2,3},{3,2},{4,5},{5,4},{6,7},{7,6},{8,9},{9,8},{10,11... | collective-permute-start | bytes 147464 | tf_op jit(solution)/shard_map/ppermute | solution.py:356
  23.6 0.8 %copy-start.4 = (bf16[48,512]{1,0:T(8,128)(2,1)S(1)}, bf16[48,512]{1,0:T(8,128)(2,1)}, u32[]{:S(2)}) copy-start(bf16[48,512]{1,0:T(8,128)(2,1)} %get-tuple-element.24.refs_0_) | copy-start | bytes 147460
  24.8 9.1 %collective-permute-start.6 = (bf16[128,512]{1,0:T(8,128)(2,1)S(1)}, bf16[128,512]{1,0:T(8,128)(2,1)S(1)}, u32[]{:S(2)}, u32[]{:S(2)}) collective-permute-start(bf16[128,512]{1,0:T(8,128)(2,1)S(1)} %get-tuple-element.31.mid_ref), channel_id=1, source_target_pairs={{0,15},{1,2},{2,1},{3,4},{4,3},{5,6},{6,5},{7,8},{8,7},{9,10},{10,... | collective-permute-start | bytes 393224 | tf_op jit(solution)/shard_map/ppermute | solution.py:356
  26.5 7.3 %collective-permute-start.5 = (bf16[128,512]{1,0:T(8,128)(2,1)S(1)}, bf16[128,512]{1,0:T(8,128)(2,1)S(1)}, u32[]{:S(2)}, u32[]{:S(2)}) collective-permute-start(bf16[128,512]{1,0:T(8,128)(2,1)S(1)} %get-tuple-element.31.mid_ref), channel_id=1, source_target_pairs={{0,1},{1,0},{2,3},{3,2},{4,5},{5,4},{6,7},{7,6},{8,9},{9,8},{10,11... | collective-permute-start | bytes 393224 | tf_op jit(solution)/shard_map/ppermute | solution.py:356
  33.9 0.9 %copy-start.3 = (bf16[128,384]{1,0:T(8,128)(2,1)S(1)}, bf16[128,384]{1,0:T(8,128)(2,1)}, u32[]{:S(2)}) copy-start(bf16[128,384]{1,0:T(8,128)(2,1)} %get-tuple-element.32.near_ref) | copy-start | bytes 294916
  36.1 0.6 %copy-start.5 = (bf16[32,512]{1,0:T(8,128)(2,1)}, bf16[32,512]{1,0:T(8,128)(2,1)S(1)}, u32[]{:S(2)}) copy-start(bf16[32,512]{1,0:T(8,128)(2,1)S(1)} %get-tuple-element.33.rest_0_) | copy-start | bytes 98308
  36.7 4.8 %collective-permute-start.7 = (bf16[32,512]{1,0:T(8,128)(2,1)S(1)}, bf16[32,512]{1,0:T(8,128)(2,1)S(1)}, u32[]{:S(2)}, u32[]{:S(2)}) collective-permute-start(bf16[32,512]{1,0:T(8,128)(2,1)S(1)} %get-tuple-element.34), channel_id=1, source_target_pairs={{0,8},{1,9},{2,10},{3,11},{4,12},{5,13},{6,14},{7,15},{8,0},{9,1},... | collective-permute-start | bytes 98312 | tf_op jit(solution)/shard_map/ppermute | solution.py:356
  36.7 6.7 %collective-permute-start.8 = (bf16[32,512]{1,0:T(8,128)(2,1)S(1)}, bf16[32,512]{1,0:T(8,128)(2,1)S(1)}, u32[]{:S(2)}, u32[]{:S(2)}) collective-permute-start(bf16[32,512]{1,0:T(8,128)(2,1)S(1)} %get-tuple-element.35), channel_id=1, source_target_pairs={{0,14},{1,15},{2,4},{3,5},{4,2},{5,3},{6,8},{7,9},{8,6},{9,7},{10,... | collective-permute-start | bytes 98312 | tf_op jit(solution)/shard_map/ppermute | solution.py:356
  39.8 6.0 %collective-permute-start.9 = (bf16[32,512]{1,0:T(8,128)(2,1)S(1)}, bf16[32,512]{1,0:T(8,128)(2,1)S(1)}, u32[]{:S(2)}, u32[]{:S(2)}) collective-permute-start(bf16[32,512]{1,0:T(8,128)(2,1)S(1)} %get-tuple-element.36), channel_id=1, source_target_pairs={{0,15},{1,2},{2,1},{3,4},{4,3},{5,6},{6,5},{7,8},{8,7},{9,10},{10,... | collective-permute-start | bytes 98312 | tf_op jit(solution)/shard_map/ppermute | solution.py:356
  41.2 4.6 %collective-permute-start.10 = (bf16[32,512]{1,0:T(8,128)(2,1)S(1)}, bf16[32,512]{1,0:T(8,128)(2,1)S(1)}, u32[]{:S(2)}, u32[]{:S(2)}) collective-permute-start(bf16[32,512]{1,0:T(8,128)(2,1)S(1)} %get-tuple-element.37), channel_id=1, source_target_pairs={{0,2},{1,3},{2,0},{3,1},{4,6},{5,7},{6,4},{7,5},{8,10},{9,11},{10,... | collective-permute-start | bytes 98312 | tf_op jit(solution)/shard_map/ppermute | solution.py:356
  41.2 4.6 %collective-permute-start.11 = (bf16[32,512]{1,0:T(8,128)(2,1)S(1)}, bf16[32,512]{1,0:T(8,128)(2,1)S(1)}, u32[]{:S(2)}, u32[]{:S(2)}) collective-permute-start(bf16[32,512]{1,0:T(8,128)(2,1)S(1)} %get-tuple-element.38), channel_id=1, source_target_pairs={{0,1},{1,0},{2,3},{3,2},{4,5},{5,4},{6,7},{7,6},{8,9},{9,8},{10,11... | collective-permute-start | bytes 98312 | tf_op jit(solution)/shard_map/ppermute | solution.py:356
  41.5 4.4 %copy-start.7 = (bf16[32,512]{1,0:T(8,128)(2,1)}, bf16[32,512]{1,0:T(8,128)(2,1)S(1)}, u32[]{:S(2)}) copy-start(bf16[32,512]{1,0:T(8,128)(2,1)S(1)} %collective-permute-done.7.rest_1_) | copy-start | bytes 98308
  43.3 2.6 %copy-start.8 = (bf16[32,512]{1,0:T(8,128)(2,1)}, bf16[32,512]{1,0:T(8,128)(2,1)S(1)}, u32[]{:S(2)}) copy-start(bf16[32,512]{1,0:T(8,128)(2,1)S(1)} %collective-permute-done.8.rest_2_) | copy-start | bytes 98308
  45.8 0.6 %copy-start.9 = (bf16[32,512]{1,0:T(8,128)(2,1)}, bf16[32,512]{1,0:T(8,128)(2,1)S(1)}, u32[]{:S(2)}) copy-start(bf16[32,512]{1,0:T(8,128)(2,1)S(1)} %collective-permute-done.9.rest_3_) | copy-start | bytes 98308
  45.8 0.6 %copy-start.10 = (bf16[32,512]{1,0:T(8,128)(2,1)}, bf16[32,512]{1,0:T(8,128)(2,1)S(1)}, u32[]{:S(2)}) copy-start(bf16[32,512]{1,0:T(8,128)(2,1)S(1)} %collective-permute-done.10.rest_4_) | copy-start | bytes 98308
  45.9 0.6 %copy-start.11 = (bf16[32,512]{1,0:T(8,128)(2,1)}, bf16[32,512]{1,0:T(8,128)(2,1)S(1)}, u32[]{:S(2)}) copy-start(bf16[32,512]{1,0:T(8,128)(2,1)S(1)} %collective-permute-done.11.rest_5_) | copy-start | bytes 98308

commit v3 on v2

v3 whole, which is shorter than its diff:
```python
import functools

import jax
import jax.numpy as jnp
from jax import lax
from jax.experimental import pallas as pl
from jax.experimental.pallas import tpu as pltpu
from jax.sharding import PartitionSpec as P

F32 = jnp.float32
BF16 = jnp.bfloat16
MIB = 1 << 20
OWN, HALF, ODD, FAR, EVEN, NEAR = range(6)
SLOTS = 6
PAD = 128


def partner(slot, me, parts):
    chip = me // 2 % 2
    core = me % 2
    step = {
        OWN: 0,
        HALF: parts // 2,
        ODD: 4 * chip - 2,
        EVEN: 2 - 4 * chip,
        FAR: 2 * core - 1,
        NEAR: 1 - 2 * core,
    }[slot]
    return (me + step + parts) % parts


def scalar_partner(slot, me, parts):
    chip = lax.rem(lax.div(me, 2), 2)
    core = lax.rem(me, 2)
    step = {
        OWN: 0,
        HALF: parts // 2,
        ODD: 4 * chip - 2,
        EVEN: 2 - 4 * chip,
        FAR: 2 * core - 1,
        NEAR: 1 - 2 * core,
    }[slot]
    return lax.rem(me + step + parts, parts)


def silu(x):
    half = 0.5 * x
    return half + half * jnp.tanh(half)


def hot_rows(ids, target):
    lanes = ids.shape[1]
    target = target.astype(BF16)
    one, zero = jnp.ones((), BF16), jnp.zeros((), BF16)
    return jnp.concatenate(
        [
            jnp.where(ids == target[:, at : at + lanes], one, zero)
            for at in range(0, target.shape[1], lanes)
        ],
        axis=1,
    )


def fill_targets(parts, per_block, block_mesh, owner_ref, tgt_ref):
    wide = tgt_ref.shape[1]
    me = lax.axis_index("nodes")
    chip = lax.rem(lax.div(me, 2), 2)
    core = lax.rem(me, 2)
    up2 = EVEN + (ODD - EVEN) * chip
    up1 = NEAR + (FAR - NEAR) * core
    off = owner_ref[...] - me
    off = jnp.where(off < 0, off + parts, off)
    slot = jnp.where(off == parts // 2, HALF, OWN)
    slot = jnp.where(off == 2, up2, slot)
    slot = jnp.where(off == parts - 2, ODD + EVEN - up2, slot)
    slot = jnp.where(off == 1, up1, slot)
    slot = jnp.where(off == parts - 1, NEAR + FAR - up1, slot)
    slot = slot.astype(F32)
    groups, lanes = owner_ref.shape
    all_blocks = tgt_ref.shape[0]
    total = jnp.zeros(tgt_ref.shape, F32)
    for r in range(groups):
        tile = lax.broadcasted_iota(jnp.int32, (all_blocks, lanes), 1) + r * lanes
        first = lax.broadcasted_iota(jnp.int32, (all_blocks, lanes), 0) * per_block
        mine = (tile >= first) & (tile < first + per_block)
        picked = jnp.where(mine, slot[r : r + 1, :], 0.0).astype(BF16)
        row = lax.broadcasted_iota(jnp.int32, (lanes, wide), 0) + r * lanes
        col = lax.broadcasted_iota(jnp.int32, (lanes, wide), 1)
        place = row - per_block * ((row * (2**19 // per_block + 1)) >> 19)
        spread = jnp.where(place == col // block_mesh, 1.0, 0.0).astype(BF16)
        total += jnp.dot(picked, spread, preferred_element_type=F32)
    col = lax.broadcasted_iota(jnp.int32, tgt_ref.shape, 1)
    tgt_ref[...] = total * block_mesh + (col % block_mesh).astype(F32)


def encode_kernel(
    parts, width, slot_hbm, owner_hbm, w_hbm, grid_hbm, enc_hbm, dec_hbm,
    lat_ref, dsum_ref, grid_ref, *rest,
):
    send_refs = rest[:SLOTS]
    (
        slot_ref, owner_ref, w_ref, enc_ref, dec_ref, wt_ref, tgt_ref, ids_ref, msum_ref,
        acc_ref, small_sems, sems,
    ) = rest[SLOTS:]
    tiles, block_mesh, block_grid = enc_ref.shape
    channels, points = grid_ref.shape
    latent = w_ref.shape[1]
    per_block = tiles * block_grid // points
    blocks = width // block_grid
    chunk = blocks * per_block
    steps = points // width
    wide = per_block * block_mesh
    rows = SLOTS * block_mesh

    def copies(step):
        cols = pl.ds(pl.multiple_of(step * width, width), width)
        some = pl.ds(step * chunk, chunk)
        return (
            pltpu.make_async_copy(grid_hbm.at[:, cols], grid_ref.at[:, cols], sems.at[0, step]),
            pltpu.make_async_copy(enc_hbm.at[some], enc_ref.at[some], sems.at[1, step]),
            pltpu.make_async_copy(dec_hbm.at[some], dec_ref.at[some], sems.at[2, step]),
        )

    small = [
        pltpu.make_async_copy(source, target, small_sems.at[i])
        for i, (source, target) in enumerate(
            ((owner_hbm, owner_ref), (w_hbm, w_ref), (slot_hbm, slot_ref))
        )
    ]
    for copy in small:
        copy.start()
    for step in range(steps):
        for copy in copies(step):
            copy.start()
    for copy in small:
        copy.wait()
    wt_ref[:, :channels] = w_ref[...].astype(F32).T.astype(BF16)
    fill_targets(parts, per_block, block_mesh, owner_ref, tgt_ref)
    ids_ref[...] = lax.broadcasted_iota(jnp.int32, ids_ref.shape, 0).astype(BF16)
    acc_ref[...] = jnp.zeros_like(acc_ref)

    @pl.loop(0, steps)
    def _(step):
        for copy in copies(step):
            copy.wait()
        cols = pl.ds(pl.multiple_of(step * width, width), width)
        for b in range(blocks):
            hot = hot_rows(ids_ref[...], tgt_ref[pl.ds(step * blocks + b, 1), :])
            some = pl.ds(step * chunk + b * per_block, per_block)
            both = jnp.concatenate(
                [
                    enc_ref[some].reshape(wide, block_grid),
                    dec_ref[some].reshape(wide, block_grid),
                ],
                axis=1,
            )
            sums = jnp.dot(hot, both, preferred_element_type=F32).astype(BF16)
            msum_ref[:, b * block_grid : (b + 1) * block_grid] = sums[:, :block_grid]
            first = pl.multiple_of((step * blocks + b) * block_grid, block_grid)
            dsum_ref[:, pl.ds(first, block_grid)] = sums[:, block_grid:]
        lat = silu(
            jnp.dot(wt_ref[:, :channels], grid_ref[:, cols], preferred_element_type=F32)
        ).astype(BF16)
        lat_ref[:, cols] = lat
        acc_ref[...] += lax.dot_general(
            lat, msum_ref[...], (((1,), (1,)), ((), ())), preferred_element_type=F32
        )

    me = lax.axis_index("nodes")
    flipped = acc_ref[...].T.astype(BF16)
    for s in range(SLOTS):
        send_refs[s][:, :latent] = flipped[s * block_mesh : (s + 1) * block_mesh, :]
        block = slot_ref[scalar_partner(s, me, parts)].astype(F32)
        send_refs[s][:, latent:] = jnp.full((block_mesh, PAD), block, F32).astype(BF16)


def encode(parts, slot_block, owners, grid_t, w_embed, enc_coef, dec_t):
    channels, points = grid_t.shape
    latent = w_embed.shape[1]
    tiles, block_mesh, block_grid = enc_coef.shape
    grid_blocks = points // block_grid
    width = 512
    steps = points // width
    rows = SLOTS * block_mesh
    wide = tiles // grid_blocks * block_mesh
    vmem = pl.BlockSpec(memory_space=pltpu.VMEM)
    hbm = pl.BlockSpec(memory_space=pl.ANY)
    return pl.pallas_call(
        functools.partial(encode_kernel, parts, width),
        in_specs=[hbm] * 6,
        out_specs=[vmem] * (3 + SLOTS),
        out_shape=[
            pltpu.VMEM((latent, points), BF16),
            pltpu.VMEM((rows, points), BF16),
            pltpu.VMEM((channels, points), BF16),
        ]
        + [jax.ShapeDtypeStruct((block_mesh, latent + PAD), BF16)] * SLOTS,
        scratch_shapes=[
            pltpu.SMEM(slot_block.shape, jnp.int32),
            pltpu.VMEM(owners.shape, jnp.int32),
            pltpu.VMEM(w_embed.shape, BF16),
            pltpu.VMEM(enc_coef.shape, BF16),
            pltpu.VMEM(dec_t.shape, BF16),
            pltpu.VMEM((latent, 256), BF16),
            pltpu.VMEM((grid_blocks, wide), F32),
            pltpu.VMEM((rows, 128), BF16),
            pltpu.VMEM((rows, width), BF16),
            pltpu.VMEM((latent, rows), F32),
            pltpu.SemaphoreType.DMA((3,)),
            pltpu.SemaphoreType.DMA((3, steps)),
        ],
        compiler_params=pltpu.CompilerParams(vmem_limit_bytes=24 * MIB),
        name="encode",
    )(
        *(
            pltpu.with_memory_space_constraint(x, pltpu.HBM)
            for x in (slot_block, owners, w_embed, grid_t, enc_coef, dec_t)
        )
    )


def prepare_kernel(parts, adj_ref, coef_ref, after_ref, near_ref):
    mesh_blocks, adj_width = adj_ref.shape
    block_mesh = coef_ref.shape[2]
    me = lax.axis_index("nodes")
    core = lax.rem(me, 2)
    columns = near_ref.shape[1]
    row = lax.broadcasted_iota(jnp.int32, (block_mesh, columns), 0)
    col = lax.broadcasted_iota(jnp.int32, (block_mesh, columns), 1)
    for b in range(mesh_blocks):
        total = jnp.zeros((block_mesh, columns), F32)
        for a in range(adj_width):
            which = adj_ref[b, a]
            listed = jnp.maximum(which, 0)
            side = lax.rem(lax.div(listed, mesh_blocks) - me + 1 + parts, parts)
            side = jnp.where(core == 0, 2 - side, side)
            place = side * mesh_blocks + lax.rem(listed, mesh_blocks)
            place = jnp.where(which >= 0, place, -columns)
            spot = jnp.where(col == place * block_mesh + row, 1.0, 0.0).astype(BF16)
            total += jnp.dot(coef_ref[b, a], spot, preferred_element_type=F32)
        near_ref[b * block_mesh : (b + 1) * block_mesh, :] = total.astype(BF16)


def prepare(parts, adj, coef, after):
    mesh_blocks, adj_width, block_mesh, _ = coef.shape
    count = mesh_blocks * block_mesh
    vmem = pl.BlockSpec(memory_space=pltpu.VMEM)
    return pl.pallas_call(
        functools.partial(prepare_kernel, parts),
        in_specs=[pl.BlockSpec(memory_space=pltpu.SMEM), vmem, vmem],
        out_specs=vmem,
        out_shape=jax.ShapeDtypeStruct((count, 3 * count), BF16),
        compiler_params=pltpu.CompilerParams(vmem_limit_bytes=8 * MIB),
        cost_estimate=pl.CostEstimate(
            flops=2 * adj_width * count * block_mesh * 3 * count,
            bytes_accessed=8 * count * 3 * count,
            transcendentals=0,
        ),
        name="prepare",
    )(adj, coef, after)


def update_kernel(*refs):
    slots = refs[:SLOTS]
    mesh_ref, w_ref, mid_ref, ids_ref = refs[SLOTS:]
    count, latent = mesh_ref.shape
    block_mesh = slots[0].shape[0]
    sums = [slot[:, :latent].astype(F32) for slot in slots]
    ids = [slot[:, latent:].astype(F32)[:1, :1] for slot in slots]
    for s in range(SLOTS):
        ids_ref[s : s + 1, :] = jnp.broadcast_to(ids[s], (1, latent))
    parts = []
    for b in range(count // block_mesh):
        total = jnp.zeros((block_mesh, latent), F32)
        for s in range(SLOTS):
            total += jnp.where(ids[s] == b, sums[s], 0.0)
        parts.append(total.astype(BF16))
    grown = jnp.dot(jnp.concatenate(parts, axis=0), w_ref[...], preferred_element_type=F32)
    mid_ref[...] = (mesh_ref[...].astype(F32) + silu(grown)).astype(BF16)


def update(slots, mesh_in, w_enc):
    vmem = pl.BlockSpec(memory_space=pltpu.VMEM)
    return pl.pallas_call(
        update_kernel,
        in_specs=[vmem] * (SLOTS + 2),
        out_specs=[vmem] * 2,
        out_shape=[
            jax.ShapeDtypeStruct(mesh_in.shape, BF16),
            jax.ShapeDtypeStruct((8, mesh_in.shape[1]), F32),
        ],
        compiler_params=pltpu.CompilerParams(vmem_limit_bytes=8 * MIB),
        name="mesh_update",
    )(*slots, mesh_in, w_enc)


def process_kernel(ids_ref, mid_ref, near_mid_ref, far_mid_ref, near_ref, gain_ref, w_ref, out_ref, *sends):
    count, latent = mid_ref.shape
    block_mesh = sends[0].shape[0]
    around = jnp.concatenate([near_mid_ref[...], mid_ref[...], far_mid_ref[...]], axis=0)
    message = jnp.dot(near_ref[...], around, preferred_element_type=F32)
    power = jnp.mean(message * message, axis=-1, keepdims=True)
    normed = (message * lax.rsqrt(power + 1e-05) * gain_ref[...]).astype(BF16)
    grown = jnp.dot(normed, w_ref[...], preferred_element_type=F32)
    grown = mid_ref[...].astype(F32) + silu(grown)
    out_ref[...] = grown.astype(BF16)
    for s in range(SLOTS):
        chosen = grown[:block_mesh, :]
        for b in range(1, count // block_mesh):
            block = grown[b * block_mesh : (b + 1) * block_mesh, :]
            chosen = jnp.where(ids_ref[s : s + 1, :] == b, block, chosen)
        sends[s][...] = chosen.astype(BF16)


def process(block_mesh, ids, mid, near_mid, far_mid, near, gain, w_proc):
    vmem = pl.BlockSpec(memory_space=pltpu.VMEM)
    latent = mid.shape[1]
    return pl.pallas_call(
        process_kernel,
        in_specs=[vmem] * 7,
        out_specs=[vmem] * (1 + SLOTS),
        out_shape=[jax.ShapeDtypeStruct(mid.shape, BF16)]
        + [jax.ShapeDtypeStruct((block_mesh, latent), BF16)] * SLOTS,
        compiler_params=pltpu.CompilerParams(vmem_limit_bytes=8 * MIB),
        name="mesh_process",
    )(ids, mid, near_mid, far_mid, near, gain, w_proc)


def decode_kernel(width, grid_ref, lat_ref, dsum_ref, w_ref, *rest):
    slots = rest[:SLOTS]
    out_hbm, back_ref, pred_ref, sems = rest[SLOTS:]
    steps = grid_ref.shape[1] // width

    def copy_out(step):
        cols = pl.ds(pl.multiple_of(step * width, width), width)
        return pltpu.make_async_copy(pred_ref.at[:, cols], out_hbm.at[:, cols], sems.at[step])

    joined = jnp.concatenate([slot[...] for slot in slots], axis=0)
    back_ref[...] = joined.astype(F32).T.astype(BF16)

    @pl.loop(0, steps)
    def _(step):
        cols = pl.ds(pl.multiple_of(step * width, width), width)
        decoded = jnp.dot(back_ref[...], dsum_ref[:, cols], preferred_element_type=F32)
        hidden = silu(lat_ref[:, cols].astype(F32) + decoded).astype(BF16)
        pred_ref[:, cols] = (
            grid_ref[:, cols].astype(F32)
            + jnp.dot(w_ref[...], hidden, preferred_element_type=F32)
        ).astype(BF16)
        copy_out(step).start()

    for step in range(steps):
        copy_out(step).wait()


def decode(grid_t, lat_t, dsum, w_out_t, slots):
    channels, points = grid_t.shape
    latent = lat_t.shape[0]
    rows = dsum.shape[0]
    width = 512
    vmem = pl.BlockSpec(memory_space=pltpu.VMEM)
    return pl.pallas_call(
        functools.partial(decode_kernel, width),
        in_specs=[vmem] * (4 + SLOTS),
        out_specs=pl.BlockSpec(memory_space=pl.ANY),
        out_shape=jax.ShapeDtypeStruct((channels, points), BF16),
        scratch_shapes=[
            pltpu.VMEM((latent, rows), BF16),
            pltpu.VMEM((channels, points), BF16),
            pltpu.SemaphoreType.DMA((points // width,)),
        ],
        compiler_params=pltpu.CompilerParams(vmem_limit_bytes=24 * MIB),
        name="decode",
    )(grid_t, lat_t, dsum, w_out_t, *slots)


def local(
    grid_in, w_embed, enc_coef, enc_owner, slot_block, mesh_in, w_enc,
    proc_adj, proc_coef, proc_gain, w_proc, dec_coef, w_out,
):
    parts = lax.axis_size("nodes")
    block_mesh = enc_coef.shape[1]

    def swap(x, slot):
        pairs = [(i, partner(slot, i, parts)) for i in range(parts)]
        return lax.ppermute(x, "nodes", pairs)

    def swap_all(xs):
        return [xs[OWN]] + [swap(xs[s], s) for s in range(1, SLOTS)]

    lat_t, dsum, grid_t, *sums = encode(
        parts, slot_block, enc_owner.reshape(-1, 128), grid_in.T, w_embed, enc_coef,
        jnp.swapaxes(dec_coef, 1, 2),
    )
    received = swap_all(sums)
    near = prepare(parts, proc_adj, proc_coef, sums[OWN])
    mid, ids = update(received, mesh_in, w_enc)
    far_mid = swap(mid, FAR)
    near_mid = swap(mid, NEAR)
    mesh_out, *sends = process(
        block_mesh, ids, mid, near_mid, far_mid, near, proc_gain.reshape(1, -1), w_proc
    )
    returned = swap_all(sends)
    pred_t = decode(grid_t, lat_t, dsum, w_out.T, returned)
    return (pred_t.T, mesh_out)


def solution(mesh):
    return jax.shard_map(
        local,
        mesh=mesh,
        in_specs=(
            P(("groups", "nodes"), None),
            P(),
            P("nodes", None, None),
            P("nodes"),
            P("nodes"),
            P(("groups", "nodes"), None),
            P(),
            P("nodes", None),
            P("nodes", None, None, None),
            P(),
            P(),
            P("nodes", None, None),
            P(),
        ),
        out_specs=(P(("groups", "nodes"), None), P(("groups", "nodes"), None)),
        check_vma=False,
    )
```

time: 56.8 us -> 45.4 us (0.80); the launches traced: 56.1 us -> 45.3 us
  Pallas kernels: 28.6 us -> 19.1 us
  waiting for transfers between devices: 9.09 us -> 12 us
  local copies, waits for them, and re-layouts: 2.9 us -> 0.03 us
  starting transfers between devices: 14.7 us -> 13.4 us
    pallas_call x3, Pallas kernels: 27 us -> 17.5 us  [the longest x1 10.5 us: encode(): pl.pallas_call(functools.partial(encode_kernel, parts, width), in_specs=[...]
    ppermute x12, waiting for transfers between devices: 9.09 us -> 12 us  [swap(): return lax.ppermute(x, 'nodes', pairs)]
    unnamed x24 -> x14, local copies, waits for them, and re-layouts: 2.9 us -> 0.03 us
    ppermute x12, starting transfers between devices: 14.7 us -> 13.4 us  [swap(): return lax.ppermute(x, 'nodes', pairs)]
  transfers between devices with their start and end apart: 12 -> 12, of which waited for: 5 -> 5; matrix products, arithmetic and copies ran while one was open for 0% -> 0% of each run, Pallas kernels for 13% -> 2%
where the time goes in v3:
time: 45.4 us; the launch traced here: 45.3 us
  Pallas kernels  19.1 us (42%)
  starting transfers between devices  13.4 us (30%)
  waiting for transfers between devices  12 us (26%)
  between operations  0.76 us (2%)
    ppermute x12, starting transfers between devices, swap(): return lax.ppermute(x, 'nodes', pairs)  13.4 us
    ppermute x12, waiting for transfers between devices, swap(): return lax.ppermute(x, 'nodes', pairs)  12 us
    pallas_call x1, Pallas kernels, encode(): pl.pallas_call(functools.partial(encode_kernel, parts, width), in_specs=[...  10.5 us
    pallas_call x1, Pallas kernels, decode(): pl.pallas_call(functools.partial(decode_kernel, width), in_specs=[vmem] *...  6.12 us
    pallas_call x1, Pallas kernels, process(): pl.pallas_call(process_kernel, in_specs=[vmem] * 7, out_specs=[vmem] * (1...  1.3 us
  transfers between devices with their start and end apart: 12, of which 5 were waited for; matrix products, arithmetic and copies ran while one was open for 0% of the time, Pallas kernels for 2%

profile of v3, /device:TPU:0, one launch (start us, length us, event | category | flops | bytes accessed | tf_op | source)
XLA Modules:
  0.0 45.3 jit_solution(13770620904294165263)
XLA Ops:
  0.6 0.0 copy-start
  0.6 0.0 copy-start.4
  0.7 0.0 copy-start.3
  0.7 0.0 copy-start.5
  0.7 0.0 copy-start.1
  0.7 0.0 copy-start.6
  0.7 10.5 %encode.1 = (bf16[512,4096]{1,0:T(8,128)(2,1)S(1)}, bf16[192,4096]{1,0:T(8,128)(2,1)S(1)}, bf16[227,4096]{1,0:T(8,128)(2,1)S(1)}, bf16[32,640]{1,0:T(8,128)(2,1)...) custom-call(s32[16]{0:T(128)} %slot_hbm.1, ...), custom_call_target="tpu_custom_call" | custom-call | tf_op jit(solution)/shard_map/encode/pallas_call | solution.py:188
  11.2 0.0 copy-start.2
  11.2 4.1 %collective-permute-start = (bf16[32,640]{1,0:T(8,128)(2,1)S(1)}, bf16[32,640]{1,0:T(8,128)(2,1)S(1)}, u32[]{:S(2)}, u32[]{:S(2)}) collective-permute-start(bf16[32,640]{1,0:T(8,128)(2,1)S(1)} %get-tuple-element.24), channel_id=1, source_target_pairs={{0,8},{1,9},{2,10},{3,11},{4,12},{5,13},{6,14},{7,15},{8,0},{9,1},... | collective-permute-start | bytes 122888 | tf_op jit(solution)/shard_map/ppermute | solution.py:386
  15.3 2.3 %collective-permute-start.1 = (bf16[32,640]{1,0:T(8,128)(2,1)S(1)}, bf16[32,640]{1,0:T(8,128)(2,1)S(1)}, u32[]{:S(2)}, u32[]{:S(2)}) collective-permute-start(bf16[32,640]{1,0:T(8,128)(2,1)S(1)} %get-tuple-element.25), channel_id=1, source_target_pairs={{0,14},{1,15},{2,4},{3,5},{4,2},{5,3},{6,8},{7,9},{8,6},{9,7},{10,... | collective-permute-start | bytes 122888 | tf_op jit(solution)/shard_map/ppermute | solution.py:386
  17.6 1.3 %collective-permute-start.2 = (bf16[32,640]{1,0:T(8,128)(2,1)S(1)}, bf16[32,640]{1,0:T(8,128)(2,1)S(1)}, u32[]{:S(2)}, u32[]{:S(2)}) collective-permute-start(bf16[32,640]{1,0:T(8,128)(2,1)S(1)} %get-tuple-element.26), channel_id=1, source_target_pairs={{0,15},{1,2},{2,1},{3,4},{4,3},{5,6},{6,5},{7,8},{8,7},{9,10},{10,... | collective-permute-start | bytes 122888 | tf_op jit(solution)/shard_map/ppermute | solution.py:386
  18.9 0.0 collective-permute-start.3
  18.9 0.7 %collective-permute-start.4 = (bf16[32,640]{1,0:T(8,128)(2,1)S(1)}, bf16[32,640]{1,0:T(8,128)(2,1)S(1)}, u32[]{:S(2)}, u32[]{:S(2)}) collective-permute-start(bf16[32,640]{1,0:T(8,128)(2,1)S(1)} %get-tuple-element.28), channel_id=1, source_target_pairs={{0,1},{1,0},{2,3},{3,2},{4,5},{5,4},{6,7},{7,6},{8,9},{9,8},{10,11... | collective-permute-start | bytes 122888 | tf_op jit(solution)/shard_map/ppermute | solution.py:386
  19.6 0.0 collective-permute-done.refs_1_
  19.6 2.4 %collective-permute-done.1.refs_2_ = bf16[32,640]{1,0:T(8,128)(2,1)S(1)} collective-permute-done((bf16[32,640]{1,0:T(8,128)(2,1)S(1)}, bf16[32,640]{1,0:T(8,128)(2,1)S(1)}, u32[]{:S(2)}, u32[]{:S(2)}) %collective-permute-start.1) | collective-permute-done | bytes 40992 | tf_op jit(solution)/shard_map/ppermute | solution.py:386
  22.0 1.7 %collective-permute-done.2.refs_3_ = bf16[32,640]{1,0:T(8,128)(2,1)S(1)} collective-permute-done((bf16[32,640]{1,0:T(8,128)(2,1)S(1)}, bf16[32,640]{1,0:T(8,128)(2,1)S(1)}, u32[]{:S(2)}, u32[]{:S(2)}) %collective-permute-start.2) | collective-permute-done | bytes 40992 | tf_op jit(solution)/shard_map/ppermute | solution.py:386
  23.7 0.0 collective-permute-done.3.refs_4_
  23.7 0.0 collective-permute-done.4.refs_5_
  23.7 0.0 copy-done
  23.7 0.0 copy-done.4
  23.7 0.3 mesh_update.1
  24.0 1.7 %collective-permute-start.6 = (bf16[128,512]{1,0:T(8,128)(2,1)S(1)}, bf16[128,512]{1,0:T(8,128)(2,1)S(1)}, u32[]{:S(2)}, u32[]{:S(2)}) collective-permute-start(bf16[128,512]{1,0:T(8,128)(2,1)S(1)} %get-tuple-element.30.mid_ref), channel_id=1, source_target_pairs={{0,15},{1,2},{2,1},{3,4},{4,3},{5,6},{6,5},{7,8},{8,7},{9,10},{10,... | collective-permute-start | bytes 393224 | tf_op jit(solution)/shard_map/ppermute | solution.py:386
  25.7 0.0 collective-permute-start.5
  25.7 0.0 copy-done.3
  25.7 0.0 copy-done.5
  25.7 0.9 %prepare.1.near_ref = bf16[128,384]{1,0:T(8,128)(2,1)S(1)} custom-call(s32[4,6]{1,0:T(4,128)S(1)} %copy-done.5, bf16[4,6,32,32]{3,2,1,0:T(8,128)(2,1)S(1)} %copy-done.3, bf16[32,640]{1,0:T(8,128)(2,1)S(1)} %get-tuple-element.23.refs_0_.after_ref), custom_call_target="tpu_custom_call" | custom-call | flops 18874368 | bytes 393216 | tf_op jit(solution)/shard_map/prepare/pallas_call | solution.py:248
  26.6 4.6 %collective-permute-done.6.far_mid_ref = bf16[128,512]{1,0:T(8,128)(2,1)S(1)} collective-permute-done((bf16[128,512]{1,0:T(8,128)(2,1)S(1)}, bf16[128,512]{1,0:T(8,128)(2,1)S(1)}, u32[]{:S(2)}, u32[]{:S(2)}) %collective-permute-start.6) | collective-permute-done | bytes 131104 | tf_op jit(solution)/shard_map/ppermute | solution.py:386
  31.2 0.0 collective-permute-done.5.near_mid_ref
  31.2 0.0 copy-done.1
  31.2 0.0 copy-done.6
  31.2 1.3 %mesh_process.1 = (bf16[128,512]{1,0:T(8,128)(2,1)}, bf16[32,512]{1,0:T(8,128)(2,1)S(1)}, bf16[32,512]{1,0:T(8,128)(2,1)S(1)}, bf16[32,512]{1,0:T(8,128)(2,1)S(1...) custom-call(f32[8,512]{1,0:T(8,128)S(1)} %get-tuple-element.29.ids_ref, ...), custom_call_target="tpu_custom_call" | custom-call | tf_op jit(solution)/shard_map/mesh_process/pallas_call | solution.py:318
  32.5 0.0 collective-permute-start.7
  32.5 0.1 collective-permute-start.8
  32.6 1.6 %collective-permute-start.9 = (bf16[32,512]{1,0:T(8,128)(2,1)S(1)}, bf16[32,512]{1,0:T(8,128)(2,1)S(1)}, u32[]{:S(2)}, u32[]{:S(2)}) collective-permute-start(bf16[32,512]{1,0:T(8,128)(2,1)S(1)} %get-tuple-element.34), channel_id=1, source_target_pairs={{0,15},{1,2},{2,1},{3,4},{4,3},{5,6},{6,5},{7,8},{8,7},{9,10},{10,... | collective-permute-start | bytes 98312 | tf_op jit(solution)/shard_map/ppermute | solution.py:386
  34.1 1.7 %collective-permute-start.10 = (bf16[32,512]{1,0:T(8,128)(2,1)S(1)}, bf16[32,512]{1,0:T(8,128)(2,1)S(1)}, u32[]{:S(2)}, u32[]{:S(2)}) collective-permute-start(bf16[32,512]{1,0:T(8,128)(2,1)S(1)} %get-tuple-element.35), channel_id=1, source_target_pairs={{0,2},{1,3},{2,0},{3,1},{4,6},{5,7},{6,4},{7,5},{8,10},{9,11},{10,... | collective-permute-start | bytes 98312 | tf_op jit(solution)/shard_map/ppermute | solution.py:386
  35.9 0.0 collective-permute-start.11
  35.9 1.7 %collective-permute-done.7.rest_1_ = bf16[32,512]{1,0:T(8,128)(2,1)S(1)} collective-permute-done((bf16[32,512]{1,0:T(8,128)(2,1)S(1)}, bf16[32,512]{1,0:T(8,128)(2,1)S(1)}, u32[]{:S(2)}, u32[]{:S(2)}) %collective-permute-start.7) | collective-permute-done | bytes 32800 | tf_op jit(solution)/shard_map/ppermute | solution.py:386
  37.5 1.6 %collective-permute-done.8.rest_2_ = bf16[32,512]{1,0:T(8,128)(2,1)S(1)} collective-permute-done((bf16[32,512]{1,0:T(8,128)(2,1)S(1)}, bf16[32,512]{1,0:T(8,128)(2,1)S(1)}, u32[]{:S(2)}, u32[]{:S(2)}) %collective-permute-start.8) | collective-permute-done | bytes 32800 | tf_op jit(solution)/shard_map/ppermute | solution.py:386
  39.1 0.0 collective-permute-done.9.rest_3_
  39.1 0.0 collective-permute-done.10.rest_4_
  39.1 0.0 collective-permute-done.11.rest_5_
  39.1 0.0 copy-done.2
  39.2 6.1 %decode.1 = bf16[227,4096]{1,0:T(8,128)(2,1)} custom-call(bf16[227,4096]{1,0:T(8,128)(2,1)S(1)} %get-tuple-element.20.grid_ref, bf16[512,4096]{1,0:T(8,128)(2,1)S(1)} %get-tuple-element.21.lat_ref, bf16[192,4096]{1,0:T(8,128)(2,1)S(1)} %get-tuple-element.22.dsum_ref, bf16[227,512]{1,0:T(8,128)(2,1)S(1)} %bitcast.6, ...), custom_call_target="tpu_custom_call" | custom-call | tf_op jit(solution)/shard_map/decode/pallas_call | solution.py:362
Async XLA Ops:
  0.6 23.1 %copy-start = (bf16[512,512]{1,0:T(8,128)(2,1)S(1)}, bf16[512,512]{1,0:T(8,128)(2,1)}, u32[]{:S(2)}) copy-start(bf16[512,512]{1,0:T(8,128)(2,1)} %refs_7_.1) | copy-start | bytes 1572868
  0.6 23.1 %copy-start.4 = (bf16[128,512]{1,0:T(8,128)(2,1)S(1)}, bf16[128,512]{1,0:T(8,128)(2,1)}, u32[]{:S(2)}) copy-start(bf16[128,512]{1,0:T(8,128)(2,1)} %refs_6_.1) | copy-start | bytes 393220
  0.7 25.1 %copy-start.3 = (bf16[4,6,32,32]{3,2,1,0:T(8,128)(2,1)S(1)}, bf16[4,6,32,32]{3,2,1,0:T(8,128)(2,1)}, u32[]{:S(2)}) copy-start(bf16[4,6,32,32]{3,2,1,0:T(8,128)(2,1)} %coef_ref.1) | copy-start | bytes 147460
  0.7 25.1 %copy-start.5 = (s32[4,6]{1,0:T(4,128)S(1)}, s32[4,6]{1,0:T(4,128)}, u32[]{:S(2)}) copy-start(s32[4,6]{1,0:T(4,128)} %adj_ref.1) | copy-start | bytes 292
  0.7 30.5 %copy-start.1 = (bf16[512,512]{1,0:T(8,128)(2,1)S(1)}, bf16[512,512]{1,0:T(8,128)(2,1)}, u32[]{:S(2)}) copy-start(bf16[512,512]{1,0:T(8,128)(2,1)} %w_ref.1) | copy-start | bytes 1572868
  0.7 30.5 %copy-start.6 = (f32[512]{0:T(512)S(1)}, f32[512]{0:T(512)}, u32[]{:S(2)}) copy-start(f32[512]{0:T(512)} %param.22) | copy-start | bytes 6148
  11.2 28.0 %copy-start.2 = (bf16[512,227]{0,1:T(8,128)(2,1)S(1)}, bf16[512,227]{0,1:T(8,128)(2,1)}, u32[]{:S(2)}) copy-start(bf16[512,227]{0,1:T(8,128)(2,1)} %param.25) | copy-start | bytes 697348
  11.2 8.4 %collective-permute-start = (bf16[32,640]{1,0:T(8,128)(2,1)S(1)}, bf16[32,640]{1,0:T(8,128)(2,1)S(1)}, u32[]{:S(2)}, u32[]{:S(2)}) collective-permute-start(bf16[32,640]{1,0:T(8,128)(2,1)S(1)} %get-tuple-element.24), channel_id=1, source_target_pairs={{0,8},{1,9},{2,10},{3,11},{4,12},{5,13},{6,14},{7,15},{8,0},{9,1},... | collective-permute-start | bytes 122888 | tf_op jit(solution)/shard_map/ppermute | solution.py:386
  15.3 6.7 %collective-permute-start.1 = (bf16[32,640]{1,0:T(8,128)(2,1)S(1)}, bf16[32,640]{1,0:T(8,128)(2,1)S(1)}, u32[]{:S(2)}, u32[]{:S(2)}) collective-permute-start(bf16[32,640]{1,0:T(8,128)(2,1)S(1)} %get-tuple-element.25), channel_id=1, source_target_pairs={{0,14},{1,15},{2,4},{3,5},{4,2},{5,3},{6,8},{7,9},{8,6},{9,7},{10,... | collective-permute-start | bytes 122888 | tf_op jit(solution)/shard_map/ppermute | solution.py:386
  17.6 6.1 %collective-permute-start.2 = (bf16[32,640]{1,0:T(8,128)(2,1)S(1)}, bf16[32,640]{1,0:T(8,128)(2,1)S(1)}, u32[]{:S(2)}, u32[]{:S(2)}) collective-permute-start(bf16[32,640]{1,0:T(8,128)(2,1)S(1)} %get-tuple-element.26), channel_id=1, source_target_pairs={{0,15},{1,2},{2,1},{3,4},{4,3},{5,6},{6,5},{7,8},{8,7},{9,10},{10,... | collective-permute-start | bytes 122888 | tf_op jit(solution)/shard_map/ppermute | solution.py:386
  18.9 4.8 %collective-permute-start.3 = (bf16[32,640]{1,0:T(8,128)(2,1)S(1)}, bf16[32,640]{1,0:T(8,128)(2,1)S(1)}, u32[]{:S(2)}, u32[]{:S(2)}) collective-permute-start(bf16[32,640]{1,0:T(8,128)(2,1)S(1)} %get-tuple-element.27), channel_id=1, source_target_pairs={{0,2},{1,3},{2,0},{3,1},{4,6},{5,7},{6,4},{7,5},{8,10},{9,11},{10,... | collective-permute-start | bytes 122888 | tf_op jit(solution)/shard_map/ppermute | solution.py:386
  18.9 4.8 %collective-permute-start.4 = (bf16[32,640]{1,0:T(8,128)(2,1)S(1)}, bf16[32,640]{1,0:T(8,128)(2,1)S(1)}, u32[]{:S(2)}, u32[]{:S(2)}) collective-permute-start(bf16[32,640]{1,0:T(8,128)(2,1)S(1)} %get-tuple-element.28), channel_id=1, source_target_pairs={{0,1},{1,0},{2,3},{3,2},{4,5},{5,4},{6,7},{7,6},{8,9},{9,8},{10,11... | collective-permute-start | bytes 122888 | tf_op jit(solution)/shard_map/ppermute | solution.py:386
  24.0 7.2 %collective-permute-start.6 = (bf16[128,512]{1,0:T(8,128)(2,1)S(1)}, bf16[128,512]{1,0:T(8,128)(2,1)S(1)}, u32[]{:S(2)}, u32[]{:S(2)}) collective-permute-start(bf16[128,512]{1,0:T(8,128)(2,1)S(1)} %get-tuple-element.30.mid_ref), channel_id=1, source_target_pairs={{0,15},{1,2},{2,1},{3,4},{4,3},{5,6},{6,5},{7,8},{8,7},{9,10},{10,... | collective-permute-start | bytes 393224 | tf_op jit(solution)/shard_map/ppermute | solution.py:386
  25.7 5.5 %collective-permute-start.5 = (bf16[128,512]{1,0:T(8,128)(2,1)S(1)}, bf16[128,512]{1,0:T(8,128)(2,1)S(1)}, u32[]{:S(2)}, u32[]{:S(2)}) collective-permute-start(bf16[128,512]{1,0:T(8,128)(2,1)S(1)} %get-tuple-element.30.mid_ref), channel_id=1, source_target_pairs={{0,1},{1,0},{2,3},{3,2},{4,5},{5,4},{6,7},{7,6},{8,9},{9,8},{10,11... | collective-permute-start | bytes 393224 | tf_op jit(solution)/shard_map/ppermute | solution.py:386
  32.5 5.0 %collective-permute-start.7 = (bf16[32,512]{1,0:T(8,128)(2,1)S(1)}, bf16[32,512]{1,0:T(8,128)(2,1)S(1)}, u32[]{:S(2)}, u32[]{:S(2)}) collective-permute-start(bf16[32,512]{1,0:T(8,128)(2,1)S(1)} %get-tuple-element.32), channel_id=1, source_target_pairs={{0,8},{1,9},{2,10},{3,11},{4,12},{5,13},{6,14},{7,15},{8,0},{9,1},... | collective-permute-start | bytes 98312 | tf_op jit(solution)/shard_map/ppermute | solution.py:386
  32.5 6.6 %collective-permute-start.8 = (bf16[32,512]{1,0:T(8,128)(2,1)S(1)}, bf16[32,512]{1,0:T(8,128)(2,1)S(1)}, u32[]{:S(2)}, u32[]{:S(2)}) collective-permute-start(bf16[32,512]{1,0:T(8,128)(2,1)S(1)} %get-tuple-element.33), channel_id=1, source_target_pairs={{0,14},{1,15},{2,4},{3,5},{4,2},{5,3},{6,8},{7,9},{8,6},{9,7},{10,... | collective-permute-start | bytes 98312 | tf_op jit(solution)/shard_map/ppermute | solution.py:386
  32.6 6.5 %collective-permute-start.9 = (bf16[32,512]{1,0:T(8,128)(2,1)S(1)}, bf16[32,512]{1,0:T(8,128)(2,1)S(1)}, u32[]{:S(2)}, u32[]{:S(2)}) collective-permute-start(bf16[32,512]{1,0:T(8,128)(2,1)S(1)} %get-tuple-element.34), channel_id=1, source_target_pairs={{0,15},{1,2},{2,1},{3,4},{4,3},{5,6},{6,5},{7,8},{8,7},{9,10},{10,... | collective-permute-start | bytes 98312 | tf_op jit(solution)/shard_map/ppermute | solution.py:386
  34.1 5.0 %collective-permute-start.10 = (bf16[32,512]{1,0:T(8,128)(2,1)S(1)}, bf16[32,512]{1,0:T(8,128)(2,1)S(1)}, u32[]{:S(2)}, u32[]{:S(2)}) collective-permute-start(bf16[32,512]{1,0:T(8,128)(2,1)S(1)} %get-tuple-element.35), channel_id=1, source_target_pairs={{0,2},{1,3},{2,0},{3,1},{4,6},{5,7},{6,4},{7,5},{8,10},{9,11},{10,... | collective-permute-start | bytes 98312 | tf_op jit(solution)/shard_map/ppermute | solution.py:386
  35.9 3.3 %collective-permute-start.11 = (bf16[32,512]{1,0:T(8,128)(2,1)S(1)}, bf16[32,512]{1,0:T(8,128)(2,1)S(1)}, u32[]{:S(2)}, u32[]{:S(2)}) collective-permute-start(bf16[32,512]{1,0:T(8,128)(2,1)S(1)} %get-tuple-element.36), channel_id=1, source_target_pairs={{0,1},{1,0},{2,3},{3,2},{4,5},{5,4},{6,7},{7,6},{8,9},{9,8},{10,11... | collective-permute-start | bytes 98312 | tf_op jit(solution)/shard_map/ppermute | solution.py:386

commit v4 on v3

--- a/solution.py
+++ b/solution.py
@@ -10,37 +10,27 @@
 F32 = jnp.float32
 BF16 = jnp.bfloat16
 MIB = 1 << 20
-OWN, HALF, ODD, FAR, EVEN, NEAR = range(6)
 SLOTS = 6
-PAD = 128
-
-
-def partner(slot, me, parts):
-    chip = me // 2 % 2
-    core = me % 2
-    step = {
-        OWN: 0,
-        HALF: parts // 2,
-        ODD: 4 * chip - 2,
-        EVEN: 2 - 4 * chip,
-        FAR: 2 * core - 1,
-        NEAR: 1 - 2 * core,
-    }[slot]
-    return (me + step + parts) % parts
-
-
-def scalar_partner(slot, me, parts):
-    chip = lax.rem(lax.div(me, 2), 2)
-    core = lax.rem(me, 2)
-    step = {
-        OWN: 0,
-        HALF: parts // 2,
-        ODD: 4 * chip - 2,
-        EVEN: 2 - 4 * chip,
-        FAR: 2 * core - 1,
-        NEAR: 1 - 2 * core,
-    }[slot]
-    return lax.rem(me + step + parts, parts)
+HALF = 5
+SQUAD = 4
+LANES = 128
+
+
+def offsets_of(parts):
+    return (0, 1, 2, -2, -1, parts // 2)
+
+
+def squads_of(parts, first):
+    return [
+        [(at + first + i) % parts for i in range(SQUAD)] for at in range(0, parts, SQUAD)
+    ]
+
+
+def seat(me, offset):
+    even = lax.rem(me, SQUAD) + offset
+    inside = (even >= 0) & (even < SQUAD)
+    odd = jnp.clip(lax.rem(me + 2, SQUAD) + offset, 0, SQUAD - 1)
+    return jnp.clip(even, 0, SQUAD - 1), inside, odd
 
 
 def silu(x):
@@ -64,17 +54,9 @@
 def fill_targets(parts, per_block, block_mesh, owner_ref, tgt_ref):
     wide = tgt_ref.shape[1]
     me = lax.axis_index("nodes")
-    chip = lax.rem(lax.div(me, 2), 2)
-    core = lax.rem(me, 2)
-    up2 = EVEN + (ODD - EVEN) * chip
-    up1 = NEAR + (FAR - NEAR) * core
     off = owner_ref[...] - me
     off = jnp.where(off < 0, off + parts, off)
-    slot = jnp.where(off == parts // 2, HALF, OWN)
-    slot = jnp.where(off == 2, up2, slot)
-    slot = jnp.where(off == parts - 2, ODD + EVEN - up2, slot)
-    slot = jnp.where(off == 1, up1, slot)
-    slot = jnp.where(off == parts - 1, NEAR + FAR - up1, slot)
+    slot = jnp.where(off == parts // 2, HALF, jnp.where(off > 2, off - parts + HALF, off))
     slot = slot.astype(F32)
     groups, lanes = owner_ref.shape
     all_blocks = tgt_ref.shape[0]
@@ -97,11 +79,11 @@
     parts, width, slot_hbm, owner_hbm, w_hbm, grid_hbm, enc_hbm, dec_hbm,
     lat_ref, dsum_ref, grid_ref, *rest,
 ):
-    send_refs = rest[:SLOTS]
+    even_ref, odd_ref, half_ref = rest[:3]
     (
         slot_ref, owner_ref, w_ref, enc_ref, dec_ref, wt_ref, tgt_ref, ids_ref, msum_ref,
         acc_ref, small_sems, sems,
-    ) = rest[SLOTS:]
+    ) = rest[3:]
     tiles, block_mesh, block_grid = enc_ref.shape
     channels, points = grid_ref.shape
     latent = w_ref.shape[1]
@@ -132,12 +114,15 @@
     for step in range(steps):
         for copy in copies(step):
             copy.start()
+    for ref in (even_ref, odd_ref):
+        ref[:, :, :latent] = jnp.zeros((SQUAD, block_mesh, latent), BF16)
+        ref[:, :, latent:] = jnp.full((SQUAD, block_mesh, LANES), -1.0, BF16)
+    ids_ref[...] = lax.broadcasted_iota(jnp.int32, ids_ref.shape, 0).astype(BF16)
+    acc_ref[...] = jnp.zeros_like(acc_ref)
     for copy in small:
         copy.wait()
     wt_ref[:, :channels] = w_ref[...].astype(F32).T.astype(BF16)
     fill_targets(parts, per_block, block_mesh, owner_ref, tgt_ref)
-    ids_ref[...] = lax.broadcasted_iota(jnp.int32, ids_ref.shape, 0).astype(BF16)
-    acc_ref[...] = jnp.zeros_like(acc_ref)
 
     @pl.loop(0, steps)
     def _(step):
@@ -168,10 +153,24 @@
 
     me = lax.axis_index("nodes")
     flipped = acc_ref[...].T.astype(BF16)
-    for s in range(SLOTS):
-        send_refs[s][:, :latent] = flipped[s * block_mesh : (s + 1) * block_mesh, :]
-        block = slot_ref[scalar_partner(s, me, parts)].astype(F32)
-        send_refs[s][:, latent:] = jnp.full((block_mesh, PAD), block, F32).astype(BF16)
+    for s, offset in enumerate(offsets_of(parts)):
+        block = slot_ref[lax.rem(me + offset + parts, parts)].astype(F32)
+        block = jnp.full((block_mesh, LANES), block, F32).astype(BF16)
+        mine = jnp.concatenate([flipped[s * block_mesh : (s + 1) * block_mesh, :], block], axis=1)
+        if s == HALF:
+            half_ref[...] = mine
+            continue
+        even, inside, odd = seat(me, offset)
+
+        @pl.when(inside)
+        def _():
+            even_ref[even] = mine
+
+        if offset != 0:
+
+            @pl.when(jnp.logical_not(inside))
+            def _():
+                odd_ref[odd] = mine
 
 
 def encode(parts, slot_block, owners, grid_t, w_embed, enc_coef, dec_t):
@@ -188,13 +187,14 @@
     return pl.pallas_call(
         functools.partial(encode_kernel, parts, width),
         in_specs=[hbm] * 6,
-        out_specs=[vmem] * (3 + SLOTS),
+        out_specs=[vmem] * 6,
         out_shape=[
             pltpu.VMEM((latent, points), BF16),
             pltpu.VMEM((rows, points), BF16),
             pltpu.VMEM((channels, points), BF16),
         ]
-        + [jax.ShapeDtypeStruct((block_mesh, latent + PAD), BF16)] * SLOTS,
+        + [jax.ShapeDtypeStruct((SQUAD, block_mesh, latent + LANES), BF16)] * 2
+        + [jax.ShapeDtypeStruct((block_mesh, latent + LANES), BF16)],
         scratch_shapes=[
             pltpu.SMEM(slot_block.shape, jnp.int32),
             pltpu.VMEM(owners.shape, jnp.int32),
@@ -260,43 +260,45 @@
     )(adj, coef, after)
 
 
-def update_kernel(*refs):
-    slots = refs[:SLOTS]
-    mesh_ref, w_ref, mid_ref, ids_ref = refs[SLOTS:]
+def update_kernel(even_ref, odd_ref, half_ref, mesh_ref, w_ref, mid_ref, ids_ref):
     count, latent = mesh_ref.shape
-    block_mesh = slots[0].shape[0]
-    sums = [slot[:, :latent].astype(F32) for slot in slots]
-    ids = [slot[:, latent:].astype(F32)[:1, :1] for slot in slots]
-    for s in range(SLOTS):
-        ids_ref[s : s + 1, :] = jnp.broadcast_to(ids[s], (1, latent))
-    parts = []
+    block_mesh = half_ref.shape[0]
+    chunks = [ref[i] for ref in (even_ref, odd_ref) for i in range(SQUAD)] + [half_ref[...]]
+    sums = [chunk[:, :latent].astype(F32) for chunk in chunks]
+    ids = [chunk[:, latent:].astype(F32)[:1, :1] for chunk in chunks]
+    for i, block in enumerate(ids):
+        ids_ref[i : i + 1, :] = jnp.broadcast_to(block, (1, latent))
+    blocks = []
     for b in range(count // block_mesh):
         total = jnp.zeros((block_mesh, latent), F32)
-        for s in range(SLOTS):
-            total += jnp.where(ids[s] == b, sums[s], 0.0)
-        parts.append(total.astype(BF16))
-    grown = jnp.dot(jnp.concatenate(parts, axis=0), w_ref[...], preferred_element_type=F32)
+        for block, part in zip(ids, sums):
+            total += jnp.where(block == b, part, 0.0)
+        blocks.append(total.astype(BF16))
+    grown = jnp.dot(jnp.concatenate(blocks, axis=0), w_ref[...], preferred_element_type=F32)
     mid_ref[...] = (mesh_ref[...].astype(F32) + silu(grown)).astype(BF16)
 
 
-def update(slots, mesh_in, w_enc):
+def update(even, odd, half, mesh_in, w_enc):
     vmem = pl.BlockSpec(memory_space=pltpu.VMEM)
     return pl.pallas_call(
         update_kernel,
-        in_specs=[vmem] * (SLOTS + 2),
+        in_specs=[vmem] * 5,
         out_specs=[vmem] * 2,
         out_shape=[
             jax.ShapeDtypeStruct(mesh_in.shape, BF16),
-            jax.ShapeDtypeStruct((8, mesh_in.shape[1]), F32),
+            jax.ShapeDtypeStruct((16, mesh_in.shape[1]), F32),
         ],
         compiler_params=pltpu.CompilerParams(vmem_limit_bytes=8 * MIB),
         name="mesh_update",
-    )(*slots, mesh_in, w_enc)
-
-
-def process_kernel(ids_ref, mid_ref, near_mid_ref, far_mid_ref, near_ref, gain_ref, w_ref, out_ref, *sends):
+    )(even, odd, half, mesh_in, w_enc)
+
+
+def process_kernel(
+    ids_ref, mid_ref, near_mid_ref, far_mid_ref, near_ref, gain_ref, w_ref,
+    out_ref, even_ref, odd_ref, half_ref,
+):
     count, latent = mid_ref.shape
-    block_mesh = sends[0].shape[0]
+    block_mesh = half_ref.shape[0]
     around = jnp.concatenate([near_mid_ref[...], mid_ref[...], far_mid_ref[...]], axis=0)
     message = jnp.dot(near_ref[...], around, preferred_element_type=F32)
     power = jnp.mean(message * message, axis=-1, keepdims=True)
@@ -304,12 +306,17 @@
     grown = jnp.dot(normed, w_ref[...], preferred_element_type=F32)
     grown = mid_ref[...].astype(F32) + silu(grown)
     out_ref[...] = grown.astype(BF16)
-    for s in range(SLOTS):
+    for i in range(2 * SQUAD + 1):
         chosen = grown[:block_mesh, :]
         for b in range(1, count // block_mesh):
             block = grown[b * block_mesh : (b + 1) * block_mesh, :]
-            chosen = jnp.where(ids_ref[s : s + 1, :] == b, block, chosen)
-        sends[s][...] = chosen.astype(BF16)
+            chosen = jnp.where(ids_ref[i : i + 1, :] == b, block, chosen)
+        if i < SQUAD:
+            even_ref[i] = chosen.astype(BF16)
+        elif i < 2 * SQUAD:
+            odd_ref[i - SQUAD] = chosen.astype(BF16)
+        else:
+            half_ref[...] = chosen.astype(BF16)
 
 
 def process(block_mesh, ids, mid, near_mid, far_mid, near, gain, w_proc):
@@ -318,25 +325,45 @@
     return pl.pallas_call(
         process_kernel,
         in_specs=[vmem] * 7,
-        out_specs=[vmem] * (1 + SLOTS),
+        out_specs=[vmem] * 4,
         out_shape=[jax.ShapeDtypeStruct(mid.shape, BF16)]
-        + [jax.ShapeDtypeStruct((block_mesh, latent), BF16)] * SLOTS,
+        + [jax.ShapeDtypeStruct((SQUAD, block_mesh, latent), BF16)] * 2
+        + [jax.ShapeDtypeStruct((block_mesh, latent), BF16)],
         compiler_params=pltpu.CompilerParams(vmem_limit_bytes=8 * MIB),
         name="mesh_process",
     )(ids, mid, near_mid, far_mid, near, gain, w_proc)
 
 
-def decode_kernel(width, grid_ref, lat_ref, dsum_ref, w_ref, *rest):
-    slots = rest[:SLOTS]
-    out_hbm, back_ref, pred_ref, sems = rest[SLOTS:]
+def decode_kernel(
+    parts, width, grid_ref, lat_ref, dsum_ref, w_ref, even_ref, odd_ref, half_ref,
+    out_hbm, join_ref, back_ref, pred_ref, sems,
+):
     steps = grid_ref.shape[1] // width
 
     def copy_out(step):
         cols = pl.ds(pl.multiple_of(step * width, width), width)
         return pltpu.make_async_copy(pred_ref.at[:, cols], out_hbm.at[:, cols], sems.at[step])
 
-    joined = jnp.concatenate([slot[...] for slot in slots], axis=0)
-    back_ref[...] = joined.astype(F32).T.astype(BF16)
+    me = lax.axis_index("nodes")
+    block_mesh = half_ref.shape[0]
+    for s, offset in enumerate(offsets_of(parts)):
+        rows = slice(s * block_mesh, (s + 1) * block_mesh)
+        if s == HALF:
+            join_ref[rows, :] = half_ref[...].astype(F32)
+            continue
+        even, inside, odd = seat(me, offset)
+
+        @pl.when(inside)
+        def _():
+            join_ref[rows, :] = even_ref[even].astype(F32)
+
+        if offset != 0:
+
+            @pl.when(jnp.logical_not(inside))
+            def _():
+                join_ref[rows, :] = odd_ref[odd].astype(F32)
+
+    back_ref[...] = join_ref[...].T.astype(BF16)
 
     @pl.loop(0, steps)
     def _(step):
@@ -353,25 +380,26 @@
         copy_out(step).wait()
 
 
-def decode(grid_t, lat_t, dsum, w_out_t, slots):
+def decode(parts, grid_t, lat_t, dsum, w_out_t, even, odd, half):
     channels, points = grid_t.shape
     latent = lat_t.shape[0]
     rows = dsum.shape[0]
     width = 512
     vmem = pl.BlockSpec(memory_space=pltpu.VMEM)
     return pl.pallas_call(
-        functools.partial(decode_kernel, width),
-        in_specs=[vmem] * (4 + SLOTS),
+        functools.partial(decode_kernel, parts, width),
+        in_specs=[vmem] * 7,
         out_specs=pl.BlockSpec(memory_space=pl.ANY),
         out_shape=jax.ShapeDtypeStruct((channels, points), BF16),
         scratch_shapes=[
+            pltpu.VMEM((rows, latent), F32),
             pltpu.VMEM((latent, rows), BF16),
             pltpu.VMEM((channels, points), BF16),
             pltpu.SemaphoreType.DMA((points // width,)),
         ],
         compiler_params=pltpu.CompilerParams(vmem_limit_bytes=24 * MIB),
         name="decode",
-    )(grid_t, lat_t, dsum, w_out_t, *slots)
+    )(grid_t, lat_t, dsum, w_out_t, even, odd, half)
 
 
 def local(
@@ -381,27 +409,32 @@
     parts = lax.axis_size("nodes")
     block_mesh = enc_coef.shape[1]
 
-    def swap(x, slot):
-        pairs = [(i, partner(slot, i, parts)) for i in range(parts)]
-        return lax.ppermute(x, "nodes", pairs)
-
-    def swap_all(xs):
-        return [xs[OWN]] + [swap(xs[s], s) for s in range(1, SLOTS)]
+    def swap(x, to):
+        return lax.ppermute(x, "nodes", [(i, to(i) % parts) for i in range(parts)])
+
+    def exchange(even, odd, half):
+        half = swap(half, lambda i: i + parts // 2)
+        odd, even = (
+            lax.all_to_all(
+                x, "nodes", split_axis=0, concat_axis=0, tiled=True,
+                axis_index_groups=squads_of(parts, first),
+            )
+            for x, first in ((odd, 2), (even, 0))
+        )
+        return even, odd, half
 
     lat_t, dsum, grid_t, *sums = encode(
         parts, slot_block, enc_owner.reshape(-1, 128), grid_in.T, w_embed, enc_coef,
         jnp.swapaxes(dec_coef, 1, 2),
     )
-    received = swap_all(sums)
-    near = prepare(parts, proc_adj, proc_coef, sums[OWN])
-    mid, ids = update(received, mesh_in, w_enc)
-    far_mid = swap(mid, FAR)
-    near_mid = swap(mid, NEAR)
+    near = prepare(parts, proc_adj, proc_coef, sums[-1])
+    mid, ids = update(*exchange(*sums), mesh_in, w_enc)
+    far_mid = swap(mid, lambda i: i + 2 * (i % 2) - 1)
+    near_mid = swap(mid, lambda i: i + 1 - 2 * (i % 2))
     mesh_out, *sends = process(
         block_mesh, ids, mid, near_mid, far_mid, near, proc_gain.reshape(1, -1), w_proc
     )
-    returned = swap_all(sends)
-    pred_t = decode(grid_t, lat_t, dsum, w_out.T, returned)
+    pred_t = decode(parts, grid_t, lat_t, dsum, w_out.T, *exchange(*sends))
     return (pred_t.T, mesh_out)
 
 

time: 45.4 us -> 79.6 us (1.75)
  blocking collectives: 0 us -> 16.8 us
  local copies, waits for them, and re-layouts: 0.03 us -> 12.2 us
  starting transfers between devices: 13.4 us -> 15.6 us
  Pallas kernels: 19.1 us -> 21 us
    all_to_all x0 -> x2, blocking collectives: none -> 16.8 us  [exchange(): lax.all_to_all(x, 'nodes', split_axis=0, concat_axis=0, tiled=True, axis_...]
    all_to_all x0 -> x2, starting transfers between devices: none -> 13.7 us  [exchange(): lax.all_to_all(x, 'nodes', split_axis=0, concat_axis=0, tiled=True, axis_...]
    unnamed x14 -> x26, local copies, waits for them, and re-layouts: 0.03 us -> 12.2 us
    ppermute x12 -> x4, starting transfers between devices: 13.4 us -> 1.92 us  [swap(): return lax.ppermute(x, 'nodes', [(i, to(i) % parts) for i in range(parts)])]
    pallas_call x3, Pallas kernels: 7.73 us -> 9.71 us  [the longest x1 7.08 us: decode(): pl.pallas_call(functools.partial(decode_kernel, parts, width), in_specs=[...]
    ppermute x12 -> x4, waiting for transfers between devices: 12 us -> 12.6 us  [swap(): return lax.ppermute(x, 'nodes', [(i, to(i) % parts) for i in range(parts)])]
  transfers between devices with their start and end apart: 12 -> 6, of which waited for: 5 -> 3; matrix products, arithmetic and copies ran while one was open for 0% -> 0% of each run, Pallas kernels for 2% -> 1%
where the time goes in v4:
time: 79.6 us; the launch traced here: 78.9 us
  Pallas kernels  21 us (26%)
  blocking collectives  16.8 us (21%)
  starting transfers between devices  15.6 us (20%)
  waiting for transfers between devices  12.6 us (16%)
  local copies, waits for them, and re-layouts  12.2 us (15%)
    all_to_all x2, blocking collectives, exchange(): lax.all_to_all(x, 'nodes', split_axis=0, concat_axis=0, tiled=True, axis_...  16.8 us
    all_to_all x2, starting transfers between devices, exchange(): lax.all_to_all(x, 'nodes', split_axis=0, concat_axis=0, tiled=True, axis_...  13.7 us
    ppermute x4, waiting for transfers between devices, swap(): return lax.ppermute(x, 'nodes', [(i, to(i) % parts) for i in range(parts)])  12.6 us
    unnamed x26, local copies, waits for them, and re-layouts  12.2 us
    pallas_call x1, Pallas kernels, encode(): pl.pallas_call(functools.partial(encode_kernel, parts, width), in_specs=[...  10.4 us
    pallas_call x1, Pallas kernels, decode(): pl.pallas_call(functools.partial(decode_kernel, parts, width), in_specs=[...  7.08 us
    ppermute x4, starting transfers between devices, swap(): return lax.ppermute(x, 'nodes', [(i, to(i) % parts) for i in range(parts)])  1.92 us
  transfers between devices with their start and end apart: 6, of which 3 were waited for; matrix products, arithmetic and copies ran while one was open for 0% of the time, Pallas kernels for 1%

profile of v4, /device:TPU:0, one launch (start us, length us, event | category | flops | bytes accessed | tf_op | source)
XLA Modules:
  0.0 78.9 jit_solution(943876017195724479)
XLA Ops:
  0.6 10.4 %encode.1 = (bf16[512,4096]{1,0:T(8,128)(2,1)S(1)}, bf16[192,4096]{1,0:T(8,128)(2,1)S(1)}, bf16[227,4096]{1,0:T(8,128)(2,1)S(1)}, bf16[4,32,640]{2,1,0:T(8,128)(...) custom-call(s32[16]{0:T(128)} %slot_hbm.1, s32[3,128]{1,0:T(4,128)} %bitcast.11, ...), custom_call_target="tpu_custom_call" | custom-call | tf_op jit(solution)/shard_map/encode/pallas_call | solution.py:187
  11.1 0.0 copy-start
  11.1 1.9 %copy-done = bf16[512,4096]{1,0:T(8,128)(2,1)} copy-done((bf16[512,4096]{1,0:T(8,128)(2,1)}, bf16[512,4096]{1,0:T(8,128)(2,1)S(1)}, u32[]{:S(2)}) %copy-start) | copy-done | bytes 4194328
  13.0 0.0 copy-start.8
  13.0 9.1 %all_to_all.20.even_ref = bf16[4,32,640]{2,1,0:T(8,128)(2,1)} all-to-all(bf16[4,32,640]{2,1,0:T(8,128)(2,1)S(1)} %get-tuple-element.17), channel_id=1, replica_groups={{0,1,2,3},{4,5,6,7},{8,9,10,11},{12,13,14,15},{16,17,18,19},{20,21,22,2..., dimensions={0} | all-to-all | bytes 327680 | tf_op jit(solution)/shard_map/all_to_all | solution.py:418
  22.1 0.0 copy-done.8
  22.1 7.7 %all-to-all-start.1 = ((bf16[4,32,640]{2,1,0:T(8,128)(2,1)}), bf16[4,32,640]{2,1,0:T(8,128)(2,1)}, u32[]{:S(2)}, u32[]{:S(2)}) async-start(bf16[4,32,640]{2,1,0:T(8,128)(2,1)} %copy-done.8), calls=%async_computation.1 | async-start | bytes 327680 | tf_op jit(solution)/shard_map/all_to_all | solution.py:418
  29.8 0.0 collective-permute-start
  29.8 5.0 %collective-permute-done.half_ref = bf16[32,640]{1,0:T(8,128)(2,1)S(1)} collective-permute-done((bf16[32,640]{1,0:T(8,128)(2,1)S(1)}, bf16[32,640]{1,0:T(8,128)(2,1)S(1)}, u32[]{:S(2)}, u32[]{:S(2)}) %collective-permute-start) | collective-permute-done | bytes 40992 | tf_op jit(solution)/shard_map/ppermute | solution.py:413
  34.9 0.0 all-to-all-done.1.odd_ref
  34.9 0.0 copy-start.2
  34.9 0.9 %copy-done.2 = bf16[4,32,640]{2,1,0:T(8,128)(2,1)S(1)} copy-done((bf16[4,32,640]{2,1,0:T(8,128)(2,1)S(1)}, bf16[4,32,640]{2,1,0:T(8,128)(2,1)}, u32[]{:S(2)}) %copy-start.2) | copy-done | bytes 163864
  35.8 0.0 copy-start.4
  35.8 1.0 %copy-done.4 = bf16[512,512]{1,0:T(8,128)(2,1)S(1)} copy-done((bf16[512,512]{1,0:T(8,128)(2,1)S(1)}, bf16[512,512]{1,0:T(8,128)(2,1)}, u32[]{:S(2)}) %copy-start.4) | copy-done | bytes 524312
  36.9 0.0 copy-start.10
  36.9 0.9 %copy-done.10 = bf16[128,512]{1,0:T(8,128)(2,1)S(1)} copy-done((bf16[128,512]{1,0:T(8,128)(2,1)S(1)}, bf16[128,512]{1,0:T(8,128)(2,1)}, u32[]{:S(2)}) %copy-start.10) | copy-done | bytes 131096
  37.8 1.3 %mesh_update.1 = (bf16[128,512]{1,0:T(8,128)(2,1)S(1)}, f32[16,512]{1,0:T(8,128)S(1)}) custom-call(bf16[4,32,640]{2,1,0:T(8,128)(2,1)S(1)} %copy-done.2, bf16[4,32,640]{2,1,0:T(8,128)(2,1)} %all-to-all-done.1.odd_ref, bf16[32,640]{1,0:T(8,128)(2,1)S(1)} %collective-permute-done.half_ref, bf16[128,512]{1,0:T(8,128)(2,1)S(1)} %copy-done.10, ...), custom_call_target="tpu_custom_call" | custom-call | tf_op jit(solution)/shard_map/mesh_update/pallas_call | solution.py:283
  39.0 1.9 %collective-permute-start.2 = (bf16[128,512]{1,0:T(8,128)(2,1)S(1)}, bf16[128,512]{1,0:T(8,128)(2,1)S(1)}, u32[]{:S(2)}, u32[]{:S(2)}) collective-permute-start(bf16[128,512]{1,0:T(8,128)(2,1)S(1)} %get-tuple-element.21.mid_ref), channel_id=1, source_target_pairs={{0,15},{1,2},{2,1},{3,4},{4,3},{5,6},{6,5},{7,8},{8,7},{9,10},{10,... | collective-permute-start | bytes 393224 | tf_op jit(solution)/shard_map/ppermute | solution.py:413
  40.9 0.0 collective-permute-start.1
  41.0 0.0 copy-start.7
  41.0 0.9 %copy-done.7 = bf16[4,6,32,32]{3,2,1,0:T(8,128)(2,1)S(1)} copy-done((bf16[4,6,32,32]{3,2,1,0:T(8,128)(2,1)S(1)}, bf16[4,6,32,32]{3,2,1,0:T(8,128)(2,1)}, u32[]{:S(2)}) %copy-start.7) | copy-done | bytes 49176
  41.9 0.0 copy-start.11
  41.9 0.7 copy-done.11
  42.6 0.9 %prepare.1.near_ref = bf16[128,384]{1,0:T(8,128)(2,1)S(1)} custom-call(s32[4,6]{1,0:T(4,128)S(1)} %copy-done.11, bf16[4,6,32,32]{3,2,1,0:T(8,128)(2,1)S(1)} %copy-done.7, bf16[32,640]{1,0:T(8,128)(2,1)S(1)} %get-tuple-element.19.after_ref), custom_call_target="tpu_custom_call" | custom-call | flops 18874368 | bytes 393216 | tf_op jit(solution)/shard_map/prepare/pallas_call | solution.py:248
  43.4 2.7 %collective-permute-done.2.far_mid_ref = bf16[128,512]{1,0:T(8,128)(2,1)S(1)} collective-permute-done((bf16[128,512]{1,0:T(8,128)(2,1)S(1)}, bf16[128,512]{1,0:T(8,128)(2,1)S(1)}, u32[]{:S(2)}, u32[]{:S(2)}) %collective-permute-start.2) | collective-permute-done | bytes 131104 | tf_op jit(solution)/shard_map/ppermute | solution.py:413
  46.2 0.0 collective-permute-done.1.near_mid_ref
  46.2 0.0 copy-start.5
  46.2 1.0 %copy-done.5 = bf16[512,512]{1,0:T(8,128)(2,1)S(1)} copy-done((bf16[512,512]{1,0:T(8,128)(2,1)S(1)}, bf16[512,512]{1,0:T(8,128)(2,1)}, u32[]{:S(2)}) %copy-start.5) | copy-done | bytes 524312
  47.2 0.0 copy-start.12
  47.2 0.7 copy-done.12
  47.9 1.4 %mesh_process.1 = (bf16[128,512]{1,0:T(8,128)(2,1)}, bf16[4,32,512]{2,1,0:T(8,128)(2,1)S(1)}, bf16[4,32,512]{2,1,0:T(8,128)(2,1)S(1)}, bf16[32,512]{1,0:T(8,128)(2,1)S(1)}) custom-call(f32[16,512]{1,0:T(8,128)S(1)} %get-tuple-element.20.ids_ref, bf16[128,512]{1,0:T(8,128)(2,1)S(1)} %get-tuple-element.21.mid_ref, ...), custom_call_target="tpu_custom_call" | custom-call | tf_op jit(solution)/shard_map/mesh_process/pallas_call | solution.py:325
  49.3 0.0 copy-start.9
  49.3 7.7 %all_to_all.21.even_ref = bf16[4,32,512]{2,1,0:T(8,128)(2,1)} all-to-all(bf16[4,32,512]{2,1,0:T(8,128)(2,1)S(1)} %get-tuple-element.22), channel_id=1, replica_groups={{0,1,2,3},{4,5,6,7},{8,9,10,11},{12,13,14,15},{16,17,18,19},{20,21,22,2..., dimensions={0} | all-to-all | bytes 262144 | tf_op jit(solution)/shard_map/all_to_all | solution.py:418
  56.9 0.0 copy-done.9
  57.0 6.0 %all-to-all-start.3 = ((bf16[4,32,512]{2,1,0:T(8,128)(2,1)}), bf16[4,32,512]{2,1,0:T(8,128)(2,1)}, u32[]{:S(2)}, u32[]{:S(2)}) async-start(bf16[4,32,512]{2,1,0:T(8,128)(2,1)} %copy-done.9), calls=%async_computation.3 | async-start | bytes 262144 | tf_op jit(solution)/shard_map/all_to_all | solution.py:418
  62.9 0.0 collective-permute-start.3
  62.9 4.8 %collective-permute-done.3.half_ref = bf16[32,512]{1,0:T(8,128)(2,1)S(1)} collective-permute-done((bf16[32,512]{1,0:T(8,128)(2,1)S(1)}, bf16[32,512]{1,0:T(8,128)(2,1)S(1)}, u32[]{:S(2)}, u32[]{:S(2)}) %collective-permute-start.3) | collective-permute-done | bytes 32800 | tf_op jit(solution)/shard_map/ppermute | solution.py:413
  67.8 0.0 all-to-all-done.3.odd_ref
  67.8 0.0 copy-start.1
  67.8 2.2 %copy-done.1 = bf16[512,4096]{1,0:T(8,128)(2,1)S(1)} copy-done((bf16[512,4096]{1,0:T(8,128)(2,1)S(1)}, bf16[512,4096]{1,0:T(8,128)(2,1)}, u32[]{:S(2)}) %copy-start.1) | copy-done | bytes 4194328
  69.9 0.0 copy-start.3
  70.0 0.9 %copy-done.3 = bf16[4,32,512]{2,1,0:T(8,128)(2,1)S(1)} copy-done((bf16[4,32,512]{2,1,0:T(8,128)(2,1)S(1)}, bf16[4,32,512]{2,1,0:T(8,128)(2,1)}, u32[]{:S(2)}) %copy-start.3) | copy-done | bytes 131096
  70.9 0.0 copy-start.6
  70.9 0.9 %copy-done.6 = bf16[512,227]{0,1:T(8,128)(2,1)S(1)} copy-done((bf16[512,227]{0,1:T(8,128)(2,1)S(1)}, bf16[512,227]{0,1:T(8,128)(2,1)}, u32[]{:S(2)}) %copy-start.6) | copy-done | bytes 232472
  71.8 7.1 %decode.1 = bf16[227,4096]{1,0:T(8,128)(2,1)} custom-call(bf16[227,4096]{1,0:T(8,128)(2,1)S(1)} %get-tuple-element.14.grid_ref, bf16[512,4096]{1,0:T(8,128)(2,1)S(1)} %copy-done.1, bf16[192,4096]{1,0:T(8,128)(2,1)S(1)} %get-tuple-element.16.dsum_ref, bf16[227,512]{1,0:T(8,128)(2,1)S(1)} %bitcast.6, bf16[4,32,512]{2,1,0:T(8,128)(2,1)S(1)} %copy-done.3, ...), custom_call_target="tpu_custom_call" | custom-call | tf_op jit(solution)/shard_map/decode/pallas_call | solution.py:389
Async XLA Ops:
  11.1 1.9 %copy-start = (bf16[512,4096]{1,0:T(8,128)(2,1)}, bf16[512,4096]{1,0:T(8,128)(2,1)S(1)}, u32[]{:S(2)}) copy-start(bf16[512,4096]{1,0:T(8,128)(2,1)S(1)} %get-tuple-element.15.lat_ref) | copy-start | bytes 12582916
  13.0 9.1 %copy-start.8 = (bf16[4,32,640]{2,1,0:T(8,128)(2,1)}, bf16[4,32,640]{2,1,0:T(8,128)(2,1)S(1)}, u32[]{:S(2)}) copy-start(bf16[4,32,640]{2,1,0:T(8,128)(2,1)S(1)} %get-tuple-element.18) | copy-start | bytes 491524
  22.1 12.8 %all-to-all-start.1 = ((bf16[4,32,640]{2,1,0:T(8,128)(2,1)}), bf16[4,32,640]{2,1,0:T(8,128)(2,1)}, u32[]{:S(2)}, u32[]{:S(2)}) async-start(bf16[4,32,640]{2,1,0:T(8,128)(2,1)} %copy-done.8), calls=%async_computation.1 | async-start | bytes 327680 | tf_op jit(solution)/shard_map/all_to_all | solution.py:418
  29.8 5.1 %collective-permute-start = (bf16[32,640]{1,0:T(8,128)(2,1)S(1)}, bf16[32,640]{1,0:T(8,128)(2,1)S(1)}, u32[]{:S(2)}, u32[]{:S(2)}) collective-permute-start(bf16[32,640]{1,0:T(8,128)(2,1)S(1)} %get-tuple-element.19.after_ref), channel_id=1, source_target_pairs={{0,8},{1,9},{2,10},{3,11},{4,12},{5,13},{6,14},{7,15},{8,0},{9,1},... | collective-permute-start | bytes 122888 | tf_op jit(solution)/shard_map/ppermute | solution.py:413
  34.9 0.9 %copy-start.2 = (bf16[4,32,640]{2,1,0:T(8,128)(2,1)S(1)}, bf16[4,32,640]{2,1,0:T(8,128)(2,1)}, u32[]{:S(2)}) copy-start(bf16[4,32,640]{2,1,0:T(8,128)(2,1)} %all_to_all.20.even_ref) | copy-start | bytes 491524
  35.8 1.0 %copy-start.4 = (bf16[512,512]{1,0:T(8,128)(2,1)S(1)}, bf16[512,512]{1,0:T(8,128)(2,1)}, u32[]{:S(2)}) copy-start(bf16[512,512]{1,0:T(8,128)(2,1)} %w_ref.2) | copy-start | bytes 1572868
  36.9 0.9 %copy-start.10 = (bf16[128,512]{1,0:T(8,128)(2,1)S(1)}, bf16[128,512]{1,0:T(8,128)(2,1)}, u32[]{:S(2)}) copy-start(bf16[128,512]{1,0:T(8,128)(2,1)} %mesh_ref.1) | copy-start | bytes 393220
  39.0 7.2 %collective-permute-start.2 = (bf16[128,512]{1,0:T(8,128)(2,1)S(1)}, bf16[128,512]{1,0:T(8,128)(2,1)S(1)}, u32[]{:S(2)}, u32[]{:S(2)}) collective-permute-start(bf16[128,512]{1,0:T(8,128)(2,1)S(1)} %get-tuple-element.21.mid_ref), channel_id=1, source_target_pairs={{0,15},{1,2},{2,1},{3,4},{4,3},{5,6},{6,5},{7,8},{8,7},{9,10},{10,... | collective-permute-start | bytes 393224 | tf_op jit(solution)/shard_map/ppermute | solution.py:413
  40.9 5.2 %collective-permute-start.1 = (bf16[128,512]{1,0:T(8,128)(2,1)S(1)}, bf16[128,512]{1,0:T(8,128)(2,1)S(1)}, u32[]{:S(2)}, u32[]{:S(2)}) collective-permute-start(bf16[128,512]{1,0:T(8,128)(2,1)S(1)} %get-tuple-element.21.mid_ref), channel_id=1, source_target_pairs={{0,1},{1,0},{2,3},{3,2},{4,5},{5,4},{6,7},{7,6},{8,9},{9,8},{10,11... | collective-permute-start | bytes 393224 | tf_op jit(solution)/shard_map/ppermute | solution.py:413
  41.0 0.9 %copy-start.7 = (bf16[4,6,32,32]{3,2,1,0:T(8,128)(2,1)S(1)}, bf16[4,6,32,32]{3,2,1,0:T(8,128)(2,1)}, u32[]{:S(2)}) copy-start(bf16[4,6,32,32]{3,2,1,0:T(8,128)(2,1)} %coef_ref.1) | copy-start | bytes 147460
  41.9 0.7 copy-start.11
  46.2 1.0 %copy-start.5 = (bf16[512,512]{1,0:T(8,128)(2,1)S(1)}, bf16[512,512]{1,0:T(8,128)(2,1)}, u32[]{:S(2)}) copy-start(bf16[512,512]{1,0:T(8,128)(2,1)} %w_ref.3) | copy-start | bytes 1572868
  47.2 0.7 copy-start.12
  49.3 7.7 %copy-start.9 = (bf16[4,32,512]{2,1,0:T(8,128)(2,1)}, bf16[4,32,512]{2,1,0:T(8,128)(2,1)S(1)}, u32[]{:S(2)}) copy-start(bf16[4,32,512]{2,1,0:T(8,128)(2,1)S(1)} %get-tuple-element.23) | copy-start | bytes 393220
  57.0 10.8 %all-to-all-start.3 = ((bf16[4,32,512]{2,1,0:T(8,128)(2,1)}), bf16[4,32,512]{2,1,0:T(8,128)(2,1)}, u32[]{:S(2)}, u32[]{:S(2)}) async-start(bf16[4,32,512]{2,1,0:T(8,128)(2,1)} %copy-done.9), calls=%async_computation.3 | async-start | bytes 262144 | tf_op jit(solution)/shard_map/all_to_all | solution.py:418
  62.9 4.8 %collective-permute-start.3 = (bf16[32,512]{1,0:T(8,128)(2,1)S(1)}, bf16[32,512]{1,0:T(8,128)(2,1)S(1)}, u32[]{:S(2)}, u32[]{:S(2)}) collective-permute-start(bf16[32,512]{1,0:T(8,128)(2,1)S(1)} %get-tuple-element.24), channel_id=1, source_target_pairs={{0,8},{1,9},{2,10},{3,11},{4,12},{5,13},{6,14},{7,15},{8,0},{9,1},... | collective-permute-start | bytes 98312 | tf_op jit(solution)/shard_map/ppermute | solution.py:413
  67.8 2.2 %copy-start.1 = (bf16[512,4096]{1,0:T(8,128)(2,1)S(1)}, bf16[512,4096]{1,0:T(8,128)(2,1)}, u32[]{:S(2)}) copy-start(bf16[512,4096]{1,0:T(8,128)(2,1)} %copy-done) | copy-start | bytes 12582916
  69.9 0.9 %copy-start.3 = (bf16[4,32,512]{2,1,0:T(8,128)(2,1)S(1)}, bf16[4,32,512]{2,1,0:T(8,128)(2,1)}, u32[]{:S(2)}) copy-start(bf16[4,32,512]{2,1,0:T(8,128)(2,1)} %all_to_all.21.even_ref) | copy-start | bytes 393220
  70.9 0.9 %copy-start.6 = (bf16[512,227]{0,1:T(8,128)(2,1)S(1)}, bf16[512,227]{0,1:T(8,128)(2,1)}, u32[]{:S(2)}) copy-start(bf16[512,227]{0,1:T(8,128)(2,1)} %param.25) | copy-start | bytes 697348

commit v5 on v3

--- a/solution.py
+++ b/solution.py
@@ -13,6 +13,7 @@
 OWN, HALF, ODD, FAR, EVEN, NEAR = range(6)
 SLOTS = 6
 PAD = 128
+AHEAD = 3
 
 
 def partner(slot, me, parts):
@@ -100,7 +101,7 @@
     send_refs = rest[:SLOTS]
     (
         slot_ref, owner_ref, w_ref, enc_ref, dec_ref, wt_ref, tgt_ref, ids_ref, msum_ref,
-        acc_ref, small_sems, sems,
+        hold_ref, acc_ref, small_sems, sems,
     ) = rest[SLOTS:]
     tiles, block_mesh, block_grid = enc_ref.shape
     channels, points = grid_ref.shape
@@ -129,43 +130,64 @@
     ]
     for copy in small:
         copy.start()
-    for step in range(steps):
+    def start(step):
         for copy in copies(step):
             copy.start()
+
+    for step in range(AHEAD):
+        start(step)
+    ids_ref[...] = lax.broadcasted_iota(jnp.int32, ids_ref.shape, 0).astype(BF16)
+    acc_ref[...] = jnp.zeros_like(acc_ref)
+    msum_ref[1] = jnp.zeros(msum_ref.shape[1:], BF16)
+    hold_ref[1] = jnp.zeros(hold_ref.shape[1:], BF16)
     for copy in small:
         copy.wait()
     wt_ref[:, :channels] = w_ref[...].astype(F32).T.astype(BF16)
     fill_targets(parts, per_block, block_mesh, owner_ref, tgt_ref)
-    ids_ref[...] = lax.broadcasted_iota(jnp.int32, ids_ref.shape, 0).astype(BF16)
-    acc_ref[...] = jnp.zeros_like(acc_ref)
-
-    @pl.loop(0, steps)
-    def _(step):
-        for copy in copies(step):
-            copy.wait()
-        cols = pl.ds(pl.multiple_of(step * width, width), width)
-        for b in range(blocks):
-            hot = hot_rows(ids_ref[...], tgt_ref[pl.ds(step * blocks + b, 1), :])
-            some = pl.ds(step * chunk + b * per_block, per_block)
-            both = jnp.concatenate(
-                [
-                    enc_ref[some].reshape(wide, block_grid),
-                    dec_ref[some].reshape(wide, block_grid),
-                ],
-                axis=1,
-            )
-            sums = jnp.dot(hot, both, preferred_element_type=F32).astype(BF16)
-            msum_ref[:, b * block_grid : (b + 1) * block_grid] = sums[:, :block_grid]
-            first = pl.multiple_of((step * blocks + b) * block_grid, block_grid)
-            dsum_ref[:, pl.ds(first, block_grid)] = sums[:, block_grid:]
-        lat = silu(
-            jnp.dot(wt_ref[:, :channels], grid_ref[:, cols], preferred_element_type=F32)
-        ).astype(BF16)
-        lat_ref[:, cols] = lat
+
+    def collect(slot):
         acc_ref[...] += lax.dot_general(
-            lat, msum_ref[...], (((1,), (1,)), ((), ())), preferred_element_type=F32
+            hold_ref[slot], msum_ref[slot], (((1,), (1,)), ((), ())), preferred_element_type=F32
         )
 
+    @pl.loop(0, steps // 2)
+    def _(pair):
+        for slot in range(2):
+            step = 2 * pair + slot
+
+            @pl.when(step + AHEAD < steps)
+            def _():
+                start(step + AHEAD)
+
+            for copy in copies(step):
+                copy.wait()
+            collect(1 - slot)
+            cols = pl.ds(pl.multiple_of(step * width, width), width)
+            for b in range(blocks):
+                hot = hot_rows(ids_ref[...], tgt_ref[pl.ds(step * blocks + b, 1), :])
+                some = pl.ds(step * chunk + b * per_block, per_block)
+                both = jnp.concatenate(
+                    [
+                        enc_ref[some].reshape(wide, block_grid),
+                        dec_ref[some].reshape(wide, block_grid),
+                    ],
+                    axis=1,
+                )
+                sums = jnp.dot(hot, both, preferred_element_type=F32).astype(BF16)
+                msum_ref[slot, :, b * block_grid : (b + 1) * block_grid] = sums[:, :block_grid]
+                first = pl.multiple_of((step * blocks + b) * block_grid, block_grid)
+                dsum_ref[:, pl.ds(first, block_grid)] = sums[:, block_grid:]
+            for half in range(0, width, 256):
+                part = pl.ds(pl.multiple_of(step * width + half, 256), 256)
+                lat = silu(
+                    jnp.dot(
+                        wt_ref[:, :channels], grid_ref[:, part], preferred_element_type=F32
+                    )
+                ).astype(BF16)
+                lat_ref[:, part] = lat
+                hold_ref[slot, :, half : half + 256] = lat
+
+    collect(1)
     me = lax.axis_index("nodes")
     flipped = acc_ref[...].T.astype(BF16)
     for s in range(SLOTS):
@@ -204,7 +226,8 @@
             pltpu.VMEM((latent, 256), BF16),
             pltpu.VMEM((grid_blocks, wide), F32),
             pltpu.VMEM((rows, 128), BF16),
-            pltpu.VMEM((rows, width), BF16),
+            pltpu.VMEM((2, rows, width), BF16),
+            pltpu.VMEM((2, latent, width), BF16),
             pltpu.VMEM((latent, rows), F32),
             pltpu.SemaphoreType.DMA((3,)),
             pltpu.SemaphoreType.DMA((3, steps)),
@@ -328,7 +351,7 @@
 
 def decode_kernel(width, grid_ref, lat_ref, dsum_ref, w_ref, *rest):
     slots = rest[:SLOTS]
-    out_hbm, back_ref, pred_ref, sems = rest[SLOTS:]
+    out_hbm, back_ref, pred_ref, hold_ref, sems = rest[SLOTS:]
     steps = grid_ref.shape[1] // width
 
     def copy_out(step):
@@ -338,17 +361,33 @@
     joined = jnp.concatenate([slot[...] for slot in slots], axis=0)
     back_ref[...] = joined.astype(F32).T.astype(BF16)
 
-    @pl.loop(0, steps)
-    def _(step):
+    hold_ref[1] = jnp.zeros(hold_ref.shape[1:], BF16)
+
+    def predict(step, slot):
         cols = pl.ds(pl.multiple_of(step * width, width), width)
-        decoded = jnp.dot(back_ref[...], dsum_ref[:, cols], preferred_element_type=F32)
-        hidden = silu(lat_ref[:, cols].astype(F32) + decoded).astype(BF16)
         pred_ref[:, cols] = (
             grid_ref[:, cols].astype(F32)
-            + jnp.dot(w_ref[...], hidden, preferred_element_type=F32)
+            + jnp.dot(w_ref[...], hold_ref[slot], preferred_element_type=F32)
         ).astype(BF16)
-        copy_out(step).start()
-
+
+    @pl.loop(0, steps // 2)
+    def _(pair):
+        for slot in range(2):
+            step = 2 * pair + slot
+            before = jnp.maximum(step - 1, 0)
+            predict(before, 1 - slot)
+            for half in range(0, width, 256):
+                part = pl.ds(pl.multiple_of(step * width + half, 256), 256)
+                decoded = jnp.dot(back_ref[...], dsum_ref[:, part], preferred_element_type=F32)
+                hidden = silu(lat_ref[:, part].astype(F32) + decoded)
+                hold_ref[slot, :, half : half + 256] = hidden.astype(BF16)
+
+            @pl.when(step > 0)
+            def _():
+                copy_out(before).start()
+
+    predict(steps - 1, 1)
+    copy_out(steps - 1).start()
     for step in range(steps):
         copy_out(step).wait()
 
@@ -367,6 +406,7 @@
         scratch_shapes=[
             pltpu.VMEM((latent, rows), BF16),
             pltpu.VMEM((channels, points), BF16),
+            pltpu.VMEM((2, latent, width), BF16),
             pltpu.SemaphoreType.DMA((points // width,)),
         ],
         compiler_params=pltpu.CompilerParams(vmem_limit_bytes=24 * MIB),

time: 45.4 us -> 42.8 us (0.943)
  Pallas kernels: 19.1 us -> 16.5 us
    pallas_call x1, Pallas kernels: 10.5 us -> 8.53 us  [encode(): pl.pallas_call(functools.partial(encode_kernel, parts, width), in_specs=[...]
    pallas_call x1, Pallas kernels: 6.12 us -> 5.46 us  [decode(): pl.pallas_call(functools.partial(decode_kernel, width), in_specs=[vmem] *...]
where the time goes in v5:
time: 42.8 us; the launch traced here: 42.7 us
  Pallas kernels  16.5 us (39%)
  starting transfers between devices  13.4 us (31%)
  waiting for transfers between devices  12 us (28%)
  between operations  0.76 us (2%)
    ppermute x12, starting transfers between devices, swap(): return lax.ppermute(x, 'nodes', pairs)  13.4 us
    ppermute x12, waiting for transfers between devices, swap(): return lax.ppermute(x, 'nodes', pairs)  12 us
    pallas_call x1, Pallas kernels, encode(): pl.pallas_call(functools.partial(encode_kernel, parts, width), in_specs=[...  8.53 us
    pallas_call x1, Pallas kernels, decode(): pl.pallas_call(functools.partial(decode_kernel, width), in_specs=[vmem] *...  5.46 us
    pallas_call x1, Pallas kernels, process(): pl.pallas_call(process_kernel, in_specs=[vmem] * 7, out_specs=[vmem] * (1...  1.31 us
    pallas_call x1, Pallas kernels, prepare(): pl.pallas_call(functools.partial(prepare_kernel, parts), in_specs=[pl.Blo...  0.88 us
  transfers between devices with their start and end apart: 12, of which 5 were waited for; matrix products, arithmetic and copies ran while one was open for 0% of the time, Pallas kernels for 2%

profile of v5, /device:TPU:0, one launch (start us, length us, event | category | flops | bytes accessed | tf_op | source)
XLA Modules:
  0.0 42.7 jit_solution(499430662689187793)
XLA Ops:
  0.6 0.0 copy-start
  0.6 0.0 copy-start.4
  0.7 0.0 copy-start.3
  0.7 0.0 copy-start.5
  0.7 0.0 copy-start.1
  0.7 0.0 copy-start.6
  0.7 8.5 %encode.1 = (bf16[512,4096]{1,0:T(8,128)(2,1)S(1)}, bf16[192,4096]{1,0:T(8,128)(2,1)S(1)}, bf16[227,4096]{1,0:T(8,128)(2,1)S(1)}, bf16[32,640]{1,0:T(8,128)(2,1)...) custom-call(s32[16]{0:T(128)} %slot_hbm.1, ...), custom_call_target="tpu_custom_call" | custom-call | tf_op jit(solution)/shard_map/encode/pallas_call | solution.py:210
  9.2 0.0 copy-start.2
  9.2 4.1 %collective-permute-start = (bf16[32,640]{1,0:T(8,128)(2,1)S(1)}, bf16[32,640]{1,0:T(8,128)(2,1)S(1)}, u32[]{:S(2)}, u32[]{:S(2)}) collective-permute-start(bf16[32,640]{1,0:T(8,128)(2,1)S(1)} %get-tuple-element.24), channel_id=1, source_target_pairs={{0,8},{1,9},{2,10},{3,11},{4,12},{5,13},{6,14},{7,15},{8,0},{9,1},... | collective-permute-start | bytes 122888 | tf_op jit(solution)/shard_map/ppermute | solution.py:426
  13.3 2.3 %collective-permute-start.1 = (bf16[32,640]{1,0:T(8,128)(2,1)S(1)}, bf16[32,640]{1,0:T(8,128)(2,1)S(1)}, u32[]{:S(2)}, u32[]{:S(2)}) collective-permute-start(bf16[32,640]{1,0:T(8,128)(2,1)S(1)} %get-tuple-element.25), channel_id=1, source_target_pairs={{0,14},{1,15},{2,4},{3,5},{4,2},{5,3},{6,8},{7,9},{8,6},{9,7},{10,... | collective-permute-start | bytes 122888 | tf_op jit(solution)/shard_map/ppermute | solution.py:426
  15.7 1.3 %collective-permute-start.2 = (bf16[32,640]{1,0:T(8,128)(2,1)S(1)}, bf16[32,640]{1,0:T(8,128)(2,1)S(1)}, u32[]{:S(2)}, u32[]{:S(2)}) collective-permute-start(bf16[32,640]{1,0:T(8,128)(2,1)S(1)} %get-tuple-element.26), channel_id=1, source_target_pairs={{0,15},{1,2},{2,1},{3,4},{4,3},{5,6},{6,5},{7,8},{8,7},{9,10},{10,... | collective-permute-start | bytes 122888 | tf_op jit(solution)/shard_map/ppermute | solution.py:426
  17.0 0.0 collective-permute-start.3
  17.0 0.7 %collective-permute-start.4 = (bf16[32,640]{1,0:T(8,128)(2,1)S(1)}, bf16[32,640]{1,0:T(8,128)(2,1)S(1)}, u32[]{:S(2)}, u32[]{:S(2)}) collective-permute-start(bf16[32,640]{1,0:T(8,128)(2,1)S(1)} %get-tuple-element.28), channel_id=1, source_target_pairs={{0,1},{1,0},{2,3},{3,2},{4,5},{5,4},{6,7},{7,6},{8,9},{9,8},{10,11... | collective-permute-start | bytes 122888 | tf_op jit(solution)/shard_map/ppermute | solution.py:426
  17.6 0.0 collective-permute-done.refs_1_
  17.6 2.4 %collective-permute-done.1.refs_2_ = bf16[32,640]{1,0:T(8,128)(2,1)S(1)} collective-permute-done((bf16[32,640]{1,0:T(8,128)(2,1)S(1)}, bf16[32,640]{1,0:T(8,128)(2,1)S(1)}, u32[]{:S(2)}, u32[]{:S(2)}) %collective-permute-start.1) | collective-permute-done | bytes 40992 | tf_op jit(solution)/shard_map/ppermute | solution.py:426
  20.0 1.7 %collective-permute-done.2.refs_3_ = bf16[32,640]{1,0:T(8,128)(2,1)S(1)} collective-permute-done((bf16[32,640]{1,0:T(8,128)(2,1)S(1)}, bf16[32,640]{1,0:T(8,128)(2,1)S(1)}, u32[]{:S(2)}, u32[]{:S(2)}) %collective-permute-start.2) | collective-permute-done | bytes 40992 | tf_op jit(solution)/shard_map/ppermute | solution.py:426
  21.8 0.0 collective-permute-done.3.refs_4_
  21.8 0.0 collective-permute-done.4.refs_5_
  21.8 0.0 copy-done
  21.8 0.0 copy-done.4
  21.8 0.3 mesh_update.1
  22.1 1.7 %collective-permute-start.6 = (bf16[128,512]{1,0:T(8,128)(2,1)S(1)}, bf16[128,512]{1,0:T(8,128)(2,1)S(1)}, u32[]{:S(2)}, u32[]{:S(2)}) collective-permute-start(bf16[128,512]{1,0:T(8,128)(2,1)S(1)} %get-tuple-element.30.mid_ref), channel_id=1, source_target_pairs={{0,15},{1,2},{2,1},{3,4},{4,3},{5,6},{6,5},{7,8},{8,7},{9,10},{10,... | collective-permute-start | bytes 393224 | tf_op jit(solution)/shard_map/ppermute | solution.py:426
  23.8 0.0 collective-permute-start.5
  23.8 0.0 copy-done.3
  23.8 0.0 copy-done.5
  23.8 0.9 %prepare.1.near_ref = bf16[128,384]{1,0:T(8,128)(2,1)S(1)} custom-call(s32[4,6]{1,0:T(4,128)S(1)} %copy-done.5, bf16[4,6,32,32]{3,2,1,0:T(8,128)(2,1)S(1)} %copy-done.3, bf16[32,640]{1,0:T(8,128)(2,1)S(1)} %get-tuple-element.23.refs_0_.after_ref), custom_call_target="tpu_custom_call" | custom-call | flops 18874368 | bytes 393216 | tf_op jit(solution)/shard_map/prepare/pallas_call | solution.py:271
  24.7 4.6 %collective-permute-done.6.far_mid_ref = bf16[128,512]{1,0:T(8,128)(2,1)S(1)} collective-permute-done((bf16[128,512]{1,0:T(8,128)(2,1)S(1)}, bf16[128,512]{1,0:T(8,128)(2,1)S(1)}, u32[]{:S(2)}, u32[]{:S(2)}) %collective-permute-start.6) | collective-permute-done | bytes 131104 | tf_op jit(solution)/shard_map/ppermute | solution.py:426
  29.3 0.0 collective-permute-done.5.near_mid_ref
  29.3 0.0 copy-done.1
  29.3 0.0 copy-done.6
  29.3 1.3 %mesh_process.1 = (bf16[128,512]{1,0:T(8,128)(2,1)}, bf16[32,512]{1,0:T(8,128)(2,1)S(1)}, bf16[32,512]{1,0:T(8,128)(2,1)S(1)}, bf16[32,512]{1,0:T(8,128)(2,1)S(1...) custom-call(f32[8,512]{1,0:T(8,128)S(1)} %get-tuple-element.29.ids_ref, ...), custom_call_target="tpu_custom_call" | custom-call | tf_op jit(solution)/shard_map/mesh_process/pallas_call | solution.py:341
  30.6 0.0 collective-permute-start.7
  30.6 0.1 collective-permute-start.8
  30.7 1.6 %collective-permute-start.9 = (bf16[32,512]{1,0:T(8,128)(2,1)S(1)}, bf16[32,512]{1,0:T(8,128)(2,1)S(1)}, u32[]{:S(2)}, u32[]{:S(2)}) collective-permute-start(bf16[32,512]{1,0:T(8,128)(2,1)S(1)} %get-tuple-element.34), channel_id=1, source_target_pairs={{0,15},{1,2},{2,1},{3,4},{4,3},{5,6},{6,5},{7,8},{8,7},{9,10},{10,... | collective-permute-start | bytes 98312 | tf_op jit(solution)/shard_map/ppermute | solution.py:426
  32.2 1.7 %collective-permute-start.10 = (bf16[32,512]{1,0:T(8,128)(2,1)S(1)}, bf16[32,512]{1,0:T(8,128)(2,1)S(1)}, u32[]{:S(2)}, u32[]{:S(2)}) collective-permute-start(bf16[32,512]{1,0:T(8,128)(2,1)S(1)} %get-tuple-element.35), channel_id=1, source_target_pairs={{0,2},{1,3},{2,0},{3,1},{4,6},{5,7},{6,4},{7,5},{8,10},{9,11},{10,... | collective-permute-start | bytes 98312 | tf_op jit(solution)/shard_map/ppermute | solution.py:426
  33.9 0.0 collective-permute-start.11
  33.9 1.7 %collective-permute-done.7.rest_1_ = bf16[32,512]{1,0:T(8,128)(2,1)S(1)} collective-permute-done((bf16[32,512]{1,0:T(8,128)(2,1)S(1)}, bf16[32,512]{1,0:T(8,128)(2,1)S(1)}, u32[]{:S(2)}, u32[]{:S(2)}) %collective-permute-start.7) | collective-permute-done | bytes 32800 | tf_op jit(solution)/shard_map/ppermute | solution.py:426
  35.6 1.6 %collective-permute-done.8.rest_2_ = bf16[32,512]{1,0:T(8,128)(2,1)S(1)} collective-permute-done((bf16[32,512]{1,0:T(8,128)(2,1)S(1)}, bf16[32,512]{1,0:T(8,128)(2,1)S(1)}, u32[]{:S(2)}, u32[]{:S(2)}) %collective-permute-start.8) | collective-permute-done | bytes 32800 | tf_op jit(solution)/shard_map/ppermute | solution.py:426
  37.2 0.0 collective-permute-done.9.rest_3_
  37.2 0.0 collective-permute-done.10.rest_4_
  37.2 0.0 collective-permute-done.11.rest_5_
  37.2 0.0 copy-done.2
  37.2 5.5 %decode.1 = bf16[227,4096]{1,0:T(8,128)(2,1)} custom-call(bf16[227,4096]{1,0:T(8,128)(2,1)S(1)} %get-tuple-element.20.grid_ref, bf16[512,4096]{1,0:T(8,128)(2,1)S(1)} %get-tuple-element.21.lat_ref, bf16[192,4096]{1,0:T(8,128)(2,1)S(1)} %get-tuple-element.22.dsum_ref, bf16[227,512]{1,0:T(8,128)(2,1)S(1)} %bitcast.6, ...), custom_call_target="tpu_custom_call" | custom-call | tf_op jit(solution)/shard_map/decode/pallas_call | solution.py:401
Async XLA Ops:
  0.6 21.2 %copy-start = (bf16[512,512]{1,0:T(8,128)(2,1)S(1)}, bf16[512,512]{1,0:T(8,128)(2,1)}, u32[]{:S(2)}) copy-start(bf16[512,512]{1,0:T(8,128)(2,1)} %refs_7_.1) | copy-start | bytes 1572868
  0.6 21.2 %copy-start.4 = (bf16[128,512]{1,0:T(8,128)(2,1)S(1)}, bf16[128,512]{1,0:T(8,128)(2,1)}, u32[]{:S(2)}) copy-start(bf16[128,512]{1,0:T(8,128)(2,1)} %refs_6_.1) | copy-start | bytes 393220
  0.7 23.1 %copy-start.3 = (bf16[4,6,32,32]{3,2,1,0:T(8,128)(2,1)S(1)}, bf16[4,6,32,32]{3,2,1,0:T(8,128)(2,1)}, u32[]{:S(2)}) copy-start(bf16[4,6,32,32]{3,2,1,0:T(8,128)(2,1)} %coef_ref.1) | copy-start | bytes 147460
  0.7 23.1 %copy-start.5 = (s32[4,6]{1,0:T(4,128)S(1)}, s32[4,6]{1,0:T(4,128)}, u32[]{:S(2)}) copy-start(s32[4,6]{1,0:T(4,128)} %adj_ref.1) | copy-start | bytes 292
  0.7 28.6 %copy-start.1 = (bf16[512,512]{1,0:T(8,128)(2,1)S(1)}, bf16[512,512]{1,0:T(8,128)(2,1)}, u32[]{:S(2)}) copy-start(bf16[512,512]{1,0:T(8,128)(2,1)} %w_ref.1) | copy-start | bytes 1572868
  0.7 28.6 %copy-start.6 = (f32[512]{0:T(512)S(1)}, f32[512]{0:T(512)}, u32[]{:S(2)}) copy-start(f32[512]{0:T(512)} %param.22) | copy-start | bytes 6148
  9.2 28.0 %copy-start.2 = (bf16[512,227]{0,1:T(8,128)(2,1)S(1)}, bf16[512,227]{0,1:T(8,128)(2,1)}, u32[]{:S(2)}) copy-start(bf16[512,227]{0,1:T(8,128)(2,1)} %param.25) | copy-start | bytes 697348
  9.2 8.4 %collective-permute-start = (bf16[32,640]{1,0:T(8,128)(2,1)S(1)}, bf16[32,640]{1,0:T(8,128)(2,1)S(1)}, u32[]{:S(2)}, u32[]{:S(2)}) collective-permute-start(bf16[32,640]{1,0:T(8,128)(2,1)S(1)} %get-tuple-element.24), channel_id=1, source_target_pairs={{0,8},{1,9},{2,10},{3,11},{4,12},{5,13},{6,14},{7,15},{8,0},{9,1},... | collective-permute-start | bytes 122888 | tf_op jit(solution)/shard_map/ppermute | solution.py:426
  13.3 6.7 %collective-permute-start.1 = (bf16[32,640]{1,0:T(8,128)(2,1)S(1)}, bf16[32,640]{1,0:T(8,128)(2,1)S(1)}, u32[]{:S(2)}, u32[]{:S(2)}) collective-permute-start(bf16[32,640]{1,0:T(8,128)(2,1)S(1)} %get-tuple-element.25), channel_id=1, source_target_pairs={{0,14},{1,15},{2,4},{3,5},{4,2},{5,3},{6,8},{7,9},{8,6},{9,7},{10,... | collective-permute-start | bytes 122888 | tf_op jit(solution)/shard_map/ppermute | solution.py:426
  15.7 6.1 %collective-permute-start.2 = (bf16[32,640]{1,0:T(8,128)(2,1)S(1)}, bf16[32,640]{1,0:T(8,128)(2,1)S(1)}, u32[]{:S(2)}, u32[]{:S(2)}) collective-permute-start(bf16[32,640]{1,0:T(8,128)(2,1)S(1)} %get-tuple-element.26), channel_id=1, source_target_pairs={{0,15},{1,2},{2,1},{3,4},{4,3},{5,6},{6,5},{7,8},{8,7},{9,10},{10,... | collective-permute-start | bytes 122888 | tf_op jit(solution)/shard_map/ppermute | solution.py:426
  17.0 4.8 %collective-permute-start.3 = (bf16[32,640]{1,0:T(8,128)(2,1)S(1)}, bf16[32,640]{1,0:T(8,128)(2,1)S(1)}, u32[]{:S(2)}, u32[]{:S(2)}) collective-permute-start(bf16[32,640]{1,0:T(8,128)(2,1)S(1)} %get-tuple-element.27), channel_id=1, source_target_pairs={{0,2},{1,3},{2,0},{3,1},{4,6},{5,7},{6,4},{7,5},{8,10},{9,11},{10,... | collective-permute-start | bytes 122888 | tf_op jit(solution)/shard_map/ppermute | solution.py:426
  17.0 4.8 %collective-permute-start.4 = (bf16[32,640]{1,0:T(8,128)(2,1)S(1)}, bf16[32,640]{1,0:T(8,128)(2,1)S(1)}, u32[]{:S(2)}, u32[]{:S(2)}) collective-permute-start(bf16[32,640]{1,0:T(8,128)(2,1)S(1)} %get-tuple-element.28), channel_id=1, source_target_pairs={{0,1},{1,0},{2,3},{3,2},{4,5},{5,4},{6,7},{7,6},{8,9},{9,8},{10,11... | collective-permute-start | bytes 122888 | tf_op jit(solution)/shard_map/ppermute | solution.py:426
  22.1 7.2 %collective-permute-start.6 = (bf16[128,512]{1,0:T(8,128)(2,1)S(1)}, bf16[128,512]{1,0:T(8,128)(2,1)S(1)}, u32[]{:S(2)}, u32[]{:S(2)}) collective-permute-start(bf16[128,512]{1,0:T(8,128)(2,1)S(1)} %get-tuple-element.30.mid_ref), channel_id=1, source_target_pairs={{0,15},{1,2},{2,1},{3,4},{4,3},{5,6},{6,5},{7,8},{8,7},{9,10},{10,... | collective-permute-start | bytes 393224 | tf_op jit(solution)/shard_map/ppermute | solution.py:426
  23.8 5.5 %collective-permute-start.5 = (bf16[128,512]{1,0:T(8,128)(2,1)S(1)}, bf16[128,512]{1,0:T(8,128)(2,1)S(1)}, u32[]{:S(2)}, u32[]{:S(2)}) collective-permute-start(bf16[128,512]{1,0:T(8,128)(2,1)S(1)} %get-tuple-element.30.mid_ref), channel_id=1, source_target_pairs={{0,1},{1,0},{2,3},{3,2},{4,5},{5,4},{6,7},{7,6},{8,9},{9,8},{10,11... | collective-permute-start | bytes 393224 | tf_op jit(solution)/shard_map/ppermute | solution.py:426
  30.6 5.0 %collective-permute-start.7 = (bf16[32,512]{1,0:T(8,128)(2,1)S(1)}, bf16[32,512]{1,0:T(8,128)(2,1)S(1)}, u32[]{:S(2)}, u32[]{:S(2)}) collective-permute-start(bf16[32,512]{1,0:T(8,128)(2,1)S(1)} %get-tuple-element.32), channel_id=1, source_target_pairs={{0,8},{1,9},{2,10},{3,11},{4,12},{5,13},{6,14},{7,15},{8,0},{9,1},... | collective-permute-start | bytes 98312 | tf_op jit(solution)/shard_map/ppermute | solution.py:426
  30.6 6.6 %collective-permute-start.8 = (bf16[32,512]{1,0:T(8,128)(2,1)S(1)}, bf16[32,512]{1,0:T(8,128)(2,1)S(1)}, u32[]{:S(2)}, u32[]{:S(2)}) collective-permute-start(bf16[32,512]{1,0:T(8,128)(2,1)S(1)} %get-tuple-element.33), channel_id=1, source_target_pairs={{0,14},{1,15},{2,4},{3,5},{4,2},{5,3},{6,8},{7,9},{8,6},{9,7},{10,... | collective-permute-start | bytes 98312 | tf_op jit(solution)/shard_map/ppermute | solution.py:426
  30.7 6.5 %collective-permute-start.9 = (bf16[32,512]{1,0:T(8,128)(2,1)S(1)}, bf16[32,512]{1,0:T(8,128)(2,1)S(1)}, u32[]{:S(2)}, u32[]{:S(2)}) collective-permute-start(bf16[32,512]{1,0:T(8,128)(2,1)S(1)} %get-tuple-element.34), channel_id=1, source_target_pairs={{0,15},{1,2},{2,1},{3,4},{4,3},{5,6},{6,5},{7,8},{8,7},{9,10},{10,... | collective-permute-start | bytes 98312 | tf_op jit(solution)/shard_map/ppermute | solution.py:426
  32.2 5.0 %collective-permute-start.10 = (bf16[32,512]{1,0:T(8,128)(2,1)S(1)}, bf16[32,512]{1,0:T(8,128)(2,1)S(1)}, u32[]{:S(2)}, u32[]{:S(2)}) collective-permute-start(bf16[32,512]{1,0:T(8,128)(2,1)S(1)} %get-tuple-element.35), channel_id=1, source_target_pairs={{0,2},{1,3},{2,0},{3,1},{4,6},{5,7},{6,4},{7,5},{8,10},{9,11},{10,... | collective-permute-start | bytes 98312 | tf_op jit(solution)/shard_map/ppermute | solution.py:426
  33.9 3.3 %collective-permute-start.11 = (bf16[32,512]{1,0:T(8,128)(2,1)S(1)}, bf16[32,512]{1,0:T(8,128)(2,1)S(1)}, u32[]{:S(2)}, u32[]{:S(2)}) collective-permute-start(bf16[32,512]{1,0:T(8,128)(2,1)S(1)} %get-tuple-element.36), channel_id=1, source_target_pairs={{0,1},{1,0},{2,3},{3,2},{4,5},{5,4},{6,7},{7,6},{8,9},{9,8},{10,11... | collective-permute-start | bytes 98312 | tf_op jit(solution)/shard_map/ppermute | solution.py:426

commit v6 on v5

--- a/solution.py
+++ b/solution.py
@@ -14,6 +14,7 @@
 SLOTS = 6
 PAD = 128
 AHEAD = 3
+TALL = 128
 
 
 def partner(slot, me, parts):
@@ -146,9 +147,11 @@
     fill_targets(parts, per_block, block_mesh, owner_ref, tgt_ref)
 
     def collect(slot):
-        acc_ref[...] += lax.dot_general(
-            hold_ref[slot], msum_ref[slot], (((1,), (1,)), ((), ())), preferred_element_type=F32
-        )
+        for top in range(0, latent, TALL):
+            acc_ref[top : top + TALL, :] += lax.dot_general(
+                hold_ref[slot, top : top + TALL, :], msum_ref[slot], (((1,), (1,)), ((), ())),
+                preferred_element_type=F32,
+            )
 
     @pl.loop(0, steps // 2)
     def _(pair):
@@ -179,13 +182,14 @@
                 dsum_ref[:, pl.ds(first, block_grid)] = sums[:, block_grid:]
             for half in range(0, width, 256):
                 part = pl.ds(pl.multiple_of(step * width + half, 256), 256)
-                lat = silu(
-                    jnp.dot(
-                        wt_ref[:, :channels], grid_ref[:, part], preferred_element_type=F32
+                for top in range(0, latent, TALL):
+                    lat = jnp.dot(
+                        wt_ref[top : top + TALL, :channels], grid_ref[:, part],
+                        preferred_element_type=F32,
                     )
-                ).astype(BF16)
-                lat_ref[:, part] = lat
-                hold_ref[slot, :, half : half + 256] = lat
+                    lat = silu(lat).astype(BF16)
+                    lat_ref[top : top + TALL, part] = lat
+                    hold_ref[slot, top : top + TALL, half : half + 256] = lat
 
     collect(1)
     me = lax.axis_index("nodes")
@@ -353,6 +357,8 @@
     slots = rest[:SLOTS]
     out_hbm, back_ref, pred_ref, hold_ref, sems = rest[SLOTS:]
     steps = grid_ref.shape[1] // width
+    channels = grid_ref.shape[0]
+    latent = lat_ref.shape[0]
 
     def copy_out(step):
         cols = pl.ds(pl.multiple_of(step * width, width), width)
@@ -364,11 +370,15 @@
     hold_ref[1] = jnp.zeros(hold_ref.shape[1:], BF16)
 
     def predict(step, slot):
-        cols = pl.ds(pl.multiple_of(step * width, width), width)
-        pred_ref[:, cols] = (
-            grid_ref[:, cols].astype(F32)
-            + jnp.dot(w_ref[...], hold_ref[slot], preferred_element_type=F32)
-        ).astype(BF16)
+        for half in range(0, width, 256):
+            part = pl.ds(pl.multiple_of(step * width + half, 256), 256)
+            for top in range(0, channels, TALL):
+                rows = slice(top, min(top + TALL, channels))
+                pred = jnp.dot(
+                    w_ref[rows, :], hold_ref[slot, :, half : half + 256],
+                    preferred_element_type=F32,
+                )
+                pred_ref[rows, part] = (grid_ref[rows, part].astype(F32) + pred).astype(BF16)
 
     @pl.loop(0, steps // 2)
     def _(pair):
@@ -378,9 +388,13 @@
             predict(before, 1 - slot)
             for half in range(0, width, 256):
                 part = pl.ds(pl.multiple_of(step * width + half, 256), 256)
-                decoded = jnp.dot(back_ref[...], dsum_ref[:, part], preferred_element_type=F32)
-                hidden = silu(lat_ref[:, part].astype(F32) + decoded)
-                hold_ref[slot, :, half : half + 256] = hidden.astype(BF16)
+                for top in range(0, latent, TALL):
+                    rows = slice(top, top + TALL)
+                    decoded = jnp.dot(
+                        back_ref[rows, :], dsum_ref[:, part], preferred_element_type=F32
+                    )
+                    hidden = silu(lat_ref[rows, part].astype(F32) + decoded)
+                    hold_ref[slot, rows, half : half + 256] = hidden.astype(BF16)
 
             @pl.when(step > 0)
             def _():

time: 42.8 us -> 43.8 us (1.023)
  Pallas kernels: 16.5 us -> 17.5 us
    pallas_call x1, Pallas kernels: 8.53 us -> 9.4 us  [encode(): pl.pallas_call(functools.partial(encode_kernel, parts, width), in_specs=[...]
where the time goes in v6:
time: 43.8 us; the launch traced here: 43.7 us
  Pallas kernels  17.5 us (40%)
  starting transfers between devices  13.4 us (31%)
  waiting for transfers between devices  12 us (27%)
  between operations  0.76 us (2%)
    ppermute x12, starting transfers between devices, swap(): return lax.ppermute(x, 'nodes', pairs)  13.4 us
    ppermute x12, waiting for transfers between devices, swap(): return lax.ppermute(x, 'nodes', pairs)  12 us
    pallas_call x1, Pallas kernels, encode(): pl.pallas_call(functools.partial(encode_kernel, parts, width), in_specs=[...  9.4 us
    pallas_call x1, Pallas kernels, decode(): pl.pallas_call(functools.partial(decode_kernel, width), in_specs=[vmem] *...  5.58 us
    pallas_call x1, Pallas kernels, process(): pl.pallas_call(process_kernel, in_specs=[vmem] * 7, out_specs=[vmem] * (1...  1.31 us
    pallas_call x1, Pallas kernels, prepare(): pl.pallas_call(functools.partial(prepare_kernel, parts), in_specs=[pl.Blo...  0.88 us
  transfers between devices with their start and end apart: 12, of which 5 were waited for; matrix products, arithmetic and copies ran while one was open for 0% of the time, Pallas kernels for 2%

profile of v6, /device:TPU:0, one launch (start us, length us, event | category | flops | bytes accessed | tf_op | source)
XLA Modules:
  0.0 43.7 jit_solution(13002288772194168284)
XLA Ops:
  0.6 0.0 copy-start
  0.6 0.0 copy-start.4
  0.7 0.0 copy-start.3
  0.7 0.0 copy-start.5
  0.7 0.0 copy-start.1
  0.7 0.0 copy-start.6
  0.7 9.4 %encode.1 = (bf16[512,4096]{1,0:T(8,128)(2,1)S(1)}, bf16[192,4096]{1,0:T(8,128)(2,1)S(1)}, bf16[227,4096]{1,0:T(8,128)(2,1)S(1)}, bf16[32,640]{1,0:T(8,128)(2,1)...) custom-call(s32[16]{0:T(128)} %slot_hbm.1, ...), custom_call_target="tpu_custom_call" | custom-call | tf_op jit(solution)/shard_map/encode/pallas_call | solution.py:214
  10.1 0.0 copy-start.2
  10.1 4.1 %collective-permute-start = (bf16[32,640]{1,0:T(8,128)(2,1)S(1)}, bf16[32,640]{1,0:T(8,128)(2,1)S(1)}, u32[]{:S(2)}, u32[]{:S(2)}) collective-permute-start(bf16[32,640]{1,0:T(8,128)(2,1)S(1)} %get-tuple-element.24), channel_id=1, source_target_pairs={{0,8},{1,9},{2,10},{3,11},{4,12},{5,13},{6,14},{7,15},{8,0},{9,1},... | collective-permute-start | bytes 122888 | tf_op jit(solution)/shard_map/ppermute | solution.py:440
  14.2 2.3 %collective-permute-start.1 = (bf16[32,640]{1,0:T(8,128)(2,1)S(1)}, bf16[32,640]{1,0:T(8,128)(2,1)S(1)}, u32[]{:S(2)}, u32[]{:S(2)}) collective-permute-start(bf16[32,640]{1,0:T(8,128)(2,1)S(1)} %get-tuple-element.25), channel_id=1, source_target_pairs={{0,14},{1,15},{2,4},{3,5},{4,2},{5,3},{6,8},{7,9},{8,6},{9,7},{10,... | collective-permute-start | bytes 122888 | tf_op jit(solution)/shard_map/ppermute | solution.py:440
  16.5 1.3 %collective-permute-start.2 = (bf16[32,640]{1,0:T(8,128)(2,1)S(1)}, bf16[32,640]{1,0:T(8,128)(2,1)S(1)}, u32[]{:S(2)}, u32[]{:S(2)}) collective-permute-start(bf16[32,640]{1,0:T(8,128)(2,1)S(1)} %get-tuple-element.26), channel_id=1, source_target_pairs={{0,15},{1,2},{2,1},{3,4},{4,3},{5,6},{6,5},{7,8},{8,7},{9,10},{10,... | collective-permute-start | bytes 122888 | tf_op jit(solution)/shard_map/ppermute | solution.py:440
  17.8 0.0 collective-permute-start.3
  17.8 0.7 %collective-permute-start.4 = (bf16[32,640]{1,0:T(8,128)(2,1)S(1)}, bf16[32,640]{1,0:T(8,128)(2,1)S(1)}, u32[]{:S(2)}, u32[]{:S(2)}) collective-permute-start(bf16[32,640]{1,0:T(8,128)(2,1)S(1)} %get-tuple-element.28), channel_id=1, source_target_pairs={{0,1},{1,0},{2,3},{3,2},{4,5},{5,4},{6,7},{7,6},{8,9},{9,8},{10,11... | collective-permute-start | bytes 122888 | tf_op jit(solution)/shard_map/ppermute | solution.py:440
  18.5 0.0 collective-permute-done.refs_1_
  18.5 2.4 %collective-permute-done.1.refs_2_ = bf16[32,640]{1,0:T(8,128)(2,1)S(1)} collective-permute-done((bf16[32,640]{1,0:T(8,128)(2,1)S(1)}, bf16[32,640]{1,0:T(8,128)(2,1)S(1)}, u32[]{:S(2)}, u32[]{:S(2)}) %collective-permute-start.1) | collective-permute-done | bytes 40992 | tf_op jit(solution)/shard_map/ppermute | solution.py:440
  20.9 1.7 %collective-permute-done.2.refs_3_ = bf16[32,640]{1,0:T(8,128)(2,1)S(1)} collective-permute-done((bf16[32,640]{1,0:T(8,128)(2,1)S(1)}, bf16[32,640]{1,0:T(8,128)(2,1)S(1)}, u32[]{:S(2)}, u32[]{:S(2)}) %collective-permute-start.2) | collective-permute-done | bytes 40992 | tf_op jit(solution)/shard_map/ppermute | solution.py:440
  22.6 0.0 collective-permute-done.3.refs_4_
  22.6 0.0 collective-permute-done.4.refs_5_
  22.6 0.0 copy-done
  22.7 0.0 copy-done.4
  22.7 0.3 mesh_update.1
  23.0 1.7 %collective-permute-start.6 = (bf16[128,512]{1,0:T(8,128)(2,1)S(1)}, bf16[128,512]{1,0:T(8,128)(2,1)S(1)}, u32[]{:S(2)}, u32[]{:S(2)}) collective-permute-start(bf16[128,512]{1,0:T(8,128)(2,1)S(1)} %get-tuple-element.30.mid_ref), channel_id=1, source_target_pairs={{0,15},{1,2},{2,1},{3,4},{4,3},{5,6},{6,5},{7,8},{8,7},{9,10},{10,... | collective-permute-start | bytes 393224 | tf_op jit(solution)/shard_map/ppermute | solution.py:440
  24.6 0.0 collective-permute-start.5
  24.6 0.0 copy-done.3
  24.6 0.0 copy-done.5
  24.7 0.9 %prepare.1.near_ref = bf16[128,384]{1,0:T(8,128)(2,1)S(1)} custom-call(s32[4,6]{1,0:T(4,128)S(1)} %copy-done.5, bf16[4,6,32,32]{3,2,1,0:T(8,128)(2,1)S(1)} %copy-done.3, bf16[32,640]{1,0:T(8,128)(2,1)S(1)} %get-tuple-element.23.refs_0_.after_ref), custom_call_target="tpu_custom_call" | custom-call | flops 18874368 | bytes 393216 | tf_op jit(solution)/shard_map/prepare/pallas_call | solution.py:275
  25.5 4.6 %collective-permute-done.6.far_mid_ref = bf16[128,512]{1,0:T(8,128)(2,1)S(1)} collective-permute-done((bf16[128,512]{1,0:T(8,128)(2,1)S(1)}, bf16[128,512]{1,0:T(8,128)(2,1)S(1)}, u32[]{:S(2)}, u32[]{:S(2)}) %collective-permute-start.6) | collective-permute-done | bytes 131104 | tf_op jit(solution)/shard_map/ppermute | solution.py:440
  30.1 0.0 collective-permute-done.5.near_mid_ref
  30.1 0.0 copy-done.1
  30.1 0.0 copy-done.6
  30.1 1.3 %mesh_process.1 = (bf16[128,512]{1,0:T(8,128)(2,1)}, bf16[32,512]{1,0:T(8,128)(2,1)S(1)}, bf16[32,512]{1,0:T(8,128)(2,1)S(1)}, bf16[32,512]{1,0:T(8,128)(2,1)S(1...) custom-call(f32[8,512]{1,0:T(8,128)S(1)} %get-tuple-element.29.ids_ref, ...), custom_call_target="tpu_custom_call" | custom-call | tf_op jit(solution)/shard_map/mesh_process/pallas_call | solution.py:345
  31.5 0.0 collective-permute-start.7
  31.5 0.1 collective-permute-start.8
  31.5 1.6 %collective-permute-start.9 = (bf16[32,512]{1,0:T(8,128)(2,1)S(1)}, bf16[32,512]{1,0:T(8,128)(2,1)S(1)}, u32[]{:S(2)}, u32[]{:S(2)}) collective-permute-start(bf16[32,512]{1,0:T(8,128)(2,1)S(1)} %get-tuple-element.34), channel_id=1, source_target_pairs={{0,15},{1,2},{2,1},{3,4},{4,3},{5,6},{6,5},{7,8},{8,7},{9,10},{10,... | collective-permute-start | bytes 98312 | tf_op jit(solution)/shard_map/ppermute | solution.py:440
  33.1 1.7 %collective-permute-start.10 = (bf16[32,512]{1,0:T(8,128)(2,1)S(1)}, bf16[32,512]{1,0:T(8,128)(2,1)S(1)}, u32[]{:S(2)}, u32[]{:S(2)}) collective-permute-start(bf16[32,512]{1,0:T(8,128)(2,1)S(1)} %get-tuple-element.35), channel_id=1, source_target_pairs={{0,2},{1,3},{2,0},{3,1},{4,6},{5,7},{6,4},{7,5},{8,10},{9,11},{10,... | collective-permute-start | bytes 98312 | tf_op jit(solution)/shard_map/ppermute | solution.py:440
  34.8 0.0 collective-permute-start.11
  34.8 1.7 %collective-permute-done.7.rest_1_ = bf16[32,512]{1,0:T(8,128)(2,1)S(1)} collective-permute-done((bf16[32,512]{1,0:T(8,128)(2,1)S(1)}, bf16[32,512]{1,0:T(8,128)(2,1)S(1)}, u32[]{:S(2)}, u32[]{:S(2)}) %collective-permute-start.7) | collective-permute-done | bytes 32800 | tf_op jit(solution)/shard_map/ppermute | solution.py:440
  36.5 1.6 %collective-permute-done.8.rest_2_ = bf16[32,512]{1,0:T(8,128)(2,1)S(1)} collective-permute-done((bf16[32,512]{1,0:T(8,128)(2,1)S(1)}, bf16[32,512]{1,0:T(8,128)(2,1)S(1)}, u32[]{:S(2)}, u32[]{:S(2)}) %collective-permute-start.8) | collective-permute-done | bytes 32800 | tf_op jit(solution)/shard_map/ppermute | solution.py:440
  38.1 0.0 collective-permute-done.9.rest_3_
  38.1 0.0 collective-permute-done.10.rest_4_
  38.1 0.0 collective-permute-done.11.rest_5_
  38.1 0.0 copy-done.2
  38.1 5.6 %decode.1 = bf16[227,4096]{1,0:T(8,128)(2,1)} custom-call(bf16[227,4096]{1,0:T(8,128)(2,1)S(1)} %get-tuple-element.20.grid_ref, bf16[512,4096]{1,0:T(8,128)(2,1)S(1)} %get-tuple-element.21.lat_ref, bf16[192,4096]{1,0:T(8,128)(2,1)S(1)} %get-tuple-element.22.dsum_ref, bf16[227,512]{1,0:T(8,128)(2,1)S(1)} %bitcast.6, ...), custom_call_target="tpu_custom_call" | custom-call | tf_op jit(solution)/shard_map/decode/pallas_call | solution.py:415
Async XLA Ops:
  0.6 22.0 %copy-start = (bf16[512,512]{1,0:T(8,128)(2,1)S(1)}, bf16[512,512]{1,0:T(8,128)(2,1)}, u32[]{:S(2)}) copy-start(bf16[512,512]{1,0:T(8,128)(2,1)} %refs_7_.1) | copy-start | bytes 1572868
  0.6 22.0 %copy-start.4 = (bf16[128,512]{1,0:T(8,128)(2,1)S(1)}, bf16[128,512]{1,0:T(8,128)(2,1)}, u32[]{:S(2)}) copy-start(bf16[128,512]{1,0:T(8,128)(2,1)} %refs_6_.1) | copy-start | bytes 393220
  0.7 24.0 %copy-start.3 = (bf16[4,6,32,32]{3,2,1,0:T(8,128)(2,1)S(1)}, bf16[4,6,32,32]{3,2,1,0:T(8,128)(2,1)}, u32[]{:S(2)}) copy-start(bf16[4,6,32,32]{3,2,1,0:T(8,128)(2,1)} %coef_ref.1) | copy-start | bytes 147460
  0.7 24.0 %copy-start.5 = (s32[4,6]{1,0:T(4,128)S(1)}, s32[4,6]{1,0:T(4,128)}, u32[]{:S(2)}) copy-start(s32[4,6]{1,0:T(4,128)} %adj_ref.1) | copy-start | bytes 292
  0.7 29.5 %copy-start.1 = (bf16[512,512]{1,0:T(8,128)(2,1)S(1)}, bf16[512,512]{1,0:T(8,128)(2,1)}, u32[]{:S(2)}) copy-start(bf16[512,512]{1,0:T(8,128)(2,1)} %w_ref.1) | copy-start | bytes 1572868
  0.7 29.5 %copy-start.6 = (f32[512]{0:T(512)S(1)}, f32[512]{0:T(512)}, u32[]{:S(2)}) copy-start(f32[512]{0:T(512)} %param.22) | copy-start | bytes 6148
  10.1 28.0 %copy-start.2 = (bf16[512,227]{0,1:T(8,128)(2,1)S(1)}, bf16[512,227]{0,1:T(8,128)(2,1)}, u32[]{:S(2)}) copy-start(bf16[512,227]{0,1:T(8,128)(2,1)} %param.25) | copy-start | bytes 697348
  10.1 8.4 %collective-permute-start = (bf16[32,640]{1,0:T(8,128)(2,1)S(1)}, bf16[32,640]{1,0:T(8,128)(2,1)S(1)}, u32[]{:S(2)}, u32[]{:S(2)}) collective-permute-start(bf16[32,640]{1,0:T(8,128)(2,1)S(1)} %get-tuple-element.24), channel_id=1, source_target_pairs={{0,8},{1,9},{2,10},{3,11},{4,12},{5,13},{6,14},{7,15},{8,0},{9,1},... | collective-permute-start | bytes 122888 | tf_op jit(solution)/shard_map/ppermute | solution.py:440
  14.2 6.7 %collective-permute-start.1 = (bf16[32,640]{1,0:T(8,128)(2,1)S(1)}, bf16[32,640]{1,0:T(8,128)(2,1)S(1)}, u32[]{:S(2)}, u32[]{:S(2)}) collective-permute-start(bf16[32,640]{1,0:T(8,128)(2,1)S(1)} %get-tuple-element.25), channel_id=1, source_target_pairs={{0,14},{1,15},{2,4},{3,5},{4,2},{5,3},{6,8},{7,9},{8,6},{9,7},{10,... | collective-permute-start | bytes 122888 | tf_op jit(solution)/shard_map/ppermute | solution.py:440
  16.5 6.1 %collective-permute-start.2 = (bf16[32,640]{1,0:T(8,128)(2,1)S(1)}, bf16[32,640]{1,0:T(8,128)(2,1)S(1)}, u32[]{:S(2)}, u32[]{:S(2)}) collective-permute-start(bf16[32,640]{1,0:T(8,128)(2,1)S(1)} %get-tuple-element.26), channel_id=1, source_target_pairs={{0,15},{1,2},{2,1},{3,4},{4,3},{5,6},{6,5},{7,8},{8,7},{9,10},{10,... | collective-permute-start | bytes 122888 | tf_op jit(solution)/shard_map/ppermute | solution.py:440
  17.8 4.8 %collective-permute-start.3 = (bf16[32,640]{1,0:T(8,128)(2,1)S(1)}, bf16[32,640]{1,0:T(8,128)(2,1)S(1)}, u32[]{:S(2)}, u32[]{:S(2)}) collective-permute-start(bf16[32,640]{1,0:T(8,128)(2,1)S(1)} %get-tuple-element.27), channel_id=1, source_target_pairs={{0,2},{1,3},{2,0},{3,1},{4,6},{5,7},{6,4},{7,5},{8,10},{9,11},{10,... | collective-permute-start | bytes 122888 | tf_op jit(solution)/shard_map/ppermute | solution.py:440
  17.8 4.8 %collective-permute-start.4 = (bf16[32,640]{1,0:T(8,128)(2,1)S(1)}, bf16[32,640]{1,0:T(8,128)(2,1)S(1)}, u32[]{:S(2)}, u32[]{:S(2)}) collective-permute-start(bf16[32,640]{1,0:T(8,128)(2,1)S(1)} %get-tuple-element.28), channel_id=1, source_target_pairs={{0,1},{1,0},{2,3},{3,2},{4,5},{5,4},{6,7},{7,6},{8,9},{9,8},{10,11... | collective-permute-start | bytes 122888 | tf_op jit(solution)/shard_map/ppermute | solution.py:440
  23.0 7.2 %collective-permute-start.6 = (bf16[128,512]{1,0:T(8,128)(2,1)S(1)}, bf16[128,512]{1,0:T(8,128)(2,1)S(1)}, u32[]{:S(2)}, u32[]{:S(2)}) collective-permute-start(bf16[128,512]{1,0:T(8,128)(2,1)S(1)} %get-tuple-element.30.mid_ref), channel_id=1, source_target_pairs={{0,15},{1,2},{2,1},{3,4},{4,3},{5,6},{6,5},{7,8},{8,7},{9,10},{10,... | collective-permute-start | bytes 393224 | tf_op jit(solution)/shard_map/ppermute | solution.py:440
  24.6 5.5 %collective-permute-start.5 = (bf16[128,512]{1,0:T(8,128)(2,1)S(1)}, bf16[128,512]{1,0:T(8,128)(2,1)S(1)}, u32[]{:S(2)}, u32[]{:S(2)}) collective-permute-start(bf16[128,512]{1,0:T(8,128)(2,1)S(1)} %get-tuple-element.30.mid_ref), channel_id=1, source_target_pairs={{0,1},{1,0},{2,3},{3,2},{4,5},{5,4},{6,7},{7,6},{8,9},{9,8},{10,11... | collective-permute-start | bytes 393224 | tf_op jit(solution)/shard_map/ppermute | solution.py:440
  31.5 5.0 %collective-permute-start.7 = (bf16[32,512]{1,0:T(8,128)(2,1)S(1)}, bf16[32,512]{1,0:T(8,128)(2,1)S(1)}, u32[]{:S(2)}, u32[]{:S(2)}) collective-permute-start(bf16[32,512]{1,0:T(8,128)(2,1)S(1)} %get-tuple-element.32), channel_id=1, source_target_pairs={{0,8},{1,9},{2,10},{3,11},{4,12},{5,13},{6,14},{7,15},{8,0},{9,1},... | collective-permute-start | bytes 98312 | tf_op jit(solution)/shard_map/ppermute | solution.py:440
  31.5 6.6 %collective-permute-start.8 = (bf16[32,512]{1,0:T(8,128)(2,1)S(1)}, bf16[32,512]{1,0:T(8,128)(2,1)S(1)}, u32[]{:S(2)}, u32[]{:S(2)}) collective-permute-start(bf16[32,512]{1,0:T(8,128)(2,1)S(1)} %get-tuple-element.33), channel_id=1, source_target_pairs={{0,14},{1,15},{2,4},{3,5},{4,2},{5,3},{6,8},{7,9},{8,6},{9,7},{10,... | collective-permute-start | bytes 98312 | tf_op jit(solution)/shard_map/ppermute | solution.py:440
  31.5 6.5 %collective-permute-start.9 = (bf16[32,512]{1,0:T(8,128)(2,1)S(1)}, bf16[32,512]{1,0:T(8,128)(2,1)S(1)}, u32[]{:S(2)}, u32[]{:S(2)}) collective-permute-start(bf16[32,512]{1,0:T(8,128)(2,1)S(1)} %get-tuple-element.34), channel_id=1, source_target_pairs={{0,15},{1,2},{2,1},{3,4},{4,3},{5,6},{6,5},{7,8},{8,7},{9,10},{10,... | collective-permute-start | bytes 98312 | tf_op jit(solution)/shard_map/ppermute | solution.py:440
  33.1 5.0 %collective-permute-start.10 = (bf16[32,512]{1,0:T(8,128)(2,1)S(1)}, bf16[32,512]{1,0:T(8,128)(2,1)S(1)}, u32[]{:S(2)}, u32[]{:S(2)}) collective-permute-start(bf16[32,512]{1,0:T(8,128)(2,1)S(1)} %get-tuple-element.35), channel_id=1, source_target_pairs={{0,2},{1,3},{2,0},{3,1},{4,6},{5,7},{6,4},{7,5},{8,10},{9,11},{10,... | collective-permute-start | bytes 98312 | tf_op jit(solution)/shard_map/ppermute | solution.py:440
  34.8 3.3 %collective-permute-start.11 = (bf16[32,512]{1,0:T(8,128)(2,1)S(1)}, bf16[32,512]{1,0:T(8,128)(2,1)S(1)}, u32[]{:S(2)}, u32[]{:S(2)}) collective-permute-start(bf16[32,512]{1,0:T(8,128)(2,1)S(1)} %get-tuple-element.36), channel_id=1, source_target_pairs={{0,1},{1,0},{2,3},{3,2},{4,5},{5,4},{6,7},{7,6},{8,9},{9,8},{10,11... | collective-permute-start | bytes 98312 | tf_op jit(solution)/shard_map/ppermute | solution.py:440

commit v7 on v5

--- a/solution.py
+++ b/solution.py
@@ -45,8 +45,7 @@
 
 
 def silu(x):
-    half = 0.5 * x
-    return half + half * jnp.tanh(half)
+    return x * pl.reciprocal(1.0 + jnp.exp(-x), approx=True)
 
 
 def hot_rows(ids, target):

time: 42.8 us -> 43.8 us (1.023)
  Pallas kernels: 16.5 us -> 17.4 us
    pallas_call x1, Pallas kernels: 8.53 us -> 9.09 us  [encode(): pl.pallas_call(functools.partial(encode_kernel, parts, width), in_specs=[...]
where the time goes in v7:
time: 43.8 us; the launch traced here: 43.6 us
  Pallas kernels  17.4 us (40%)
  starting transfers between devices  13.4 us (31%)
  waiting for transfers between devices  12 us (27%)
  between operations  0.76 us (2%)
    ppermute x12, starting transfers between devices, swap(): return lax.ppermute(x, 'nodes', pairs)  13.4 us
    ppermute x12, waiting for transfers between devices, swap(): return lax.ppermute(x, 'nodes', pairs)  12 us
    pallas_call x1, Pallas kernels, encode(): pl.pallas_call(functools.partial(encode_kernel, parts, width), in_specs=[...  9.09 us
    pallas_call x1, Pallas kernels, decode(): pl.pallas_call(functools.partial(decode_kernel, width), in_specs=[vmem] *...  5.81 us
    pallas_call x1, Pallas kernels, process(): pl.pallas_call(process_kernel, in_specs=[vmem] * 7, out_specs=[vmem] * (1...  1.32 us
    pallas_call x1, Pallas kernels, prepare(): pl.pallas_call(functools.partial(prepare_kernel, parts), in_specs=[pl.Blo...  0.88 us
  transfers between devices with their start and end apart: 12, of which 5 were waited for; matrix products, arithmetic and copies ran while one was open for 0% of the time, Pallas kernels for 2%

profile of v7, /device:TPU:0, one launch (start us, length us, event | category | flops | bytes accessed | tf_op | source)
XLA Modules:
  0.0 43.6 jit_solution(7321390172739036113)
XLA Ops:
  0.6 0.0 copy-start
  0.6 0.0 copy-start.4
  0.7 0.0 copy-start.3
  0.7 0.0 copy-start.5
  0.7 0.0 copy-start.1
  0.7 0.0 copy-start.6
  0.7 9.1 %encode.1 = (bf16[512,4096]{1,0:T(8,128)(2,1)S(1)}, bf16[192,4096]{1,0:T(8,128)(2,1)S(1)}, bf16[227,4096]{1,0:T(8,128)(2,1)S(1)}, bf16[32,640]{1,0:T(8,128)(2,1)...) custom-call(s32[16]{0:T(128)} %slot_hbm.1, ...), custom_call_target="tpu_custom_call" | custom-call | tf_op jit(solution)/shard_map/encode/pallas_call | solution.py:209
  9.8 0.0 copy-start.2
  9.8 4.1 %collective-permute-start = (bf16[32,640]{1,0:T(8,128)(2,1)S(1)}, bf16[32,640]{1,0:T(8,128)(2,1)S(1)}, u32[]{:S(2)}, u32[]{:S(2)}) collective-permute-start(bf16[32,640]{1,0:T(8,128)(2,1)S(1)} %get-tuple-element.24), channel_id=1, source_target_pairs={{0,8},{1,9},{2,10},{3,11},{4,12},{5,13},{6,14},{7,15},{8,0},{9,1},... | collective-permute-start | bytes 122888 | tf_op jit(solution)/shard_map/ppermute | solution.py:425
  13.9 2.3 %collective-permute-start.1 = (bf16[32,640]{1,0:T(8,128)(2,1)S(1)}, bf16[32,640]{1,0:T(8,128)(2,1)S(1)}, u32[]{:S(2)}, u32[]{:S(2)}) collective-permute-start(bf16[32,640]{1,0:T(8,128)(2,1)S(1)} %get-tuple-element.25), channel_id=1, source_target_pairs={{0,14},{1,15},{2,4},{3,5},{4,2},{5,3},{6,8},{7,9},{8,6},{9,7},{10,... | collective-permute-start | bytes 122888 | tf_op jit(solution)/shard_map/ppermute | solution.py:425
  16.2 1.3 %collective-permute-start.2 = (bf16[32,640]{1,0:T(8,128)(2,1)S(1)}, bf16[32,640]{1,0:T(8,128)(2,1)S(1)}, u32[]{:S(2)}, u32[]{:S(2)}) collective-permute-start(bf16[32,640]{1,0:T(8,128)(2,1)S(1)} %get-tuple-element.26), channel_id=1, source_target_pairs={{0,15},{1,2},{2,1},{3,4},{4,3},{5,6},{6,5},{7,8},{8,7},{9,10},{10,... | collective-permute-start | bytes 122888 | tf_op jit(solution)/shard_map/ppermute | solution.py:425
  17.5 0.0 collective-permute-start.3
  17.5 0.7 %collective-permute-start.4 = (bf16[32,640]{1,0:T(8,128)(2,1)S(1)}, bf16[32,640]{1,0:T(8,128)(2,1)S(1)}, u32[]{:S(2)}, u32[]{:S(2)}) collective-permute-start(bf16[32,640]{1,0:T(8,128)(2,1)S(1)} %get-tuple-element.28), channel_id=1, source_target_pairs={{0,1},{1,0},{2,3},{3,2},{4,5},{5,4},{6,7},{7,6},{8,9},{9,8},{10,11... | collective-permute-start | bytes 122888 | tf_op jit(solution)/shard_map/ppermute | solution.py:425
  18.2 0.0 collective-permute-done.refs_1_
  18.2 2.4 %collective-permute-done.1.refs_2_ = bf16[32,640]{1,0:T(8,128)(2,1)S(1)} collective-permute-done((bf16[32,640]{1,0:T(8,128)(2,1)S(1)}, bf16[32,640]{1,0:T(8,128)(2,1)S(1)}, u32[]{:S(2)}, u32[]{:S(2)}) %collective-permute-start.1) | collective-permute-done | bytes 40992 | tf_op jit(solution)/shard_map/ppermute | solution.py:425
  20.6 1.7 %collective-permute-done.2.refs_3_ = bf16[32,640]{1,0:T(8,128)(2,1)S(1)} collective-permute-done((bf16[32,640]{1,0:T(8,128)(2,1)S(1)}, bf16[32,640]{1,0:T(8,128)(2,1)S(1)}, u32[]{:S(2)}, u32[]{:S(2)}) %collective-permute-start.2) | collective-permute-done | bytes 40992 | tf_op jit(solution)/shard_map/ppermute | solution.py:425
  22.3 0.0 collective-permute-done.3.refs_4_
  22.3 0.0 collective-permute-done.4.refs_5_
  22.3 0.0 copy-done
  22.3 0.0 copy-done.4
  22.4 0.3 mesh_update.1
  22.7 1.7 %collective-permute-start.6 = (bf16[128,512]{1,0:T(8,128)(2,1)S(1)}, bf16[128,512]{1,0:T(8,128)(2,1)S(1)}, u32[]{:S(2)}, u32[]{:S(2)}) collective-permute-start(bf16[128,512]{1,0:T(8,128)(2,1)S(1)} %get-tuple-element.30.mid_ref), channel_id=1, source_target_pairs={{0,15},{1,2},{2,1},{3,4},{4,3},{5,6},{6,5},{7,8},{8,7},{9,10},{10,... | collective-permute-start | bytes 393224 | tf_op jit(solution)/shard_map/ppermute | solution.py:425
  24.4 0.0 collective-permute-start.5
  24.4 0.0 copy-done.3
  24.4 0.0 copy-done.5
  24.4 0.9 %prepare.1.near_ref = bf16[128,384]{1,0:T(8,128)(2,1)S(1)} custom-call(s32[4,6]{1,0:T(4,128)S(1)} %copy-done.5, bf16[4,6,32,32]{3,2,1,0:T(8,128)(2,1)S(1)} %copy-done.3, bf16[32,640]{1,0:T(8,128)(2,1)S(1)} %get-tuple-element.23.refs_0_.after_ref), custom_call_target="tpu_custom_call" | custom-call | flops 18874368 | bytes 393216 | tf_op jit(solution)/shard_map/prepare/pallas_call | solution.py:270
  25.3 4.6 %collective-permute-done.6.far_mid_ref = bf16[128,512]{1,0:T(8,128)(2,1)S(1)} collective-permute-done((bf16[128,512]{1,0:T(8,128)(2,1)S(1)}, bf16[128,512]{1,0:T(8,128)(2,1)S(1)}, u32[]{:S(2)}, u32[]{:S(2)}) %collective-permute-start.6) | collective-permute-done | bytes 131104 | tf_op jit(solution)/shard_map/ppermute | solution.py:425
  29.8 0.0 collective-permute-done.5.near_mid_ref
  29.9 0.0 copy-done.1
  29.9 0.0 copy-done.6
  29.9 1.3 %mesh_process.1 = (bf16[128,512]{1,0:T(8,128)(2,1)}, bf16[32,512]{1,0:T(8,128)(2,1)S(1)}, bf16[32,512]{1,0:T(8,128)(2,1)S(1)}, bf16[32,512]{1,0:T(8,128)(2,1)S(1...) custom-call(f32[8,512]{1,0:T(8,128)S(1)} %get-tuple-element.29.ids_ref, ...), custom_call_target="tpu_custom_call" | custom-call | tf_op jit(solution)/shard_map/mesh_process/pallas_call | solution.py:340
  31.2 0.0 collective-permute-start.7
  31.2 0.1 collective-permute-start.8
  31.3 1.6 %collective-permute-start.9 = (bf16[32,512]{1,0:T(8,128)(2,1)S(1)}, bf16[32,512]{1,0:T(8,128)(2,1)S(1)}, u32[]{:S(2)}, u32[]{:S(2)}) collective-permute-start(bf16[32,512]{1,0:T(8,128)(2,1)S(1)} %get-tuple-element.34), channel_id=1, source_target_pairs={{0,15},{1,2},{2,1},{3,4},{4,3},{5,6},{6,5},{7,8},{8,7},{9,10},{10,... | collective-permute-start | bytes 98312 | tf_op jit(solution)/shard_map/ppermute | solution.py:425
  32.8 1.7 %collective-permute-start.10 = (bf16[32,512]{1,0:T(8,128)(2,1)S(1)}, bf16[32,512]{1,0:T(8,128)(2,1)S(1)}, u32[]{:S(2)}, u32[]{:S(2)}) collective-permute-start(bf16[32,512]{1,0:T(8,128)(2,1)S(1)} %get-tuple-element.35), channel_id=1, source_target_pairs={{0,2},{1,3},{2,0},{3,1},{4,6},{5,7},{6,4},{7,5},{8,10},{9,11},{10,... | collective-permute-start | bytes 98312 | tf_op jit(solution)/shard_map/ppermute | solution.py:425
  34.5 0.0 collective-permute-start.11
  34.5 1.7 %collective-permute-done.7.rest_1_ = bf16[32,512]{1,0:T(8,128)(2,1)S(1)} collective-permute-done((bf16[32,512]{1,0:T(8,128)(2,1)S(1)}, bf16[32,512]{1,0:T(8,128)(2,1)S(1)}, u32[]{:S(2)}, u32[]{:S(2)}) %collective-permute-start.7) | collective-permute-done | bytes 32800 | tf_op jit(solution)/shard_map/ppermute | solution.py:425
  36.2 1.6 %collective-permute-done.8.rest_2_ = bf16[32,512]{1,0:T(8,128)(2,1)S(1)} collective-permute-done((bf16[32,512]{1,0:T(8,128)(2,1)S(1)}, bf16[32,512]{1,0:T(8,128)(2,1)S(1)}, u32[]{:S(2)}, u32[]{:S(2)}) %collective-permute-start.8) | collective-permute-done | bytes 32800 | tf_op jit(solution)/shard_map/ppermute | solution.py:425
  37.8 0.0 collective-permute-done.9.rest_3_
  37.8 0.0 collective-permute-done.10.rest_4_
  37.8 0.0 collective-permute-done.11.rest_5_
  37.8 0.0 copy-done.2
  37.8 5.8 %decode.1 = bf16[227,4096]{1,0:T(8,128)(2,1)} custom-call(bf16[227,4096]{1,0:T(8,128)(2,1)S(1)} %get-tuple-element.20.grid_ref, bf16[512,4096]{1,0:T(8,128)(2,1)S(1)} %get-tuple-element.21.lat_ref, bf16[192,4096]{1,0:T(8,128)(2,1)S(1)} %get-tuple-element.22.dsum_ref, bf16[227,512]{1,0:T(8,128)(2,1)S(1)} %bitcast.6, ...), custom_call_target="tpu_custom_call" | custom-call | tf_op jit(solution)/shard_map/decode/pallas_call | solution.py:400
Async XLA Ops:
  0.6 21.7 %copy-start = (bf16[512,512]{1,0:T(8,128)(2,1)S(1)}, bf16[512,512]{1,0:T(8,128)(2,1)}, u32[]{:S(2)}) copy-start(bf16[512,512]{1,0:T(8,128)(2,1)} %refs_7_.1) | copy-start | bytes 1572868
  0.6 21.7 %copy-start.4 = (bf16[128,512]{1,0:T(8,128)(2,1)S(1)}, bf16[128,512]{1,0:T(8,128)(2,1)}, u32[]{:S(2)}) copy-start(bf16[128,512]{1,0:T(8,128)(2,1)} %refs_6_.1) | copy-start | bytes 393220
  0.7 23.7 %copy-start.3 = (bf16[4,6,32,32]{3,2,1,0:T(8,128)(2,1)S(1)}, bf16[4,6,32,32]{3,2,1,0:T(8,128)(2,1)}, u32[]{:S(2)}) copy-start(bf16[4,6,32,32]{3,2,1,0:T(8,128)(2,1)} %coef_ref.1) | copy-start | bytes 147460
  0.7 23.7 %copy-start.5 = (s32[4,6]{1,0:T(4,128)S(1)}, s32[4,6]{1,0:T(4,128)}, u32[]{:S(2)}) copy-start(s32[4,6]{1,0:T(4,128)} %adj_ref.1) | copy-start | bytes 292
  0.7 29.2 %copy-start.1 = (bf16[512,512]{1,0:T(8,128)(2,1)S(1)}, bf16[512,512]{1,0:T(8,128)(2,1)}, u32[]{:S(2)}) copy-start(bf16[512,512]{1,0:T(8,128)(2,1)} %w_ref.1) | copy-start | bytes 1572868
  0.7 29.2 %copy-start.6 = (f32[512]{0:T(512)S(1)}, f32[512]{0:T(512)}, u32[]{:S(2)}) copy-start(f32[512]{0:T(512)} %param.22) | copy-start | bytes 6148
  9.8 28.0 %copy-start.2 = (bf16[512,227]{0,1:T(8,128)(2,1)S(1)}, bf16[512,227]{0,1:T(8,128)(2,1)}, u32[]{:S(2)}) copy-start(bf16[512,227]{0,1:T(8,128)(2,1)} %param.25) | copy-start | bytes 697348
  9.8 8.4 %collective-permute-start = (bf16[32,640]{1,0:T(8,128)(2,1)S(1)}, bf16[32,640]{1,0:T(8,128)(2,1)S(1)}, u32[]{:S(2)}, u32[]{:S(2)}) collective-permute-start(bf16[32,640]{1,0:T(8,128)(2,1)S(1)} %get-tuple-element.24), channel_id=1, source_target_pairs={{0,8},{1,9},{2,10},{3,11},{4,12},{5,13},{6,14},{7,15},{8,0},{9,1},... | collective-permute-start | bytes 122888 | tf_op jit(solution)/shard_map/ppermute | solution.py:425
  13.9 6.7 %collective-permute-start.1 = (bf16[32,640]{1,0:T(8,128)(2,1)S(1)}, bf16[32,640]{1,0:T(8,128)(2,1)S(1)}, u32[]{:S(2)}, u32[]{:S(2)}) collective-permute-start(bf16[32,640]{1,0:T(8,128)(2,1)S(1)} %get-tuple-element.25), channel_id=1, source_target_pairs={{0,14},{1,15},{2,4},{3,5},{4,2},{5,3},{6,8},{7,9},{8,6},{9,7},{10,... | collective-permute-start | bytes 122888 | tf_op jit(solution)/shard_map/ppermute | solution.py:425
  16.2 6.1 %collective-permute-start.2 = (bf16[32,640]{1,0:T(8,128)(2,1)S(1)}, bf16[32,640]{1,0:T(8,128)(2,1)S(1)}, u32[]{:S(2)}, u32[]{:S(2)}) collective-permute-start(bf16[32,640]{1,0:T(8,128)(2,1)S(1)} %get-tuple-element.26), channel_id=1, source_target_pairs={{0,15},{1,2},{2,1},{3,4},{4,3},{5,6},{6,5},{7,8},{8,7},{9,10},{10,... | collective-permute-start | bytes 122888 | tf_op jit(solution)/shard_map/ppermute | solution.py:425
  17.5 4.8 %collective-permute-start.3 = (bf16[32,640]{1,0:T(8,128)(2,1)S(1)}, bf16[32,640]{1,0:T(8,128)(2,1)S(1)}, u32[]{:S(2)}, u32[]{:S(2)}) collective-permute-start(bf16[32,640]{1,0:T(8,128)(2,1)S(1)} %get-tuple-element.27), channel_id=1, source_target_pairs={{0,2},{1,3},{2,0},{3,1},{4,6},{5,7},{6,4},{7,5},{8,10},{9,11},{10,... | collective-permute-start | bytes 122888 | tf_op jit(solution)/shard_map/ppermute | solution.py:425
  17.5 4.8 %collective-permute-start.4 = (bf16[32,640]{1,0:T(8,128)(2,1)S(1)}, bf16[32,640]{1,0:T(8,128)(2,1)S(1)}, u32[]{:S(2)}, u32[]{:S(2)}) collective-permute-start(bf16[32,640]{1,0:T(8,128)(2,1)S(1)} %get-tuple-element.28), channel_id=1, source_target_pairs={{0,1},{1,0},{2,3},{3,2},{4,5},{5,4},{6,7},{7,6},{8,9},{9,8},{10,11... | collective-permute-start | bytes 122888 | tf_op jit(solution)/shard_map/ppermute | solution.py:425
  22.7 7.2 %collective-permute-start.6 = (bf16[128,512]{1,0:T(8,128)(2,1)S(1)}, bf16[128,512]{1,0:T(8,128)(2,1)S(1)}, u32[]{:S(2)}, u32[]{:S(2)}) collective-permute-start(bf16[128,512]{1,0:T(8,128)(2,1)S(1)} %get-tuple-element.30.mid_ref), channel_id=1, source_target_pairs={{0,15},{1,2},{2,1},{3,4},{4,3},{5,6},{6,5},{7,8},{8,7},{9,10},{10,... | collective-permute-start | bytes 393224 | tf_op jit(solution)/shard_map/ppermute | solution.py:425
  24.4 5.5 %collective-permute-start.5 = (bf16[128,512]{1,0:T(8,128)(2,1)S(1)}, bf16[128,512]{1,0:T(8,128)(2,1)S(1)}, u32[]{:S(2)}, u32[]{:S(2)}) collective-permute-start(bf16[128,512]{1,0:T(8,128)(2,1)S(1)} %get-tuple-element.30.mid_ref), channel_id=1, source_target_pairs={{0,1},{1,0},{2,3},{3,2},{4,5},{5,4},{6,7},{7,6},{8,9},{9,8},{10,11... | collective-permute-start | bytes 393224 | tf_op jit(solution)/shard_map/ppermute | solution.py:425
  31.2 5.0 %collective-permute-start.7 = (bf16[32,512]{1,0:T(8,128)(2,1)S(1)}, bf16[32,512]{1,0:T(8,128)(2,1)S(1)}, u32[]{:S(2)}, u32[]{:S(2)}) collective-permute-start(bf16[32,512]{1,0:T(8,128)(2,1)S(1)} %get-tuple-element.32), channel_id=1, source_target_pairs={{0,8},{1,9},{2,10},{3,11},{4,12},{5,13},{6,14},{7,15},{8,0},{9,1},... | collective-permute-start | bytes 98312 | tf_op jit(solution)/shard_map/ppermute | solution.py:425
  31.2 6.6 %collective-permute-start.8 = (bf16[32,512]{1,0:T(8,128)(2,1)S(1)}, bf16[32,512]{1,0:T(8,128)(2,1)S(1)}, u32[]{:S(2)}, u32[]{:S(2)}) collective-permute-start(bf16[32,512]{1,0:T(8,128)(2,1)S(1)} %get-tuple-element.33), channel_id=1, source_target_pairs={{0,14},{1,15},{2,4},{3,5},{4,2},{5,3},{6,8},{7,9},{8,6},{9,7},{10,... | collective-permute-start | bytes 98312 | tf_op jit(solution)/shard_map/ppermute | solution.py:425
  31.3 6.5 %collective-permute-start.9 = (bf16[32,512]{1,0:T(8,128)(2,1)S(1)}, bf16[32,512]{1,0:T(8,128)(2,1)S(1)}, u32[]{:S(2)}, u32[]{:S(2)}) collective-permute-start(bf16[32,512]{1,0:T(8,128)(2,1)S(1)} %get-tuple-element.34), channel_id=1, source_target_pairs={{0,15},{1,2},{2,1},{3,4},{4,3},{5,6},{6,5},{7,8},{8,7},{9,10},{10,... | collective-permute-start | bytes 98312 | tf_op jit(solution)/shard_map/ppermute | solution.py:425
  32.8 5.0 %collective-permute-start.10 = (bf16[32,512]{1,0:T(8,128)(2,1)S(1)}, bf16[32,512]{1,0:T(8,128)(2,1)S(1)}, u32[]{:S(2)}, u32[]{:S(2)}) collective-permute-start(bf16[32,512]{1,0:T(8,128)(2,1)S(1)} %get-tuple-element.35), channel_id=1, source_target_pairs={{0,2},{1,3},{2,0},{3,1},{4,6},{5,7},{6,4},{7,5},{8,10},{9,11},{10,... | collective-permute-start | bytes 98312 | tf_op jit(solution)/shard_map/ppermute | solution.py:425
  34.5 3.3 %collective-permute-start.11 = (bf16[32,512]{1,0:T(8,128)(2,1)S(1)}, bf16[32,512]{1,0:T(8,128)(2,1)S(1)}, u32[]{:S(2)}, u32[]{:S(2)}) collective-permute-start(bf16[32,512]{1,0:T(8,128)(2,1)S(1)} %get-tuple-element.36), channel_id=1, source_target_pairs={{0,1},{1,0},{2,3},{3,2},{4,5},{5,4},{6,7},{7,6},{8,9},{9,8},{10,11... | collective-permute-start | bytes 98312 | tf_op jit(solution)/shard_map/ppermute | solution.py:425

commit v8 on v3

--- a/solution.py
+++ b/solution.py
@@ -13,6 +13,7 @@
 OWN, HALF, ODD, FAR, EVEN, NEAR = range(6)
 SLOTS = 6
 PAD = 128
+AHEAD = 3
 
 
 def partner(slot, me, parts):
@@ -100,7 +101,7 @@
     send_refs = rest[:SLOTS]
     (
         slot_ref, owner_ref, w_ref, enc_ref, dec_ref, wt_ref, tgt_ref, ids_ref, msum_ref,
-        acc_ref, small_sems, sems,
+        hold_ref, acc_ref, small_sems, sems,
     ) = rest[SLOTS:]
     tiles, block_mesh, block_grid = enc_ref.shape
     channels, points = grid_ref.shape
@@ -113,7 +114,7 @@
     rows = SLOTS * block_mesh
 
     def copies(step):
-        cols = pl.ds(pl.multiple_of(step * width, width), width)
+        cols = pl.ds(step * width, width)
         some = pl.ds(step * chunk, chunk)
         return (
             pltpu.make_async_copy(grid_hbm.at[:, cols], grid_ref.at[:, cols], sems.at[0, step]),
@@ -129,21 +130,32 @@
     ]
     for copy in small:
         copy.start()
-    for step in range(steps):
+    def start(step):
         for copy in copies(step):
             copy.start()
+
+    for step in range(AHEAD):
+        start(step)
+    ids_ref[...] = lax.broadcasted_iota(jnp.int32, ids_ref.shape, 0).astype(BF16)
+    acc_ref[...] = jnp.zeros_like(acc_ref)
     for copy in small:
         copy.wait()
     wt_ref[:, :channels] = w_ref[...].astype(F32).T.astype(BF16)
     fill_targets(parts, per_block, block_mesh, owner_ref, tgt_ref)
-    ids_ref[...] = lax.broadcasted_iota(jnp.int32, ids_ref.shape, 0).astype(BF16)
-    acc_ref[...] = jnp.zeros_like(acc_ref)
-
-    @pl.loop(0, steps)
-    def _(step):
+
+    def collect(slot):
+        acc_ref[...] += lax.dot_general(
+            hold_ref[slot], msum_ref[slot], (((1,), (1,)), ((), ())), preferred_element_type=F32
+        )
+
+    for step in range(steps):
+        slot = step % 2
+        if step + AHEAD < steps:
+            start(step + AHEAD)
         for copy in copies(step):
             copy.wait()
-        cols = pl.ds(pl.multiple_of(step * width, width), width)
+        if step > 0:
+            collect(1 - slot)
         for b in range(blocks):
             hot = hot_rows(ids_ref[...], tgt_ref[pl.ds(step * blocks + b, 1), :])
             some = pl.ds(step * chunk + b * per_block, per_block)
@@ -155,17 +167,20 @@
                 axis=1,
             )
             sums = jnp.dot(hot, both, preferred_element_type=F32).astype(BF16)
-            msum_ref[:, b * block_grid : (b + 1) * block_grid] = sums[:, :block_grid]
-            first = pl.multiple_of((step * blocks + b) * block_grid, block_grid)
+            msum_ref[slot, :, b * block_grid : (b + 1) * block_grid] = sums[:, :block_grid]
+            first = (step * blocks + b) * block_grid
             dsum_ref[:, pl.ds(first, block_grid)] = sums[:, block_grid:]
-        lat = silu(
-            jnp.dot(wt_ref[:, :channels], grid_ref[:, cols], preferred_element_type=F32)
-        ).astype(BF16)
-        lat_ref[:, cols] = lat
-        acc_ref[...] += lax.dot_general(
-            lat, msum_ref[...], (((1,), (1,)), ((), ())), preferred_element_type=F32
-        )
-
+        for half in range(0, width, 256):
+            part = pl.ds(step * width + half, 256)
+            lat = silu(
+                jnp.dot(
+                    wt_ref[:, :channels], grid_ref[:, part], preferred_element_type=F32
+                )
+            ).astype(BF16)
+            lat_ref[:, part] = lat
+            hold_ref[slot, :, half : half + 256] = lat
+
+    collect(1)
     me = lax.axis_index("nodes")
     flipped = acc_ref[...].T.astype(BF16)
     for s in range(SLOTS):
@@ -204,7 +219,8 @@
             pltpu.VMEM((latent, 256), BF16),
             pltpu.VMEM((grid_blocks, wide), F32),
             pltpu.VMEM((rows, 128), BF16),
-            pltpu.VMEM((rows, width), BF16),
+            pltpu.VMEM((2, rows, width), BF16),
+            pltpu.VMEM((2, latent, width), BF16),
             pltpu.VMEM((latent, rows), F32),
             pltpu.SemaphoreType.DMA((3,)),
             pltpu.SemaphoreType.DMA((3, steps)),
@@ -328,27 +344,35 @@
 
 def decode_kernel(width, grid_ref, lat_ref, dsum_ref, w_ref, *rest):
     slots = rest[:SLOTS]
-    out_hbm, back_ref, pred_ref, sems = rest[SLOTS:]
+    out_hbm, back_ref, pred_ref, hold_ref, sems = rest[SLOTS:]
     steps = grid_ref.shape[1] // width
 
     def copy_out(step):
-        cols = pl.ds(pl.multiple_of(step * width, width), width)
+        cols = pl.ds(step * width, width)
         return pltpu.make_async_copy(pred_ref.at[:, cols], out_hbm.at[:, cols], sems.at[step])
 
     joined = jnp.concatenate([slot[...] for slot in slots], axis=0)
     back_ref[...] = joined.astype(F32).T.astype(BF16)
 
-    @pl.loop(0, steps)
-    def _(step):
-        cols = pl.ds(pl.multiple_of(step * width, width), width)
-        decoded = jnp.dot(back_ref[...], dsum_ref[:, cols], preferred_element_type=F32)
-        hidden = silu(lat_ref[:, cols].astype(F32) + decoded).astype(BF16)
+    def predict(step, slot):
+        cols = pl.ds(step * width, width)
         pred_ref[:, cols] = (
             grid_ref[:, cols].astype(F32)
-            + jnp.dot(w_ref[...], hidden, preferred_element_type=F32)
+            + jnp.dot(w_ref[...], hold_ref[slot], preferred_element_type=F32)
         ).astype(BF16)
-        copy_out(step).start()
-
+
+    for step in range(steps):
+        slot = step % 2
+        if step > 0:
+            predict(step - 1, 1 - slot)
+            copy_out(step - 1).start()
+        for half in range(0, width, 256):
+            part = pl.ds(step * width + half, 256)
+            decoded = jnp.dot(back_ref[...], dsum_ref[:, part], preferred_element_type=F32)
+            hidden = silu(lat_ref[:, part].astype(F32) + decoded)
+            hold_ref[slot, :, half : half + 256] = hidden.astype(BF16)
+    predict(steps - 1, (steps - 1) % 2)
+    copy_out(steps - 1).start()
     for step in range(steps):
         copy_out(step).wait()
 
@@ -367,6 +391,7 @@
         scratch_shapes=[
             pltpu.VMEM((latent, rows), BF16),
             pltpu.VMEM((channels, points), BF16),
+            pltpu.VMEM((2, latent, width), BF16),
             pltpu.SemaphoreType.DMA((points // width,)),
         ],
         compiler_params=pltpu.CompilerParams(vmem_limit_bytes=24 * MIB),

time: 45.4 us -> 42.1 us (0.927)
  Pallas kernels: 19.1 us -> 15.7 us
    pallas_call x1, Pallas kernels: 10.5 us -> 8.19 us  [encode(): pl.pallas_call(functools.partial(encode_kernel, parts, width), in_specs=[...]
    pallas_call x1, Pallas kernels: 6.12 us -> 5.06 us  [decode(): pl.pallas_call(functools.partial(decode_kernel, width), in_specs=[vmem] *...]
where the time goes in v8:
time: 42.1 us; the launch traced here: 41.9 us
  Pallas kernels  15.7 us (37%)
  starting transfers between devices  13.4 us (32%)
  waiting for transfers between devices  12 us (29%)
  between operations  0.76 us (2%)
    ppermute x12, starting transfers between devices, swap(): return lax.ppermute(x, 'nodes', pairs)  13.4 us
    ppermute x12, waiting for transfers between devices, swap(): return lax.ppermute(x, 'nodes', pairs)  12 us
    pallas_call x1, Pallas kernels, encode(): pl.pallas_call(functools.partial(encode_kernel, parts, width), in_specs=[...  8.19 us
    pallas_call x1, Pallas kernels, decode(): pl.pallas_call(functools.partial(decode_kernel, width), in_specs=[vmem] *...  5.06 us
    pallas_call x1, Pallas kernels, process(): pl.pallas_call(process_kernel, in_specs=[vmem] * 7, out_specs=[vmem] * (1...  1.31 us
    pallas_call x1, Pallas kernels, prepare(): pl.pallas_call(functools.partial(prepare_kernel, parts), in_specs=[pl.Blo...  0.88 us
  transfers between devices with their start and end apart: 12, of which 5 were waited for; matrix products, arithmetic and copies ran while one was open for 0% of the time, Pallas kernels for 2%

profile of v8, /device:TPU:0, one launch (start us, length us, event | category | flops | bytes accessed | tf_op | source)
XLA Modules:
  0.0 41.9 jit_solution(6038511962667700053)
XLA Ops:
  0.6 0.0 copy-start
  0.6 0.0 copy-start.4
  0.7 0.0 copy-start.3
  0.7 0.0 copy-start.5
  0.7 0.0 copy-start.1
  0.7 0.0 copy-start.6
  0.7 8.2 %encode.1 = (bf16[512,4096]{1,0:T(8,128)(2,1)S(1)}, bf16[192,4096]{1,0:T(8,128)(2,1)S(1)}, bf16[227,4096]{1,0:T(8,128)(2,1)S(1)}, bf16[32,640]{1,0:T(8,128)(2,1)...) custom-call(s32[16]{0:T(128)} %slot_hbm.1, ...), custom_call_target="tpu_custom_call" | custom-call | tf_op jit(solution)/shard_map/encode/pallas_call | solution.py:203
  8.9 0.0 copy-start.2
  8.9 4.1 %collective-permute-start = (bf16[32,640]{1,0:T(8,128)(2,1)S(1)}, bf16[32,640]{1,0:T(8,128)(2,1)S(1)}, u32[]{:S(2)}, u32[]{:S(2)}) collective-permute-start(bf16[32,640]{1,0:T(8,128)(2,1)S(1)} %get-tuple-element.24), channel_id=1, source_target_pairs={{0,8},{1,9},{2,10},{3,11},{4,12},{5,13},{6,14},{7,15},{8,0},{9,1},... | collective-permute-start | bytes 122888 | tf_op jit(solution)/shard_map/ppermute | solution.py:411
  13.0 2.3 %collective-permute-start.1 = (bf16[32,640]{1,0:T(8,128)(2,1)S(1)}, bf16[32,640]{1,0:T(8,128)(2,1)S(1)}, u32[]{:S(2)}, u32[]{:S(2)}) collective-permute-start(bf16[32,640]{1,0:T(8,128)(2,1)S(1)} %get-tuple-element.25), channel_id=1, source_target_pairs={{0,14},{1,15},{2,4},{3,5},{4,2},{5,3},{6,8},{7,9},{8,6},{9,7},{10,... | collective-permute-start | bytes 122888 | tf_op jit(solution)/shard_map/ppermute | solution.py:411
  15.3 1.3 %collective-permute-start.2 = (bf16[32,640]{1,0:T(8,128)(2,1)S(1)}, bf16[32,640]{1,0:T(8,128)(2,1)S(1)}, u32[]{:S(2)}, u32[]{:S(2)}) collective-permute-start(bf16[32,640]{1,0:T(8,128)(2,1)S(1)} %get-tuple-element.26), channel_id=1, source_target_pairs={{0,15},{1,2},{2,1},{3,4},{4,3},{5,6},{6,5},{7,8},{8,7},{9,10},{10,... | collective-permute-start | bytes 122888 | tf_op jit(solution)/shard_map/ppermute | solution.py:411
  16.6 0.0 collective-permute-start.3
  16.6 0.7 %collective-permute-start.4 = (bf16[32,640]{1,0:T(8,128)(2,1)S(1)}, bf16[32,640]{1,0:T(8,128)(2,1)S(1)}, u32[]{:S(2)}, u32[]{:S(2)}) collective-permute-start(bf16[32,640]{1,0:T(8,128)(2,1)S(1)} %get-tuple-element.28), channel_id=1, source_target_pairs={{0,1},{1,0},{2,3},{3,2},{4,5},{5,4},{6,7},{7,6},{8,9},{9,8},{10,11... | collective-permute-start | bytes 122888 | tf_op jit(solution)/shard_map/ppermute | solution.py:411
  17.3 0.0 collective-permute-done.refs_1_
  17.3 2.4 %collective-permute-done.1.refs_2_ = bf16[32,640]{1,0:T(8,128)(2,1)S(1)} collective-permute-done((bf16[32,640]{1,0:T(8,128)(2,1)S(1)}, bf16[32,640]{1,0:T(8,128)(2,1)S(1)}, u32[]{:S(2)}, u32[]{:S(2)}) %collective-permute-start.1) | collective-permute-done | bytes 40992 | tf_op jit(solution)/shard_map/ppermute | solution.py:411
  19.7 1.7 %collective-permute-done.2.refs_3_ = bf16[32,640]{1,0:T(8,128)(2,1)S(1)} collective-permute-done((bf16[32,640]{1,0:T(8,128)(2,1)S(1)}, bf16[32,640]{1,0:T(8,128)(2,1)S(1)}, u32[]{:S(2)}, u32[]{:S(2)}) %collective-permute-start.2) | collective-permute-done | bytes 40992 | tf_op jit(solution)/shard_map/ppermute | solution.py:411
  21.4 0.0 collective-permute-done.3.refs_4_
  21.4 0.0 collective-permute-done.4.refs_5_
  21.4 0.0 copy-done
  21.5 0.0 copy-done.4
  21.5 0.3 mesh_update.1
  21.8 1.7 %collective-permute-start.6 = (bf16[128,512]{1,0:T(8,128)(2,1)S(1)}, bf16[128,512]{1,0:T(8,128)(2,1)S(1)}, u32[]{:S(2)}, u32[]{:S(2)}) collective-permute-start(bf16[128,512]{1,0:T(8,128)(2,1)S(1)} %get-tuple-element.30.mid_ref), channel_id=1, source_target_pairs={{0,15},{1,2},{2,1},{3,4},{4,3},{5,6},{6,5},{7,8},{8,7},{9,10},{10,... | collective-permute-start | bytes 393224 | tf_op jit(solution)/shard_map/ppermute | solution.py:411
  23.4 0.0 collective-permute-start.5
  23.4 0.0 copy-done.3
  23.4 0.0 copy-done.5
  23.4 0.9 %prepare.1.near_ref = bf16[128,384]{1,0:T(8,128)(2,1)S(1)} custom-call(s32[4,6]{1,0:T(4,128)S(1)} %copy-done.5, bf16[4,6,32,32]{3,2,1,0:T(8,128)(2,1)S(1)} %copy-done.3, bf16[32,640]{1,0:T(8,128)(2,1)S(1)} %get-tuple-element.23.refs_0_.after_ref), custom_call_target="tpu_custom_call" | custom-call | flops 18874368 | bytes 393216 | tf_op jit(solution)/shard_map/prepare/pallas_call | solution.py:264
  24.3 4.6 %collective-permute-done.6.far_mid_ref = bf16[128,512]{1,0:T(8,128)(2,1)S(1)} collective-permute-done((bf16[128,512]{1,0:T(8,128)(2,1)S(1)}, bf16[128,512]{1,0:T(8,128)(2,1)S(1)}, u32[]{:S(2)}, u32[]{:S(2)}) %collective-permute-start.6) | collective-permute-done | bytes 131104 | tf_op jit(solution)/shard_map/ppermute | solution.py:411
  28.9 0.0 collective-permute-done.5.near_mid_ref
  28.9 0.0 copy-done.1
  28.9 0.0 copy-done.6
  28.9 1.3 %mesh_process.1 = (bf16[128,512]{1,0:T(8,128)(2,1)}, bf16[32,512]{1,0:T(8,128)(2,1)S(1)}, bf16[32,512]{1,0:T(8,128)(2,1)S(1)}, bf16[32,512]{1,0:T(8,128)(2,1)S(1...) custom-call(f32[8,512]{1,0:T(8,128)S(1)} %get-tuple-element.29.ids_ref, ...), custom_call_target="tpu_custom_call" | custom-call | tf_op jit(solution)/shard_map/mesh_process/pallas_call | solution.py:334
  30.2 0.0 collective-permute-start.7
  30.2 0.1 collective-permute-start.8
  30.3 1.6 %collective-permute-start.9 = (bf16[32,512]{1,0:T(8,128)(2,1)S(1)}, bf16[32,512]{1,0:T(8,128)(2,1)S(1)}, u32[]{:S(2)}, u32[]{:S(2)}) collective-permute-start(bf16[32,512]{1,0:T(8,128)(2,1)S(1)} %get-tuple-element.34), channel_id=1, source_target_pairs={{0,15},{1,2},{2,1},{3,4},{4,3},{5,6},{6,5},{7,8},{8,7},{9,10},{10,... | collective-permute-start | bytes 98312 | tf_op jit(solution)/shard_map/ppermute | solution.py:411
  31.9 1.7 %collective-permute-start.10 = (bf16[32,512]{1,0:T(8,128)(2,1)S(1)}, bf16[32,512]{1,0:T(8,128)(2,1)S(1)}, u32[]{:S(2)}, u32[]{:S(2)}) collective-permute-start(bf16[32,512]{1,0:T(8,128)(2,1)S(1)} %get-tuple-element.35), channel_id=1, source_target_pairs={{0,2},{1,3},{2,0},{3,1},{4,6},{5,7},{6,4},{7,5},{8,10},{9,11},{10,... | collective-permute-start | bytes 98312 | tf_op jit(solution)/shard_map/ppermute | solution.py:411
  33.6 0.0 collective-permute-start.11
  33.6 1.7 %collective-permute-done.7.rest_1_ = bf16[32,512]{1,0:T(8,128)(2,1)S(1)} collective-permute-done((bf16[32,512]{1,0:T(8,128)(2,1)S(1)}, bf16[32,512]{1,0:T(8,128)(2,1)S(1)}, u32[]{:S(2)}, u32[]{:S(2)}) %collective-permute-start.7) | collective-permute-done | bytes 32800 | tf_op jit(solution)/shard_map/ppermute | solution.py:411
  35.3 1.6 %collective-permute-done.8.rest_2_ = bf16[32,512]{1,0:T(8,128)(2,1)S(1)} collective-permute-done((bf16[32,512]{1,0:T(8,128)(2,1)S(1)}, bf16[32,512]{1,0:T(8,128)(2,1)S(1)}, u32[]{:S(2)}, u32[]{:S(2)}) %collective-permute-start.8) | collective-permute-done | bytes 32800 | tf_op jit(solution)/shard_map/ppermute | solution.py:411
  36.9 0.0 collective-permute-done.9.rest_3_
  36.9 0.0 collective-permute-done.10.rest_4_
  36.9 0.0 collective-permute-done.11.rest_5_
  36.9 0.0 copy-done.2
  36.9 5.1 %decode.1 = bf16[227,4096]{1,0:T(8,128)(2,1)} custom-call(bf16[227,4096]{1,0:T(8,128)(2,1)S(1)} %get-tuple-element.20.grid_ref, bf16[512,4096]{1,0:T(8,128)(2,1)S(1)} %get-tuple-element.21.lat_ref, bf16[192,4096]{1,0:T(8,128)(2,1)S(1)} %get-tuple-element.22.dsum_ref, bf16[227,512]{1,0:T(8,128)(2,1)S(1)} %bitcast.6, ...), custom_call_target="tpu_custom_call" | custom-call | tf_op jit(solution)/shard_map/decode/pallas_call | solution.py:386
Async XLA Ops:
  0.6 20.8 %copy-start = (bf16[512,512]{1,0:T(8,128)(2,1)S(1)}, bf16[512,512]{1,0:T(8,128)(2,1)}, u32[]{:S(2)}) copy-start(bf16[512,512]{1,0:T(8,128)(2,1)} %refs_7_.1) | copy-start | bytes 1572868
  0.6 20.8 %copy-start.4 = (bf16[128,512]{1,0:T(8,128)(2,1)S(1)}, bf16[128,512]{1,0:T(8,128)(2,1)}, u32[]{:S(2)}) copy-start(bf16[128,512]{1,0:T(8,128)(2,1)} %refs_6_.1) | copy-start | bytes 393220
  0.7 22.8 %copy-start.3 = (bf16[4,6,32,32]{3,2,1,0:T(8,128)(2,1)S(1)}, bf16[4,6,32,32]{3,2,1,0:T(8,128)(2,1)}, u32[]{:S(2)}) copy-start(bf16[4,6,32,32]{3,2,1,0:T(8,128)(2,1)} %coef_ref.1) | copy-start | bytes 147460
  0.7 22.8 %copy-start.5 = (s32[4,6]{1,0:T(4,128)S(1)}, s32[4,6]{1,0:T(4,128)}, u32[]{:S(2)}) copy-start(s32[4,6]{1,0:T(4,128)} %adj_ref.1) | copy-start | bytes 292
  0.7 28.3 %copy-start.1 = (bf16[512,512]{1,0:T(8,128)(2,1)S(1)}, bf16[512,512]{1,0:T(8,128)(2,1)}, u32[]{:S(2)}) copy-start(bf16[512,512]{1,0:T(8,128)(2,1)} %w_ref.1) | copy-start | bytes 1572868
  0.7 28.3 %copy-start.6 = (f32[512]{0:T(512)S(1)}, f32[512]{0:T(512)}, u32[]{:S(2)}) copy-start(f32[512]{0:T(512)} %param.22) | copy-start | bytes 6148
  8.9 28.0 %copy-start.2 = (bf16[512,227]{0,1:T(8,128)(2,1)S(1)}, bf16[512,227]{0,1:T(8,128)(2,1)}, u32[]{:S(2)}) copy-start(bf16[512,227]{0,1:T(8,128)(2,1)} %param.25) | copy-start | bytes 697348
  8.9 8.4 %collective-permute-start = (bf16[32,640]{1,0:T(8,128)(2,1)S(1)}, bf16[32,640]{1,0:T(8,128)(2,1)S(1)}, u32[]{:S(2)}, u32[]{:S(2)}) collective-permute-start(bf16[32,640]{1,0:T(8,128)(2,1)S(1)} %get-tuple-element.24), channel_id=1, source_target_pairs={{0,8},{1,9},{2,10},{3,11},{4,12},{5,13},{6,14},{7,15},{8,0},{9,1},... | collective-permute-start | bytes 122888 | tf_op jit(solution)/shard_map/ppermute | solution.py:411
  13.0 6.7 %collective-permute-start.1 = (bf16[32,640]{1,0:T(8,128)(2,1)S(1)}, bf16[32,640]{1,0:T(8,128)(2,1)S(1)}, u32[]{:S(2)}, u32[]{:S(2)}) collective-permute-start(bf16[32,640]{1,0:T(8,128)(2,1)S(1)} %get-tuple-element.25), channel_id=1, source_target_pairs={{0,14},{1,15},{2,4},{3,5},{4,2},{5,3},{6,8},{7,9},{8,6},{9,7},{10,... | collective-permute-start | bytes 122888 | tf_op jit(solution)/shard_map/ppermute | solution.py:411
  15.3 6.1 %collective-permute-start.2 = (bf16[32,640]{1,0:T(8,128)(2,1)S(1)}, bf16[32,640]{1,0:T(8,128)(2,1)S(1)}, u32[]{:S(2)}, u32[]{:S(2)}) collective-permute-start(bf16[32,640]{1,0:T(8,128)(2,1)S(1)} %get-tuple-element.26), channel_id=1, source_target_pairs={{0,15},{1,2},{2,1},{3,4},{4,3},{5,6},{6,5},{7,8},{8,7},{9,10},{10,... | collective-permute-start | bytes 122888 | tf_op jit(solution)/shard_map/ppermute | solution.py:411
  16.6 4.8 %collective-permute-start.3 = (bf16[32,640]{1,0:T(8,128)(2,1)S(1)}, bf16[32,640]{1,0:T(8,128)(2,1)S(1)}, u32[]{:S(2)}, u32[]{:S(2)}) collective-permute-start(bf16[32,640]{1,0:T(8,128)(2,1)S(1)} %get-tuple-element.27), channel_id=1, source_target_pairs={{0,2},{1,3},{2,0},{3,1},{4,6},{5,7},{6,4},{7,5},{8,10},{9,11},{10,... | collective-permute-start | bytes 122888 | tf_op jit(solution)/shard_map/ppermute | solution.py:411
  16.6 4.8 %collective-permute-start.4 = (bf16[32,640]{1,0:T(8,128)(2,1)S(1)}, bf16[32,640]{1,0:T(8,128)(2,1)S(1)}, u32[]{:S(2)}, u32[]{:S(2)}) collective-permute-start(bf16[32,640]{1,0:T(8,128)(2,1)S(1)} %get-tuple-element.28), channel_id=1, source_target_pairs={{0,1},{1,0},{2,3},{3,2},{4,5},{5,4},{6,7},{7,6},{8,9},{9,8},{10,11... | collective-permute-start | bytes 122888 | tf_op jit(solution)/shard_map/ppermute | solution.py:411
  21.8 7.2 %collective-permute-start.6 = (bf16[128,512]{1,0:T(8,128)(2,1)S(1)}, bf16[128,512]{1,0:T(8,128)(2,1)S(1)}, u32[]{:S(2)}, u32[]{:S(2)}) collective-permute-start(bf16[128,512]{1,0:T(8,128)(2,1)S(1)} %get-tuple-element.30.mid_ref), channel_id=1, source_target_pairs={{0,15},{1,2},{2,1},{3,4},{4,3},{5,6},{6,5},{7,8},{8,7},{9,10},{10,... | collective-permute-start | bytes 393224 | tf_op jit(solution)/shard_map/ppermute | solution.py:411
  23.4 5.5 %collective-permute-start.5 = (bf16[128,512]{1,0:T(8,128)(2,1)S(1)}, bf16[128,512]{1,0:T(8,128)(2,1)S(1)}, u32[]{:S(2)}, u32[]{:S(2)}) collective-permute-start(bf16[128,512]{1,0:T(8,128)(2,1)S(1)} %get-tuple-element.30.mid_ref), channel_id=1, source_target_pairs={{0,1},{1,0},{2,3},{3,2},{4,5},{5,4},{6,7},{7,6},{8,9},{9,8},{10,11... | collective-permute-start | bytes 393224 | tf_op jit(solution)/shard_map/ppermute | solution.py:411
  30.2 5.0 %collective-permute-start.7 = (bf16[32,512]{1,0:T(8,128)(2,1)S(1)}, bf16[32,512]{1,0:T(8,128)(2,1)S(1)}, u32[]{:S(2)}, u32[]{:S(2)}) collective-permute-start(bf16[32,512]{1,0:T(8,128)(2,1)S(1)} %get-tuple-element.32), channel_id=1, source_target_pairs={{0,8},{1,9},{2,10},{3,11},{4,12},{5,13},{6,14},{7,15},{8,0},{9,1},... | collective-permute-start | bytes 98312 | tf_op jit(solution)/shard_map/ppermute | solution.py:411
  30.2 6.6 %collective-permute-start.8 = (bf16[32,512]{1,0:T(8,128)(2,1)S(1)}, bf16[32,512]{1,0:T(8,128)(2,1)S(1)}, u32[]{:S(2)}, u32[]{:S(2)}) collective-permute-start(bf16[32,512]{1,0:T(8,128)(2,1)S(1)} %get-tuple-element.33), channel_id=1, source_target_pairs={{0,14},{1,15},{2,4},{3,5},{4,2},{5,3},{6,8},{7,9},{8,6},{9,7},{10,... | collective-permute-start | bytes 98312 | tf_op jit(solution)/shard_map/ppermute | solution.py:411
  30.3 6.5 %collective-permute-start.9 = (bf16[32,512]{1,0:T(8,128)(2,1)S(1)}, bf16[32,512]{1,0:T(8,128)(2,1)S(1)}, u32[]{:S(2)}, u32[]{:S(2)}) collective-permute-start(bf16[32,512]{1,0:T(8,128)(2,1)S(1)} %get-tuple-element.34), channel_id=1, source_target_pairs={{0,15},{1,2},{2,1},{3,4},{4,3},{5,6},{6,5},{7,8},{8,7},{9,10},{10,... | collective-permute-start | bytes 98312 | tf_op jit(solution)/shard_map/ppermute | solution.py:411
  31.9 5.0 %collective-permute-start.10 = (bf16[32,512]{1,0:T(8,128)(2,1)S(1)}, bf16[32,512]{1,0:T(8,128)(2,1)S(1)}, u32[]{:S(2)}, u32[]{:S(2)}) collective-permute-start(bf16[32,512]{1,0:T(8,128)(2,1)S(1)} %get-tuple-element.35), channel_id=1, source_target_pairs={{0,2},{1,3},{2,0},{3,1},{4,6},{5,7},{6,4},{7,5},{8,10},{9,11},{10,... | collective-permute-start | bytes 98312 | tf_op jit(solution)/shard_map/ppermute | solution.py:411
  33.6 3.3 %collective-permute-start.11 = (bf16[32,512]{1,0:T(8,128)(2,1)S(1)}, bf16[32,512]{1,0:T(8,128)(2,1)S(1)}, u32[]{:S(2)}, u32[]{:S(2)}) collective-permute-start(bf16[32,512]{1,0:T(8,128)(2,1)S(1)} %get-tuple-element.36), channel_id=1, source_target_pairs={{0,1},{1,0},{2,3},{3,2},{4,5},{5,4},{6,7},{7,6},{8,9},{9,8},{10,11... | collective-permute-start | bytes 98312 | tf_op jit(solution)/shard_map/ppermute | solution.py:411

commit v9 on v8

--- a/solution.py
+++ b/solution.py
@@ -276,8 +276,12 @@
     )(adj, coef, after)
 
 
-def update_kernel(*refs):
-    slots = refs[:SLOTS]
+def other_half(parts, ref):
+    return ref[jnp.where(lax.axis_index("nodes") < parts // 2, 1, 0)]
+
+
+def update_kernel(parts, *refs):
+    slots = [other_half(parts, r) if s == HALF else r[...] for s, r in enumerate(refs[:SLOTS])]
     mesh_ref, w_ref, mid_ref, ids_ref = refs[SLOTS:]
     count, latent = mesh_ref.shape
     block_mesh = slots[0].shape[0]
@@ -295,10 +299,10 @@
     mid_ref[...] = (mesh_ref[...].astype(F32) + silu(grown)).astype(BF16)
 
 
-def update(slots, mesh_in, w_enc):
+def update(parts, slots, mesh_in, w_enc):
     vmem = pl.BlockSpec(memory_space=pltpu.VMEM)
     return pl.pallas_call(
-        update_kernel,
+        functools.partial(update_kernel, parts),
         in_specs=[vmem] * (SLOTS + 2),
         out_specs=[vmem] * 2,
         out_shape=[
@@ -342,7 +346,7 @@
     )(ids, mid, near_mid, far_mid, near, gain, w_proc)
 
 
-def decode_kernel(width, grid_ref, lat_ref, dsum_ref, w_ref, *rest):
+def decode_kernel(parts, width, grid_ref, lat_ref, dsum_ref, w_ref, *rest):
     slots = rest[:SLOTS]
     out_hbm, back_ref, pred_ref, hold_ref, sems = rest[SLOTS:]
     steps = grid_ref.shape[1] // width
@@ -351,7 +355,9 @@
         cols = pl.ds(step * width, width)
         return pltpu.make_async_copy(pred_ref.at[:, cols], out_hbm.at[:, cols], sems.at[step])
 
-    joined = jnp.concatenate([slot[...] for slot in slots], axis=0)
+    joined = jnp.concatenate(
+        [other_half(parts, r) if s == HALF else r[...] for s, r in enumerate(slots)], axis=0
+    )
     back_ref[...] = joined.astype(F32).T.astype(BF16)
 
     def predict(step, slot):
@@ -377,14 +383,14 @@
         copy_out(step).wait()
 
 
-def decode(grid_t, lat_t, dsum, w_out_t, slots):
+def decode(parts, grid_t, lat_t, dsum, w_out_t, slots):
     channels, points = grid_t.shape
     latent = lat_t.shape[0]
     rows = dsum.shape[0]
     width = 512
     vmem = pl.BlockSpec(memory_space=pltpu.VMEM)
     return pl.pallas_call(
-        functools.partial(decode_kernel, width),
+        functools.partial(decode_kernel, parts, width),
         in_specs=[vmem] * (4 + SLOTS),
         out_specs=pl.BlockSpec(memory_space=pl.ANY),
         out_shape=jax.ShapeDtypeStruct((channels, points), BF16),
@@ -410,8 +416,13 @@
         pairs = [(i, partner(slot, i, parts)) for i in range(parts)]
         return lax.ppermute(x, "nodes", pairs)
 
+    def both_halves(x):
+        pairs = [[i, i + parts // 2] for i in range(parts // 2)]
+        return lax.all_gather(x, "nodes", axis=0, axis_index_groups=pairs)
+
     def swap_all(xs):
-        return [xs[OWN]] + [swap(xs[s], s) for s in range(1, SLOTS)]
+        far = both_halves(xs[HALF])
+        return [xs[OWN], far] + [swap(xs[s], s) for s in range(2, SLOTS)]
 
     lat_t, dsum, grid_t, *sums = encode(
         parts, slot_block, enc_owner.reshape(-1, 128), grid_in.T, w_embed, enc_coef,
@@ -419,14 +430,14 @@
     )
     received = swap_all(sums)
     near = prepare(parts, proc_adj, proc_coef, sums[OWN])
-    mid, ids = update(received, mesh_in, w_enc)
+    mid, ids = update(parts, received, mesh_in, w_enc)
     far_mid = swap(mid, FAR)
     near_mid = swap(mid, NEAR)
     mesh_out, *sends = process(
         block_mesh, ids, mid, near_mid, far_mid, near, proc_gain.reshape(1, -1), w_proc
     )
     returned = swap_all(sends)
-    pred_t = decode(grid_t, lat_t, dsum, w_out.T, returned)
+    pred_t = decode(parts, grid_t, lat_t, dsum, w_out.T, returned)
     return (pred_t.T, mesh_out)
 
 

time: 42.1 us -> 45.2 us (1.074)
  blocking collectives: 0 us -> 11.5 us
  waiting for transfers between devices: 12 us -> 4.55 us
  starting transfers between devices: 13.4 us -> 12.4 us
    all_gather x0 -> x2, blocking collectives: none -> 11.5 us  [both_halves(): return lax.all_gather(x, 'nodes', axis=0, axis_index_groups=pairs)]
    ppermute x12 -> x10, waiting for transfers between devices: 12 us -> 4.55 us  [swap(): return lax.ppermute(x, 'nodes', pairs)]
    ppermute x12 -> x10, starting transfers between devices: 13.4 us -> 12.4 us  [swap(): return lax.ppermute(x, 'nodes', pairs)]
  transfers between devices with their start and end apart: 12 -> 10, of which waited for: 5 -> 1; matrix products, arithmetic and copies ran while one was open for 0% -> 0% of each run, Pallas kernels for 2% -> 2%
where the time goes in v9:
time: 45.2 us; the launch traced here: 45 us
  Pallas kernels  15.8 us (35%)
  starting transfers between devices  12.4 us (27%)
  blocking collectives  11.5 us (25%)
  waiting for transfers between devices  4.55 us (10%)
  between operations  0.78 us (2%)
    ppermute x10, starting transfers between devices, swap(): return lax.ppermute(x, 'nodes', pairs)  12.4 us
    all_gather x2, blocking collectives, both_halves(): return lax.all_gather(x, 'nodes', axis=0, axis_index_groups=pairs)  11.5 us
    pallas_call x1, Pallas kernels, encode(): pl.pallas_call(functools.partial(encode_kernel, parts, width), in_specs=[...  8.19 us
    pallas_call x1, Pallas kernels, decode(): pl.pallas_call(functools.partial(decode_kernel, parts, width), in_specs=[...  5.07 us
    ppermute x10, waiting for transfers between devices, swap(): return lax.ppermute(x, 'nodes', pairs)  4.55 us
    pallas_call x1, Pallas kernels, process(): pl.pallas_call(process_kernel, in_specs=[vmem] * 7, out_specs=[vmem] * (1...  1.31 us
  transfers between devices with their start and end apart: 10, of which 1 were waited for; matrix products, arithmetic and copies ran while one was open for 0% of the time, Pallas kernels for 2%

profile of v9, /device:TPU:0, one launch (start us, length us, event | category | flops | bytes accessed | tf_op | source)
XLA Modules:
  0.0 45.0 jit_solution(149387873816866139)
XLA Ops:
  0.6 0.0 copy-start
  0.6 0.0 copy-start.4
  0.7 0.0 copy-start.3
  0.7 0.0 copy-start.5
  0.7 0.0 copy-start.1
  0.7 0.0 copy-start.6
  0.7 8.2 %encode.1 = (bf16[512,4096]{1,0:T(8,128)(2,1)S(1)}, bf16[192,4096]{1,0:T(8,128)(2,1)S(1)}, bf16[227,4096]{1,0:T(8,128)(2,1)S(1)}, bf16[32,640]{1,0:T(8,128)(2,1)...) custom-call(s32[16]{0:T(128)} %slot_hbm.1, ...), custom_call_target="tpu_custom_call" | custom-call | tf_op jit(solution)/shard_map/encode/pallas_call | solution.py:203
  8.9 0.0 copy-start.2
  8.9 6.1 %collective-permute-start = (bf16[32,640]{1,0:T(8,128)(2,1)S(1)}, bf16[32,640]{1,0:T(8,128)(2,1)S(1)}, u32[]{:S(2)}, u32[]{:S(2)}) collective-permute-start(bf16[32,640]{1,0:T(8,128)(2,1)S(1)} %get-tuple-element.25), channel_id=1, source_target_pairs={{0,14},{1,15},{2,4},{3,5},{4,2},{5,3},{6,8},{7,9},{8,6},{9,7},{10,... | collective-permute-start | bytes 122888 | tf_op jit(solution)/shard_map/ppermute | solution.py:417
  15.0 0.0 collective-permute-start.1
  15.0 1.2 %collective-permute-start.2 = (bf16[32,640]{1,0:T(8,128)(2,1)S(1)}, bf16[32,640]{1,0:T(8,128)(2,1)S(1)}, u32[]{:S(2)}, u32[]{:S(2)}) collective-permute-start(bf16[32,640]{1,0:T(8,128)(2,1)S(1)} %get-tuple-element.27), channel_id=1, source_target_pairs={{0,2},{1,3},{2,0},{3,1},{4,6},{5,7},{6,4},{7,5},{8,10},{9,11},{10,... | collective-permute-start | bytes 122888 | tf_op jit(solution)/shard_map/ppermute | solution.py:417
  16.2 0.0 collective-permute-start.3
  16.2 6.0 %all-gather = bf16[64,640]{1,0:T(8,128)(2,1)S(1)} all-gather(bf16[32,640]{1,0:T(8,128)(2,1)S(1)} %get-tuple-element.24), channel_id=2, replica_groups={{0,8},{1,9},{2,10},{3,11},{4,12},{5,13},{6,14},{7,15},{16,24},{17,25},{..., dimensions={0}, use_global_device_ids=true | all-gather | bytes 122880 | tf_op jit(solution)/shard_map/all_gather | solution.py:421
  22.2 0.0 collective-permute-done.refs_2_
  22.2 0.0 collective-permute-done.1.refs_3_
  22.2 0.0 collective-permute-done.2.refs_4_
  22.2 0.0 collective-permute-done.3.refs_5_
  22.2 0.0 copy-done
  22.2 0.0 copy-done.4
  22.2 0.3 mesh_update.1
  22.5 1.7 %collective-permute-start.5 = (bf16[128,512]{1,0:T(8,128)(2,1)S(1)}, bf16[128,512]{1,0:T(8,128)(2,1)S(1)}, u32[]{:S(2)}, u32[]{:S(2)}) collective-permute-start(bf16[128,512]{1,0:T(8,128)(2,1)S(1)} %get-tuple-element.30.mid_ref), channel_id=1, source_target_pairs={{0,15},{1,2},{2,1},{3,4},{4,3},{5,6},{6,5},{7,8},{8,7},{9,10},{10,... | collective-permute-start | bytes 393224 | tf_op jit(solution)/shard_map/ppermute | solution.py:417
  24.3 0.0 collective-permute-start.4
  24.3 0.0 copy-done.3
  24.3 0.0 copy-done.5
  24.3 0.9 %prepare.1.near_ref = bf16[128,384]{1,0:T(8,128)(2,1)S(1)} custom-call(s32[4,6]{1,0:T(4,128)S(1)} %copy-done.5, bf16[4,6,32,32]{3,2,1,0:T(8,128)(2,1)S(1)} %copy-done.3, bf16[32,640]{1,0:T(8,128)(2,1)S(1)} %get-tuple-element.23.refs_0_.after_ref), custom_call_target="tpu_custom_call" | custom-call | flops 18874368 | bytes 393216 | tf_op jit(solution)/shard_map/prepare/pallas_call | solution.py:264
  25.2 4.5 %collective-permute-done.5.far_mid_ref = bf16[128,512]{1,0:T(8,128)(2,1)S(1)} collective-permute-done((bf16[128,512]{1,0:T(8,128)(2,1)S(1)}, bf16[128,512]{1,0:T(8,128)(2,1)S(1)}, u32[]{:S(2)}, u32[]{:S(2)}) %collective-permute-start.5) | collective-permute-done | bytes 131104 | tf_op jit(solution)/shard_map/ppermute | solution.py:417
  29.7 0.0 collective-permute-done.4.near_mid_ref
  29.7 0.0 copy-done.1
  29.7 0.0 copy-done.6
  29.7 1.3 %mesh_process.1 = (bf16[128,512]{1,0:T(8,128)(2,1)}, bf16[32,512]{1,0:T(8,128)(2,1)S(1)}, bf16[32,512]{1,0:T(8,128)(2,1)S(1)}, bf16[32,512]{1,0:T(8,128)(2,1)S(1...) custom-call(f32[8,512]{1,0:T(8,128)S(1)} %get-tuple-element.29.ids_ref, ...), custom_call_target="tpu_custom_call" | custom-call | tf_op jit(solution)/shard_map/mesh_process/pallas_call | solution.py:338
  31.0 0.5 %collective-permute-start.6 = (bf16[32,512]{1,0:T(8,128)(2,1)S(1)}, bf16[32,512]{1,0:T(8,128)(2,1)S(1)}, u32[]{:S(2)}, u32[]{:S(2)}) collective-permute-start(bf16[32,512]{1,0:T(8,128)(2,1)S(1)} %get-tuple-element.33), channel_id=1, source_target_pairs={{0,14},{1,15},{2,4},{3,5},{4,2},{5,3},{6,8},{7,9},{8,6},{9,7},{10,... | collective-permute-start | bytes 98312 | tf_op jit(solution)/shard_map/ppermute | solution.py:417
  31.5 1.2 %collective-permute-start.7 = (bf16[32,512]{1,0:T(8,128)(2,1)S(1)}, bf16[32,512]{1,0:T(8,128)(2,1)S(1)}, u32[]{:S(2)}, u32[]{:S(2)}) collective-permute-start(bf16[32,512]{1,0:T(8,128)(2,1)S(1)} %get-tuple-element.34), channel_id=1, source_target_pairs={{0,15},{1,2},{2,1},{3,4},{4,3},{5,6},{6,5},{7,8},{8,7},{9,10},{10,... | collective-permute-start | bytes 98312 | tf_op jit(solution)/shard_map/ppermute | solution.py:417
  32.7 1.7 %collective-permute-start.8 = (bf16[32,512]{1,0:T(8,128)(2,1)S(1)}, bf16[32,512]{1,0:T(8,128)(2,1)S(1)}, u32[]{:S(2)}, u32[]{:S(2)}) collective-permute-start(bf16[32,512]{1,0:T(8,128)(2,1)S(1)} %get-tuple-element.35), channel_id=1, source_target_pairs={{0,2},{1,3},{2,0},{3,1},{4,6},{5,7},{6,4},{7,5},{8,10},{9,11},{10,... | collective-permute-start | bytes 98312 | tf_op jit(solution)/shard_map/ppermute | solution.py:417
  34.4 0.0 collective-permute-start.9
  34.4 5.5 %all-gather.1 = bf16[64,512]{1,0:T(8,128)(2,1)S(1)} all-gather(bf16[32,512]{1,0:T(8,128)(2,1)S(1)} %get-tuple-element.32), channel_id=3, replica_groups={{0,8},{1,9},{2,10},{3,11},{4,12},{5,13},{6,14},{7,15},{16,24},{17,25},{..., dimensions={0}, use_global_device_ids=true | all-gather | bytes 98304 | tf_op jit(solution)/shard_map/all_gather | solution.py:421
  39.9 0.0 collective-permute-done.6.rest_2_
  39.9 0.0 collective-permute-done.7.rest_3_
  39.9 0.0 collective-permute-done.8.rest_4_
  39.9 0.0 collective-permute-done.9.rest_5_
  39.9 0.0 copy-done.2
  39.9 5.1 %decode.1 = bf16[227,4096]{1,0:T(8,128)(2,1)} custom-call(bf16[227,4096]{1,0:T(8,128)(2,1)S(1)} %get-tuple-element.20.grid_ref, bf16[512,4096]{1,0:T(8,128)(2,1)S(1)} %get-tuple-element.21.lat_ref, bf16[192,4096]{1,0:T(8,128)(2,1)S(1)} %get-tuple-element.22.dsum_ref, bf16[227,512]{1,0:T(8,128)(2,1)S(1)} %bitcast.10, ...), custom_call_target="tpu_custom_call" | custom-call | tf_op jit(solution)/shard_map/decode/pallas_call | solution.py:392
Async XLA Ops:
  0.6 21.6 %copy-start = (bf16[512,512]{1,0:T(8,128)(2,1)S(1)}, bf16[512,512]{1,0:T(8,128)(2,1)}, u32[]{:S(2)}) copy-start(bf16[512,512]{1,0:T(8,128)(2,1)} %refs_7_.1) | copy-start | bytes 1572868
  0.6 21.6 %copy-start.4 = (bf16[128,512]{1,0:T(8,128)(2,1)S(1)}, bf16[128,512]{1,0:T(8,128)(2,1)}, u32[]{:S(2)}) copy-start(bf16[128,512]{1,0:T(8,128)(2,1)} %refs_6_.1) | copy-start | bytes 393220
  0.7 23.6 %copy-start.3 = (bf16[4,6,32,32]{3,2,1,0:T(8,128)(2,1)S(1)}, bf16[4,6,32,32]{3,2,1,0:T(8,128)(2,1)}, u32[]{:S(2)}) copy-start(bf16[4,6,32,32]{3,2,1,0:T(8,128)(2,1)} %coef_ref.1) | copy-start | bytes 147460
  0.7 23.6 %copy-start.5 = (s32[4,6]{1,0:T(4,128)S(1)}, s32[4,6]{1,0:T(4,128)}, u32[]{:S(2)}) copy-start(s32[4,6]{1,0:T(4,128)} %adj_ref.1) | copy-start | bytes 292
  0.7 29.0 %copy-start.1 = (bf16[512,512]{1,0:T(8,128)(2,1)S(1)}, bf16[512,512]{1,0:T(8,128)(2,1)}, u32[]{:S(2)}) copy-start(bf16[512,512]{1,0:T(8,128)(2,1)} %w_ref.1) | copy-start | bytes 1572868
  0.7 29.0 %copy-start.6 = (f32[512]{0:T(512)S(1)}, f32[512]{0:T(512)}, u32[]{:S(2)}) copy-start(f32[512]{0:T(512)} %param.22) | copy-start | bytes 6148
  8.9 31.0 %copy-start.2 = (bf16[512,227]{0,1:T(8,128)(2,1)S(1)}, bf16[512,227]{0,1:T(8,128)(2,1)}, u32[]{:S(2)}) copy-start(bf16[512,227]{0,1:T(8,128)(2,1)} %param.25) | copy-start | bytes 697348
  8.9 13.3 %collective-permute-start = (bf16[32,640]{1,0:T(8,128)(2,1)S(1)}, bf16[32,640]{1,0:T(8,128)(2,1)S(1)}, u32[]{:S(2)}, u32[]{:S(2)}) collective-permute-start(bf16[32,640]{1,0:T(8,128)(2,1)S(1)} %get-tuple-element.25), channel_id=1, source_target_pairs={{0,14},{1,15},{2,4},{3,5},{4,2},{5,3},{6,8},{7,9},{8,6},{9,7},{10,... | collective-permute-start | bytes 122888 | tf_op jit(solution)/shard_map/ppermute | solution.py:417
  15.0 7.2 %collective-permute-start.1 = (bf16[32,640]{1,0:T(8,128)(2,1)S(1)}, bf16[32,640]{1,0:T(8,128)(2,1)S(1)}, u32[]{:S(2)}, u32[]{:S(2)}) collective-permute-start(bf16[32,640]{1,0:T(8,128)(2,1)S(1)} %get-tuple-element.26), channel_id=1, source_target_pairs={{0,15},{1,2},{2,1},{3,4},{4,3},{5,6},{6,5},{7,8},{8,7},{9,10},{10,... | collective-permute-start | bytes 122888 | tf_op jit(solution)/shard_map/ppermute | solution.py:417
  15.0 7.2 %collective-permute-start.2 = (bf16[32,640]{1,0:T(8,128)(2,1)S(1)}, bf16[32,640]{1,0:T(8,128)(2,1)S(1)}, u32[]{:S(2)}, u32[]{:S(2)}) collective-permute-start(bf16[32,640]{1,0:T(8,128)(2,1)S(1)} %get-tuple-element.27), channel_id=1, source_target_pairs={{0,2},{1,3},{2,0},{3,1},{4,6},{5,7},{6,4},{7,5},{8,10},{9,11},{10,... | collective-permute-start | bytes 122888 | tf_op jit(solution)/shard_map/ppermute | solution.py:417
  16.2 6.0 %collective-permute-start.3 = (bf16[32,640]{1,0:T(8,128)(2,1)S(1)}, bf16[32,640]{1,0:T(8,128)(2,1)S(1)}, u32[]{:S(2)}, u32[]{:S(2)}) collective-permute-start(bf16[32,640]{1,0:T(8,128)(2,1)S(1)} %get-tuple-element.28), channel_id=1, source_target_pairs={{0,1},{1,0},{2,3},{3,2},{4,5},{5,4},{6,7},{7,6},{8,9},{9,8},{10,11... | collective-permute-start | bytes 122888 | tf_op jit(solution)/shard_map/ppermute | solution.py:417
  22.5 7.2 %collective-permute-start.5 = (bf16[128,512]{1,0:T(8,128)(2,1)S(1)}, bf16[128,512]{1,0:T(8,128)(2,1)S(1)}, u32[]{:S(2)}, u32[]{:S(2)}) collective-permute-start(bf16[128,512]{1,0:T(8,128)(2,1)S(1)} %get-tuple-element.30.mid_ref), channel_id=1, source_target_pairs={{0,15},{1,2},{2,1},{3,4},{4,3},{5,6},{6,5},{7,8},{8,7},{9,10},{10,... | collective-permute-start | bytes 393224 | tf_op jit(solution)/shard_map/ppermute | solution.py:417
  24.3 5.4 %collective-permute-start.4 = (bf16[128,512]{1,0:T(8,128)(2,1)S(1)}, bf16[128,512]{1,0:T(8,128)(2,1)S(1)}, u32[]{:S(2)}, u32[]{:S(2)}) collective-permute-start(bf16[128,512]{1,0:T(8,128)(2,1)S(1)} %get-tuple-element.30.mid_ref), channel_id=1, source_target_pairs={{0,1},{1,0},{2,3},{3,2},{4,5},{5,4},{6,7},{7,6},{8,9},{9,8},{10,11... | collective-permute-start | bytes 393224 | tf_op jit(solution)/shard_map/ppermute | solution.py:417
  31.0 8.9 %collective-permute-start.6 = (bf16[32,512]{1,0:T(8,128)(2,1)S(1)}, bf16[32,512]{1,0:T(8,128)(2,1)S(1)}, u32[]{:S(2)}, u32[]{:S(2)}) collective-permute-start(bf16[32,512]{1,0:T(8,128)(2,1)S(1)} %get-tuple-element.33), channel_id=1, source_target_pairs={{0,14},{1,15},{2,4},{3,5},{4,2},{5,3},{6,8},{7,9},{8,6},{9,7},{10,... | collective-permute-start | bytes 98312 | tf_op jit(solution)/shard_map/ppermute | solution.py:417
  31.5 8.4 %collective-permute-start.7 = (bf16[32,512]{1,0:T(8,128)(2,1)S(1)}, bf16[32,512]{1,0:T(8,128)(2,1)S(1)}, u32[]{:S(2)}, u32[]{:S(2)}) collective-permute-start(bf16[32,512]{1,0:T(8,128)(2,1)S(1)} %get-tuple-element.34), channel_id=1, source_target_pairs={{0,15},{1,2},{2,1},{3,4},{4,3},{5,6},{6,5},{7,8},{8,7},{9,10},{10,... | collective-permute-start | bytes 98312 | tf_op jit(solution)/shard_map/ppermute | solution.py:417
  32.7 7.2 %collective-permute-start.8 = (bf16[32,512]{1,0:T(8,128)(2,1)S(1)}, bf16[32,512]{1,0:T(8,128)(2,1)S(1)}, u32[]{:S(2)}, u32[]{:S(2)}) collective-permute-start(bf16[32,512]{1,0:T(8,128)(2,1)S(1)} %get-tuple-element.35), channel_id=1, source_target_pairs={{0,2},{1,3},{2,0},{3,1},{4,6},{5,7},{6,4},{7,5},{8,10},{9,11},{10,... | collective-permute-start | bytes 98312 | tf_op jit(solution)/shard_map/ppermute | solution.py:417
  34.4 5.5 %collective-permute-start.9 = (bf16[32,512]{1,0:T(8,128)(2,1)S(1)}, bf16[32,512]{1,0:T(8,128)(2,1)S(1)}, u32[]{:S(2)}, u32[]{:S(2)}) collective-permute-start(bf16[32,512]{1,0:T(8,128)(2,1)S(1)} %get-tuple-element.36), channel_id=1, source_target_pairs={{0,1},{1,0},{2,3},{3,2},{4,5},{5,4},{6,7},{7,6},{8,9},{9,8},{10,11... | collective-permute-start | bytes 98312 | tf_op jit(solution)/shard_map/ppermute | solution.py:417

commit v10 on v8

--- a/solution.py
+++ b/solution.py
@@ -44,9 +44,12 @@
     return lax.rem(me + step + parts, parts)
 
 
+def silu_of_half(half):
+    return half + half * jnp.tanh(half)
+
+
 def silu(x):
-    half = 0.5 * x
-    return half + half * jnp.tanh(half)
+    return silu_of_half(0.5 * x)
 
 
 def hot_rows(ids, target):
@@ -140,7 +143,7 @@
     acc_ref[...] = jnp.zeros_like(acc_ref)
     for copy in small:
         copy.wait()
-    wt_ref[:, :channels] = w_ref[...].astype(F32).T.astype(BF16)
+    wt_ref[:, :channels] = (0.5 * w_ref[...].astype(F32)).T.astype(BF16)
     fill_targets(parts, per_block, block_mesh, owner_ref, tgt_ref)
 
     def collect(slot):
@@ -172,7 +175,7 @@
             dsum_ref[:, pl.ds(first, block_grid)] = sums[:, block_grid:]
         for half in range(0, width, 256):
             part = pl.ds(step * width + half, 256)
-            lat = silu(
+            lat = silu_of_half(
                 jnp.dot(
                     wt_ref[:, :channels], grid_ref[:, part], preferred_element_type=F32
                 )
@@ -352,7 +355,7 @@
         return pltpu.make_async_copy(pred_ref.at[:, cols], out_hbm.at[:, cols], sems.at[step])
 
     joined = jnp.concatenate([slot[...] for slot in slots], axis=0)
-    back_ref[...] = joined.astype(F32).T.astype(BF16)
+    back_ref[...] = joined.T
 
     def predict(step, slot):
         cols = pl.ds(step * width, width)
@@ -411,7 +414,10 @@
         return lax.ppermute(x, "nodes", pairs)
 
     def swap_all(xs):
-        return [xs[OWN]] + [swap(xs[s], s) for s in range(1, SLOTS)]
+        out = {OWN: xs[OWN]}
+        for s in (ODD, HALF, FAR, EVEN, NEAR):
+            out[s] = swap(xs[s], s)
+        return [out[s] for s in range(SLOTS)]
 
     lat_t, dsum, grid_t, *sums = encode(
         parts, slot_block, enc_owner.reshape(-1, 128), grid_in.T, w_embed, enc_coef,

time: 42.1 us -> 41.9 us (level)
  no operation moved by 1% of the time
where the time goes in v10:
time: 41.9 us; the launch traced here: 41.7 us
  Pallas kernels  15.5 us (37%)
  starting transfers between devices  13.4 us (32%)
  waiting for transfers between devices  12 us (29%)
  between operations  0.76 us (2%)
    ppermute x12, starting transfers between devices, swap(): return lax.ppermute(x, 'nodes', pairs)  13.4 us
    ppermute x12, waiting for transfers between devices, swap(): return lax.ppermute(x, 'nodes', pairs)  12 us
    pallas_call x1, Pallas kernels, encode(): pl.pallas_call(functools.partial(encode_kernel, parts, width), in_specs=[...  8.03 us
    pallas_call x1, Pallas kernels, decode(): pl.pallas_call(functools.partial(decode_kernel, width), in_specs=[vmem] *...  5.02 us
    pallas_call x1, Pallas kernels, process(): pl.pallas_call(process_kernel, in_specs=[vmem] * 7, out_specs=[vmem] * (1...  1.31 us
    pallas_call x1, Pallas kernels, prepare(): pl.pallas_call(functools.partial(prepare_kernel, parts), in_specs=[pl.Blo...  0.88 us
  transfers between devices with their start and end apart: 12, of which 5 were waited for; matrix products, arithmetic and copies ran while one was open for 0% of the time, Pallas kernels for 2%

profile of v10, /device:TPU:0, one launch (start us, length us, event | category | flops | bytes accessed | tf_op | source)
XLA Modules:
  0.0 41.7 jit_solution(7561764541365902592)
XLA Ops:
  0.6 0.0 copy-start
  0.6 0.0 copy-start.4
  0.7 0.0 copy-start.3
  0.7 0.0 copy-start.5
  0.7 0.0 copy-start.1
  0.7 0.0 copy-start.6
  0.7 8.0 %encode.1 = (bf16[512,4096]{1,0:T(8,128)(2,1)S(1)}, bf16[192,4096]{1,0:T(8,128)(2,1)S(1)}, bf16[227,4096]{1,0:T(8,128)(2,1)S(1)}, bf16[32,640]{1,0:T(8,128)(2,1)...) custom-call(s32[16]{0:T(128)} %slot_hbm.1, ...), custom_call_target="tpu_custom_call" | custom-call | tf_op jit(solution)/shard_map/encode/pallas_call | solution.py:206
  8.7 0.0 copy-start.2
  8.7 4.1 %collective-permute-start = (bf16[32,640]{1,0:T(8,128)(2,1)S(1)}, bf16[32,640]{1,0:T(8,128)(2,1)S(1)}, u32[]{:S(2)}, u32[]{:S(2)}) collective-permute-start(bf16[32,640]{1,0:T(8,128)(2,1)S(1)} %get-tuple-element.24), channel_id=1, source_target_pairs={{0,8},{1,9},{2,10},{3,11},{4,12},{5,13},{6,14},{7,15},{8,0},{9,1},... | collective-permute-start | bytes 122888 | tf_op jit(solution)/shard_map/ppermute | solution.py:414
  12.8 2.3 %collective-permute-start.1 = (bf16[32,640]{1,0:T(8,128)(2,1)S(1)}, bf16[32,640]{1,0:T(8,128)(2,1)S(1)}, u32[]{:S(2)}, u32[]{:S(2)}) collective-permute-start(bf16[32,640]{1,0:T(8,128)(2,1)S(1)} %get-tuple-element.25), channel_id=1, source_target_pairs={{0,14},{1,15},{2,4},{3,5},{4,2},{5,3},{6,8},{7,9},{8,6},{9,7},{10,... | collective-permute-start | bytes 122888 | tf_op jit(solution)/shard_map/ppermute | solution.py:414
  15.1 1.3 %collective-permute-start.2 = (bf16[32,640]{1,0:T(8,128)(2,1)S(1)}, bf16[32,640]{1,0:T(8,128)(2,1)S(1)}, u32[]{:S(2)}, u32[]{:S(2)}) collective-permute-start(bf16[32,640]{1,0:T(8,128)(2,1)S(1)} %get-tuple-element.26), channel_id=1, source_target_pairs={{0,15},{1,2},{2,1},{3,4},{4,3},{5,6},{6,5},{7,8},{8,7},{9,10},{10,... | collective-permute-start | bytes 122888 | tf_op jit(solution)/shard_map/ppermute | solution.py:414
  16.4 0.0 collective-permute-start.3
  16.4 0.7 %collective-permute-start.4 = (bf16[32,640]{1,0:T(8,128)(2,1)S(1)}, bf16[32,640]{1,0:T(8,128)(2,1)S(1)}, u32[]{:S(2)}, u32[]{:S(2)}) collective-permute-start(bf16[32,640]{1,0:T(8,128)(2,1)S(1)} %get-tuple-element.28), channel_id=1, source_target_pairs={{0,1},{1,0},{2,3},{3,2},{4,5},{5,4},{6,7},{7,6},{8,9},{9,8},{10,11... | collective-permute-start | bytes 122888 | tf_op jit(solution)/shard_map/ppermute | solution.py:414
  17.1 0.0 collective-permute-done.refs_1_
  17.1 2.4 %collective-permute-done.1.refs_2_ = bf16[32,640]{1,0:T(8,128)(2,1)S(1)} collective-permute-done((bf16[32,640]{1,0:T(8,128)(2,1)S(1)}, bf16[32,640]{1,0:T(8,128)(2,1)S(1)}, u32[]{:S(2)}, u32[]{:S(2)}) %collective-permute-start.1) | collective-permute-done | bytes 40992 | tf_op jit(solution)/shard_map/ppermute | solution.py:414
  19.5 1.7 %collective-permute-done.2.refs_3_ = bf16[32,640]{1,0:T(8,128)(2,1)S(1)} collective-permute-done((bf16[32,640]{1,0:T(8,128)(2,1)S(1)}, bf16[32,640]{1,0:T(8,128)(2,1)S(1)}, u32[]{:S(2)}, u32[]{:S(2)}) %collective-permute-start.2) | collective-permute-done | bytes 40992 | tf_op jit(solution)/shard_map/ppermute | solution.py:414
  21.3 0.0 collective-permute-done.3.refs_4_
  21.3 0.0 collective-permute-done.4.refs_5_
  21.3 0.0 copy-done
  21.3 0.0 copy-done.4
  21.3 0.3 mesh_update.1
  21.6 1.7 %collective-permute-start.6 = (bf16[128,512]{1,0:T(8,128)(2,1)S(1)}, bf16[128,512]{1,0:T(8,128)(2,1)S(1)}, u32[]{:S(2)}, u32[]{:S(2)}) collective-permute-start(bf16[128,512]{1,0:T(8,128)(2,1)S(1)} %get-tuple-element.30.mid_ref), channel_id=1, source_target_pairs={{0,15},{1,2},{2,1},{3,4},{4,3},{5,6},{6,5},{7,8},{8,7},{9,10},{10,... | collective-permute-start | bytes 393224 | tf_op jit(solution)/shard_map/ppermute | solution.py:414
  23.3 0.0 collective-permute-start.5
  23.3 0.0 copy-done.3
  23.3 0.0 copy-done.5
  23.3 0.9 %prepare.1.near_ref = bf16[128,384]{1,0:T(8,128)(2,1)S(1)} custom-call(s32[4,6]{1,0:T(4,128)S(1)} %copy-done.5, bf16[4,6,32,32]{3,2,1,0:T(8,128)(2,1)S(1)} %copy-done.3, bf16[32,640]{1,0:T(8,128)(2,1)S(1)} %get-tuple-element.23.refs_0_.after_ref), custom_call_target="tpu_custom_call" | custom-call | flops 18874368 | bytes 393216 | tf_op jit(solution)/shard_map/prepare/pallas_call | solution.py:267
  24.2 4.6 %collective-permute-done.6.far_mid_ref = bf16[128,512]{1,0:T(8,128)(2,1)S(1)} collective-permute-done((bf16[128,512]{1,0:T(8,128)(2,1)S(1)}, bf16[128,512]{1,0:T(8,128)(2,1)S(1)}, u32[]{:S(2)}, u32[]{:S(2)}) %collective-permute-start.6) | collective-permute-done | bytes 131104 | tf_op jit(solution)/shard_map/ppermute | solution.py:414
  28.8 0.0 collective-permute-done.5.near_mid_ref
  28.8 0.0 copy-done.1
  28.8 0.0 copy-done.6
  28.8 1.3 %mesh_process.1 = (bf16[128,512]{1,0:T(8,128)(2,1)}, bf16[32,512]{1,0:T(8,128)(2,1)S(1)}, bf16[32,512]{1,0:T(8,128)(2,1)S(1)}, bf16[32,512]{1,0:T(8,128)(2,1)S(1...) custom-call(f32[8,512]{1,0:T(8,128)S(1)} %get-tuple-element.29.ids_ref, ...), custom_call_target="tpu_custom_call" | custom-call | tf_op jit(solution)/shard_map/mesh_process/pallas_call | solution.py:337
  30.1 0.0 collective-permute-start.7
  30.1 0.1 collective-permute-start.8
  30.2 1.6 %collective-permute-start.9 = (bf16[32,512]{1,0:T(8,128)(2,1)S(1)}, bf16[32,512]{1,0:T(8,128)(2,1)S(1)}, u32[]{:S(2)}, u32[]{:S(2)}) collective-permute-start(bf16[32,512]{1,0:T(8,128)(2,1)S(1)} %get-tuple-element.34), channel_id=1, source_target_pairs={{0,15},{1,2},{2,1},{3,4},{4,3},{5,6},{6,5},{7,8},{8,7},{9,10},{10,... | collective-permute-start | bytes 98312 | tf_op jit(solution)/shard_map/ppermute | solution.py:414
  31.7 1.7 %collective-permute-start.10 = (bf16[32,512]{1,0:T(8,128)(2,1)S(1)}, bf16[32,512]{1,0:T(8,128)(2,1)S(1)}, u32[]{:S(2)}, u32[]{:S(2)}) collective-permute-start(bf16[32,512]{1,0:T(8,128)(2,1)S(1)} %get-tuple-element.35), channel_id=1, source_target_pairs={{0,2},{1,3},{2,0},{3,1},{4,6},{5,7},{6,4},{7,5},{8,10},{9,11},{10,... | collective-permute-start | bytes 98312 | tf_op jit(solution)/shard_map/ppermute | solution.py:414
  33.4 0.0 collective-permute-start.11
  33.4 1.7 %collective-permute-done.7.rest_1_ = bf16[32,512]{1,0:T(8,128)(2,1)S(1)} collective-permute-done((bf16[32,512]{1,0:T(8,128)(2,1)S(1)}, bf16[32,512]{1,0:T(8,128)(2,1)S(1)}, u32[]{:S(2)}, u32[]{:S(2)}) %collective-permute-start.7) | collective-permute-done | bytes 32800 | tf_op jit(solution)/shard_map/ppermute | solution.py:414
  35.1 1.6 %collective-permute-done.8.rest_2_ = bf16[32,512]{1,0:T(8,128)(2,1)S(1)} collective-permute-done((bf16[32,512]{1,0:T(8,128)(2,1)S(1)}, bf16[32,512]{1,0:T(8,128)(2,1)S(1)}, u32[]{:S(2)}, u32[]{:S(2)}) %collective-permute-start.8) | collective-permute-done | bytes 32800 | tf_op jit(solution)/shard_map/ppermute | solution.py:414
  36.7 0.0 collective-permute-done.9.rest_3_
  36.7 0.0 collective-permute-done.10.rest_4_
  36.7 0.0 collective-permute-done.11.rest_5_
  36.7 0.0 copy-done.2
  36.7 5.0 %decode.1 = bf16[227,4096]{1,0:T(8,128)(2,1)} custom-call(bf16[227,4096]{1,0:T(8,128)(2,1)S(1)} %get-tuple-element.20.grid_ref, bf16[512,4096]{1,0:T(8,128)(2,1)S(1)} %get-tuple-element.21.lat_ref, bf16[192,4096]{1,0:T(8,128)(2,1)S(1)} %get-tuple-element.22.dsum_ref, bf16[227,512]{1,0:T(8,128)(2,1)S(1)} %bitcast.6, ...), custom_call_target="tpu_custom_call" | custom-call | tf_op jit(solution)/shard_map/decode/pallas_call | solution.py:389
Async XLA Ops:
  0.6 20.6 %copy-start = (bf16[512,512]{1,0:T(8,128)(2,1)S(1)}, bf16[512,512]{1,0:T(8,128)(2,1)}, u32[]{:S(2)}) copy-start(bf16[512,512]{1,0:T(8,128)(2,1)} %refs_7_.1) | copy-start | bytes 1572868
  0.6 20.6 %copy-start.4 = (bf16[128,512]{1,0:T(8,128)(2,1)S(1)}, bf16[128,512]{1,0:T(8,128)(2,1)}, u32[]{:S(2)}) copy-start(bf16[128,512]{1,0:T(8,128)(2,1)} %refs_6_.1) | copy-start | bytes 393220
  0.7 22.6 %copy-start.3 = (bf16[4,6,32,32]{3,2,1,0:T(8,128)(2,1)S(1)}, bf16[4,6,32,32]{3,2,1,0:T(8,128)(2,1)}, u32[]{:S(2)}) copy-start(bf16[4,6,32,32]{3,2,1,0:T(8,128)(2,1)} %coef_ref.1) | copy-start | bytes 147460
  0.7 22.6 %copy-start.5 = (s32[4,6]{1,0:T(4,128)S(1)}, s32[4,6]{1,0:T(4,128)}, u32[]{:S(2)}) copy-start(s32[4,6]{1,0:T(4,128)} %adj_ref.1) | copy-start | bytes 292
  0.7 28.1 %copy-start.1 = (bf16[512,512]{1,0:T(8,128)(2,1)S(1)}, bf16[512,512]{1,0:T(8,128)(2,1)}, u32[]{:S(2)}) copy-start(bf16[512,512]{1,0:T(8,128)(2,1)} %w_ref.1) | copy-start | bytes 1572868
  0.7 28.1 %copy-start.6 = (f32[512]{0:T(512)S(1)}, f32[512]{0:T(512)}, u32[]{:S(2)}) copy-start(f32[512]{0:T(512)} %param.22) | copy-start | bytes 6148
  8.7 28.0 %copy-start.2 = (bf16[512,227]{0,1:T(8,128)(2,1)S(1)}, bf16[512,227]{0,1:T(8,128)(2,1)}, u32[]{:S(2)}) copy-start(bf16[512,227]{0,1:T(8,128)(2,1)} %param.25) | copy-start | bytes 697348
  8.7 8.4 %collective-permute-start = (bf16[32,640]{1,0:T(8,128)(2,1)S(1)}, bf16[32,640]{1,0:T(8,128)(2,1)S(1)}, u32[]{:S(2)}, u32[]{:S(2)}) collective-permute-start(bf16[32,640]{1,0:T(8,128)(2,1)S(1)} %get-tuple-element.24), channel_id=1, source_target_pairs={{0,8},{1,9},{2,10},{3,11},{4,12},{5,13},{6,14},{7,15},{8,0},{9,1},... | collective-permute-start | bytes 122888 | tf_op jit(solution)/shard_map/ppermute | solution.py:414
  12.8 6.7 %collective-permute-start.1 = (bf16[32,640]{1,0:T(8,128)(2,1)S(1)}, bf16[32,640]{1,0:T(8,128)(2,1)S(1)}, u32[]{:S(2)}, u32[]{:S(2)}) collective-permute-start(bf16[32,640]{1,0:T(8,128)(2,1)S(1)} %get-tuple-element.25), channel_id=1, source_target_pairs={{0,14},{1,15},{2,4},{3,5},{4,2},{5,3},{6,8},{7,9},{8,6},{9,7},{10,... | collective-permute-start | bytes 122888 | tf_op jit(solution)/shard_map/ppermute | solution.py:414
  15.1 6.1 %collective-permute-start.2 = (bf16[32,640]{1,0:T(8,128)(2,1)S(1)}, bf16[32,640]{1,0:T(8,128)(2,1)S(1)}, u32[]{:S(2)}, u32[]{:S(2)}) collective-permute-start(bf16[32,640]{1,0:T(8,128)(2,1)S(1)} %get-tuple-element.26), channel_id=1, source_target_pairs={{0,15},{1,2},{2,1},{3,4},{4,3},{5,6},{6,5},{7,8},{8,7},{9,10},{10,... | collective-permute-start | bytes 122888 | tf_op jit(solution)/shard_map/ppermute | solution.py:414
  16.4 4.8 %collective-permute-start.3 = (bf16[32,640]{1,0:T(8,128)(2,1)S(1)}, bf16[32,640]{1,0:T(8,128)(2,1)S(1)}, u32[]{:S(2)}, u32[]{:S(2)}) collective-permute-start(bf16[32,640]{1,0:T(8,128)(2,1)S(1)} %get-tuple-element.27), channel_id=1, source_target_pairs={{0,2},{1,3},{2,0},{3,1},{4,6},{5,7},{6,4},{7,5},{8,10},{9,11},{10,... | collective-permute-start | bytes 122888 | tf_op jit(solution)/shard_map/ppermute | solution.py:414
  16.4 4.8 %collective-permute-start.4 = (bf16[32,640]{1,0:T(8,128)(2,1)S(1)}, bf16[32,640]{1,0:T(8,128)(2,1)S(1)}, u32[]{:S(2)}, u32[]{:S(2)}) collective-permute-start(bf16[32,640]{1,0:T(8,128)(2,1)S(1)} %get-tuple-element.28), channel_id=1, source_target_pairs={{0,1},{1,0},{2,3},{3,2},{4,5},{5,4},{6,7},{7,6},{8,9},{9,8},{10,11... | collective-permute-start | bytes 122888 | tf_op jit(solution)/shard_map/ppermute | solution.py:414
  21.6 7.2 %collective-permute-start.6 = (bf16[128,512]{1,0:T(8,128)(2,1)S(1)}, bf16[128,512]{1,0:T(8,128)(2,1)S(1)}, u32[]{:S(2)}, u32[]{:S(2)}) collective-permute-start(bf16[128,512]{1,0:T(8,128)(2,1)S(1)} %get-tuple-element.30.mid_ref), channel_id=1, source_target_pairs={{0,15},{1,2},{2,1},{3,4},{4,3},{5,6},{6,5},{7,8},{8,7},{9,10},{10,... | collective-permute-start | bytes 393224 | tf_op jit(solution)/shard_map/ppermute | solution.py:414
  23.3 5.5 %collective-permute-start.5 = (bf16[128,512]{1,0:T(8,128)(2,1)S(1)}, bf16[128,512]{1,0:T(8,128)(2,1)S(1)}, u32[]{:S(2)}, u32[]{:S(2)}) collective-permute-start(bf16[128,512]{1,0:T(8,128)(2,1)S(1)} %get-tuple-element.30.mid_ref), channel_id=1, source_target_pairs={{0,1},{1,0},{2,3},{3,2},{4,5},{5,4},{6,7},{7,6},{8,9},{9,8},{10,11... | collective-permute-start | bytes 393224 | tf_op jit(solution)/shard_map/ppermute | solution.py:414
  30.1 5.0 %collective-permute-start.7 = (bf16[32,512]{1,0:T(8,128)(2,1)S(1)}, bf16[32,512]{1,0:T(8,128)(2,1)S(1)}, u32[]{:S(2)}, u32[]{:S(2)}) collective-permute-start(bf16[32,512]{1,0:T(8,128)(2,1)S(1)} %get-tuple-element.32), channel_id=1, source_target_pairs={{0,8},{1,9},{2,10},{3,11},{4,12},{5,13},{6,14},{7,15},{8,0},{9,1},... | collective-permute-start | bytes 98312 | tf_op jit(solution)/shard_map/ppermute | solution.py:414
  30.1 6.6 %collective-permute-start.8 = (bf16[32,512]{1,0:T(8,128)(2,1)S(1)}, bf16[32,512]{1,0:T(8,128)(2,1)S(1)}, u32[]{:S(2)}, u32[]{:S(2)}) collective-permute-start(bf16[32,512]{1,0:T(8,128)(2,1)S(1)} %get-tuple-element.33), channel_id=1, source_target_pairs={{0,14},{1,15},{2,4},{3,5},{4,2},{5,3},{6,8},{7,9},{8,6},{9,7},{10,... | collective-permute-start | bytes 98312 | tf_op jit(solution)/shard_map/ppermute | solution.py:414
  30.2 6.5 %collective-permute-start.9 = (bf16[32,512]{1,0:T(8,128)(2,1)S(1)}, bf16[32,512]{1,0:T(8,128)(2,1)S(1)}, u32[]{:S(2)}, u32[]{:S(2)}) collective-permute-start(bf16[32,512]{1,0:T(8,128)(2,1)S(1)} %get-tuple-element.34), channel_id=1, source_target_pairs={{0,15},{1,2},{2,1},{3,4},{4,3},{5,6},{6,5},{7,8},{8,7},{9,10},{10,... | collective-permute-start | bytes 98312 | tf_op jit(solution)/shard_map/ppermute | solution.py:414
  31.7 5.0 %collective-permute-start.10 = (bf16[32,512]{1,0:T(8,128)(2,1)S(1)}, bf16[32,512]{1,0:T(8,128)(2,1)S(1)}, u32[]{:S(2)}, u32[]{:S(2)}) collective-permute-start(bf16[32,512]{1,0:T(8,128)(2,1)S(1)} %get-tuple-element.35), channel_id=1, source_target_pairs={{0,2},{1,3},{2,0},{3,1},{4,6},{5,7},{6,4},{7,5},{8,10},{9,11},{10,... | collective-permute-start | bytes 98312 | tf_op jit(solution)/shard_map/ppermute | solution.py:414
  33.4 3.3 %collective-permute-start.11 = (bf16[32,512]{1,0:T(8,128)(2,1)S(1)}, bf16[32,512]{1,0:T(8,128)(2,1)S(1)}, u32[]{:S(2)}, u32[]{:S(2)}) collective-permute-start(bf16[32,512]{1,0:T(8,128)(2,1)S(1)} %get-tuple-element.36), channel_id=1, source_target_pairs={{0,1},{1,0},{2,3},{3,2},{4,5},{5,4},{6,7},{7,6},{8,9},{9,8},{10,11... | collective-permute-start | bytes 98312 | tf_op jit(solution)/shard_map/ppermute | solution.py:414

commit v11 on v10

--- a/solution.py
+++ b/solution.py
@@ -10,7 +10,7 @@
 F32 = jnp.float32
 BF16 = jnp.bfloat16
 MIB = 1 << 20
-OWN, HALF, ODD, FAR, EVEN, NEAR = range(6)
+OWN, ODD, HALF, FAR, EVEN, NEAR = range(6)
 SLOTS = 6
 PAD = 128
 AHEAD = 3
@@ -65,8 +65,17 @@
     )
 
 
-def fill_targets(parts, per_block, block_mesh, owner_ref, tgt_ref):
-    wide = tgt_ref.shape[1]
+def spreads(per_block, block_mesh, groups, lanes, wide):
+    out = []
+    for r in range(groups):
+        row = lax.broadcasted_iota(jnp.int32, (lanes, wide), 0) + r * lanes
+        col = lax.broadcasted_iota(jnp.int32, (lanes, wide), 1)
+        place = row - per_block * ((row * (2**19 // per_block + 1)) >> 19)
+        out.append(jnp.where(place == col // block_mesh, 1.0, 0.0).astype(BF16))
+    return out
+
+
+def fill_targets(parts, per_block, block_mesh, spread_ref, owner_ref, tgt_ref):
     me = lax.axis_index("nodes")
     chip = lax.rem(lax.div(me, 2), 2)
     core = lax.rem(me, 2)
@@ -88,11 +97,7 @@
         first = lax.broadcasted_iota(jnp.int32, (all_blocks, lanes), 0) * per_block
         mine = (tile >= first) & (tile < first + per_block)
         picked = jnp.where(mine, slot[r : r + 1, :], 0.0).astype(BF16)
-        row = lax.broadcasted_iota(jnp.int32, (lanes, wide), 0) + r * lanes
-        col = lax.broadcasted_iota(jnp.int32, (lanes, wide), 1)
-        place = row - per_block * ((row * (2**19 // per_block + 1)) >> 19)
-        spread = jnp.where(place == col // block_mesh, 1.0, 0.0).astype(BF16)
-        total += jnp.dot(picked, spread, preferred_element_type=F32)
+        total += jnp.dot(picked, spread_ref[r], preferred_element_type=F32)
     col = lax.broadcasted_iota(jnp.int32, tgt_ref.shape, 1)
     tgt_ref[...] = total * block_mesh + (col % block_mesh).astype(F32)
 
@@ -104,7 +109,7 @@
     send_refs = rest[:SLOTS]
     (
         slot_ref, owner_ref, w_ref, enc_ref, dec_ref, wt_ref, tgt_ref, ids_ref, msum_ref,
-        hold_ref, acc_ref, small_sems, sems,
+        hold_ref, acc_ref, spread_ref, small_sems, sems,
     ) = rest[SLOTS:]
     tiles, block_mesh, block_grid = enc_ref.shape
     channels, points = grid_ref.shape
@@ -137,14 +142,17 @@
         for copy in copies(step):
             copy.start()
 
-    for step in range(AHEAD):
-        start(step)
+    start(0)
     ids_ref[...] = lax.broadcasted_iota(jnp.int32, ids_ref.shape, 0).astype(BF16)
     acc_ref[...] = jnp.zeros_like(acc_ref)
+    for r, spread in enumerate(spreads(per_block, block_mesh, *owner_ref.shape, wide)):
+        spread_ref[r] = spread
     for copy in small:
         copy.wait()
+    for step in range(1, AHEAD):
+        start(step)
     wt_ref[:, :channels] = (0.5 * w_ref[...].astype(F32)).T.astype(BF16)
-    fill_targets(parts, per_block, block_mesh, owner_ref, tgt_ref)
+    fill_targets(parts, per_block, block_mesh, spread_ref, owner_ref, tgt_ref)
 
     def collect(slot):
         acc_ref[...] += lax.dot_general(
@@ -185,7 +193,7 @@
 
     collect(1)
     me = lax.axis_index("nodes")
-    flipped = acc_ref[...].T.astype(BF16)
+    flipped = acc_ref[...].astype(BF16).T
     for s in range(SLOTS):
         send_refs[s][:, :latent] = flipped[s * block_mesh : (s + 1) * block_mesh, :]
         block = slot_ref[scalar_partner(s, me, parts)].astype(F32)
@@ -225,6 +233,7 @@
             pltpu.VMEM((2, rows, width), BF16),
             pltpu.VMEM((2, latent, width), BF16),
             pltpu.VMEM((latent, rows), F32),
+            pltpu.VMEM((*owners.shape, wide), BF16),
             pltpu.SemaphoreType.DMA((3,)),
             pltpu.SemaphoreType.DMA((3, steps)),
         ],
@@ -238,12 +247,13 @@
     )
 
 
-def prepare_kernel(parts, adj_ref, coef_ref, after_ref, near_ref):
+def prepare_kernel(parts, adj_ref, coef_ref, mid_ref, near_ref, part_ref, all_ref):
     mesh_blocks, adj_width = adj_ref.shape
     block_mesh = coef_ref.shape[2]
     me = lax.axis_index("nodes")
     core = lax.rem(me, 2)
-    columns = near_ref.shape[1]
+    count = mid_ref.shape[0]
+    columns = all_ref.shape[1]
     row = lax.broadcasted_iota(jnp.int32, (block_mesh, columns), 0)
     col = lax.broadcasted_iota(jnp.int32, (block_mesh, columns), 1)
     for b in range(mesh_blocks):
@@ -252,23 +262,31 @@
             which = adj_ref[b, a]
             listed = jnp.maximum(which, 0)
             side = lax.rem(lax.div(listed, mesh_blocks) - me + 1 + parts, parts)
-            side = jnp.where(core == 0, 2 - side, side)
+            side = jnp.where(side == 1, 2, jnp.where((side == 2) == (core == 0), 0, 1))
             place = side * mesh_blocks + lax.rem(listed, mesh_blocks)
             place = jnp.where(which >= 0, place, -columns)
             spot = jnp.where(col == place * block_mesh + row, 1.0, 0.0).astype(BF16)
             total += jnp.dot(coef_ref[b, a], spot, preferred_element_type=F32)
-        near_ref[b * block_mesh : (b + 1) * block_mesh, :] = total.astype(BF16)
-
-
-def prepare(parts, adj, coef, after):
+        all_ref[b * block_mesh : (b + 1) * block_mesh, :] = total.astype(BF16)
+    near_ref[...] = all_ref[:, : 2 * count]
+    part_ref[...] = jnp.dot(
+        all_ref[:, 2 * count :], mid_ref[...], preferred_element_type=F32
+    )
+
+
+def prepare(parts, adj, coef, mid):
     mesh_blocks, adj_width, block_mesh, _ = coef.shape
     count = mesh_blocks * block_mesh
     vmem = pl.BlockSpec(memory_space=pltpu.VMEM)
     return pl.pallas_call(
         functools.partial(prepare_kernel, parts),
         in_specs=[pl.BlockSpec(memory_space=pltpu.SMEM), vmem, vmem],
-        out_specs=vmem,
-        out_shape=jax.ShapeDtypeStruct((count, 3 * count), BF16),
+        out_specs=[vmem] * 2,
+        out_shape=[
+            jax.ShapeDtypeStruct((count, 2 * count), BF16),
+            jax.ShapeDtypeStruct(mid.shape, F32),
+        ],
+        scratch_shapes=[pltpu.VMEM((count, 3 * count), BF16)],
         compiler_params=pltpu.CompilerParams(vmem_limit_bytes=8 * MIB),
         cost_estimate=pl.CostEstimate(
             flops=2 * adj_width * count * block_mesh * 3 * count,
@@ -276,7 +294,7 @@
             transcendentals=0,
         ),
         name="prepare",
-    )(adj, coef, after)
+    )(adj, coef, mid)
 
 
 def update_kernel(*refs):
@@ -313,11 +331,13 @@
     )(*slots, mesh_in, w_enc)
 
 
-def process_kernel(ids_ref, mid_ref, near_mid_ref, far_mid_ref, near_ref, gain_ref, w_ref, out_ref, *sends):
+def process_kernel(
+    ids_ref, mid_ref, near_mid_ref, far_mid_ref, near_ref, part_ref, gain_ref, w_ref, out_ref, *sends
+):
     count, latent = mid_ref.shape
     block_mesh = sends[0].shape[0]
-    around = jnp.concatenate([near_mid_ref[...], mid_ref[...], far_mid_ref[...]], axis=0)
-    message = jnp.dot(near_ref[...], around, preferred_element_type=F32)
+    around = jnp.concatenate([near_mid_ref[...], far_mid_ref[...]], axis=0)
+    message = part_ref[...] + jnp.dot(near_ref[...], around, preferred_element_type=F32)
     power = jnp.mean(message * message, axis=-1, keepdims=True)
     normed = (message * lax.rsqrt(power + 1e-05) * gain_ref[...]).astype(BF16)
     grown = jnp.dot(normed, w_ref[...], preferred_element_type=F32)
@@ -331,18 +351,18 @@
         sends[s][...] = chosen.astype(BF16)
 
 
-def process(block_mesh, ids, mid, near_mid, far_mid, near, gain, w_proc):
+def process(block_mesh, ids, mid, near_mid, far_mid, near, part, gain, w_proc):
     vmem = pl.BlockSpec(memory_space=pltpu.VMEM)
     latent = mid.shape[1]
     return pl.pallas_call(
         process_kernel,
-        in_specs=[vmem] * 7,
+        in_specs=[vmem] * 8,
         out_specs=[vmem] * (1 + SLOTS),
         out_shape=[jax.ShapeDtypeStruct(mid.shape, BF16)]
         + [jax.ShapeDtypeStruct((block_mesh, latent), BF16)] * SLOTS,
         compiler_params=pltpu.CompilerParams(vmem_limit_bytes=8 * MIB),
         name="mesh_process",
-    )(ids, mid, near_mid, far_mid, near, gain, w_proc)
+    )(ids, mid, near_mid, far_mid, near, part, gain, w_proc)
 
 
 def decode_kernel(width, grid_ref, lat_ref, dsum_ref, w_ref, *rest):
@@ -414,22 +434,19 @@
         return lax.ppermute(x, "nodes", pairs)
 
     def swap_all(xs):
-        out = {OWN: xs[OWN]}
-        for s in (ODD, HALF, FAR, EVEN, NEAR):
-            out[s] = swap(xs[s], s)
-        return [out[s] for s in range(SLOTS)]
+        return [xs[OWN]] + [swap(xs[s], s) for s in range(1, SLOTS)]
 
     lat_t, dsum, grid_t, *sums = encode(
         parts, slot_block, enc_owner.reshape(-1, 128), grid_in.T, w_embed, enc_coef,
         jnp.swapaxes(dec_coef, 1, 2),
     )
     received = swap_all(sums)
-    near = prepare(parts, proc_adj, proc_coef, sums[OWN])
     mid, ids = update(received, mesh_in, w_enc)
     far_mid = swap(mid, FAR)
     near_mid = swap(mid, NEAR)
+    near, part = prepare(parts, proc_adj, proc_coef, mid)
     mesh_out, *sends = process(
-        block_mesh, ids, mid, near_mid, far_mid, near, proc_gain.reshape(1, -1), w_proc
+        block_mesh, ids, mid, near_mid, far_mid, near, part, proc_gain.reshape(1, -1), w_proc
     )
     returned = swap_all(sends)
     pred_t = decode(grid_t, lat_t, dsum, w_out.T, returned)

time: 41.9 us -> 41.3 us (0.986)
  starting transfers between devices: 13.4 us -> 12.8 us
    ppermute x12, starting transfers between devices: 13.4 us -> 12.8 us  [swap(): return lax.ppermute(x, 'nodes', pairs)]
  transfers between devices with their start and end apart: 12 -> 12, of which waited for: 5 -> 4; matrix products, arithmetic and copies ran while one was open for 0% -> 0% of each run, Pallas kernels for 2% -> 3%
where the time goes in v11:
time: 41.3 us; the launch traced here: 41.2 us
  Pallas kernels  15.6 us (38%)
  starting transfers between devices  12.8 us (31%)
  waiting for transfers between devices  12 us (29%)
  between operations  0.76 us (2%)
    ppermute x12, starting transfers between devices, swap(): return lax.ppermute(x, 'nodes', pairs)  12.8 us
    ppermute x12, waiting for transfers between devices, swap(): return lax.ppermute(x, 'nodes', pairs)  12 us
    pallas_call x1, Pallas kernels, encode(): pl.pallas_call(functools.partial(encode_kernel, parts, width), in_specs=[...  7.86 us
    pallas_call x1, Pallas kernels, decode(): pl.pallas_call(functools.partial(decode_kernel, width), in_specs=[vmem] *...  5.01 us
    pallas_call x1, Pallas kernels, process(): pl.pallas_call(process_kernel, in_specs=[vmem] * 8, out_specs=[vmem] * (1...  1.27 us
    pallas_call x1, Pallas kernels, prepare(): pl.pallas_call(functools.partial(prepare_kernel, parts), in_specs=[pl.Blo...  1.11 us
  transfers between devices with their start and end apart: 12, of which 4 were waited for; matrix products, arithmetic and copies ran while one was open for 0% of the time, Pallas kernels for 3%

profile of v11, /device:TPU:0, one launch (start us, length us, event | category | flops | bytes accessed | tf_op | source)
XLA Modules:
  0.0 41.2 jit_solution(14918947513049879560)
XLA Ops:
  0.6 0.0 copy-start.1
  0.6 0.0 copy-start.4
  0.7 0.0 copy-start.3
  0.7 0.0 copy-start.5
  0.7 0.0 copy-start
  0.7 0.0 copy-start.6
  0.7 7.9 %encode.1 = (bf16[512,4096]{1,0:T(8,128)(2,1)S(1)}, bf16[192,4096]{1,0:T(8,128)(2,1)S(1)}, bf16[227,4096]{1,0:T(8,128)(2,1)S(1)}, bf16[32,640]{1,0:T(8,128)(2,1)...) custom-call(s32[16]{0:T(128)} %slot_hbm.1, ...), custom_call_target="tpu_custom_call" | custom-call | tf_op jit(solution)/shard_map/encode/pallas_call | solution.py:214
  8.6 0.0 copy-start.2
  8.6 6.1 %collective-permute-start = (bf16[32,640]{1,0:T(8,128)(2,1)S(1)}, bf16[32,640]{1,0:T(8,128)(2,1)S(1)}, u32[]{:S(2)}, u32[]{:S(2)}) collective-permute-start(bf16[32,640]{1,0:T(8,128)(2,1)S(1)} %get-tuple-element.26), channel_id=1, source_target_pairs={{0,14},{1,15},{2,4},{3,5},{4,2},{5,3},{6,8},{7,9},{8,6},{9,7},{10,... | collective-permute-start | bytes 122888 | tf_op jit(solution)/shard_map/ppermute | solution.py:434
  14.6 0.0 collective-permute-start.1
  14.7 0.7 %collective-permute-start.2 = (bf16[32,640]{1,0:T(8,128)(2,1)S(1)}, bf16[32,640]{1,0:T(8,128)(2,1)S(1)}, u32[]{:S(2)}, u32[]{:S(2)}) collective-permute-start(bf16[32,640]{1,0:T(8,128)(2,1)S(1)} %get-tuple-element.28), channel_id=1, source_target_pairs={{0,15},{1,2},{2,1},{3,4},{4,3},{5,6},{6,5},{7,8},{8,7},{9,10},{10,... | collective-permute-start | bytes 122888 | tf_op jit(solution)/shard_map/ppermute | solution.py:434
  15.4 0.5 %collective-permute-start.3 = (bf16[32,640]{1,0:T(8,128)(2,1)S(1)}, bf16[32,640]{1,0:T(8,128)(2,1)S(1)}, u32[]{:S(2)}, u32[]{:S(2)}) collective-permute-start(bf16[32,640]{1,0:T(8,128)(2,1)S(1)} %get-tuple-element.29), channel_id=1, source_target_pairs={{0,2},{1,3},{2,0},{3,1},{4,6},{5,7},{6,4},{7,5},{8,10},{9,11},{10,... | collective-permute-start | bytes 122888 | tf_op jit(solution)/shard_map/ppermute | solution.py:434
  15.8 1.1 %collective-permute-start.4 = (bf16[32,640]{1,0:T(8,128)(2,1)S(1)}, bf16[32,640]{1,0:T(8,128)(2,1)S(1)}, u32[]{:S(2)}, u32[]{:S(2)}) collective-permute-start(bf16[32,640]{1,0:T(8,128)(2,1)S(1)} %get-tuple-element.30), channel_id=1, source_target_pairs={{0,1},{1,0},{2,3},{3,2},{4,5},{5,4},{6,7},{7,6},{8,9},{9,8},{10,11... | collective-permute-start | bytes 122888 | tf_op jit(solution)/shard_map/ppermute | solution.py:434
  17.0 0.0 collective-permute-done.refs_1_
  17.0 2.6 %collective-permute-done.1.refs_2_ = bf16[32,640]{1,0:T(8,128)(2,1)S(1)} collective-permute-done((bf16[32,640]{1,0:T(8,128)(2,1)S(1)}, bf16[32,640]{1,0:T(8,128)(2,1)S(1)}, u32[]{:S(2)}, u32[]{:S(2)}) %collective-permute-start.1) | collective-permute-done | bytes 40992 | tf_op jit(solution)/shard_map/ppermute | solution.py:434
  19.6 1.2 %collective-permute-done.2.refs_3_ = bf16[32,640]{1,0:T(8,128)(2,1)S(1)} collective-permute-done((bf16[32,640]{1,0:T(8,128)(2,1)S(1)}, bf16[32,640]{1,0:T(8,128)(2,1)S(1)}, u32[]{:S(2)}, u32[]{:S(2)}) %collective-permute-start.2) | collective-permute-done | bytes 40992 | tf_op jit(solution)/shard_map/ppermute | solution.py:434
  20.8 0.0 collective-permute-done.3.refs_4_
  20.8 0.0 collective-permute-done.4.refs_5_
  20.8 0.0 copy-done.1
  20.8 0.0 copy-done.4
  20.8 0.3 mesh_update.1
  21.1 1.4 %collective-permute-start.6 = (bf16[128,512]{1,0:T(8,128)(2,1)S(1)}, bf16[128,512]{1,0:T(8,128)(2,1)S(1)}, u32[]{:S(2)}, u32[]{:S(2)}) collective-permute-start(bf16[128,512]{1,0:T(8,128)(2,1)S(1)} %get-tuple-element.32.mid_ref), channel_id=1, source_target_pairs={{0,15},{1,2},{2,1},{3,4},{4,3},{5,6},{6,5},{7,8},{8,7},{9,10},{10,... | collective-permute-start | bytes 393224 | tf_op jit(solution)/shard_map/ppermute | solution.py:434
  22.5 0.0 collective-permute-start.5
  22.5 0.0 copy-done.3
  22.5 0.0 copy-done.5
  22.5 1.1 %prepare.1 = (bf16[128,256]{1,0:T(8,128)(2,1)S(1)}, f32[128,512]{1,0:T(8,128)S(1)}) custom-call(s32[4,6]{1,0:T(4,128)S(1)} %copy-done.5, bf16[4,6,32,32]{3,2,1,0:T(8,128)(2,1)S(1)} %copy-done.3, bf16[128,512]{1,0:T(8,128)(2,1)S(1)} %get-tuple-element.32.mid_ref), custom_call_target="tpu_custom_call" | custom-call | flops 18874368 | bytes 393216 | tf_op jit(solution)/shard_map/prepare/pallas_call | solution.py:281
  23.6 4.6 %collective-permute-done.6.far_mid_ref = bf16[128,512]{1,0:T(8,128)(2,1)S(1)} collective-permute-done((bf16[128,512]{1,0:T(8,128)(2,1)S(1)}, bf16[128,512]{1,0:T(8,128)(2,1)S(1)}, u32[]{:S(2)}, u32[]{:S(2)}) %collective-permute-start.6) | collective-permute-done | bytes 131104 | tf_op jit(solution)/shard_map/ppermute | solution.py:434
  28.3 0.0 collective-permute-done.5.near_mid_ref
  28.3 0.0 copy-done
  28.3 0.0 copy-done.6
  28.3 1.3 %mesh_process.1 = (bf16[128,512]{1,0:T(8,128)(2,1)}, bf16[32,512]{1,0:T(8,128)(2,1)S(1)}, bf16[32,512]{1,0:T(8,128)(2,1)S(1)}, bf16[32,512]{1,0:T(8,128)(2,1)S(1...) custom-call(f32[8,512]{1,0:T(8,128)S(1)} %get-tuple-element.31.ids_ref, ...), custom_call_target="tpu_custom_call" | custom-call | tf_op jit(solution)/shard_map/mesh_process/pallas_call | solution.py:357
  29.5 0.0 collective-permute-start.7
  29.5 0.0 collective-permute-start.8
  29.6 1.3 %collective-permute-start.9 = (bf16[32,512]{1,0:T(8,128)(2,1)S(1)}, bf16[32,512]{1,0:T(8,128)(2,1)S(1)}, u32[]{:S(2)}, u32[]{:S(2)}) collective-permute-start(bf16[32,512]{1,0:T(8,128)(2,1)S(1)} %get-tuple-element.38), channel_id=1, source_target_pairs={{0,15},{1,2},{2,1},{3,4},{4,3},{5,6},{6,5},{7,8},{8,7},{9,10},{10,... | collective-permute-start | bytes 98312 | tf_op jit(solution)/shard_map/ppermute | solution.py:434
  30.9 1.7 %collective-permute-start.10 = (bf16[32,512]{1,0:T(8,128)(2,1)S(1)}, bf16[32,512]{1,0:T(8,128)(2,1)S(1)}, u32[]{:S(2)}, u32[]{:S(2)}) collective-permute-start(bf16[32,512]{1,0:T(8,128)(2,1)S(1)} %get-tuple-element.39), channel_id=1, source_target_pairs={{0,2},{1,3},{2,0},{3,1},{4,6},{5,7},{6,4},{7,5},{8,10},{9,11},{10,... | collective-permute-start | bytes 98312 | tf_op jit(solution)/shard_map/ppermute | solution.py:434
  32.6 0.0 collective-permute-start.11
  32.6 3.5 %collective-permute-done.7.rest_1_ = bf16[32,512]{1,0:T(8,128)(2,1)S(1)} collective-permute-done((bf16[32,512]{1,0:T(8,128)(2,1)S(1)}, bf16[32,512]{1,0:T(8,128)(2,1)S(1)}, u32[]{:S(2)}, u32[]{:S(2)}) %collective-permute-start.7) | collective-permute-done | bytes 32800 | tf_op jit(solution)/shard_map/ppermute | solution.py:434
  36.2 0.0 collective-permute-done.8.rest_2_
  36.2 0.0 collective-permute-done.9.rest_3_
  36.2 0.0 collective-permute-done.10.rest_4_
  36.2 0.0 collective-permute-done.11.rest_5_
  36.2 0.0 copy-done.2
  36.2 5.0 %decode.1 = bf16[227,4096]{1,0:T(8,128)(2,1)} custom-call(bf16[227,4096]{1,0:T(8,128)(2,1)S(1)} %get-tuple-element.22.grid_ref, bf16[512,4096]{1,0:T(8,128)(2,1)S(1)} %get-tuple-element.23.lat_ref, bf16[192,4096]{1,0:T(8,128)(2,1)S(1)} %get-tuple-element.24.dsum_ref, bf16[227,512]{1,0:T(8,128)(2,1)S(1)} %bitcast.6, ...), custom_call_target="tpu_custom_call" | custom-call | tf_op jit(solution)/shard_map/decode/pallas_call | solution.py:409
Async XLA Ops:
  0.6 20.2 %copy-start.1 = (bf16[512,512]{1,0:T(8,128)(2,1)S(1)}, bf16[512,512]{1,0:T(8,128)(2,1)}, u32[]{:S(2)}) copy-start(bf16[512,512]{1,0:T(8,128)(2,1)} %refs_7_.1) | copy-start | bytes 1572868
  0.6 20.1 %copy-start.4 = (bf16[128,512]{1,0:T(8,128)(2,1)S(1)}, bf16[128,512]{1,0:T(8,128)(2,1)}, u32[]{:S(2)}) copy-start(bf16[128,512]{1,0:T(8,128)(2,1)} %refs_6_.1) | copy-start | bytes 393220
  0.7 21.8 %copy-start.3 = (bf16[4,6,32,32]{3,2,1,0:T(8,128)(2,1)S(1)}, bf16[4,6,32,32]{3,2,1,0:T(8,128)(2,1)}, u32[]{:S(2)}) copy-start(bf16[4,6,32,32]{3,2,1,0:T(8,128)(2,1)} %coef_ref.1) | copy-start | bytes 147460
  0.7 21.8 %copy-start.5 = (s32[4,6]{1,0:T(4,128)S(1)}, s32[4,6]{1,0:T(4,128)}, u32[]{:S(2)}) copy-start(s32[4,6]{1,0:T(4,128)} %adj_ref.1) | copy-start | bytes 292
  0.7 27.6 %copy-start = (bf16[512,512]{1,0:T(8,128)(2,1)S(1)}, bf16[512,512]{1,0:T(8,128)(2,1)}, u32[]{:S(2)}) copy-start(bf16[512,512]{1,0:T(8,128)(2,1)} %w_ref.1) | copy-start | bytes 1572868
  0.7 27.6 %copy-start.6 = (f32[512]{0:T(512)S(1)}, f32[512]{0:T(512)}, u32[]{:S(2)}) copy-start(f32[512]{0:T(512)} %param.22) | copy-start | bytes 6148
  8.6 27.6 %copy-start.2 = (bf16[512,227]{0,1:T(8,128)(2,1)S(1)}, bf16[512,227]{0,1:T(8,128)(2,1)}, u32[]{:S(2)}) copy-start(bf16[512,227]{0,1:T(8,128)(2,1)} %param.25) | copy-start | bytes 697348
  8.6 8.4 %collective-permute-start = (bf16[32,640]{1,0:T(8,128)(2,1)S(1)}, bf16[32,640]{1,0:T(8,128)(2,1)S(1)}, u32[]{:S(2)}, u32[]{:S(2)}) collective-permute-start(bf16[32,640]{1,0:T(8,128)(2,1)S(1)} %get-tuple-element.26), channel_id=1, source_target_pairs={{0,14},{1,15},{2,4},{3,5},{4,2},{5,3},{6,8},{7,9},{8,6},{9,7},{10,... | collective-permute-start | bytes 122888 | tf_op jit(solution)/shard_map/ppermute | solution.py:434
  14.6 4.9 %collective-permute-start.1 = (bf16[32,640]{1,0:T(8,128)(2,1)S(1)}, bf16[32,640]{1,0:T(8,128)(2,1)S(1)}, u32[]{:S(2)}, u32[]{:S(2)}) collective-permute-start(bf16[32,640]{1,0:T(8,128)(2,1)S(1)} %get-tuple-element.27), channel_id=1, source_target_pairs={{0,8},{1,9},{2,10},{3,11},{4,12},{5,13},{6,14},{7,15},{8,0},{9,1},... | collective-permute-start | bytes 122888 | tf_op jit(solution)/shard_map/ppermute | solution.py:434
  14.7 6.1 %collective-permute-start.2 = (bf16[32,640]{1,0:T(8,128)(2,1)S(1)}, bf16[32,640]{1,0:T(8,128)(2,1)S(1)}, u32[]{:S(2)}, u32[]{:S(2)}) collective-permute-start(bf16[32,640]{1,0:T(8,128)(2,1)S(1)} %get-tuple-element.28), channel_id=1, source_target_pairs={{0,15},{1,2},{2,1},{3,4},{4,3},{5,6},{6,5},{7,8},{8,7},{9,10},{10,... | collective-permute-start | bytes 122888 | tf_op jit(solution)/shard_map/ppermute | solution.py:434
  15.4 5.4 %collective-permute-start.3 = (bf16[32,640]{1,0:T(8,128)(2,1)S(1)}, bf16[32,640]{1,0:T(8,128)(2,1)S(1)}, u32[]{:S(2)}, u32[]{:S(2)}) collective-permute-start(bf16[32,640]{1,0:T(8,128)(2,1)S(1)} %get-tuple-element.29), channel_id=1, source_target_pairs={{0,2},{1,3},{2,0},{3,1},{4,6},{5,7},{6,4},{7,5},{8,10},{9,11},{10,... | collective-permute-start | bytes 122888 | tf_op jit(solution)/shard_map/ppermute | solution.py:434
  15.8 4.9 %collective-permute-start.4 = (bf16[32,640]{1,0:T(8,128)(2,1)S(1)}, bf16[32,640]{1,0:T(8,128)(2,1)S(1)}, u32[]{:S(2)}, u32[]{:S(2)}) collective-permute-start(bf16[32,640]{1,0:T(8,128)(2,1)S(1)} %get-tuple-element.30), channel_id=1, source_target_pairs={{0,1},{1,0},{2,3},{3,2},{4,5},{5,4},{6,7},{7,6},{8,9},{9,8},{10,11... | collective-permute-start | bytes 122888 | tf_op jit(solution)/shard_map/ppermute | solution.py:434
  21.1 7.2 %collective-permute-start.6 = (bf16[128,512]{1,0:T(8,128)(2,1)S(1)}, bf16[128,512]{1,0:T(8,128)(2,1)S(1)}, u32[]{:S(2)}, u32[]{:S(2)}) collective-permute-start(bf16[128,512]{1,0:T(8,128)(2,1)S(1)} %get-tuple-element.32.mid_ref), channel_id=1, source_target_pairs={{0,15},{1,2},{2,1},{3,4},{4,3},{5,6},{6,5},{7,8},{8,7},{9,10},{10,... | collective-permute-start | bytes 393224 | tf_op jit(solution)/shard_map/ppermute | solution.py:434
  22.5 5.8 %collective-permute-start.5 = (bf16[128,512]{1,0:T(8,128)(2,1)S(1)}, bf16[128,512]{1,0:T(8,128)(2,1)S(1)}, u32[]{:S(2)}, u32[]{:S(2)}) collective-permute-start(bf16[128,512]{1,0:T(8,128)(2,1)S(1)} %get-tuple-element.32.mid_ref), channel_id=1, source_target_pairs={{0,1},{1,0},{2,3},{3,2},{4,5},{5,4},{6,7},{7,6},{8,9},{9,8},{10,11... | collective-permute-start | bytes 393224 | tf_op jit(solution)/shard_map/ppermute | solution.py:434
  29.5 6.6 %collective-permute-start.7 = (bf16[32,512]{1,0:T(8,128)(2,1)S(1)}, bf16[32,512]{1,0:T(8,128)(2,1)S(1)}, u32[]{:S(2)}, u32[]{:S(2)}) collective-permute-start(bf16[32,512]{1,0:T(8,128)(2,1)S(1)} %get-tuple-element.36), channel_id=1, source_target_pairs={{0,14},{1,15},{2,4},{3,5},{4,2},{5,3},{6,8},{7,9},{8,6},{9,7},{10,... | collective-permute-start | bytes 98312 | tf_op jit(solution)/shard_map/ppermute | solution.py:434
  29.5 6.6 %collective-permute-start.8 = (bf16[32,512]{1,0:T(8,128)(2,1)S(1)}, bf16[32,512]{1,0:T(8,128)(2,1)S(1)}, u32[]{:S(2)}, u32[]{:S(2)}) collective-permute-start(bf16[32,512]{1,0:T(8,128)(2,1)S(1)} %get-tuple-element.37), channel_id=1, source_target_pairs={{0,8},{1,9},{2,10},{3,11},{4,12},{5,13},{6,14},{7,15},{8,0},{9,1},... | collective-permute-start | bytes 98312 | tf_op jit(solution)/shard_map/ppermute | solution.py:434
  29.6 6.6 %collective-permute-start.9 = (bf16[32,512]{1,0:T(8,128)(2,1)S(1)}, bf16[32,512]{1,0:T(8,128)(2,1)S(1)}, u32[]{:S(2)}, u32[]{:S(2)}) collective-permute-start(bf16[32,512]{1,0:T(8,128)(2,1)S(1)} %get-tuple-element.38), channel_id=1, source_target_pairs={{0,15},{1,2},{2,1},{3,4},{4,3},{5,6},{6,5},{7,8},{8,7},{9,10},{10,... | collective-permute-start | bytes 98312 | tf_op jit(solution)/shard_map/ppermute | solution.py:434
  30.9 5.3 %collective-permute-start.10 = (bf16[32,512]{1,0:T(8,128)(2,1)S(1)}, bf16[32,512]{1,0:T(8,128)(2,1)S(1)}, u32[]{:S(2)}, u32[]{:S(2)}) collective-permute-start(bf16[32,512]{1,0:T(8,128)(2,1)S(1)} %get-tuple-element.39), channel_id=1, source_target_pairs={{0,2},{1,3},{2,0},{3,1},{4,6},{5,7},{6,4},{7,5},{8,10},{9,11},{10,... | collective-permute-start | bytes 98312 | tf_op jit(solution)/shard_map/ppermute | solution.py:434
  32.6 3.6 %collective-permute-start.11 = (bf16[32,512]{1,0:T(8,128)(2,1)S(1)}, bf16[32,512]{1,0:T(8,128)(2,1)S(1)}, u32[]{:S(2)}, u32[]{:S(2)}) collective-permute-start(bf16[32,512]{1,0:T(8,128)(2,1)S(1)} %get-tuple-element.40), channel_id=1, source_target_pairs={{0,1},{1,0},{2,3},{3,2},{4,5},{5,4},{6,7},{7,6},{8,9},{9,8},{10,11... | collective-permute-start | bytes 98312 | tf_op jit(solution)/shard_map/ppermute | solution.py:434

commit v12 on v11

--- a/solution.py
+++ b/solution.py
@@ -10,7 +10,7 @@
 F32 = jnp.float32
 BF16 = jnp.bfloat16
 MIB = 1 << 20
-OWN, ODD, HALF, FAR, EVEN, NEAR = range(6)
+OWN, FAR, HALF, ODD, EVEN, NEAR = range(6)
 SLOTS = 6
 PAD = 128
 AHEAD = 3
@@ -181,15 +181,14 @@
             msum_ref[slot, :, b * block_grid : (b + 1) * block_grid] = sums[:, :block_grid]
             first = (step * blocks + b) * block_grid
             dsum_ref[:, pl.ds(first, block_grid)] = sums[:, block_grid:]
-        for half in range(0, width, 256):
-            part = pl.ds(step * width + half, 256)
-            lat = silu_of_half(
-                jnp.dot(
-                    wt_ref[:, :channels], grid_ref[:, part], preferred_element_type=F32
-                )
-            ).astype(BF16)
+        for at in range(0, width, 256):
+            part = pl.ds(step * width + at, 256)
+            half = jnp.dot(
+                wt_ref[:, :channels], grid_ref[:, part], preferred_element_type=F32
+            )
+            lat = silu_of_half(half.astype(BF16))
             lat_ref[:, part] = lat
-            hold_ref[slot, :, half : half + 256] = lat
+            hold_ref[slot, :, at : at + 256] = lat
 
     collect(1)
     me = lax.axis_index("nodes")
@@ -392,8 +391,8 @@
         for half in range(0, width, 256):
             part = pl.ds(step * width + half, 256)
             decoded = jnp.dot(back_ref[...], dsum_ref[:, part], preferred_element_type=F32)
-            hidden = silu(lat_ref[:, part].astype(F32) + decoded)
-            hold_ref[slot, :, half : half + 256] = hidden.astype(BF16)
+            halved = 0.5 * (lat_ref[:, part].astype(F32) + decoded)
+            hold_ref[slot, :, half : half + 256] = silu_of_half(halved.astype(BF16))
     predict(steps - 1, (steps - 1) % 2)
     copy_out(steps - 1).start()
     for step in range(steps):

time: 41.3 us -> 41.5 us (level)
  Pallas kernels: 15.6 us -> 14.7 us
  starting transfers between devices: 12.8 us -> 13.6 us
    pallas_call x1, Pallas kernels: 5.01 us -> 4.11 us  [decode(): pl.pallas_call(functools.partial(decode_kernel, width), in_specs=[vmem] *...]
    ppermute x12, starting transfers between devices: 12.8 us -> 13.6 us  [swap(): return lax.ppermute(x, 'nodes', pairs)]
  transfers between devices with their start and end apart: 12 -> 12, of which waited for: 4 -> 5; matrix products, arithmetic and copies ran while one was open for 0% -> 0% of each run, Pallas kernels for 3% -> 3%
where the time goes in v12:
time: 41.5 us; the launch traced here: 41.4 us
  Pallas kernels  14.7 us (35%)
  starting transfers between devices  13.6 us (33%)
  waiting for transfers between devices  12.3 us (30%)
  between operations  0.75 us (2%)
    ppermute x12, starting transfers between devices, swap(): return lax.ppermute(x, 'nodes', pairs)  13.6 us
    ppermute x12, waiting for transfers between devices, swap(): return lax.ppermute(x, 'nodes', pairs)  12.3 us
    pallas_call x1, Pallas kernels, encode(): pl.pallas_call(functools.partial(encode_kernel, parts, width), in_specs=[...  7.87 us
    pallas_call x1, Pallas kernels, decode(): pl.pallas_call(functools.partial(decode_kernel, width), in_specs=[vmem] *...  4.11 us
    pallas_call x1, Pallas kernels, process(): pl.pallas_call(process_kernel, in_specs=[vmem] * 8, out_specs=[vmem] * (1...  1.27 us
    pallas_call x1, Pallas kernels, prepare(): pl.pallas_call(functools.partial(prepare_kernel, parts), in_specs=[pl.Blo...  1.11 us
  transfers between devices with their start and end apart: 12, of which 5 were waited for; matrix products, arithmetic and copies ran while one was open for 0% of the time, Pallas kernels for 3%

profile of v12, /device:TPU:0, one launch (start us, length us, event | category | flops | bytes accessed | tf_op | source)
XLA Modules:
  0.0 41.4 jit_solution(15430944976876968868)
XLA Ops:
  0.6 0.0 copy-start.1
  0.6 0.0 copy-start.4
  0.7 0.0 copy-start.3
  0.7 0.0 copy-start.5
  0.7 0.0 copy-start
  0.7 0.0 copy-start.6
  0.7 7.9 %encode.1 = (bf16[512,4096]{1,0:T(8,128)(2,1)S(1)}, bf16[192,4096]{1,0:T(8,128)(2,1)S(1)}, bf16[227,4096]{1,0:T(8,128)(2,1)S(1)}, bf16[32,640]{1,0:T(8,128)(2,1)...) custom-call(s32[16]{0:T(128)} %slot_hbm.1, ...), custom_call_target="tpu_custom_call" | custom-call | tf_op jit(solution)/shard_map/encode/pallas_call | solution.py:213
  8.6 0.0 copy-start.2
  8.6 5.5 %collective-permute-start = (bf16[32,640]{1,0:T(8,128)(2,1)S(1)}, bf16[32,640]{1,0:T(8,128)(2,1)S(1)}, u32[]{:S(2)}, u32[]{:S(2)}) collective-permute-start(bf16[32,640]{1,0:T(8,128)(2,1)S(1)} %get-tuple-element.26), channel_id=1, source_target_pairs={{0,15},{1,2},{2,1},{3,4},{4,3},{5,6},{6,5},{7,8},{8,7},{9,10},{10,... | collective-permute-start | bytes 122888 | tf_op jit(solution)/shard_map/ppermute | solution.py:433
  14.1 0.0 collective-permute-start.1
  14.1 1.0 %collective-permute-start.2 = (bf16[32,640]{1,0:T(8,128)(2,1)S(1)}, bf16[32,640]{1,0:T(8,128)(2,1)S(1)}, u32[]{:S(2)}, u32[]{:S(2)}) collective-permute-start(bf16[32,640]{1,0:T(8,128)(2,1)S(1)} %get-tuple-element.28), channel_id=1, source_target_pairs={{0,14},{1,15},{2,4},{3,5},{4,2},{5,3},{6,8},{7,9},{8,6},{9,7},{10,... | collective-permute-start | bytes 122888 | tf_op jit(solution)/shard_map/ppermute | solution.py:433
  15.1 1.5 %collective-permute-start.3 = (bf16[32,640]{1,0:T(8,128)(2,1)S(1)}, bf16[32,640]{1,0:T(8,128)(2,1)S(1)}, u32[]{:S(2)}, u32[]{:S(2)}) collective-permute-start(bf16[32,640]{1,0:T(8,128)(2,1)S(1)} %get-tuple-element.29), channel_id=1, source_target_pairs={{0,2},{1,3},{2,0},{3,1},{4,6},{5,7},{6,4},{7,5},{8,10},{9,11},{10,... | collective-permute-start | bytes 122888 | tf_op jit(solution)/shard_map/ppermute | solution.py:433
  16.6 0.0 collective-permute-start.4
  16.6 0.0 collective-permute-done.refs_1_
  16.6 2.4 %collective-permute-done.1.refs_2_ = bf16[32,640]{1,0:T(8,128)(2,1)S(1)} collective-permute-done((bf16[32,640]{1,0:T(8,128)(2,1)S(1)}, bf16[32,640]{1,0:T(8,128)(2,1)S(1)}, u32[]{:S(2)}, u32[]{:S(2)}) %collective-permute-start.1) | collective-permute-done | bytes 40992 | tf_op jit(solution)/shard_map/ppermute | solution.py:433
  19.0 1.8 %collective-permute-done.2.refs_3_ = bf16[32,640]{1,0:T(8,128)(2,1)S(1)} collective-permute-done((bf16[32,640]{1,0:T(8,128)(2,1)S(1)}, bf16[32,640]{1,0:T(8,128)(2,1)S(1)}, u32[]{:S(2)}, u32[]{:S(2)}) %collective-permute-start.2) | collective-permute-done | bytes 40992 | tf_op jit(solution)/shard_map/ppermute | solution.py:433
  20.8 0.0 collective-permute-done.3.refs_4_
  20.8 0.0 collective-permute-done.4.refs_5_
  20.8 0.0 copy-done.1
  20.8 0.0 copy-done.4
  20.8 0.3 mesh_update.1
  21.1 1.1 %collective-permute-start.6 = (bf16[128,512]{1,0:T(8,128)(2,1)S(1)}, bf16[128,512]{1,0:T(8,128)(2,1)S(1)}, u32[]{:S(2)}, u32[]{:S(2)}) collective-permute-start(bf16[128,512]{1,0:T(8,128)(2,1)S(1)} %get-tuple-element.32.mid_ref), channel_id=1, source_target_pairs={{0,15},{1,2},{2,1},{3,4},{4,3},{5,6},{6,5},{7,8},{8,7},{9,10},{10,... | collective-permute-start | bytes 393224 | tf_op jit(solution)/shard_map/ppermute | solution.py:433
  22.2 0.0 collective-permute-start.5
  22.2 0.0 copy-done.3
  22.2 0.0 copy-done.5
  22.2 1.1 %prepare.1 = (bf16[128,256]{1,0:T(8,128)(2,1)S(1)}, f32[128,512]{1,0:T(8,128)S(1)}) custom-call(s32[4,6]{1,0:T(4,128)S(1)} %copy-done.5, bf16[4,6,32,32]{3,2,1,0:T(8,128)(2,1)S(1)} %copy-done.3, bf16[128,512]{1,0:T(8,128)(2,1)S(1)} %get-tuple-element.32.mid_ref), custom_call_target="tpu_custom_call" | custom-call | flops 18874368 | bytes 393216 | tf_op jit(solution)/shard_map/prepare/pallas_call | solution.py:280
  23.3 4.9 %collective-permute-done.6.far_mid_ref = bf16[128,512]{1,0:T(8,128)(2,1)S(1)} collective-permute-done((bf16[128,512]{1,0:T(8,128)(2,1)S(1)}, bf16[128,512]{1,0:T(8,128)(2,1)S(1)}, u32[]{:S(2)}, u32[]{:S(2)}) %collective-permute-start.6) | collective-permute-done | bytes 131104 | tf_op jit(solution)/shard_map/ppermute | solution.py:433
  28.3 0.0 collective-permute-done.5.near_mid_ref
  28.3 0.0 copy-done
  28.3 0.0 copy-done.6
  28.3 1.3 %mesh_process.1 = (bf16[128,512]{1,0:T(8,128)(2,1)}, bf16[32,512]{1,0:T(8,128)(2,1)S(1)}, bf16[32,512]{1,0:T(8,128)(2,1)S(1)}, bf16[32,512]{1,0:T(8,128)(2,1)S(1...) custom-call(f32[8,512]{1,0:T(8,128)S(1)} %get-tuple-element.31.ids_ref, ...), custom_call_target="tpu_custom_call" | custom-call | tf_op jit(solution)/shard_map/mesh_process/pallas_call | solution.py:356
  29.6 1.0 %collective-permute-start.7 = (bf16[32,512]{1,0:T(8,128)(2,1)S(1)}, bf16[32,512]{1,0:T(8,128)(2,1)S(1)}, u32[]{:S(2)}, u32[]{:S(2)}) collective-permute-start(bf16[32,512]{1,0:T(8,128)(2,1)S(1)} %get-tuple-element.36), channel_id=1, source_target_pairs={{0,15},{1,2},{2,1},{3,4},{4,3},{5,6},{6,5},{7,8},{8,7},{9,10},{10,... | collective-permute-start | bytes 98312 | tf_op jit(solution)/shard_map/ppermute | solution.py:433
  30.6 0.0 collective-permute-start.8
  30.6 1.7 %collective-permute-start.9 = (bf16[32,512]{1,0:T(8,128)(2,1)S(1)}, bf16[32,512]{1,0:T(8,128)(2,1)S(1)}, u32[]{:S(2)}, u32[]{:S(2)}) collective-permute-start(bf16[32,512]{1,0:T(8,128)(2,1)S(1)} %get-tuple-element.38), channel_id=1, source_target_pairs={{0,14},{1,15},{2,4},{3,5},{4,2},{5,3},{6,8},{7,9},{8,6},{9,7},{10,... | collective-permute-start | bytes 98312 | tf_op jit(solution)/shard_map/ppermute | solution.py:433
  32.3 0.0 collective-permute-start.10
  32.3 1.8 %collective-permute-start.11 = (bf16[32,512]{1,0:T(8,128)(2,1)S(1)}, bf16[32,512]{1,0:T(8,128)(2,1)S(1)}, u32[]{:S(2)}, u32[]{:S(2)}) collective-permute-start(bf16[32,512]{1,0:T(8,128)(2,1)S(1)} %get-tuple-element.40), channel_id=1, source_target_pairs={{0,1},{1,0},{2,3},{3,2},{4,5},{5,4},{6,7},{7,6},{8,9},{9,8},{10,11... | collective-permute-start | bytes 98312 | tf_op jit(solution)/shard_map/ppermute | solution.py:433
  34.1 1.5 %collective-permute-done.7.rest_1_ = bf16[32,512]{1,0:T(8,128)(2,1)S(1)} collective-permute-done((bf16[32,512]{1,0:T(8,128)(2,1)S(1)}, bf16[32,512]{1,0:T(8,128)(2,1)S(1)}, u32[]{:S(2)}, u32[]{:S(2)}) %collective-permute-start.7) | collective-permute-done | bytes 32800 | tf_op jit(solution)/shard_map/ppermute | solution.py:433
  35.6 0.0 collective-permute-done.8.rest_2_
  35.6 1.6 %collective-permute-done.9.rest_3_ = bf16[32,512]{1,0:T(8,128)(2,1)S(1)} collective-permute-done((bf16[32,512]{1,0:T(8,128)(2,1)S(1)}, bf16[32,512]{1,0:T(8,128)(2,1)S(1)}, u32[]{:S(2)}, u32[]{:S(2)}) %collective-permute-start.9) | collective-permute-done | bytes 32800 | tf_op jit(solution)/shard_map/ppermute | solution.py:433
  37.2 0.0 collective-permute-done.10.rest_4_
  37.2 0.0 collective-permute-done.11.rest_5_
  37.2 0.0 copy-done.2
  37.2 4.1 %decode.1 = bf16[227,4096]{1,0:T(8,128)(2,1)} custom-call(bf16[227,4096]{1,0:T(8,128)(2,1)S(1)} %get-tuple-element.22.grid_ref, bf16[512,4096]{1,0:T(8,128)(2,1)S(1)} %get-tuple-element.23.lat_ref, bf16[192,4096]{1,0:T(8,128)(2,1)S(1)} %get-tuple-element.24.dsum_ref, bf16[227,512]{1,0:T(8,128)(2,1)S(1)} %bitcast.6, ...), custom_call_target="tpu_custom_call" | custom-call | tf_op jit(solution)/shard_map/decode/pallas_call | solution.py:408
Async XLA Ops:
  0.6 20.2 %copy-start.1 = (bf16[512,512]{1,0:T(8,128)(2,1)S(1)}, bf16[512,512]{1,0:T(8,128)(2,1)}, u32[]{:S(2)}) copy-start(bf16[512,512]{1,0:T(8,128)(2,1)} %refs_7_.1) | copy-start | bytes 1572868
  0.6 20.2 %copy-start.4 = (bf16[128,512]{1,0:T(8,128)(2,1)S(1)}, bf16[128,512]{1,0:T(8,128)(2,1)}, u32[]{:S(2)}) copy-start(bf16[128,512]{1,0:T(8,128)(2,1)} %refs_6_.1) | copy-start | bytes 393220
  0.7 21.6 %copy-start.3 = (bf16[4,6,32,32]{3,2,1,0:T(8,128)(2,1)S(1)}, bf16[4,6,32,32]{3,2,1,0:T(8,128)(2,1)}, u32[]{:S(2)}) copy-start(bf16[4,6,32,32]{3,2,1,0:T(8,128)(2,1)} %coef_ref.1) | copy-start | bytes 147460
  0.7 21.6 %copy-start.5 = (s32[4,6]{1,0:T(4,128)S(1)}, s32[4,6]{1,0:T(4,128)}, u32[]{:S(2)}) copy-start(s32[4,6]{1,0:T(4,128)} %adj_ref.1) | copy-start | bytes 292
  0.7 27.6 %copy-start = (bf16[512,512]{1,0:T(8,128)(2,1)S(1)}, bf16[512,512]{1,0:T(8,128)(2,1)}, u32[]{:S(2)}) copy-start(bf16[512,512]{1,0:T(8,128)(2,1)} %w_ref.1) | copy-start | bytes 1572868
  0.7 27.6 %copy-start.6 = (f32[512]{0:T(512)S(1)}, f32[512]{0:T(512)}, u32[]{:S(2)}) copy-start(f32[512]{0:T(512)} %param.22) | copy-start | bytes 6148
  8.6 28.7 %copy-start.2 = (bf16[512,227]{0,1:T(8,128)(2,1)S(1)}, bf16[512,227]{0,1:T(8,128)(2,1)}, u32[]{:S(2)}) copy-start(bf16[512,227]{0,1:T(8,128)(2,1)} %param.25) | copy-start | bytes 697348
  8.6 8.0 %collective-permute-start = (bf16[32,640]{1,0:T(8,128)(2,1)S(1)}, bf16[32,640]{1,0:T(8,128)(2,1)S(1)}, u32[]{:S(2)}, u32[]{:S(2)}) collective-permute-start(bf16[32,640]{1,0:T(8,128)(2,1)S(1)} %get-tuple-element.26), channel_id=1, source_target_pairs={{0,15},{1,2},{2,1},{3,4},{4,3},{5,6},{6,5},{7,8},{8,7},{9,10},{10,... | collective-permute-start | bytes 122888 | tf_op jit(solution)/shard_map/ppermute | solution.py:433
  14.1 4.9 %collective-permute-start.1 = (bf16[32,640]{1,0:T(8,128)(2,1)S(1)}, bf16[32,640]{1,0:T(8,128)(2,1)S(1)}, u32[]{:S(2)}, u32[]{:S(2)}) collective-permute-start(bf16[32,640]{1,0:T(8,128)(2,1)S(1)} %get-tuple-element.27), channel_id=1, source_target_pairs={{0,8},{1,9},{2,10},{3,11},{4,12},{5,13},{6,14},{7,15},{8,0},{9,1},... | collective-permute-start | bytes 122888 | tf_op jit(solution)/shard_map/ppermute | solution.py:433
  14.1 6.7 %collective-permute-start.2 = (bf16[32,640]{1,0:T(8,128)(2,1)S(1)}, bf16[32,640]{1,0:T(8,128)(2,1)S(1)}, u32[]{:S(2)}, u32[]{:S(2)}) collective-permute-start(bf16[32,640]{1,0:T(8,128)(2,1)S(1)} %get-tuple-element.28), channel_id=1, source_target_pairs={{0,14},{1,15},{2,4},{3,5},{4,2},{5,3},{6,8},{7,9},{8,6},{9,7},{10,... | collective-permute-start | bytes 122888 | tf_op jit(solution)/shard_map/ppermute | solution.py:433
  15.1 5.7 %collective-permute-start.3 = (bf16[32,640]{1,0:T(8,128)(2,1)S(1)}, bf16[32,640]{1,0:T(8,128)(2,1)S(1)}, u32[]{:S(2)}, u32[]{:S(2)}) collective-permute-start(bf16[32,640]{1,0:T(8,128)(2,1)S(1)} %get-tuple-element.29), channel_id=1, source_target_pairs={{0,2},{1,3},{2,0},{3,1},{4,6},{5,7},{6,4},{7,5},{8,10},{9,11},{10,... | collective-permute-start | bytes 122888 | tf_op jit(solution)/shard_map/ppermute | solution.py:433
  16.6 4.2 %collective-permute-start.4 = (bf16[32,640]{1,0:T(8,128)(2,1)S(1)}, bf16[32,640]{1,0:T(8,128)(2,1)S(1)}, u32[]{:S(2)}, u32[]{:S(2)}) collective-permute-start(bf16[32,640]{1,0:T(8,128)(2,1)S(1)} %get-tuple-element.30), channel_id=1, source_target_pairs={{0,1},{1,0},{2,3},{3,2},{4,5},{5,4},{6,7},{7,6},{8,9},{9,8},{10,11... | collective-permute-start | bytes 122888 | tf_op jit(solution)/shard_map/ppermute | solution.py:433
  21.1 7.2 %collective-permute-start.6 = (bf16[128,512]{1,0:T(8,128)(2,1)S(1)}, bf16[128,512]{1,0:T(8,128)(2,1)S(1)}, u32[]{:S(2)}, u32[]{:S(2)}) collective-permute-start(bf16[128,512]{1,0:T(8,128)(2,1)S(1)} %get-tuple-element.32.mid_ref), channel_id=1, source_target_pairs={{0,15},{1,2},{2,1},{3,4},{4,3},{5,6},{6,5},{7,8},{8,7},{9,10},{10,... | collective-permute-start | bytes 393224 | tf_op jit(solution)/shard_map/ppermute | solution.py:433
  22.2 6.1 %collective-permute-start.5 = (bf16[128,512]{1,0:T(8,128)(2,1)S(1)}, bf16[128,512]{1,0:T(8,128)(2,1)S(1)}, u32[]{:S(2)}, u32[]{:S(2)}) collective-permute-start(bf16[128,512]{1,0:T(8,128)(2,1)S(1)} %get-tuple-element.32.mid_ref), channel_id=1, source_target_pairs={{0,1},{1,0},{2,3},{3,2},{4,5},{5,4},{6,7},{7,6},{8,9},{9,8},{10,11... | collective-permute-start | bytes 393224 | tf_op jit(solution)/shard_map/ppermute | solution.py:433
  29.6 6.0 %collective-permute-start.7 = (bf16[32,512]{1,0:T(8,128)(2,1)S(1)}, bf16[32,512]{1,0:T(8,128)(2,1)S(1)}, u32[]{:S(2)}, u32[]{:S(2)}) collective-permute-start(bf16[32,512]{1,0:T(8,128)(2,1)S(1)} %get-tuple-element.36), channel_id=1, source_target_pairs={{0,15},{1,2},{2,1},{3,4},{4,3},{5,6},{6,5},{7,8},{8,7},{9,10},{10,... | collective-permute-start | bytes 98312 | tf_op jit(solution)/shard_map/ppermute | solution.py:433
  30.6 5.0 %collective-permute-start.8 = (bf16[32,512]{1,0:T(8,128)(2,1)S(1)}, bf16[32,512]{1,0:T(8,128)(2,1)S(1)}, u32[]{:S(2)}, u32[]{:S(2)}) collective-permute-start(bf16[32,512]{1,0:T(8,128)(2,1)S(1)} %get-tuple-element.37), channel_id=1, source_target_pairs={{0,8},{1,9},{2,10},{3,11},{4,12},{5,13},{6,14},{7,15},{8,0},{9,1},... | collective-permute-start | bytes 98312 | tf_op jit(solution)/shard_map/ppermute | solution.py:433
  30.6 6.7 %collective-permute-start.9 = (bf16[32,512]{1,0:T(8,128)(2,1)S(1)}, bf16[32,512]{1,0:T(8,128)(2,1)S(1)}, u32[]{:S(2)}, u32[]{:S(2)}) collective-permute-start(bf16[32,512]{1,0:T(8,128)(2,1)S(1)} %get-tuple-element.38), channel_id=1, source_target_pairs={{0,14},{1,15},{2,4},{3,5},{4,2},{5,3},{6,8},{7,9},{8,6},{9,7},{10,... | collective-permute-start | bytes 98312 | tf_op jit(solution)/shard_map/ppermute | solution.py:433
  32.3 4.9 %collective-permute-start.10 = (bf16[32,512]{1,0:T(8,128)(2,1)S(1)}, bf16[32,512]{1,0:T(8,128)(2,1)S(1)}, u32[]{:S(2)}, u32[]{:S(2)}) collective-permute-start(bf16[32,512]{1,0:T(8,128)(2,1)S(1)} %get-tuple-element.39), channel_id=1, source_target_pairs={{0,2},{1,3},{2,0},{3,1},{4,6},{5,7},{6,4},{7,5},{8,10},{9,11},{10,... | collective-permute-start | bytes 98312 | tf_op jit(solution)/shard_map/ppermute | solution.py:433
  32.3 4.9 %collective-permute-start.11 = (bf16[32,512]{1,0:T(8,128)(2,1)S(1)}, bf16[32,512]{1,0:T(8,128)(2,1)S(1)}, u32[]{:S(2)}, u32[]{:S(2)}) collective-permute-start(bf16[32,512]{1,0:T(8,128)(2,1)S(1)} %get-tuple-element.40), channel_id=1, source_target_pairs={{0,1},{1,0},{2,3},{3,2},{4,5},{5,4},{6,7},{7,6},{8,9},{9,8},{10,11... | collective-permute-start | bytes 98312 | tf_op jit(solution)/shard_map/ppermute | solution.py:433

commit v13 on v11

--- a/solution.py
+++ b/solution.py
@@ -375,7 +375,7 @@
         return pltpu.make_async_copy(pred_ref.at[:, cols], out_hbm.at[:, cols], sems.at[step])
 
     joined = jnp.concatenate([slot[...] for slot in slots], axis=0)
-    back_ref[...] = joined.T
+    back_ref[...] = (BF16(0.5) * joined).T
 
     def predict(step, slot):
         cols = pl.ds(step * width, width)
@@ -392,8 +392,8 @@
         for half in range(0, width, 256):
             part = pl.ds(step * width + half, 256)
             decoded = jnp.dot(back_ref[...], dsum_ref[:, part], preferred_element_type=F32)
-            hidden = silu(lat_ref[:, part].astype(F32) + decoded)
-            hold_ref[slot, :, half : half + 256] = hidden.astype(BF16)
+            halved = BF16(0.5) * lat_ref[:, part] + decoded.astype(BF16)
+            hold_ref[slot, :, half : half + 256] = silu_of_half(halved)
     predict(steps - 1, (steps - 1) % 2)
     copy_out(steps - 1).start()
     for step in range(steps):

time: 41.3 us -> 40.1 us (0.971)
  Pallas kernels: 15.6 us -> 14.4 us
    pallas_call x1, Pallas kernels: 5.01 us -> 3.81 us  [decode(): pl.pallas_call(functools.partial(decode_kernel, width), in_specs=[vmem] *...]
where the time goes in v13:
time: 40.1 us; the launch traced here: 40 us
  Pallas kernels  14.4 us (36%)
  starting transfers between devices  12.8 us (32%)
  waiting for transfers between devices  12 us (30%)
  between operations  0.76 us (2%)
    ppermute x12, starting transfers between devices, swap(): return lax.ppermute(x, 'nodes', pairs)  12.8 us
    ppermute x12, waiting for transfers between devices, swap(): return lax.ppermute(x, 'nodes', pairs)  12 us
    pallas_call x1, Pallas kernels, encode(): pl.pallas_call(functools.partial(encode_kernel, parts, width), in_specs=[...  7.86 us
    pallas_call x1, Pallas kernels, decode(): pl.pallas_call(functools.partial(decode_kernel, width), in_specs=[vmem] *...  3.81 us
    pallas_call x1, Pallas kernels, process(): pl.pallas_call(process_kernel, in_specs=[vmem] * 8, out_specs=[vmem] * (1...  1.27 us
    pallas_call x1, Pallas kernels, prepare(): pl.pallas_call(functools.partial(prepare_kernel, parts), in_specs=[pl.Blo...  1.11 us
  transfers between devices with their start and end apart: 12, of which 4 were waited for; matrix products, arithmetic and copies ran while one was open for 0% of the time, Pallas kernels for 3%

profile of v13, /device:TPU:0, one launch (start us, length us, event | category | flops | bytes accessed | tf_op | source)
XLA Modules:
  0.0 40.0 jit_solution(9481512763815352992)
XLA Ops:
  0.6 0.0 copy-start.1
  0.6 0.0 copy-start.4
  0.7 0.0 copy-start.3
  0.7 0.0 copy-start.5
  0.7 0.0 copy-start
  0.7 0.0 copy-start.6
  0.7 7.9 %encode.1 = (bf16[512,4096]{1,0:T(8,128)(2,1)S(1)}, bf16[192,4096]{1,0:T(8,128)(2,1)S(1)}, bf16[227,4096]{1,0:T(8,128)(2,1)S(1)}, bf16[32,640]{1,0:T(8,128)(2,1)...) custom-call(s32[16]{0:T(128)} %slot_hbm.1, ...), custom_call_target="tpu_custom_call" | custom-call | tf_op jit(solution)/shard_map/encode/pallas_call | solution.py:214
  8.6 0.0 copy-start.2
  8.6 6.1 %collective-permute-start = (bf16[32,640]{1,0:T(8,128)(2,1)S(1)}, bf16[32,640]{1,0:T(8,128)(2,1)S(1)}, u32[]{:S(2)}, u32[]{:S(2)}) collective-permute-start(bf16[32,640]{1,0:T(8,128)(2,1)S(1)} %get-tuple-element.26), channel_id=1, source_target_pairs={{0,14},{1,15},{2,4},{3,5},{4,2},{5,3},{6,8},{7,9},{8,6},{9,7},{10,... | collective-permute-start | bytes 122888 | tf_op jit(solution)/shard_map/ppermute | solution.py:434
  14.6 0.0 collective-permute-start.1
  14.7 0.7 %collective-permute-start.2 = (bf16[32,640]{1,0:T(8,128)(2,1)S(1)}, bf16[32,640]{1,0:T(8,128)(2,1)S(1)}, u32[]{:S(2)}, u32[]{:S(2)}) collective-permute-start(bf16[32,640]{1,0:T(8,128)(2,1)S(1)} %get-tuple-element.28), channel_id=1, source_target_pairs={{0,15},{1,2},{2,1},{3,4},{4,3},{5,6},{6,5},{7,8},{8,7},{9,10},{10,... | collective-permute-start | bytes 122888 | tf_op jit(solution)/shard_map/ppermute | solution.py:434
  15.4 0.5 %collective-permute-start.3 = (bf16[32,640]{1,0:T(8,128)(2,1)S(1)}, bf16[32,640]{1,0:T(8,128)(2,1)S(1)}, u32[]{:S(2)}, u32[]{:S(2)}) collective-permute-start(bf16[32,640]{1,0:T(8,128)(2,1)S(1)} %get-tuple-element.29), channel_id=1, source_target_pairs={{0,2},{1,3},{2,0},{3,1},{4,6},{5,7},{6,4},{7,5},{8,10},{9,11},{10,... | collective-permute-start | bytes 122888 | tf_op jit(solution)/shard_map/ppermute | solution.py:434
  15.8 1.1 %collective-permute-start.4 = (bf16[32,640]{1,0:T(8,128)(2,1)S(1)}, bf16[32,640]{1,0:T(8,128)(2,1)S(1)}, u32[]{:S(2)}, u32[]{:S(2)}) collective-permute-start(bf16[32,640]{1,0:T(8,128)(2,1)S(1)} %get-tuple-element.30), channel_id=1, source_target_pairs={{0,1},{1,0},{2,3},{3,2},{4,5},{5,4},{6,7},{7,6},{8,9},{9,8},{10,11... | collective-permute-start | bytes 122888 | tf_op jit(solution)/shard_map/ppermute | solution.py:434
  17.0 0.0 collective-permute-done.refs_1_
  17.0 2.6 %collective-permute-done.1.refs_2_ = bf16[32,640]{1,0:T(8,128)(2,1)S(1)} collective-permute-done((bf16[32,640]{1,0:T(8,128)(2,1)S(1)}, bf16[32,640]{1,0:T(8,128)(2,1)S(1)}, u32[]{:S(2)}, u32[]{:S(2)}) %collective-permute-start.1) | collective-permute-done | bytes 40992 | tf_op jit(solution)/shard_map/ppermute | solution.py:434
  19.6 1.2 %collective-permute-done.2.refs_3_ = bf16[32,640]{1,0:T(8,128)(2,1)S(1)} collective-permute-done((bf16[32,640]{1,0:T(8,128)(2,1)S(1)}, bf16[32,640]{1,0:T(8,128)(2,1)S(1)}, u32[]{:S(2)}, u32[]{:S(2)}) %collective-permute-start.2) | collective-permute-done | bytes 40992 | tf_op jit(solution)/shard_map/ppermute | solution.py:434
  20.8 0.0 collective-permute-done.3.refs_4_
  20.8 0.0 collective-permute-done.4.refs_5_
  20.8 0.0 copy-done.1
  20.8 0.0 copy-done.4
  20.8 0.3 mesh_update.1
  21.1 1.4 %collective-permute-start.6 = (bf16[128,512]{1,0:T(8,128)(2,1)S(1)}, bf16[128,512]{1,0:T(8,128)(2,1)S(1)}, u32[]{:S(2)}, u32[]{:S(2)}) collective-permute-start(bf16[128,512]{1,0:T(8,128)(2,1)S(1)} %get-tuple-element.32.mid_ref), channel_id=1, source_target_pairs={{0,15},{1,2},{2,1},{3,4},{4,3},{5,6},{6,5},{7,8},{8,7},{9,10},{10,... | collective-permute-start | bytes 393224 | tf_op jit(solution)/shard_map/ppermute | solution.py:434
  22.5 0.0 collective-permute-start.5
  22.5 0.0 copy-done.3
  22.5 0.0 copy-done.5
  22.5 1.1 %prepare.1 = (bf16[128,256]{1,0:T(8,128)(2,1)S(1)}, f32[128,512]{1,0:T(8,128)S(1)}) custom-call(s32[4,6]{1,0:T(4,128)S(1)} %copy-done.5, bf16[4,6,32,32]{3,2,1,0:T(8,128)(2,1)S(1)} %copy-done.3, bf16[128,512]{1,0:T(8,128)(2,1)S(1)} %get-tuple-element.32.mid_ref), custom_call_target="tpu_custom_call" | custom-call | flops 18874368 | bytes 393216 | tf_op jit(solution)/shard_map/prepare/pallas_call | solution.py:281
  23.6 4.6 %collective-permute-done.6.far_mid_ref = bf16[128,512]{1,0:T(8,128)(2,1)S(1)} collective-permute-done((bf16[128,512]{1,0:T(8,128)(2,1)S(1)}, bf16[128,512]{1,0:T(8,128)(2,1)S(1)}, u32[]{:S(2)}, u32[]{:S(2)}) %collective-permute-start.6) | collective-permute-done | bytes 131104 | tf_op jit(solution)/shard_map/ppermute | solution.py:434
  28.3 0.0 collective-permute-done.5.near_mid_ref
  28.3 0.0 copy-done
  28.3 0.0 copy-done.6
  28.3 1.3 %mesh_process.1 = (bf16[128,512]{1,0:T(8,128)(2,1)}, bf16[32,512]{1,0:T(8,128)(2,1)S(1)}, bf16[32,512]{1,0:T(8,128)(2,1)S(1)}, bf16[32,512]{1,0:T(8,128)(2,1)S(1...) custom-call(f32[8,512]{1,0:T(8,128)S(1)} %get-tuple-element.31.ids_ref, ...), custom_call_target="tpu_custom_call" | custom-call | tf_op jit(solution)/shard_map/mesh_process/pallas_call | solution.py:357
  29.5 0.0 collective-permute-start.7
  29.5 0.0 collective-permute-start.8
  29.6 1.3 %collective-permute-start.9 = (bf16[32,512]{1,0:T(8,128)(2,1)S(1)}, bf16[32,512]{1,0:T(8,128)(2,1)S(1)}, u32[]{:S(2)}, u32[]{:S(2)}) collective-permute-start(bf16[32,512]{1,0:T(8,128)(2,1)S(1)} %get-tuple-element.38), channel_id=1, source_target_pairs={{0,15},{1,2},{2,1},{3,4},{4,3},{5,6},{6,5},{7,8},{8,7},{9,10},{10,... | collective-permute-start | bytes 98312 | tf_op jit(solution)/shard_map/ppermute | solution.py:434
  30.9 1.7 %collective-permute-start.10 = (bf16[32,512]{1,0:T(8,128)(2,1)S(1)}, bf16[32,512]{1,0:T(8,128)(2,1)S(1)}, u32[]{:S(2)}, u32[]{:S(2)}) collective-permute-start(bf16[32,512]{1,0:T(8,128)(2,1)S(1)} %get-tuple-element.39), channel_id=1, source_target_pairs={{0,2},{1,3},{2,0},{3,1},{4,6},{5,7},{6,4},{7,5},{8,10},{9,11},{10,... | collective-permute-start | bytes 98312 | tf_op jit(solution)/shard_map/ppermute | solution.py:434
  32.6 0.0 collective-permute-start.11
  32.6 3.5 %collective-permute-done.7.rest_1_ = bf16[32,512]{1,0:T(8,128)(2,1)S(1)} collective-permute-done((bf16[32,512]{1,0:T(8,128)(2,1)S(1)}, bf16[32,512]{1,0:T(8,128)(2,1)S(1)}, u32[]{:S(2)}, u32[]{:S(2)}) %collective-permute-start.7) | collective-permute-done | bytes 32800 | tf_op jit(solution)/shard_map/ppermute | solution.py:434
  36.2 0.0 collective-permute-done.8.rest_2_
  36.2 0.0 collective-permute-done.9.rest_3_
  36.2 0.0 collective-permute-done.10.rest_4_
  36.2 0.0 collective-permute-done.11.rest_5_
  36.2 0.0 copy-done.2
  36.2 3.8 %decode.1 = bf16[227,4096]{1,0:T(8,128)(2,1)} custom-call(bf16[227,4096]{1,0:T(8,128)(2,1)S(1)} %get-tuple-element.22.grid_ref, bf16[512,4096]{1,0:T(8,128)(2,1)S(1)} %get-tuple-element.23.lat_ref, bf16[192,4096]{1,0:T(8,128)(2,1)S(1)} %get-tuple-element.24.dsum_ref, bf16[227,512]{1,0:T(8,128)(2,1)S(1)} %bitcast.6, ...), custom_call_target="tpu_custom_call" | custom-call | tf_op jit(solution)/shard_map/decode/pallas_call | solution.py:409
Async XLA Ops:
  0.6 20.2 %copy-start.1 = (bf16[512,512]{1,0:T(8,128)(2,1)S(1)}, bf16[512,512]{1,0:T(8,128)(2,1)}, u32[]{:S(2)}) copy-start(bf16[512,512]{1,0:T(8,128)(2,1)} %refs_7_.1) | copy-start | bytes 1572868
  0.6 20.1 %copy-start.4 = (bf16[128,512]{1,0:T(8,128)(2,1)S(1)}, bf16[128,512]{1,0:T(8,128)(2,1)}, u32[]{:S(2)}) copy-start(bf16[128,512]{1,0:T(8,128)(2,1)} %refs_6_.1) | copy-start | bytes 393220
  0.7 21.8 %copy-start.3 = (bf16[4,6,32,32]{3,2,1,0:T(8,128)(2,1)S(1)}, bf16[4,6,32,32]{3,2,1,0:T(8,128)(2,1)}, u32[]{:S(2)}) copy-start(bf16[4,6,32,32]{3,2,1,0:T(8,128)(2,1)} %coef_ref.1) | copy-start | bytes 147460
  0.7 21.8 %copy-start.5 = (s32[4,6]{1,0:T(4,128)S(1)}, s32[4,6]{1,0:T(4,128)}, u32[]{:S(2)}) copy-start(s32[4,6]{1,0:T(4,128)} %adj_ref.1) | copy-start | bytes 292
  0.7 27.6 %copy-start = (bf16[512,512]{1,0:T(8,128)(2,1)S(1)}, bf16[512,512]{1,0:T(8,128)(2,1)}, u32[]{:S(2)}) copy-start(bf16[512,512]{1,0:T(8,128)(2,1)} %w_ref.1) | copy-start | bytes 1572868
  0.7 27.6 %copy-start.6 = (f32[512]{0:T(512)S(1)}, f32[512]{0:T(512)}, u32[]{:S(2)}) copy-start(f32[512]{0:T(512)} %param.22) | copy-start | bytes 6148
  8.6 27.6 %copy-start.2 = (bf16[512,227]{0,1:T(8,128)(2,1)S(1)}, bf16[512,227]{0,1:T(8,128)(2,1)}, u32[]{:S(2)}) copy-start(bf16[512,227]{0,1:T(8,128)(2,1)} %param.25) | copy-start | bytes 697348
  8.6 8.4 %collective-permute-start = (bf16[32,640]{1,0:T(8,128)(2,1)S(1)}, bf16[32,640]{1,0:T(8,128)(2,1)S(1)}, u32[]{:S(2)}, u32[]{:S(2)}) collective-permute-start(bf16[32,640]{1,0:T(8,128)(2,1)S(1)} %get-tuple-element.26), channel_id=1, source_target_pairs={{0,14},{1,15},{2,4},{3,5},{4,2},{5,3},{6,8},{7,9},{8,6},{9,7},{10,... | collective-permute-start | bytes 122888 | tf_op jit(solution)/shard_map/ppermute | solution.py:434
  14.6 4.9 %collective-permute-start.1 = (bf16[32,640]{1,0:T(8,128)(2,1)S(1)}, bf16[32,640]{1,0:T(8,128)(2,1)S(1)}, u32[]{:S(2)}, u32[]{:S(2)}) collective-permute-start(bf16[32,640]{1,0:T(8,128)(2,1)S(1)} %get-tuple-element.27), channel_id=1, source_target_pairs={{0,8},{1,9},{2,10},{3,11},{4,12},{5,13},{6,14},{7,15},{8,0},{9,1},... | collective-permute-start | bytes 122888 | tf_op jit(solution)/shard_map/ppermute | solution.py:434
  14.7 6.1 %collective-permute-start.2 = (bf16[32,640]{1,0:T(8,128)(2,1)S(1)}, bf16[32,640]{1,0:T(8,128)(2,1)S(1)}, u32[]{:S(2)}, u32[]{:S(2)}) collective-permute-start(bf16[32,640]{1,0:T(8,128)(2,1)S(1)} %get-tuple-element.28), channel_id=1, source_target_pairs={{0,15},{1,2},{2,1},{3,4},{4,3},{5,6},{6,5},{7,8},{8,7},{9,10},{10,... | collective-permute-start | bytes 122888 | tf_op jit(solution)/shard_map/ppermute | solution.py:434
  15.4 5.4 %collective-permute-start.3 = (bf16[32,640]{1,0:T(8,128)(2,1)S(1)}, bf16[32,640]{1,0:T(8,128)(2,1)S(1)}, u32[]{:S(2)}, u32[]{:S(2)}) collective-permute-start(bf16[32,640]{1,0:T(8,128)(2,1)S(1)} %get-tuple-element.29), channel_id=1, source_target_pairs={{0,2},{1,3},{2,0},{3,1},{4,6},{5,7},{6,4},{7,5},{8,10},{9,11},{10,... | collective-permute-start | bytes 122888 | tf_op jit(solution)/shard_map/ppermute | solution.py:434
  15.8 4.9 %collective-permute-start.4 = (bf16[32,640]{1,0:T(8,128)(2,1)S(1)}, bf16[32,640]{1,0:T(8,128)(2,1)S(1)}, u32[]{:S(2)}, u32[]{:S(2)}) collective-permute-start(bf16[32,640]{1,0:T(8,128)(2,1)S(1)} %get-tuple-element.30), channel_id=1, source_target_pairs={{0,1},{1,0},{2,3},{3,2},{4,5},{5,4},{6,7},{7,6},{8,9},{9,8},{10,11... | collective-permute-start | bytes 122888 | tf_op jit(solution)/shard_map/ppermute | solution.py:434
  21.1 7.2 %collective-permute-start.6 = (bf16[128,512]{1,0:T(8,128)(2,1)S(1)}, bf16[128,512]{1,0:T(8,128)(2,1)S(1)}, u32[]{:S(2)}, u32[]{:S(2)}) collective-permute-start(bf16[128,512]{1,0:T(8,128)(2,1)S(1)} %get-tuple-element.32.mid_ref), channel_id=1, source_target_pairs={{0,15},{1,2},{2,1},{3,4},{4,3},{5,6},{6,5},{7,8},{8,7},{9,10},{10,... | collective-permute-start | bytes 393224 | tf_op jit(solution)/shard_map/ppermute | solution.py:434
  22.5 5.8 %collective-permute-start.5 = (bf16[128,512]{1,0:T(8,128)(2,1)S(1)}, bf16[128,512]{1,0:T(8,128)(2,1)S(1)}, u32[]{:S(2)}, u32[]{:S(2)}) collective-permute-start(bf16[128,512]{1,0:T(8,128)(2,1)S(1)} %get-tuple-element.32.mid_ref), channel_id=1, source_target_pairs={{0,1},{1,0},{2,3},{3,2},{4,5},{5,4},{6,7},{7,6},{8,9},{9,8},{10,11... | collective-permute-start | bytes 393224 | tf_op jit(solution)/shard_map/ppermute | solution.py:434
  29.5 6.6 %collective-permute-start.7 = (bf16[32,512]{1,0:T(8,128)(2,1)S(1)}, bf16[32,512]{1,0:T(8,128)(2,1)S(1)}, u32[]{:S(2)}, u32[]{:S(2)}) collective-permute-start(bf16[32,512]{1,0:T(8,128)(2,1)S(1)} %get-tuple-element.36), channel_id=1, source_target_pairs={{0,14},{1,15},{2,4},{3,5},{4,2},{5,3},{6,8},{7,9},{8,6},{9,7},{10,... | collective-permute-start | bytes 98312 | tf_op jit(solution)/shard_map/ppermute | solution.py:434
  29.5 6.6 %collective-permute-start.8 = (bf16[32,512]{1,0:T(8,128)(2,1)S(1)}, bf16[32,512]{1,0:T(8,128)(2,1)S(1)}, u32[]{:S(2)}, u32[]{:S(2)}) collective-permute-start(bf16[32,512]{1,0:T(8,128)(2,1)S(1)} %get-tuple-element.37), channel_id=1, source_target_pairs={{0,8},{1,9},{2,10},{3,11},{4,12},{5,13},{6,14},{7,15},{8,0},{9,1},... | collective-permute-start | bytes 98312 | tf_op jit(solution)/shard_map/ppermute | solution.py:434
  29.6 6.6 %collective-permute-start.9 = (bf16[32,512]{1,0:T(8,128)(2,1)S(1)}, bf16[32,512]{1,0:T(8,128)(2,1)S(1)}, u32[]{:S(2)}, u32[]{:S(2)}) collective-permute-start(bf16[32,512]{1,0:T(8,128)(2,1)S(1)} %get-tuple-element.38), channel_id=1, source_target_pairs={{0,15},{1,2},{2,1},{3,4},{4,3},{5,6},{6,5},{7,8},{8,7},{9,10},{10,... | collective-permute-start | bytes 98312 | tf_op jit(solution)/shard_map/ppermute | solution.py:434
  30.9 5.3 %collective-permute-start.10 = (bf16[32,512]{1,0:T(8,128)(2,1)S(1)}, bf16[32,512]{1,0:T(8,128)(2,1)S(1)}, u32[]{:S(2)}, u32[]{:S(2)}) collective-permute-start(bf16[32,512]{1,0:T(8,128)(2,1)S(1)} %get-tuple-element.39), channel_id=1, source_target_pairs={{0,2},{1,3},{2,0},{3,1},{4,6},{5,7},{6,4},{7,5},{8,10},{9,11},{10,... | collective-permute-start | bytes 98312 | tf_op jit(solution)/shard_map/ppermute | solution.py:434
  32.6 3.6 %collective-permute-start.11 = (bf16[32,512]{1,0:T(8,128)(2,1)S(1)}, bf16[32,512]{1,0:T(8,128)(2,1)S(1)}, u32[]{:S(2)}, u32[]{:S(2)}) collective-permute-start(bf16[32,512]{1,0:T(8,128)(2,1)S(1)} %get-tuple-element.40), channel_id=1, source_target_pairs={{0,1},{1,0},{2,3},{3,2},{4,5},{5,4},{6,7},{7,6},{8,9},{9,8},{10,11... | collective-permute-start | bytes 98312 | tf_op jit(solution)/shard_map/ppermute | solution.py:434

commit v14 on v13

--- a/solution.py
+++ b/solution.py
@@ -109,7 +109,7 @@
     send_refs = rest[:SLOTS]
     (
         slot_ref, owner_ref, w_ref, enc_ref, dec_ref, wt_ref, tgt_ref, ids_ref, msum_ref,
-        hold_ref, acc_ref, spread_ref, small_sems, sems,
+        acc_ref, spread_ref, small_sems, sems,
     ) = rest[SLOTS:]
     tiles, block_mesh, block_grid = enc_ref.shape
     channels, points = grid_ref.shape
@@ -154,9 +154,10 @@
     wt_ref[:, :channels] = (0.5 * w_ref[...].astype(F32)).T.astype(BF16)
     fill_targets(parts, per_block, block_mesh, spread_ref, owner_ref, tgt_ref)
 
-    def collect(slot):
+    def collect(step):
+        lat = lat_ref[:, step * width : (step + 1) * width]
         acc_ref[...] += lax.dot_general(
-            hold_ref[slot], msum_ref[slot], (((1,), (1,)), ((), ())), preferred_element_type=F32
+            msum_ref[step % 2], lat, (((1,), (1,)), ((), ())), preferred_element_type=F32
         )
 
     for step in range(steps):
@@ -166,7 +167,7 @@
         for copy in copies(step):
             copy.wait()
         if step > 0:
-            collect(1 - slot)
+            collect(step - 1)
         for b in range(blocks):
             hot = hot_rows(ids_ref[...], tgt_ref[pl.ds(step * blocks + b, 1), :])
             some = pl.ds(step * chunk + b * per_block, per_block)
@@ -189,13 +190,12 @@
                 )
             ).astype(BF16)
             lat_ref[:, part] = lat
-            hold_ref[slot, :, half : half + 256] = lat
-
-    collect(1)
+
+    collect(steps - 1)
     me = lax.axis_index("nodes")
-    flipped = acc_ref[...].astype(BF16).T
+    summed = acc_ref[...].astype(BF16)
     for s in range(SLOTS):
-        send_refs[s][:, :latent] = flipped[s * block_mesh : (s + 1) * block_mesh, :]
+        send_refs[s][:, :latent] = summed[s * block_mesh : (s + 1) * block_mesh, :]
         block = slot_ref[scalar_partner(s, me, parts)].astype(F32)
         send_refs[s][:, latent:] = jnp.full((block_mesh, PAD), block, F32).astype(BF16)
 
@@ -231,8 +231,7 @@
             pltpu.VMEM((grid_blocks, wide), F32),
             pltpu.VMEM((rows, 128), BF16),
             pltpu.VMEM((2, rows, width), BF16),
-            pltpu.VMEM((2, latent, width), BF16),
-            pltpu.VMEM((latent, rows), F32),
+            pltpu.VMEM((rows, latent), F32),
             pltpu.VMEM((*owners.shape, wide), BF16),
             pltpu.SemaphoreType.DMA((3,)),
             pltpu.SemaphoreType.DMA((3, steps)),

time: 40.1 us -> 40.1 us (level)
  no operation moved by 1% of the time
where the time goes in v14:
time: 40.1 us; the launch traced here: 39.9 us
  Pallas kernels  14.3 us (36%)
  starting transfers between devices  12.8 us (32%)
  waiting for transfers between devices  12 us (30%)
  between operations  0.76 us (2%)
    ppermute x12, starting transfers between devices, swap(): return lax.ppermute(x, 'nodes', pairs)  12.8 us
    ppermute x12, waiting for transfers between devices, swap(): return lax.ppermute(x, 'nodes', pairs)  12 us
    pallas_call x1, Pallas kernels, encode(): pl.pallas_call(functools.partial(encode_kernel, parts, width), in_specs=[...  7.79 us
    pallas_call x1, Pallas kernels, decode(): pl.pallas_call(functools.partial(decode_kernel, width), in_specs=[vmem] *...  3.82 us
    pallas_call x1, Pallas kernels, process(): pl.pallas_call(process_kernel, in_specs=[vmem] * 8, out_specs=[vmem] * (1...  1.27 us
    pallas_call x1, Pallas kernels, prepare(): pl.pallas_call(functools.partial(prepare_kernel, parts), in_specs=[pl.Blo...  1.11 us
  transfers between devices with their start and end apart: 12, of which 4 were waited for; matrix products, arithmetic and copies ran while one was open for 0% of the time, Pallas kernels for 3%

profile of v14, /device:TPU:0, one launch (start us, length us, event | category | flops | bytes accessed | tf_op | source)
XLA Modules:
  0.0 39.9 jit_solution(16082972604103680689)
XLA Ops:
  0.6 0.0 copy-start.1
  0.6 0.0 copy-start.4
  0.7 0.0 copy-start.3
  0.7 0.0 copy-start.5
  0.7 0.0 copy-start
  0.7 0.0 copy-start.6
  0.7 7.8 %encode.1 = (bf16[512,4096]{1,0:T(8,128)(2,1)S(1)}, bf16[192,4096]{1,0:T(8,128)(2,1)S(1)}, bf16[227,4096]{1,0:T(8,128)(2,1)S(1)}, bf16[32,640]{1,0:T(8,128)(2,1)...) custom-call(s32[16]{0:T(128)} %slot_hbm.1, ...), custom_call_target="tpu_custom_call" | custom-call | tf_op jit(solution)/shard_map/encode/pallas_call | solution.py:214
  8.5 0.0 copy-start.2
  8.5 6.1 %collective-permute-start = (bf16[32,640]{1,0:T(8,128)(2,1)S(1)}, bf16[32,640]{1,0:T(8,128)(2,1)S(1)}, u32[]{:S(2)}, u32[]{:S(2)}) collective-permute-start(bf16[32,640]{1,0:T(8,128)(2,1)S(1)} %get-tuple-element.26), channel_id=1, source_target_pairs={{0,14},{1,15},{2,4},{3,5},{4,2},{5,3},{6,8},{7,9},{8,6},{9,7},{10,... | collective-permute-start | bytes 122888 | tf_op jit(solution)/shard_map/ppermute | solution.py:433
  14.6 0.0 collective-permute-start.1
  14.6 0.7 %collective-permute-start.2 = (bf16[32,640]{1,0:T(8,128)(2,1)S(1)}, bf16[32,640]{1,0:T(8,128)(2,1)S(1)}, u32[]{:S(2)}, u32[]{:S(2)}) collective-permute-start(bf16[32,640]{1,0:T(8,128)(2,1)S(1)} %get-tuple-element.28), channel_id=1, source_target_pairs={{0,15},{1,2},{2,1},{3,4},{4,3},{5,6},{6,5},{7,8},{8,7},{9,10},{10,... | collective-permute-start | bytes 122888 | tf_op jit(solution)/shard_map/ppermute | solution.py:433
  15.3 0.5 %collective-permute-start.3 = (bf16[32,640]{1,0:T(8,128)(2,1)S(1)}, bf16[32,640]{1,0:T(8,128)(2,1)S(1)}, u32[]{:S(2)}, u32[]{:S(2)}) collective-permute-start(bf16[32,640]{1,0:T(8,128)(2,1)S(1)} %get-tuple-element.29), channel_id=1, source_target_pairs={{0,2},{1,3},{2,0},{3,1},{4,6},{5,7},{6,4},{7,5},{8,10},{9,11},{10,... | collective-permute-start | bytes 122888 | tf_op jit(solution)/shard_map/ppermute | solution.py:433
  15.8 1.1 %collective-permute-start.4 = (bf16[32,640]{1,0:T(8,128)(2,1)S(1)}, bf16[32,640]{1,0:T(8,128)(2,1)S(1)}, u32[]{:S(2)}, u32[]{:S(2)}) collective-permute-start(bf16[32,640]{1,0:T(8,128)(2,1)S(1)} %get-tuple-element.30), channel_id=1, source_target_pairs={{0,1},{1,0},{2,3},{3,2},{4,5},{5,4},{6,7},{7,6},{8,9},{9,8},{10,11... | collective-permute-start | bytes 122888 | tf_op jit(solution)/shard_map/ppermute | solution.py:433
  16.9 0.0 collective-permute-done.refs_1_
  16.9 2.6 %collective-permute-done.1.refs_2_ = bf16[32,640]{1,0:T(8,128)(2,1)S(1)} collective-permute-done((bf16[32,640]{1,0:T(8,128)(2,1)S(1)}, bf16[32,640]{1,0:T(8,128)(2,1)S(1)}, u32[]{:S(2)}, u32[]{:S(2)}) %collective-permute-start.1) | collective-permute-done | bytes 40992 | tf_op jit(solution)/shard_map/ppermute | solution.py:433
  19.5 1.2 %collective-permute-done.2.refs_3_ = bf16[32,640]{1,0:T(8,128)(2,1)S(1)} collective-permute-done((bf16[32,640]{1,0:T(8,128)(2,1)S(1)}, bf16[32,640]{1,0:T(8,128)(2,1)S(1)}, u32[]{:S(2)}, u32[]{:S(2)}) %collective-permute-start.2) | collective-permute-done | bytes 40992 | tf_op jit(solution)/shard_map/ppermute | solution.py:433
  20.7 0.0 collective-permute-done.3.refs_4_
  20.7 0.0 collective-permute-done.4.refs_5_
  20.7 0.0 copy-done.1
  20.7 0.0 copy-done.4
  20.7 0.3 mesh_update.1
  21.0 1.4 %collective-permute-start.6 = (bf16[128,512]{1,0:T(8,128)(2,1)S(1)}, bf16[128,512]{1,0:T(8,128)(2,1)S(1)}, u32[]{:S(2)}, u32[]{:S(2)}) collective-permute-start(bf16[128,512]{1,0:T(8,128)(2,1)S(1)} %get-tuple-element.32.mid_ref), channel_id=1, source_target_pairs={{0,15},{1,2},{2,1},{3,4},{4,3},{5,6},{6,5},{7,8},{8,7},{9,10},{10,... | collective-permute-start | bytes 393224 | tf_op jit(solution)/shard_map/ppermute | solution.py:433
  22.4 0.0 collective-permute-start.5
  22.4 0.0 copy-done.3
  22.4 0.0 copy-done.5
  22.4 1.1 %prepare.1 = (bf16[128,256]{1,0:T(8,128)(2,1)S(1)}, f32[128,512]{1,0:T(8,128)S(1)}) custom-call(s32[4,6]{1,0:T(4,128)S(1)} %copy-done.5, bf16[4,6,32,32]{3,2,1,0:T(8,128)(2,1)S(1)} %copy-done.3, bf16[128,512]{1,0:T(8,128)(2,1)S(1)} %get-tuple-element.32.mid_ref), custom_call_target="tpu_custom_call" | custom-call | flops 18874368 | bytes 393216 | tf_op jit(solution)/shard_map/prepare/pallas_call | solution.py:280
  23.5 4.7 %collective-permute-done.6.far_mid_ref = bf16[128,512]{1,0:T(8,128)(2,1)S(1)} collective-permute-done((bf16[128,512]{1,0:T(8,128)(2,1)S(1)}, bf16[128,512]{1,0:T(8,128)(2,1)S(1)}, u32[]{:S(2)}, u32[]{:S(2)}) %collective-permute-start.6) | collective-permute-done | bytes 131104 | tf_op jit(solution)/shard_map/ppermute | solution.py:433
  28.2 0.0 collective-permute-done.5.near_mid_ref
  28.2 0.0 copy-done
  28.2 0.0 copy-done.6
  28.2 1.3 %mesh_process.1 = (bf16[128,512]{1,0:T(8,128)(2,1)}, bf16[32,512]{1,0:T(8,128)(2,1)S(1)}, bf16[32,512]{1,0:T(8,128)(2,1)S(1)}, bf16[32,512]{1,0:T(8,128)(2,1)S(1...) custom-call(f32[8,512]{1,0:T(8,128)S(1)} %get-tuple-element.31.ids_ref, ...), custom_call_target="tpu_custom_call" | custom-call | tf_op jit(solution)/shard_map/mesh_process/pallas_call | solution.py:356
  29.5 0.0 collective-permute-start.7
  29.5 0.0 collective-permute-start.8
  29.5 1.3 %collective-permute-start.9 = (bf16[32,512]{1,0:T(8,128)(2,1)S(1)}, bf16[32,512]{1,0:T(8,128)(2,1)S(1)}, u32[]{:S(2)}, u32[]{:S(2)}) collective-permute-start(bf16[32,512]{1,0:T(8,128)(2,1)S(1)} %get-tuple-element.38), channel_id=1, source_target_pairs={{0,15},{1,2},{2,1},{3,4},{4,3},{5,6},{6,5},{7,8},{8,7},{9,10},{10,... | collective-permute-start | bytes 98312 | tf_op jit(solution)/shard_map/ppermute | solution.py:433
  30.8 1.7 %collective-permute-start.10 = (bf16[32,512]{1,0:T(8,128)(2,1)S(1)}, bf16[32,512]{1,0:T(8,128)(2,1)S(1)}, u32[]{:S(2)}, u32[]{:S(2)}) collective-permute-start(bf16[32,512]{1,0:T(8,128)(2,1)S(1)} %get-tuple-element.39), channel_id=1, source_target_pairs={{0,2},{1,3},{2,0},{3,1},{4,6},{5,7},{6,4},{7,5},{8,10},{9,11},{10,... | collective-permute-start | bytes 98312 | tf_op jit(solution)/shard_map/ppermute | solution.py:433
  32.5 0.0 collective-permute-start.11
  32.5 3.6 %collective-permute-done.7.rest_1_ = bf16[32,512]{1,0:T(8,128)(2,1)S(1)} collective-permute-done((bf16[32,512]{1,0:T(8,128)(2,1)S(1)}, bf16[32,512]{1,0:T(8,128)(2,1)S(1)}, u32[]{:S(2)}, u32[]{:S(2)}) %collective-permute-start.7) | collective-permute-done | bytes 32800 | tf_op jit(solution)/shard_map/ppermute | solution.py:433
  36.1 0.0 collective-permute-done.8.rest_2_
  36.1 0.0 collective-permute-done.9.rest_3_
  36.1 0.0 collective-permute-done.10.rest_4_
  36.1 0.0 collective-permute-done.11.rest_5_
  36.1 0.0 copy-done.2
  36.1 3.8 %decode.1 = bf16[227,4096]{1,0:T(8,128)(2,1)} custom-call(bf16[227,4096]{1,0:T(8,128)(2,1)S(1)} %get-tuple-element.22.grid_ref, bf16[512,4096]{1,0:T(8,128)(2,1)S(1)} %get-tuple-element.23.lat_ref, bf16[192,4096]{1,0:T(8,128)(2,1)S(1)} %get-tuple-element.24.dsum_ref, bf16[227,512]{1,0:T(8,128)(2,1)S(1)} %bitcast.6, ...), custom_call_target="tpu_custom_call" | custom-call | tf_op jit(solution)/shard_map/decode/pallas_call | solution.py:408
Async XLA Ops:
  0.6 20.1 %copy-start.1 = (bf16[512,512]{1,0:T(8,128)(2,1)S(1)}, bf16[512,512]{1,0:T(8,128)(2,1)}, u32[]{:S(2)}) copy-start(bf16[512,512]{1,0:T(8,128)(2,1)} %refs_7_.1) | copy-start | bytes 1572868
  0.6 20.1 %copy-start.4 = (bf16[128,512]{1,0:T(8,128)(2,1)S(1)}, bf16[128,512]{1,0:T(8,128)(2,1)}, u32[]{:S(2)}) copy-start(bf16[128,512]{1,0:T(8,128)(2,1)} %refs_6_.1) | copy-start | bytes 393220
  0.7 21.8 %copy-start.3 = (bf16[4,6,32,32]{3,2,1,0:T(8,128)(2,1)S(1)}, bf16[4,6,32,32]{3,2,1,0:T(8,128)(2,1)}, u32[]{:S(2)}) copy-start(bf16[4,6,32,32]{3,2,1,0:T(8,128)(2,1)} %coef_ref.1) | copy-start | bytes 147460
  0.7 21.7 %copy-start.5 = (s32[4,6]{1,0:T(4,128)S(1)}, s32[4,6]{1,0:T(4,128)}, u32[]{:S(2)}) copy-start(s32[4,6]{1,0:T(4,128)} %adj_ref.1) | copy-start | bytes 292
  0.7 27.5 %copy-start = (bf16[512,512]{1,0:T(8,128)(2,1)S(1)}, bf16[512,512]{1,0:T(8,128)(2,1)}, u32[]{:S(2)}) copy-start(bf16[512,512]{1,0:T(8,128)(2,1)} %w_ref.1) | copy-start | bytes 1572868
  0.7 27.5 %copy-start.6 = (f32[512]{0:T(512)S(1)}, f32[512]{0:T(512)}, u32[]{:S(2)}) copy-start(f32[512]{0:T(512)} %param.22) | copy-start | bytes 6148
  8.5 27.6 %copy-start.2 = (bf16[512,227]{0,1:T(8,128)(2,1)S(1)}, bf16[512,227]{0,1:T(8,128)(2,1)}, u32[]{:S(2)}) copy-start(bf16[512,227]{0,1:T(8,128)(2,1)} %param.25) | copy-start | bytes 697348
  8.5 8.4 %collective-permute-start = (bf16[32,640]{1,0:T(8,128)(2,1)S(1)}, bf16[32,640]{1,0:T(8,128)(2,1)S(1)}, u32[]{:S(2)}, u32[]{:S(2)}) collective-permute-start(bf16[32,640]{1,0:T(8,128)(2,1)S(1)} %get-tuple-element.26), channel_id=1, source_target_pairs={{0,14},{1,15},{2,4},{3,5},{4,2},{5,3},{6,8},{7,9},{8,6},{9,7},{10,... | collective-permute-start | bytes 122888 | tf_op jit(solution)/shard_map/ppermute | solution.py:433
  14.6 4.9 %collective-permute-start.1 = (bf16[32,640]{1,0:T(8,128)(2,1)S(1)}, bf16[32,640]{1,0:T(8,128)(2,1)S(1)}, u32[]{:S(2)}, u32[]{:S(2)}) collective-permute-start(bf16[32,640]{1,0:T(8,128)(2,1)S(1)} %get-tuple-element.27), channel_id=1, source_target_pairs={{0,8},{1,9},{2,10},{3,11},{4,12},{5,13},{6,14},{7,15},{8,0},{9,1},... | collective-permute-start | bytes 122888 | tf_op jit(solution)/shard_map/ppermute | solution.py:433
  14.6 6.1 %collective-permute-start.2 = (bf16[32,640]{1,0:T(8,128)(2,1)S(1)}, bf16[32,640]{1,0:T(8,128)(2,1)S(1)}, u32[]{:S(2)}, u32[]{:S(2)}) collective-permute-start(bf16[32,640]{1,0:T(8,128)(2,1)S(1)} %get-tuple-element.28), channel_id=1, source_target_pairs={{0,15},{1,2},{2,1},{3,4},{4,3},{5,6},{6,5},{7,8},{8,7},{9,10},{10,... | collective-permute-start | bytes 122888 | tf_op jit(solution)/shard_map/ppermute | solution.py:433
  15.3 5.4 %collective-permute-start.3 = (bf16[32,640]{1,0:T(8,128)(2,1)S(1)}, bf16[32,640]{1,0:T(8,128)(2,1)S(1)}, u32[]{:S(2)}, u32[]{:S(2)}) collective-permute-start(bf16[32,640]{1,0:T(8,128)(2,1)S(1)} %get-tuple-element.29), channel_id=1, source_target_pairs={{0,2},{1,3},{2,0},{3,1},{4,6},{5,7},{6,4},{7,5},{8,10},{9,11},{10,... | collective-permute-start | bytes 122888 | tf_op jit(solution)/shard_map/ppermute | solution.py:433
  15.8 4.9 %collective-permute-start.4 = (bf16[32,640]{1,0:T(8,128)(2,1)S(1)}, bf16[32,640]{1,0:T(8,128)(2,1)S(1)}, u32[]{:S(2)}, u32[]{:S(2)}) collective-permute-start(bf16[32,640]{1,0:T(8,128)(2,1)S(1)} %get-tuple-element.30), channel_id=1, source_target_pairs={{0,1},{1,0},{2,3},{3,2},{4,5},{5,4},{6,7},{7,6},{8,9},{9,8},{10,11... | collective-permute-start | bytes 122888 | tf_op jit(solution)/shard_map/ppermute | solution.py:433
  21.0 7.2 %collective-permute-start.6 = (bf16[128,512]{1,0:T(8,128)(2,1)S(1)}, bf16[128,512]{1,0:T(8,128)(2,1)S(1)}, u32[]{:S(2)}, u32[]{:S(2)}) collective-permute-start(bf16[128,512]{1,0:T(8,128)(2,1)S(1)} %get-tuple-element.32.mid_ref), channel_id=1, source_target_pairs={{0,15},{1,2},{2,1},{3,4},{4,3},{5,6},{6,5},{7,8},{8,7},{9,10},{10,... | collective-permute-start | bytes 393224 | tf_op jit(solution)/shard_map/ppermute | solution.py:433
  22.4 5.8 %collective-permute-start.5 = (bf16[128,512]{1,0:T(8,128)(2,1)S(1)}, bf16[128,512]{1,0:T(8,128)(2,1)S(1)}, u32[]{:S(2)}, u32[]{:S(2)}) collective-permute-start(bf16[128,512]{1,0:T(8,128)(2,1)S(1)} %get-tuple-element.32.mid_ref), channel_id=1, source_target_pairs={{0,1},{1,0},{2,3},{3,2},{4,5},{5,4},{6,7},{7,6},{8,9},{9,8},{10,11... | collective-permute-start | bytes 393224 | tf_op jit(solution)/shard_map/ppermute | solution.py:433
  29.5 6.6 %collective-permute-start.7 = (bf16[32,512]{1,0:T(8,128)(2,1)S(1)}, bf16[32,512]{1,0:T(8,128)(2,1)S(1)}, u32[]{:S(2)}, u32[]{:S(2)}) collective-permute-start(bf16[32,512]{1,0:T(8,128)(2,1)S(1)} %get-tuple-element.36), channel_id=1, source_target_pairs={{0,14},{1,15},{2,4},{3,5},{4,2},{5,3},{6,8},{7,9},{8,6},{9,7},{10,... | collective-permute-start | bytes 98312 | tf_op jit(solution)/shard_map/ppermute | solution.py:433
  29.5 6.6 %collective-permute-start.8 = (bf16[32,512]{1,0:T(8,128)(2,1)S(1)}, bf16[32,512]{1,0:T(8,128)(2,1)S(1)}, u32[]{:S(2)}, u32[]{:S(2)}) collective-permute-start(bf16[32,512]{1,0:T(8,128)(2,1)S(1)} %get-tuple-element.37), channel_id=1, source_target_pairs={{0,8},{1,9},{2,10},{3,11},{4,12},{5,13},{6,14},{7,15},{8,0},{9,1},... | collective-permute-start | bytes 98312 | tf_op jit(solution)/shard_map/ppermute | solution.py:433
  29.5 6.6 %collective-permute-start.9 = (bf16[32,512]{1,0:T(8,128)(2,1)S(1)}, bf16[32,512]{1,0:T(8,128)(2,1)S(1)}, u32[]{:S(2)}, u32[]{:S(2)}) collective-permute-start(bf16[32,512]{1,0:T(8,128)(2,1)S(1)} %get-tuple-element.38), channel_id=1, source_target_pairs={{0,15},{1,2},{2,1},{3,4},{4,3},{5,6},{6,5},{7,8},{8,7},{9,10},{10,... | collective-permute-start | bytes 98312 | tf_op jit(solution)/shard_map/ppermute | solution.py:433
  30.8 5.3 %collective-permute-start.10 = (bf16[32,512]{1,0:T(8,128)(2,1)S(1)}, bf16[32,512]{1,0:T(8,128)(2,1)S(1)}, u32[]{:S(2)}, u32[]{:S(2)}) collective-permute-start(bf16[32,512]{1,0:T(8,128)(2,1)S(1)} %get-tuple-element.39), channel_id=1, source_target_pairs={{0,2},{1,3},{2,0},{3,1},{4,6},{5,7},{6,4},{7,5},{8,10},{9,11},{10,... | collective-permute-start | bytes 98312 | tf_op jit(solution)/shard_map/ppermute | solution.py:433
  32.5 3.6 %collective-permute-start.11 = (bf16[32,512]{1,0:T(8,128)(2,1)S(1)}, bf16[32,512]{1,0:T(8,128)(2,1)S(1)}, u32[]{:S(2)}, u32[]{:S(2)}) collective-permute-start(bf16[32,512]{1,0:T(8,128)(2,1)S(1)} %get-tuple-element.40), channel_id=1, source_target_pairs={{0,1},{1,0},{2,3},{3,2},{4,5},{5,4},{6,7},{7,6},{8,9},{9,8},{10,11... | collective-permute-start | bytes 98312 | tf_op jit(solution)/shard_map/ppermute | solution.py:433

commit v15 on v14

--- a/solution.py
+++ b/solution.py
@@ -103,12 +103,12 @@
 
 
 def encode_kernel(
-    parts, width, slot_hbm, owner_hbm, w_hbm, grid_hbm, enc_hbm, dec_hbm,
-    lat_ref, dsum_ref, grid_ref, *rest,
+    parts, width, slot_hbm, owner_hbm, w_hbm, grid_hbm, enc_hbm,
+    lat_ref, tgt_ref, grid_ref, *rest,
 ):
     send_refs = rest[:SLOTS]
     (
-        slot_ref, owner_ref, w_ref, enc_ref, dec_ref, wt_ref, tgt_ref, ids_ref, msum_ref,
+        slot_ref, owner_ref, w_ref, enc_ref, wt_ref, ids_ref, msum_ref,
         acc_ref, spread_ref, small_sems, sems,
     ) = rest[SLOTS:]
     tiles, block_mesh, block_grid = enc_ref.shape
@@ -127,7 +127,6 @@
         return (
             pltpu.make_async_copy(grid_hbm.at[:, cols], grid_ref.at[:, cols], sems.at[0, step]),
             pltpu.make_async_copy(enc_hbm.at[some], enc_ref.at[some], sems.at[1, step]),
-            pltpu.make_async_copy(dec_hbm.at[some], dec_ref.at[some], sems.at[2, step]),
         )
 
     small = [
@@ -171,17 +170,9 @@
         for b in range(blocks):
             hot = hot_rows(ids_ref[...], tgt_ref[pl.ds(step * blocks + b, 1), :])
             some = pl.ds(step * chunk + b * per_block, per_block)
-            both = jnp.concatenate(
-                [
-                    enc_ref[some].reshape(wide, block_grid),
-                    dec_ref[some].reshape(wide, block_grid),
-                ],
-                axis=1,
-            )
-            sums = jnp.dot(hot, both, preferred_element_type=F32).astype(BF16)
-            msum_ref[slot, :, b * block_grid : (b + 1) * block_grid] = sums[:, :block_grid]
-            first = (step * blocks + b) * block_grid
-            dsum_ref[:, pl.ds(first, block_grid)] = sums[:, block_grid:]
+            tiles_of = enc_ref[some].reshape(wide, block_grid)
+            sums = jnp.dot(hot, tiles_of, preferred_element_type=F32).astype(BF16)
+            msum_ref[slot, :, b * block_grid : (b + 1) * block_grid] = sums
         for half in range(0, width, 256):
             part = pl.ds(step * width + half, 256)
             lat = silu_of_half(
@@ -200,7 +191,7 @@
         send_refs[s][:, latent:] = jnp.full((block_mesh, PAD), block, F32).astype(BF16)
 
 
-def encode(parts, slot_block, owners, grid_t, w_embed, enc_coef, dec_t):
+def encode(parts, slot_block, owners, grid_t, w_embed, enc_coef):
     channels, points = grid_t.shape
     latent = w_embed.shape[1]
     tiles, block_mesh, block_grid = enc_coef.shape
@@ -213,11 +204,11 @@
     hbm = pl.BlockSpec(memory_space=pl.ANY)
     return pl.pallas_call(
         functools.partial(encode_kernel, parts, width),
-        in_specs=[hbm] * 6,
+        in_specs=[hbm] * 5,
         out_specs=[vmem] * (3 + SLOTS),
         out_shape=[
             pltpu.VMEM((latent, points), BF16),
-            pltpu.VMEM((rows, points), BF16),
+            pltpu.VMEM((grid_blocks, wide), F32),
             pltpu.VMEM((channels, points), BF16),
         ]
         + [jax.ShapeDtypeStruct((block_mesh, latent + PAD), BF16)] * SLOTS,
@@ -226,24 +217,78 @@
             pltpu.VMEM(owners.shape, jnp.int32),
             pltpu.VMEM(w_embed.shape, BF16),
             pltpu.VMEM(enc_coef.shape, BF16),
-            pltpu.VMEM(dec_t.shape, BF16),
             pltpu.VMEM((latent, 256), BF16),
-            pltpu.VMEM((grid_blocks, wide), F32),
             pltpu.VMEM((rows, 128), BF16),
             pltpu.VMEM((2, rows, width), BF16),
             pltpu.VMEM((rows, latent), F32),
             pltpu.VMEM((*owners.shape, wide), BF16),
             pltpu.SemaphoreType.DMA((3,)),
-            pltpu.SemaphoreType.DMA((3, steps)),
+            pltpu.SemaphoreType.DMA((2, steps)),
         ],
         compiler_params=pltpu.CompilerParams(vmem_limit_bytes=24 * MIB),
         name="encode",
     )(
         *(
             pltpu.with_memory_space_constraint(x, pltpu.HBM)
-            for x in (slot_block, owners, w_embed, grid_t, enc_coef, dec_t)
+            for x in (slot_block, owners, w_embed, grid_t, enc_coef)
         )
     )
+
+
+def decoder_sums_kernel(tgt_ref, dec_hbm, dsum_ref, done_ref, dec_ref, ids_ref, sems):
+    tiles, block_mesh, block_grid = dec_ref.shape
+    grid_blocks, wide = tgt_ref.shape
+    per_block = tiles // grid_blocks
+    steps = sems.shape[0]
+    chunk = tiles // steps
+    blocks = grid_blocks // steps
+
+    def copy(step):
+        some = pl.ds(step * chunk, chunk)
+        return pltpu.make_async_copy(dec_hbm.at[some], dec_ref.at[some], sems.at[step])
+
+    for step in range(steps):
+        copy(step).start()
+    ids_ref[...] = lax.broadcasted_iota(jnp.int32, ids_ref.shape, 0).astype(BF16)
+    for step in range(steps):
+        copy(step).wait()
+        for g in range(step * blocks, (step + 1) * blocks):
+            hot = hot_rows(ids_ref[...], tgt_ref[g : g + 1, :])
+            some = pl.ds(g * per_block, per_block)
+            sums = jnp.dot(
+                hot, dec_ref[some].reshape(wide, block_grid), preferred_element_type=F32
+            )
+            dsum_ref[:, g * block_grid : (g + 1) * block_grid] = sums.astype(BF16)
+    done_ref[...] = jnp.zeros_like(done_ref)
+
+
+def decoder_sums(tgt, dec_t):
+    tiles, block_mesh, block_grid = dec_t.shape
+    grid_blocks, wide = tgt.shape
+    rows = SLOTS * block_mesh
+    steps = 8
+    vmem = pl.BlockSpec(memory_space=pltpu.VMEM)
+    return pl.pallas_call(
+        decoder_sums_kernel,
+        in_specs=[vmem, pl.BlockSpec(memory_space=pl.ANY)],
+        out_specs=[vmem] * 2,
+        out_shape=[
+            pltpu.VMEM((rows, grid_blocks * block_grid), BF16),
+            jax.ShapeDtypeStruct((8, 128), F32),
+        ],
+        scratch_shapes=[
+            pltpu.VMEM(dec_t.shape, BF16),
+            pltpu.VMEM((rows, 128), BF16),
+            pltpu.SemaphoreType.DMA((steps,)),
+        ],
+        compiler_params=pltpu.CompilerParams(vmem_limit_bytes=16 * MIB),
+        cost_estimate=pl.CostEstimate(
+            flops=2 * rows * wide * block_grid * grid_blocks,
+            bytes_accessed=2 * (dec_t.size + rows * grid_blocks * block_grid),
+            transcendentals=0,
+        ),
+        name="decoder_sums",
+    )(tgt, pltpu.with_memory_space_constraint(dec_t, pltpu.HBM))
 
 
 def prepare_kernel(parts, adj_ref, coef_ref, mid_ref, near_ref, part_ref, all_ref):
@@ -298,7 +343,7 @@
 
 def update_kernel(*refs):
     slots = refs[:SLOTS]
-    mesh_ref, w_ref, mid_ref, ids_ref = refs[SLOTS:]
+    mesh_ref, w_ref, after_ref, mid_ref, ids_ref = refs[SLOTS:]
     count, latent = mesh_ref.shape
     block_mesh = slots[0].shape[0]
     sums = [slot[:, :latent].astype(F32) for slot in slots]
@@ -315,11 +360,11 @@
     mid_ref[...] = (mesh_ref[...].astype(F32) + silu(grown)).astype(BF16)
 
 
-def update(slots, mesh_in, w_enc):
+def update(slots, mesh_in, w_enc, after):
     vmem = pl.BlockSpec(memory_space=pltpu.VMEM)
     return pl.pallas_call(
         update_kernel,
-        in_specs=[vmem] * (SLOTS + 2),
+        in_specs=[vmem] * (SLOTS + 3),
         out_specs=[vmem] * 2,
         out_shape=[
             jax.ShapeDtypeStruct(mesh_in.shape, BF16),
@@ -327,7 +372,7 @@
         ],
         compiler_params=pltpu.CompilerParams(vmem_limit_bytes=8 * MIB),
         name="mesh_update",
-    )(*slots, mesh_in, w_enc)
+    )(*slots, mesh_in, w_enc, after)
 
 
 def process_kernel(
@@ -435,12 +480,12 @@
     def swap_all(xs):
         return [xs[OWN]] + [swap(xs[s], s) for s in range(1, SLOTS)]
 
-    lat_t, dsum, grid_t, *sums = encode(
-        parts, slot_block, enc_owner.reshape(-1, 128), grid_in.T, w_embed, enc_coef,
-        jnp.swapaxes(dec_coef, 1, 2),
+    lat_t, tgt, grid_t, *sums = encode(
+        parts, slot_block, enc_owner.reshape(-1, 128), grid_in.T, w_embed, enc_coef
     )
     received = swap_all(sums)
-    mid, ids = update(received, mesh_in, w_enc)
+    dsum, after = decoder_sums(tgt, jnp.swapaxes(dec_coef, 1, 2))
+    mid, ids = update(received, mesh_in, w_enc, after)
     far_mid = swap(mid, FAR)
     near_mid = swap(mid, NEAR)
     near, part = prepare(parts, proc_adj, proc_coef, mid)

time: 40.1 us -> 41 us (1.022)
  waiting for transfers between devices: 12 us -> 8.3 us
  Pallas kernels: 14.3 us -> 17.3 us
  starting transfers between devices: 12.8 us -> 14.5 us
    ppermute x12, waiting for transfers between devices: 12 us -> 8.3 us  [swap(): return lax.ppermute(x, 'nodes', pairs)]
    pallas_call x1 -> x2, Pallas kernels: 0.3 us -> 4.02 us  [the longest x1 3.72 us: decoder_sums(): pl.pallas_call(decoder_sums_kernel, in_specs=[vmem, pl.BlockSpec(memory_s...]
    ppermute x12, starting transfers between devices: 12.8 us -> 14.5 us  [swap(): return lax.ppermute(x, 'nodes', pairs)]
    pallas_call x1, Pallas kernels: 7.79 us -> 7.05 us  [encode(): pl.pallas_call(functools.partial(encode_kernel, parts, width), in_specs=[...]
  transfers between devices with their start and end apart: 12 -> 12, of which waited for: 4 -> 3; matrix products, arithmetic and copies ran while one was open for 0% -> 0% of each run, Pallas kernels for 3% -> 12%
where the time goes in v15:
time: 41 us; the launch traced here: 40.9 us
  Pallas kernels  17.3 us (42%)
  starting transfers between devices  14.5 us (35%)
  waiting for transfers between devices  8.3 us (20%)
  between operations  0.74 us (2%)
    ppermute x12, starting transfers between devices, swap(): return lax.ppermute(x, 'nodes', pairs)  14.5 us
    ppermute x12, waiting for transfers between devices, swap(): return lax.ppermute(x, 'nodes', pairs)  8.3 us
    pallas_call x1, Pallas kernels, encode(): pl.pallas_call(functools.partial(encode_kernel, parts, width), in_specs=[...  7.05 us
    pallas_call x1, Pallas kernels, decode(): pl.pallas_call(functools.partial(decode_kernel, width), in_specs=[vmem] *...  3.81 us
    pallas_call x1, Pallas kernels, decoder_sums(): pl.pallas_call(decoder_sums_kernel, in_specs=[vmem, pl.BlockSpec(memory_s...  3.72 us
    pallas_call x1, Pallas kernels, process(): pl.pallas_call(process_kernel, in_specs=[vmem] * 8, out_specs=[vmem] * (1...  1.27 us
    pallas_call x1, Pallas kernels, prepare(): pl.pallas_call(functools.partial(prepare_kernel, parts), in_specs=[pl.Blo...  1.11 us
  transfers between devices with their start and end apart: 12, of which 3 were waited for; matrix products, arithmetic and copies ran while one was open for 0% of the time, Pallas kernels for 12%

profile of v15, /device:TPU:0, one launch (start us, length us, event | category | flops | bytes accessed | tf_op | source)
XLA Modules:
  0.0 40.9 jit_solution(7643197971406616379)
XLA Ops:
  0.6 7.1 %encode.1 = (bf16[512,4096]{1,0:T(8,128)(2,1)S(1)}, f32[32,384]{1,0:T(8,128)S(1)}, bf16[227,4096]{1,0:T(8,128)(2,1)S(1)}, bf16[32,640]{1,0:T(8,128)(2,1)S(1)}, b...) custom-call(s32[16]{0:T(128)} %slot_hbm.1, ...), custom_call_target="tpu_custom_call" | custom-call | tf_op jit(solution)/shard_map/encode/pallas_call | solution.py:205
  7.7 0.0 copy-start.1
  7.7 0.0 copy-start.4
  7.7 6.1 %collective-permute-start = (bf16[32,640]{1,0:T(8,128)(2,1)S(1)}, bf16[32,640]{1,0:T(8,128)(2,1)S(1)}, u32[]{:S(2)}, u32[]{:S(2)}) collective-permute-start(bf16[32,640]{1,0:T(8,128)(2,1)S(1)} %get-tuple-element.29), channel_id=1, source_target_pairs={{0,14},{1,15},{2,4},{3,5},{4,2},{5,3},{6,8},{7,9},{8,6},{9,7},{10,... | collective-permute-start | bytes 122888 | tf_op jit(solution)/shard_map/ppermute | solution.py:478
  13.8 0.0 collective-permute-start.1
  13.8 0.7 %collective-permute-start.2 = (bf16[32,640]{1,0:T(8,128)(2,1)S(1)}, bf16[32,640]{1,0:T(8,128)(2,1)S(1)}, u32[]{:S(2)}, u32[]{:S(2)}) collective-permute-start(bf16[32,640]{1,0:T(8,128)(2,1)S(1)} %get-tuple-element.31), channel_id=1, source_target_pairs={{0,15},{1,2},{2,1},{3,4},{4,3},{5,6},{6,5},{7,8},{8,7},{9,10},{10,... | collective-permute-start | bytes 122888 | tf_op jit(solution)/shard_map/ppermute | solution.py:478
  14.5 0.5 %collective-permute-start.3 = (bf16[32,640]{1,0:T(8,128)(2,1)S(1)}, bf16[32,640]{1,0:T(8,128)(2,1)S(1)}, u32[]{:S(2)}, u32[]{:S(2)}) collective-permute-start(bf16[32,640]{1,0:T(8,128)(2,1)S(1)} %get-tuple-element.32), channel_id=1, source_target_pairs={{0,2},{1,3},{2,0},{3,1},{4,6},{5,7},{6,4},{7,5},{8,10},{9,11},{10,... | collective-permute-start | bytes 122888 | tf_op jit(solution)/shard_map/ppermute | solution.py:478
  15.0 1.1 %collective-permute-start.4 = (bf16[32,640]{1,0:T(8,128)(2,1)S(1)}, bf16[32,640]{1,0:T(8,128)(2,1)S(1)}, u32[]{:S(2)}, u32[]{:S(2)}) collective-permute-start(bf16[32,640]{1,0:T(8,128)(2,1)S(1)} %get-tuple-element.33), channel_id=1, source_target_pairs={{0,1},{1,0},{2,3},{3,2},{4,5},{5,4},{6,7},{7,6},{8,9},{9,8},{10,11... | collective-permute-start | bytes 122888 | tf_op jit(solution)/shard_map/ppermute | solution.py:478
  16.1 0.0 copy-start.3
  16.1 0.0 copy-start.5
  16.1 0.0 copy-start
  16.1 0.0 copy-start.6
  16.1 3.7 %decoder_sums.1 = (bf16[192,4096]{1,0:T(8,128)(2,1)S(1)}, f32[8,128]{1,0:T(8,128)S(1)}) custom-call(f32[32,384]{1,0:T(8,128)S(1)} %get-tuple-element.26.tgt_ref, bf16[384,32,128]{2,1,0:T(8,128)(2,1)} %bitcast.8), custom_call_target="tpu_custom_call" | custom-call | flops 603979776 | bytes 4718592 | tf_op jit(solution)/shard_map/decoder_sums/pallas_call | solution.py:271
  19.8 0.0 copy-start.2
  19.9 0.0 collective-permute-done.refs_1_
  19.9 0.0 collective-permute-done.1.refs_2_
  19.9 0.0 collective-permute-done.2.refs_3_
  19.9 0.0 collective-permute-done.3.refs_4_
  19.9 0.0 collective-permute-done.4.refs_5_
  19.9 0.0 copy-done.1
  19.9 0.0 copy-done.4
  19.9 0.3 mesh_update.1
  20.2 2.2 %collective-permute-start.6 = (bf16[128,512]{1,0:T(8,128)(2,1)S(1)}, bf16[128,512]{1,0:T(8,128)(2,1)S(1)}, u32[]{:S(2)}, u32[]{:S(2)}) collective-permute-start(bf16[128,512]{1,0:T(8,128)(2,1)S(1)} %get-tuple-element.36.mid_ref), channel_id=1, source_target_pairs={{0,15},{1,2},{2,1},{3,4},{4,3},{5,6},{6,5},{7,8},{8,7},{9,10},{10,... | collective-permute-start | bytes 393224 | tf_op jit(solution)/shard_map/ppermute | solution.py:478
  22.5 0.0 collective-permute-start.5
  22.5 0.0 copy-done.3
  22.5 0.0 copy-done.5
  22.5 1.1 %prepare.1 = (bf16[128,256]{1,0:T(8,128)(2,1)S(1)}, f32[128,512]{1,0:T(8,128)S(1)}) custom-call(s32[4,6]{1,0:T(4,128)S(1)} %copy-done.5, bf16[4,6,32,32]{3,2,1,0:T(8,128)(2,1)S(1)} %copy-done.3, bf16[128,512]{1,0:T(8,128)(2,1)S(1)} %get-tuple-element.36.mid_ref), custom_call_target="tpu_custom_call" | custom-call | flops 18874368 | bytes 393216 | tf_op jit(solution)/shard_map/prepare/pallas_call | solution.py:325
  23.6 3.8 %collective-permute-done.6.far_mid_ref = bf16[128,512]{1,0:T(8,128)(2,1)S(1)} collective-permute-done((bf16[128,512]{1,0:T(8,128)(2,1)S(1)}, bf16[128,512]{1,0:T(8,128)(2,1)S(1)}, u32[]{:S(2)}, u32[]{:S(2)}) %collective-permute-start.6) | collective-permute-done | bytes 131104 | tf_op jit(solution)/shard_map/ppermute | solution.py:478
  27.4 0.0 collective-permute-done.5.near_mid_ref
  27.4 0.0 copy-done
  27.4 0.0 copy-done.6
  27.4 1.3 %mesh_process.1 = (bf16[128,512]{1,0:T(8,128)(2,1)}, bf16[32,512]{1,0:T(8,128)(2,1)S(1)}, bf16[32,512]{1,0:T(8,128)(2,1)S(1)}, bf16[32,512]{1,0:T(8,128)(2,1)S(1...) custom-call(f32[8,512]{1,0:T(8,128)S(1)} %get-tuple-element.35.ids_ref, ...), custom_call_target="tpu_custom_call" | custom-call | tf_op jit(solution)/shard_map/mesh_process/pallas_call | solution.py:401
  28.7 0.7 %collective-permute-start.7 = (bf16[32,512]{1,0:T(8,128)(2,1)S(1)}, bf16[32,512]{1,0:T(8,128)(2,1)S(1)}, u32[]{:S(2)}, u32[]{:S(2)}) collective-permute-start(bf16[32,512]{1,0:T(8,128)(2,1)S(1)} %get-tuple-element.40), channel_id=1, source_target_pairs={{0,14},{1,15},{2,4},{3,5},{4,2},{5,3},{6,8},{7,9},{8,6},{9,7},{10,... | collective-permute-start | bytes 98312 | tf_op jit(solution)/shard_map/ppermute | solution.py:478
  29.4 1.6 %collective-permute-start.8 = (bf16[32,512]{1,0:T(8,128)(2,1)S(1)}, bf16[32,512]{1,0:T(8,128)(2,1)S(1)}, u32[]{:S(2)}, u32[]{:S(2)}) collective-permute-start(bf16[32,512]{1,0:T(8,128)(2,1)S(1)} %get-tuple-element.41), channel_id=1, source_target_pairs={{0,8},{1,9},{2,10},{3,11},{4,12},{5,13},{6,14},{7,15},{8,0},{9,1},... | collective-permute-start | bytes 98312 | tf_op jit(solution)/shard_map/ppermute | solution.py:478
  31.0 1.2 %collective-permute-start.9 = (bf16[32,512]{1,0:T(8,128)(2,1)S(1)}, bf16[32,512]{1,0:T(8,128)(2,1)S(1)}, u32[]{:S(2)}, u32[]{:S(2)}) collective-permute-start(bf16[32,512]{1,0:T(8,128)(2,1)S(1)} %get-tuple-element.42), channel_id=1, source_target_pairs={{0,15},{1,2},{2,1},{3,4},{4,3},{5,6},{6,5},{7,8},{8,7},{9,10},{10,... | collective-permute-start | bytes 98312 | tf_op jit(solution)/shard_map/ppermute | solution.py:478
  32.3 0.3 collective-permute-start.10
  32.6 0.0 collective-permute-start.11
  32.6 2.8 %collective-permute-done.7.rest_1_ = bf16[32,512]{1,0:T(8,128)(2,1)S(1)} collective-permute-done((bf16[32,512]{1,0:T(8,128)(2,1)S(1)}, bf16[32,512]{1,0:T(8,128)(2,1)S(1)}, u32[]{:S(2)}, u32[]{:S(2)}) %collective-permute-start.7) | collective-permute-done | bytes 32800 | tf_op jit(solution)/shard_map/ppermute | solution.py:478
  35.4 0.0 collective-permute-done.8.rest_2_
  35.4 1.7 %collective-permute-done.9.rest_3_ = bf16[32,512]{1,0:T(8,128)(2,1)S(1)} collective-permute-done((bf16[32,512]{1,0:T(8,128)(2,1)S(1)}, bf16[32,512]{1,0:T(8,128)(2,1)S(1)}, u32[]{:S(2)}, u32[]{:S(2)}) %collective-permute-start.9) | collective-permute-done | bytes 32800 | tf_op jit(solution)/shard_map/ppermute | solution.py:478
  37.1 0.0 collective-permute-done.10.rest_4_
  37.1 0.0 collective-permute-done.11.rest_5_
  37.1 0.0 copy-done.2
  37.1 3.8 %decode.1 = bf16[227,4096]{1,0:T(8,128)(2,1)} custom-call(bf16[227,4096]{1,0:T(8,128)(2,1)S(1)} %get-tuple-element.24.grid_ref, bf16[512,4096]{1,0:T(8,128)(2,1)S(1)} %get-tuple-element.25.lat_ref, bf16[192,4096]{1,0:T(8,128)(2,1)S(1)} %get-tuple-element.27.dsum_ref, bf16[227,512]{1,0:T(8,128)(2,1)S(1)} %bitcast.6, ...), custom_call_target="tpu_custom_call" | custom-call | tf_op jit(solution)/shard_map/decode/pallas_call | solution.py:453
Async XLA Ops:
  7.7 12.2 %copy-start.1 = (bf16[512,512]{1,0:T(8,128)(2,1)S(1)}, bf16[512,512]{1,0:T(8,128)(2,1)}, u32[]{:S(2)}) copy-start(bf16[512,512]{1,0:T(8,128)(2,1)} %refs_7_.1) | copy-start | bytes 1572868
  7.7 12.2 %copy-start.4 = (bf16[128,512]{1,0:T(8,128)(2,1)S(1)}, bf16[128,512]{1,0:T(8,128)(2,1)}, u32[]{:S(2)}) copy-start(bf16[128,512]{1,0:T(8,128)(2,1)} %refs_6_.1) | copy-start | bytes 393220
  7.7 12.1 %collective-permute-start = (bf16[32,640]{1,0:T(8,128)(2,1)S(1)}, bf16[32,640]{1,0:T(8,128)(2,1)S(1)}, u32[]{:S(2)}, u32[]{:S(2)}) collective-permute-start(bf16[32,640]{1,0:T(8,128)(2,1)S(1)} %get-tuple-element.29), channel_id=1, source_target_pairs={{0,14},{1,15},{2,4},{3,5},{4,2},{5,3},{6,8},{7,9},{8,6},{9,7},{10,... | collective-permute-start | bytes 122888 | tf_op jit(solution)/shard_map/ppermute | solution.py:478
  13.8 6.1 %collective-permute-start.1 = (bf16[32,640]{1,0:T(8,128)(2,1)S(1)}, bf16[32,640]{1,0:T(8,128)(2,1)S(1)}, u32[]{:S(2)}, u32[]{:S(2)}) collective-permute-start(bf16[32,640]{1,0:T(8,128)(2,1)S(1)} %get-tuple-element.30), channel_id=1, source_target_pairs={{0,8},{1,9},{2,10},{3,11},{4,12},{5,13},{6,14},{7,15},{8,0},{9,1},... | collective-permute-start | bytes 122888 | tf_op jit(solution)/shard_map/ppermute | solution.py:478
  13.8 6.1 %collective-permute-start.2 = (bf16[32,640]{1,0:T(8,128)(2,1)S(1)}, bf16[32,640]{1,0:T(8,128)(2,1)S(1)}, u32[]{:S(2)}, u32[]{:S(2)}) collective-permute-start(bf16[32,640]{1,0:T(8,128)(2,1)S(1)} %get-tuple-element.31), channel_id=1, source_target_pairs={{0,15},{1,2},{2,1},{3,4},{4,3},{5,6},{6,5},{7,8},{8,7},{9,10},{10,... | collective-permute-start | bytes 122888 | tf_op jit(solution)/shard_map/ppermute | solution.py:478
  14.5 5.4 %collective-permute-start.3 = (bf16[32,640]{1,0:T(8,128)(2,1)S(1)}, bf16[32,640]{1,0:T(8,128)(2,1)S(1)}, u32[]{:S(2)}, u32[]{:S(2)}) collective-permute-start(bf16[32,640]{1,0:T(8,128)(2,1)S(1)} %get-tuple-element.32), channel_id=1, source_target_pairs={{0,2},{1,3},{2,0},{3,1},{4,6},{5,7},{6,4},{7,5},{8,10},{9,11},{10,... | collective-permute-start | bytes 122888 | tf_op jit(solution)/shard_map/ppermute | solution.py:478
  15.0 4.9 %collective-permute-start.4 = (bf16[32,640]{1,0:T(8,128)(2,1)S(1)}, bf16[32,640]{1,0:T(8,128)(2,1)S(1)}, u32[]{:S(2)}, u32[]{:S(2)}) collective-permute-start(bf16[32,640]{1,0:T(8,128)(2,1)S(1)} %get-tuple-element.33), channel_id=1, source_target_pairs={{0,1},{1,0},{2,3},{3,2},{4,5},{5,4},{6,7},{7,6},{8,9},{9,8},{10,11... | collective-permute-start | bytes 122888 | tf_op jit(solution)/shard_map/ppermute | solution.py:478
  16.1 6.4 %copy-start.3 = (bf16[4,6,32,32]{3,2,1,0:T(8,128)(2,1)S(1)}, bf16[4,6,32,32]{3,2,1,0:T(8,128)(2,1)}, u32[]{:S(2)}) copy-start(bf16[4,6,32,32]{3,2,1,0:T(8,128)(2,1)} %coef_ref.1) | copy-start | bytes 147460
  16.1 6.4 %copy-start.5 = (s32[4,6]{1,0:T(4,128)S(1)}, s32[4,6]{1,0:T(4,128)}, u32[]{:S(2)}) copy-start(s32[4,6]{1,0:T(4,128)} %adj_ref.1) | copy-start | bytes 292
  16.1 11.3 %copy-start = (bf16[512,512]{1,0:T(8,128)(2,1)S(1)}, bf16[512,512]{1,0:T(8,128)(2,1)}, u32[]{:S(2)}) copy-start(bf16[512,512]{1,0:T(8,128)(2,1)} %w_ref.1) | copy-start | bytes 1572868
  16.1 11.3 %copy-start.6 = (f32[512]{0:T(512)S(1)}, f32[512]{0:T(512)}, u32[]{:S(2)}) copy-start(f32[512]{0:T(512)} %param.22) | copy-start | bytes 6148
  19.8 17.2 %copy-start.2 = (bf16[512,227]{0,1:T(8,128)(2,1)S(1)}, bf16[512,227]{0,1:T(8,128)(2,1)}, u32[]{:S(2)}) copy-start(bf16[512,227]{0,1:T(8,128)(2,1)} %param.25) | copy-start | bytes 697348
  20.2 7.2 %collective-permute-start.6 = (bf16[128,512]{1,0:T(8,128)(2,1)S(1)}, bf16[128,512]{1,0:T(8,128)(2,1)S(1)}, u32[]{:S(2)}, u32[]{:S(2)}) collective-permute-start(bf16[128,512]{1,0:T(8,128)(2,1)S(1)} %get-tuple-element.36.mid_ref), channel_id=1, source_target_pairs={{0,15},{1,2},{2,1},{3,4},{4,3},{5,6},{6,5},{7,8},{8,7},{9,10},{10,... | collective-permute-start | bytes 393224 | tf_op jit(solution)/shard_map/ppermute | solution.py:478
  22.5 4.9 %collective-permute-start.5 = (bf16[128,512]{1,0:T(8,128)(2,1)S(1)}, bf16[128,512]{1,0:T(8,128)(2,1)S(1)}, u32[]{:S(2)}, u32[]{:S(2)}) collective-permute-start(bf16[128,512]{1,0:T(8,128)(2,1)S(1)} %get-tuple-element.36.mid_ref), channel_id=1, source_target_pairs={{0,1},{1,0},{2,3},{3,2},{4,5},{5,4},{6,7},{7,6},{8,9},{9,8},{10,11... | collective-permute-start | bytes 393224 | tf_op jit(solution)/shard_map/ppermute | solution.py:478
  28.7 6.7 %collective-permute-start.7 = (bf16[32,512]{1,0:T(8,128)(2,1)S(1)}, bf16[32,512]{1,0:T(8,128)(2,1)S(1)}, u32[]{:S(2)}, u32[]{:S(2)}) collective-permute-start(bf16[32,512]{1,0:T(8,128)(2,1)S(1)} %get-tuple-element.40), channel_id=1, source_target_pairs={{0,14},{1,15},{2,4},{3,5},{4,2},{5,3},{6,8},{7,9},{8,6},{9,7},{10,... | collective-permute-start | bytes 98312 | tf_op jit(solution)/shard_map/ppermute | solution.py:478
  29.4 6.0 %collective-permute-start.8 = (bf16[32,512]{1,0:T(8,128)(2,1)S(1)}, bf16[32,512]{1,0:T(8,128)(2,1)S(1)}, u32[]{:S(2)}, u32[]{:S(2)}) collective-permute-start(bf16[32,512]{1,0:T(8,128)(2,1)S(1)} %get-tuple-element.41), channel_id=1, source_target_pairs={{0,8},{1,9},{2,10},{3,11},{4,12},{5,13},{6,14},{7,15},{8,0},{9,1},... | collective-permute-start | bytes 98312 | tf_op jit(solution)/shard_map/ppermute | solution.py:478
  31.0 6.0 %collective-permute-start.9 = (bf16[32,512]{1,0:T(8,128)(2,1)S(1)}, bf16[32,512]{1,0:T(8,128)(2,1)S(1)}, u32[]{:S(2)}, u32[]{:S(2)}) collective-permute-start(bf16[32,512]{1,0:T(8,128)(2,1)S(1)} %get-tuple-element.42), channel_id=1, source_target_pairs={{0,15},{1,2},{2,1},{3,4},{4,3},{5,6},{6,5},{7,8},{8,7},{9,10},{10,... | collective-permute-start | bytes 98312 | tf_op jit(solution)/shard_map/ppermute | solution.py:478
  32.3 4.8 %collective-permute-start.10 = (bf16[32,512]{1,0:T(8,128)(2,1)S(1)}, bf16[32,512]{1,0:T(8,128)(2,1)S(1)}, u32[]{:S(2)}, u32[]{:S(2)}) collective-permute-start(bf16[32,512]{1,0:T(8,128)(2,1)S(1)} %get-tuple-element.43), channel_id=1, source_target_pairs={{0,2},{1,3},{2,0},{3,1},{4,6},{5,7},{6,4},{7,5},{8,10},{9,11},{10,... | collective-permute-start | bytes 98312 | tf_op jit(solution)/shard_map/ppermute | solution.py:478
  32.6 4.5 %collective-permute-start.11 = (bf16[32,512]{1,0:T(8,128)(2,1)S(1)}, bf16[32,512]{1,0:T(8,128)(2,1)S(1)}, u32[]{:S(2)}, u32[]{:S(2)}) collective-permute-start(bf16[32,512]{1,0:T(8,128)(2,1)S(1)} %get-tuple-element.44), channel_id=1, source_target_pairs={{0,1},{1,0},{2,3},{3,2},{4,5},{5,4},{6,7},{7,6},{8,9},{9,8},{10,11... | collective-permute-start | bytes 98312 | tf_op jit(solution)/shard_map/ppermute | solution.py:478

commit v16 on v14

--- a/solution.py
+++ b/solution.py
@@ -205,7 +205,7 @@
     latent = w_embed.shape[1]
     tiles, block_mesh, block_grid = enc_coef.shape
     grid_blocks = points // block_grid
-    width = 512
+    width = 1024
     steps = points // width
     rows = SLOTS * block_mesh
     wide = tiles // grid_blocks * block_mesh

time: 40.1 us -> 39.2 us (0.978)
  Pallas kernels: 14.3 us -> 13.4 us
    pallas_call x1, Pallas kernels: 7.79 us -> 6.9 us  [encode(): pl.pallas_call(functools.partial(encode_kernel, parts, width), in_specs=[...]
where the time goes in v16:
time: 39.2 us; the launch traced here: 39.1 us
  Pallas kernels  13.4 us (34%)
  starting transfers between devices  12.8 us (33%)
  waiting for transfers between devices  12 us (31%)
  between operations  0.76 us (2%)
    ppermute x12, starting transfers between devices, swap(): return lax.ppermute(x, 'nodes', pairs)  12.8 us
    ppermute x12, waiting for transfers between devices, swap(): return lax.ppermute(x, 'nodes', pairs)  12 us
    pallas_call x1, Pallas kernels, encode(): pl.pallas_call(functools.partial(encode_kernel, parts, width), in_specs=[...  6.9 us
    pallas_call x1, Pallas kernels, decode(): pl.pallas_call(functools.partial(decode_kernel, width), in_specs=[vmem] *...  3.82 us
    pallas_call x1, Pallas kernels, process(): pl.pallas_call(process_kernel, in_specs=[vmem] * 8, out_specs=[vmem] * (1...  1.27 us
    pallas_call x1, Pallas kernels, prepare(): pl.pallas_call(functools.partial(prepare_kernel, parts), in_specs=[pl.Blo...  1.11 us
  transfers between devices with their start and end apart: 12, of which 4 were waited for; matrix products, arithmetic and copies ran while one was open for 0% of the time, Pallas kernels for 3%

profile of v16, /device:TPU:0, one launch (start us, length us, event | category | flops | bytes accessed | tf_op | source)
XLA Modules:
  0.0 39.1 jit_solution(9659875790594038818)
XLA Ops:
  0.6 0.0 copy-start.1
  0.6 0.0 copy-start.4
  0.7 0.0 copy-start.3
  0.7 0.0 copy-start.5
  0.7 0.0 copy-start
  0.7 0.0 copy-start.6
  0.7 6.9 %encode.1 = (bf16[512,4096]{1,0:T(8,128)(2,1)S(1)}, bf16[192,4096]{1,0:T(8,128)(2,1)S(1)}, bf16[227,4096]{1,0:T(8,128)(2,1)S(1)}, bf16[32,640]{1,0:T(8,128)(2,1)...) custom-call(s32[16]{0:T(128)} %slot_hbm.1, ...), custom_call_target="tpu_custom_call" | custom-call | tf_op jit(solution)/shard_map/encode/pallas_call | solution.py:214
  7.6 0.0 copy-start.2
  7.6 6.1 %collective-permute-start = (bf16[32,640]{1,0:T(8,128)(2,1)S(1)}, bf16[32,640]{1,0:T(8,128)(2,1)S(1)}, u32[]{:S(2)}, u32[]{:S(2)}) collective-permute-start(bf16[32,640]{1,0:T(8,128)(2,1)S(1)} %get-tuple-element.26), channel_id=1, source_target_pairs={{0,14},{1,15},{2,4},{3,5},{4,2},{5,3},{6,8},{7,9},{8,6},{9,7},{10,... | collective-permute-start | bytes 122888 | tf_op jit(solution)/shard_map/ppermute | solution.py:433
  13.7 0.0 collective-permute-start.1
  13.7 0.7 %collective-permute-start.2 = (bf16[32,640]{1,0:T(8,128)(2,1)S(1)}, bf16[32,640]{1,0:T(8,128)(2,1)S(1)}, u32[]{:S(2)}, u32[]{:S(2)}) collective-permute-start(bf16[32,640]{1,0:T(8,128)(2,1)S(1)} %get-tuple-element.28), channel_id=1, source_target_pairs={{0,15},{1,2},{2,1},{3,4},{4,3},{5,6},{6,5},{7,8},{8,7},{9,10},{10,... | collective-permute-start | bytes 122888 | tf_op jit(solution)/shard_map/ppermute | solution.py:433
  14.4 0.5 %collective-permute-start.3 = (bf16[32,640]{1,0:T(8,128)(2,1)S(1)}, bf16[32,640]{1,0:T(8,128)(2,1)S(1)}, u32[]{:S(2)}, u32[]{:S(2)}) collective-permute-start(bf16[32,640]{1,0:T(8,128)(2,1)S(1)} %get-tuple-element.29), channel_id=1, source_target_pairs={{0,2},{1,3},{2,0},{3,1},{4,6},{5,7},{6,4},{7,5},{8,10},{9,11},{10,... | collective-permute-start | bytes 122888 | tf_op jit(solution)/shard_map/ppermute | solution.py:433
  14.9 1.1 %collective-permute-start.4 = (bf16[32,640]{1,0:T(8,128)(2,1)S(1)}, bf16[32,640]{1,0:T(8,128)(2,1)S(1)}, u32[]{:S(2)}, u32[]{:S(2)}) collective-permute-start(bf16[32,640]{1,0:T(8,128)(2,1)S(1)} %get-tuple-element.30), channel_id=1, source_target_pairs={{0,1},{1,0},{2,3},{3,2},{4,5},{5,4},{6,7},{7,6},{8,9},{9,8},{10,11... | collective-permute-start | bytes 122888 | tf_op jit(solution)/shard_map/ppermute | solution.py:433
  16.0 0.0 collective-permute-done.refs_1_
  16.0 2.6 %collective-permute-done.1.refs_2_ = bf16[32,640]{1,0:T(8,128)(2,1)S(1)} collective-permute-done((bf16[32,640]{1,0:T(8,128)(2,1)S(1)}, bf16[32,640]{1,0:T(8,128)(2,1)S(1)}, u32[]{:S(2)}, u32[]{:S(2)}) %collective-permute-start.1) | collective-permute-done | bytes 40992 | tf_op jit(solution)/shard_map/ppermute | solution.py:433
  18.6 1.2 %collective-permute-done.2.refs_3_ = bf16[32,640]{1,0:T(8,128)(2,1)S(1)} collective-permute-done((bf16[32,640]{1,0:T(8,128)(2,1)S(1)}, bf16[32,640]{1,0:T(8,128)(2,1)S(1)}, u32[]{:S(2)}, u32[]{:S(2)}) %collective-permute-start.2) | collective-permute-done | bytes 40992 | tf_op jit(solution)/shard_map/ppermute | solution.py:433
  19.8 0.0 collective-permute-done.3.refs_4_
  19.8 0.0 collective-permute-done.4.refs_5_
  19.8 0.0 copy-done.1
  19.8 0.0 copy-done.4
  19.8 0.3 mesh_update.1
  20.1 1.4 %collective-permute-start.6 = (bf16[128,512]{1,0:T(8,128)(2,1)S(1)}, bf16[128,512]{1,0:T(8,128)(2,1)S(1)}, u32[]{:S(2)}, u32[]{:S(2)}) collective-permute-start(bf16[128,512]{1,0:T(8,128)(2,1)S(1)} %get-tuple-element.32.mid_ref), channel_id=1, source_target_pairs={{0,15},{1,2},{2,1},{3,4},{4,3},{5,6},{6,5},{7,8},{8,7},{9,10},{10,... | collective-permute-start | bytes 393224 | tf_op jit(solution)/shard_map/ppermute | solution.py:433
  21.5 0.0 collective-permute-start.5
  21.5 0.0 copy-done.3
  21.5 0.0 copy-done.5
  21.5 1.1 %prepare.1 = (bf16[128,256]{1,0:T(8,128)(2,1)S(1)}, f32[128,512]{1,0:T(8,128)S(1)}) custom-call(s32[4,6]{1,0:T(4,128)S(1)} %copy-done.5, bf16[4,6,32,32]{3,2,1,0:T(8,128)(2,1)S(1)} %copy-done.3, bf16[128,512]{1,0:T(8,128)(2,1)S(1)} %get-tuple-element.32.mid_ref), custom_call_target="tpu_custom_call" | custom-call | flops 18874368 | bytes 393216 | tf_op jit(solution)/shard_map/prepare/pallas_call | solution.py:280
  22.6 4.7 %collective-permute-done.6.far_mid_ref = bf16[128,512]{1,0:T(8,128)(2,1)S(1)} collective-permute-done((bf16[128,512]{1,0:T(8,128)(2,1)S(1)}, bf16[128,512]{1,0:T(8,128)(2,1)S(1)}, u32[]{:S(2)}, u32[]{:S(2)}) %collective-permute-start.6) | collective-permute-done | bytes 131104 | tf_op jit(solution)/shard_map/ppermute | solution.py:433
  27.3 0.0 collective-permute-done.5.near_mid_ref
  27.3 0.0 copy-done
  27.3 0.0 copy-done.6
  27.3 1.3 %mesh_process.1 = (bf16[128,512]{1,0:T(8,128)(2,1)}, bf16[32,512]{1,0:T(8,128)(2,1)S(1)}, bf16[32,512]{1,0:T(8,128)(2,1)S(1)}, bf16[32,512]{1,0:T(8,128)(2,1)S(1...) custom-call(f32[8,512]{1,0:T(8,128)S(1)} %get-tuple-element.31.ids_ref, ...), custom_call_target="tpu_custom_call" | custom-call | tf_op jit(solution)/shard_map/mesh_process/pallas_call | solution.py:356
  28.6 0.0 collective-permute-start.7
  28.6 0.0 collective-permute-start.8
  28.6 1.3 %collective-permute-start.9 = (bf16[32,512]{1,0:T(8,128)(2,1)S(1)}, bf16[32,512]{1,0:T(8,128)(2,1)S(1)}, u32[]{:S(2)}, u32[]{:S(2)}) collective-permute-start(bf16[32,512]{1,0:T(8,128)(2,1)S(1)} %get-tuple-element.38), channel_id=1, source_target_pairs={{0,15},{1,2},{2,1},{3,4},{4,3},{5,6},{6,5},{7,8},{8,7},{9,10},{10,... | collective-permute-start | bytes 98312 | tf_op jit(solution)/shard_map/ppermute | solution.py:433
  29.9 1.7 %collective-permute-start.10 = (bf16[32,512]{1,0:T(8,128)(2,1)S(1)}, bf16[32,512]{1,0:T(8,128)(2,1)S(1)}, u32[]{:S(2)}, u32[]{:S(2)}) collective-permute-start(bf16[32,512]{1,0:T(8,128)(2,1)S(1)} %get-tuple-element.39), channel_id=1, source_target_pairs={{0,2},{1,3},{2,0},{3,1},{4,6},{5,7},{6,4},{7,5},{8,10},{9,11},{10,... | collective-permute-start | bytes 98312 | tf_op jit(solution)/shard_map/ppermute | solution.py:433
  31.6 0.0 collective-permute-start.11
  31.6 3.6 %collective-permute-done.7.rest_1_ = bf16[32,512]{1,0:T(8,128)(2,1)S(1)} collective-permute-done((bf16[32,512]{1,0:T(8,128)(2,1)S(1)}, bf16[32,512]{1,0:T(8,128)(2,1)S(1)}, u32[]{:S(2)}, u32[]{:S(2)}) %collective-permute-start.7) | collective-permute-done | bytes 32800 | tf_op jit(solution)/shard_map/ppermute | solution.py:433
  35.2 0.0 collective-permute-done.8.rest_2_
  35.2 0.0 collective-permute-done.9.rest_3_
  35.2 0.0 collective-permute-done.10.rest_4_
  35.2 0.0 collective-permute-done.11.rest_5_
  35.2 0.0 copy-done.2
  35.2 3.8 %decode.1 = bf16[227,4096]{1,0:T(8,128)(2,1)} custom-call(bf16[227,4096]{1,0:T(8,128)(2,1)S(1)} %get-tuple-element.22.grid_ref, bf16[512,4096]{1,0:T(8,128)(2,1)S(1)} %get-tuple-element.23.lat_ref, bf16[192,4096]{1,0:T(8,128)(2,1)S(1)} %get-tuple-element.24.dsum_ref, bf16[227,512]{1,0:T(8,128)(2,1)S(1)} %bitcast.6, ...), custom_call_target="tpu_custom_call" | custom-call | tf_op jit(solution)/shard_map/decode/pallas_call | solution.py:408
Async XLA Ops:
  0.6 19.2 %copy-start.1 = (bf16[512,512]{1,0:T(8,128)(2,1)S(1)}, bf16[512,512]{1,0:T(8,128)(2,1)}, u32[]{:S(2)}) copy-start(bf16[512,512]{1,0:T(8,128)(2,1)} %refs_7_.1) | copy-start | bytes 1572868
  0.6 19.2 %copy-start.4 = (bf16[128,512]{1,0:T(8,128)(2,1)S(1)}, bf16[128,512]{1,0:T(8,128)(2,1)}, u32[]{:S(2)}) copy-start(bf16[128,512]{1,0:T(8,128)(2,1)} %refs_6_.1) | copy-start | bytes 393220
  0.7 20.9 %copy-start.3 = (bf16[4,6,32,32]{3,2,1,0:T(8,128)(2,1)S(1)}, bf16[4,6,32,32]{3,2,1,0:T(8,128)(2,1)}, u32[]{:S(2)}) copy-start(bf16[4,6,32,32]{3,2,1,0:T(8,128)(2,1)} %coef_ref.1) | copy-start | bytes 147460
  0.7 20.9 %copy-start.5 = (s32[4,6]{1,0:T(4,128)S(1)}, s32[4,6]{1,0:T(4,128)}, u32[]{:S(2)}) copy-start(s32[4,6]{1,0:T(4,128)} %adj_ref.1) | copy-start | bytes 292
  0.7 26.6 %copy-start = (bf16[512,512]{1,0:T(8,128)(2,1)S(1)}, bf16[512,512]{1,0:T(8,128)(2,1)}, u32[]{:S(2)}) copy-start(bf16[512,512]{1,0:T(8,128)(2,1)} %w_ref.1) | copy-start | bytes 1572868
  0.7 26.6 %copy-start.6 = (f32[512]{0:T(512)S(1)}, f32[512]{0:T(512)}, u32[]{:S(2)}) copy-start(f32[512]{0:T(512)} %param.22) | copy-start | bytes 6148
  7.6 27.6 %copy-start.2 = (bf16[512,227]{0,1:T(8,128)(2,1)S(1)}, bf16[512,227]{0,1:T(8,128)(2,1)}, u32[]{:S(2)}) copy-start(bf16[512,227]{0,1:T(8,128)(2,1)} %param.25) | copy-start | bytes 697348
  7.6 8.4 %collective-permute-start = (bf16[32,640]{1,0:T(8,128)(2,1)S(1)}, bf16[32,640]{1,0:T(8,128)(2,1)S(1)}, u32[]{:S(2)}, u32[]{:S(2)}) collective-permute-start(bf16[32,640]{1,0:T(8,128)(2,1)S(1)} %get-tuple-element.26), channel_id=1, source_target_pairs={{0,14},{1,15},{2,4},{3,5},{4,2},{5,3},{6,8},{7,9},{8,6},{9,7},{10,... | collective-permute-start | bytes 122888 | tf_op jit(solution)/shard_map/ppermute | solution.py:433
  13.7 4.9 %collective-permute-start.1 = (bf16[32,640]{1,0:T(8,128)(2,1)S(1)}, bf16[32,640]{1,0:T(8,128)(2,1)S(1)}, u32[]{:S(2)}, u32[]{:S(2)}) collective-permute-start(bf16[32,640]{1,0:T(8,128)(2,1)S(1)} %get-tuple-element.27), channel_id=1, source_target_pairs={{0,8},{1,9},{2,10},{3,11},{4,12},{5,13},{6,14},{7,15},{8,0},{9,1},... | collective-permute-start | bytes 122888 | tf_op jit(solution)/shard_map/ppermute | solution.py:433
  13.7 6.1 %collective-permute-start.2 = (bf16[32,640]{1,0:T(8,128)(2,1)S(1)}, bf16[32,640]{1,0:T(8,128)(2,1)S(1)}, u32[]{:S(2)}, u32[]{:S(2)}) collective-permute-start(bf16[32,640]{1,0:T(8,128)(2,1)S(1)} %get-tuple-element.28), channel_id=1, source_target_pairs={{0,15},{1,2},{2,1},{3,4},{4,3},{5,6},{6,5},{7,8},{8,7},{9,10},{10,... | collective-permute-start | bytes 122888 | tf_op jit(solution)/shard_map/ppermute | solution.py:433
  14.4 5.4 %collective-permute-start.3 = (bf16[32,640]{1,0:T(8,128)(2,1)S(1)}, bf16[32,640]{1,0:T(8,128)(2,1)S(1)}, u32[]{:S(2)}, u32[]{:S(2)}) collective-permute-start(bf16[32,640]{1,0:T(8,128)(2,1)S(1)} %get-tuple-element.29), channel_id=1, source_target_pairs={{0,2},{1,3},{2,0},{3,1},{4,6},{5,7},{6,4},{7,5},{8,10},{9,11},{10,... | collective-permute-start | bytes 122888 | tf_op jit(solution)/shard_map/ppermute | solution.py:433
  14.9 4.9 %collective-permute-start.4 = (bf16[32,640]{1,0:T(8,128)(2,1)S(1)}, bf16[32,640]{1,0:T(8,128)(2,1)S(1)}, u32[]{:S(2)}, u32[]{:S(2)}) collective-permute-start(bf16[32,640]{1,0:T(8,128)(2,1)S(1)} %get-tuple-element.30), channel_id=1, source_target_pairs={{0,1},{1,0},{2,3},{3,2},{4,5},{5,4},{6,7},{7,6},{8,9},{9,8},{10,11... | collective-permute-start | bytes 122888 | tf_op jit(solution)/shard_map/ppermute | solution.py:433
  20.1 7.2 %collective-permute-start.6 = (bf16[128,512]{1,0:T(8,128)(2,1)S(1)}, bf16[128,512]{1,0:T(8,128)(2,1)S(1)}, u32[]{:S(2)}, u32[]{:S(2)}) collective-permute-start(bf16[128,512]{1,0:T(8,128)(2,1)S(1)} %get-tuple-element.32.mid_ref), channel_id=1, source_target_pairs={{0,15},{1,2},{2,1},{3,4},{4,3},{5,6},{6,5},{7,8},{8,7},{9,10},{10,... | collective-permute-start | bytes 393224 | tf_op jit(solution)/shard_map/ppermute | solution.py:433
  21.5 5.8 %collective-permute-start.5 = (bf16[128,512]{1,0:T(8,128)(2,1)S(1)}, bf16[128,512]{1,0:T(8,128)(2,1)S(1)}, u32[]{:S(2)}, u32[]{:S(2)}) collective-permute-start(bf16[128,512]{1,0:T(8,128)(2,1)S(1)} %get-tuple-element.32.mid_ref), channel_id=1, source_target_pairs={{0,1},{1,0},{2,3},{3,2},{4,5},{5,4},{6,7},{7,6},{8,9},{9,8},{10,11... | collective-permute-start | bytes 393224 | tf_op jit(solution)/shard_map/ppermute | solution.py:433
  28.6 6.6 %collective-permute-start.7 = (bf16[32,512]{1,0:T(8,128)(2,1)S(1)}, bf16[32,512]{1,0:T(8,128)(2,1)S(1)}, u32[]{:S(2)}, u32[]{:S(2)}) collective-permute-start(bf16[32,512]{1,0:T(8,128)(2,1)S(1)} %get-tuple-element.36), channel_id=1, source_target_pairs={{0,14},{1,15},{2,4},{3,5},{4,2},{5,3},{6,8},{7,9},{8,6},{9,7},{10,... | collective-permute-start | bytes 98312 | tf_op jit(solution)/shard_map/ppermute | solution.py:433
  28.6 6.6 %collective-permute-start.8 = (bf16[32,512]{1,0:T(8,128)(2,1)S(1)}, bf16[32,512]{1,0:T(8,128)(2,1)S(1)}, u32[]{:S(2)}, u32[]{:S(2)}) collective-permute-start(bf16[32,512]{1,0:T(8,128)(2,1)S(1)} %get-tuple-element.37), channel_id=1, source_target_pairs={{0,8},{1,9},{2,10},{3,11},{4,12},{5,13},{6,14},{7,15},{8,0},{9,1},... | collective-permute-start | bytes 98312 | tf_op jit(solution)/shard_map/ppermute | solution.py:433
  28.6 6.6 %collective-permute-start.9 = (bf16[32,512]{1,0:T(8,128)(2,1)S(1)}, bf16[32,512]{1,0:T(8,128)(2,1)S(1)}, u32[]{:S(2)}, u32[]{:S(2)}) collective-permute-start(bf16[32,512]{1,0:T(8,128)(2,1)S(1)} %get-tuple-element.38), channel_id=1, source_target_pairs={{0,15},{1,2},{2,1},{3,4},{4,3},{5,6},{6,5},{7,8},{8,7},{9,10},{10,... | collective-permute-start | bytes 98312 | tf_op jit(solution)/shard_map/ppermute | solution.py:433
  29.9 5.3 %collective-permute-start.10 = (bf16[32,512]{1,0:T(8,128)(2,1)S(1)}, bf16[32,512]{1,0:T(8,128)(2,1)S(1)}, u32[]{:S(2)}, u32[]{:S(2)}) collective-permute-start(bf16[32,512]{1,0:T(8,128)(2,1)S(1)} %get-tuple-element.39), channel_id=1, source_target_pairs={{0,2},{1,3},{2,0},{3,1},{4,6},{5,7},{6,4},{7,5},{8,10},{9,11},{10,... | collective-permute-start | bytes 98312 | tf_op jit(solution)/shard_map/ppermute | solution.py:433
  31.6 3.6 %collective-permute-start.11 = (bf16[32,512]{1,0:T(8,128)(2,1)S(1)}, bf16[32,512]{1,0:T(8,128)(2,1)S(1)}, u32[]{:S(2)}, u32[]{:S(2)}) collective-permute-start(bf16[32,512]{1,0:T(8,128)(2,1)S(1)} %get-tuple-element.40), channel_id=1, source_target_pairs={{0,1},{1,0},{2,3},{3,2},{4,5},{5,4},{6,7},{7,6},{8,9},{9,8},{10,11... | collective-permute-start | bytes 98312 | tf_op jit(solution)/shard_map/ppermute | solution.py:433
